TPU v7x, 32 devices: a whole 2x2x4 slice. The times are simulated.
32 devices in a mesh: dp: 4 (over z), expert: 8 (over y, x, core).
Axes of the slice: x: 2, y: 2, z: 4, core: 2. Of those that a mesh axis runs over, the one named last changes fastest.
Arguments:
- tokens: bfloat16 [12288, 768], P(('dp', 'expert')), may hold values from -6 to 6
- segments: int32 [32, 384], P(('dp', 'expert')), may hold values from 0 to 3, never falling along the last dimension, each value on 1 to 192 neighbouring positions
- routes: int32 [12288, 1], P(('dp', 'expert')), may hold values from 0 to 7; in each aligned block of 384 rows (0 to 383, 384 to 767, ...) at most 96 rows name the same one
- norm_gains: bfloat16 [3, 768], P(None, 'expert'), may hold values from 0.099609375 to 1.8984375
- norm_shifts: bfloat16 [3, 768], P(None, 'expert'), may hold values from -1 to 1
- project_in: bfloat16 [768, 2304], P(None, 'expert'), may hold values from -0.21875 to 0.21875
- project_out: bfloat16 [768, 768], P(None, 'expert'), may hold values from -0.625 to 0.625
- dense_up: bfloat16 [768, 3072], P(None, 'expert'), may hold values from -0.21875 to 0.21875
- dense_down: bfloat16 [3072, 768], P(None, 'expert'), may hold values from -0.109375 to 0.109375
- centroids: bfloat16 [8, 768], P(None, 'expert'), may hold values from -0.15625 to 0.15625
- expert_up: bfloat16 [8, 768, 3072], P('expert', None, 'dp'), may hold values from -0.21875 to 0.21875
- expert_down: bfloat16 [8, 768, 3072], P('expert', None, 'dp'), may hold values from -0.109375 to 0.109375
- cotangent: bfloat16 [12288, 768], P(('dp', 'expert')), may hold values from -6 to 6
Outputs:
- output: bfloat16 [12288, 768], P(('dp', 'expert'))
- tokens_grad: float32 [12288, 768], P(('dp', 'expert'))
- gains_grad: float32 [3, 768], P(None, 'expert')
- shifts_grad: float32 [3, 768], P(None, 'expert')
- project_in_grad: float32 [768, 2304], P(None, 'expert')
- project_out_grad: float32 [768, 768], P(None, 'expert')
- dense_up_grad: float32 [768, 3072], P(None, 'expert')
- dense_down_grad: float32 [3072, 768], P(None, 'expert')
- centroids_grad: float32 [8, 768], P(None, 'expert')
- expert_up_grad: float32 [8, 768, 3072], P('expert', None, 'dp')
- expert_down_grad: float32 [8, 768, 3072], P('expert', None, 'dp')
Inputs may be any that keep to these rules, and one draw needn't show every extreme that they name: `routes`: among the 384 tokens of one packed row no expert is chosen more than 96 times, and in every draw some expert is chosen exactly 96 times by some row. `segments`: each packed row holds 4 documents numbered in order, never falling; a document has at most 192 tokens and one has exactly that many.
All inputs are finite; a program needn't handle non-finite values.
Results may differ from a plain program's by a relative error of at most 0.019.
Values may be sent and summed in bfloat16 or wider, within the bound.
No kernel may reach another device: no remote copies, remote signals or barrier semaphores. Data moves between devices by JAX's collectives and lax.ppermute only.
A program may use at most 192 MiB of HBM per device.

v0:
```python
import jax
import jax.numpy as jnp
from jax import lax
from jax.sharding import PartitionSpec as P

HEAD_DIM = 64


def layer_norm(rows, gain, shift):
    average = jnp.mean(rows, axis=-1, keepdims=True)
    centred = rows - average
    spread = jnp.mean(centred * centred, axis=-1, keepdims=True)
    return centred * lax.rsqrt(spread + 1e-05) * gain + shift


def smooth(values):
    return jax.nn.gelu(values, approximate=True)


def contract_rows(left, right):
    return lax.dot_general(
        left, right, (((0,), (0,)), ((), ())), preferred_element_type=jnp.float32
    )


def times_transposed(left, right):
    return lax.dot_general(
        left, right, (((1,), (1,)), ((), ())), preferred_element_type=jnp.float32
    )


def on_device(
    tokens,
    segments,
    routes,
    norm_gains,
    norm_shifts,
    project_in,
    project_out,
    dense_up,
    dense_down,
    centroids,
    expert_up,
    expert_down,
    cotangent,
):
    count_tokens, width = tokens.shape
    count_heads = width // HEAD_DIM
    scale = HEAD_DIM ** (-0.5)
    gathered = (
        lax.all_gather(norm_gains, "expert", axis=1, tiled=True),
        lax.all_gather(norm_shifts, "expert", axis=1, tiled=True),
        lax.all_gather(project_in, "expert", axis=1, tiled=True),
        lax.all_gather(project_out, "expert", axis=1, tiled=True),
        lax.all_gather(dense_up, "expert", axis=1, tiled=True),
        lax.all_gather(dense_down, "expert", axis=1, tiled=True),
        lax.all_gather(centroids, "expert", axis=1, tiled=True),
    )
    gains = gathered[0].astype(jnp.float32)
    shifts = gathered[1].astype(jnp.float32)
    whole_in, whole_out, whole_up, whole_down, whole_centroids = (
        gathered[2],
        gathered[3],
        gathered[4],
        gathered[5],
        gathered[6],
    )
    expert_whole = (
        lax.all_gather(expert_up, "dp", axis=2, tiled=True),
        lax.all_gather(expert_down, "dp", axis=2, tiled=True),
    )
    own_up = expert_whole[0][0]
    own_down = expert_whole[1][0]
    rows = tokens.astype(jnp.float32)
    documents = segments[0]
    position = jnp.arange(count_tokens)
    allowed = (documents[:, None] == documents[None, :]) & (position[:, None] >= position[None, :])

    def score(queries, keys):
        raw = jnp.einsum("qhd,khd->hqk", queries, keys, preferred_element_type=jnp.float32) * scale
        return jnp.where(allowed[None], raw, -1000000000.0)

    first_in = layer_norm(rows, gains[0], shifts[0]).astype(jnp.bfloat16)
    projected = jnp.dot(first_in, whole_in, preferred_element_type=jnp.float32).astype(jnp.bfloat16)
    projected = projected.reshape(count_tokens, 3, count_heads, HEAD_DIM)
    queries = projected[:, 0]
    keys = projected[:, 1]
    values = projected[:, 2]
    scores = score(queries, keys)
    row_max = jnp.max(scores, axis=-1, keepdims=True)
    lifted = jnp.exp(scores - row_max)
    totals = jnp.sum(lifted, axis=-1, keepdims=True)
    log_total = row_max + jnp.log(totals)
    probs_low = (lifted / totals).astype(jnp.bfloat16)
    mixed = jnp.einsum("hqk,khd->qhd", probs_low, values, preferred_element_type=jnp.float32)
    mixed = mixed.reshape(count_tokens, width).astype(jnp.bfloat16)
    after_attn = rows + jnp.dot(mixed, whole_out, preferred_element_type=jnp.float32)
    second_in = layer_norm(after_attn, gains[1], shifts[1]).astype(jnp.bfloat16)
    widened = jnp.dot(second_in, whole_up, preferred_element_type=jnp.float32)
    activated = smooth(widened).astype(jnp.bfloat16)
    hidden = after_attn + jnp.dot(activated, whole_down, preferred_element_type=jnp.float32)
    moe_in = layer_norm(hidden, gains[2], shifts[2])
    moe_low = moe_in.astype(jnp.bfloat16)
    count_experts = whole_centroids.shape[0]
    capacity = 2 * count_tokens // count_experts
    chosen_ids = routes[:, 0]
    onehot_int = (
        chosen_ids[:, None] == jnp.arange(count_experts, dtype=jnp.int32)[None, :]
    ).astype(jnp.int32)
    ranks = jnp.sum((jnp.cumsum(onehot_int, axis=0) - 1) * onehot_int, axis=1)
    slots = chosen_ids * capacity + ranks
    onehot = onehot_int.astype(jnp.float32)
    chosen = jnp.dot(onehot, whole_centroids.astype(jnp.float32), precision=lax.Precision.HIGHEST)
    gates = jax.nn.sigmoid(jnp.sum(moe_in * chosen, axis=1))
    outgoing = jnp.zeros((count_experts * capacity, width), jnp.bfloat16).at[slots].set(moe_low)
    arrived = lax.all_to_all(
        outgoing.reshape(count_experts, capacity, width),
        "expert",
        split_axis=0,
        concat_axis=0,
        tiled=True,
    ).reshape(-1, width)
    expert_pre = jnp.dot(arrived, own_up, preferred_element_type=jnp.float32)
    expert_act = smooth(expert_pre).astype(jnp.bfloat16)
    expert_result = times_transposed(expert_act, own_down).astype(jnp.bfloat16)
    returned = lax.all_to_all(
        expert_result.reshape(count_experts, capacity, width),
        "expert",
        split_axis=0,
        concat_axis=0,
        tiled=True,
    )
    combined = returned.reshape(-1, width)[slots].astype(jnp.float32)
    output = (hidden + gates[:, None] * combined).astype(jnp.bfloat16)
    incoming = cotangent.astype(jnp.float32)
    scaled = (gates[:, None] * incoming).astype(jnp.bfloat16)
    gate_grad = jnp.sum(incoming * combined, axis=1)
    logit_grad = gate_grad * gates * (1.0 - gates)
    centroids_full = lax.dot_general(
        onehot,
        logit_grad[:, None] * moe_in,
        (((0,), (0,)), ((), ())),
        precision=lax.Precision.HIGHEST,
        preferred_element_type=jnp.float32,
    )
    backward_out = jnp.zeros((count_experts * capacity, width), jnp.bfloat16).at[slots].set(scaled)
    grad_arrived = lax.all_to_all(
        backward_out.reshape(count_experts, capacity, width),
        "expert",
        split_axis=0,
        concat_axis=0,
        tiled=True,
    ).reshape(-1, width)
    act_grad = jnp.dot(grad_arrived, own_down, preferred_element_type=jnp.float32)
    smooth_pull = jax.vjp(smooth, expert_pre)[1]
    pre_grad = smooth_pull(act_grad)[0].astype(jnp.bfloat16)
    up_grad_own = contract_rows(arrived, pre_grad)
    down_grad_own = contract_rows(grad_arrived, expert_act)
    rows_grad = times_transposed(pre_grad, own_up).astype(jnp.bfloat16)
    expert_sums = (
        lax.psum_scatter(
            up_grad_own[None].astype(jnp.bfloat16), "dp", scatter_dimension=2, tiled=True
        ).astype(jnp.float32),
        lax.psum_scatter(
            down_grad_own[None].astype(jnp.bfloat16), "dp", scatter_dimension=2, tiled=True
        ).astype(jnp.float32),
    )
    back_rows = lax.all_to_all(
        rows_grad.reshape(count_experts, capacity, width),
        "expert",
        split_axis=0,
        concat_axis=0,
        tiled=True,
    )
    moe_grad = (
        back_rows.reshape(-1, width)[slots].astype(jnp.float32) + logit_grad[:, None] * chosen
    )
    third_pull = jax.vjp(layer_norm, hidden, gains[2], shifts[2])[1]
    hidden_part, third_gain, third_shift = third_pull(moe_grad)
    hidden_grad = incoming + hidden_part
    down_in = hidden_grad.astype(jnp.bfloat16)
    dense_down_full = contract_rows(activated, down_in)
    activated_grad = times_transposed(down_in, whole_down)
    widened_pull = jax.vjp(smooth, widened)[1]
    widened_grad = widened_pull(activated_grad)[0].astype(jnp.bfloat16)
    dense_up_full = contract_rows(second_in, widened_grad)
    second_grad = times_transposed(widened_grad, whole_up)
    second_pull = jax.vjp(layer_norm, after_attn, gains[1], shifts[1])[1]
    after_part, second_gain, second_shift = second_pull(second_grad)
    after_grad = hidden_grad + after_part
    attn_grad = after_grad.astype(jnp.bfloat16)
    project_out_full = contract_rows(mixed, attn_grad)
    mixed_grad = (
        times_transposed(attn_grad, whole_out)
        .astype(jnp.bfloat16)
        .reshape(count_tokens, count_heads, HEAD_DIM)
    )
    probs = jnp.exp(score(queries, keys) - log_total)
    values_grad = jnp.einsum(
        "hqk,qhd->khd", probs.astype(jnp.bfloat16), mixed_grad, preferred_element_type=jnp.float32
    )
    probs_grad = jnp.einsum("qhd,khd->hqk", mixed_grad, values, preferred_element_type=jnp.float32)
    scores_grad = (
        probs * (probs_grad - jnp.sum(probs * probs_grad, axis=-1, keepdims=True))
    ).astype(jnp.bfloat16)
    queries_grad = (
        jnp.einsum("hqk,khd->qhd", scores_grad, keys, preferred_element_type=jnp.float32) * scale
    )
    keys_grad = (
        jnp.einsum("hqk,qhd->khd", scores_grad, queries, preferred_element_type=jnp.float32) * scale
    )
    projected_grad = (
        jnp.stack([queries_grad, keys_grad, values_grad], axis=1)
        .reshape(count_tokens, 3 * width)
        .astype(jnp.bfloat16)
    )
    project_in_full = contract_rows(first_in, projected_grad)
    first_grad = times_transposed(projected_grad, whole_in)
    first_pull = jax.vjp(layer_norm, rows, gains[0], shifts[0])[1]
    rows_part, first_gain, first_shift = first_pull(first_grad)
    tokens_grad = after_grad + rows_part
    gains_full = jnp.stack([first_gain, second_gain, third_gain], axis=0)
    shifts_full = jnp.stack([first_shift, second_shift, third_shift], axis=0)
    pieces = (
        lax.psum_scatter(
            gains_full.astype(jnp.bfloat16), "expert", scatter_dimension=1, tiled=True
        ).astype(jnp.float32),
        lax.psum_scatter(
            shifts_full.astype(jnp.bfloat16), "expert", scatter_dimension=1, tiled=True
        ).astype(jnp.float32),
        lax.psum_scatter(
            project_in_full.astype(jnp.bfloat16), "expert", scatter_dimension=1, tiled=True
        ).astype(jnp.float32),
        lax.psum_scatter(
            project_out_full.astype(jnp.bfloat16), "expert", scatter_dimension=1, tiled=True
        ).astype(jnp.float32),
        lax.psum_scatter(
            dense_up_full.astype(jnp.bfloat16), "expert", scatter_dimension=1, tiled=True
        ).astype(jnp.float32),
        lax.psum_scatter(
            dense_down_full.astype(jnp.bfloat16), "expert", scatter_dimension=1, tiled=True
        ).astype(jnp.float32),
        lax.psum_scatter(
            centroids_full.astype(jnp.bfloat16), "expert", scatter_dimension=1, tiled=True
        ).astype(jnp.float32),
    )
    pieces = (
        lax.psum(pieces[0].astype(jnp.bfloat16), "dp").astype(jnp.float32),
        lax.psum(pieces[1].astype(jnp.bfloat16), "dp").astype(jnp.float32),
        lax.psum(pieces[2].astype(jnp.bfloat16), "dp").astype(jnp.float32),
        lax.psum(pieces[3].astype(jnp.bfloat16), "dp").astype(jnp.float32),
        lax.psum(pieces[4].astype(jnp.bfloat16), "dp").astype(jnp.float32),
        lax.psum(pieces[5].astype(jnp.bfloat16), "dp").astype(jnp.float32),
        lax.psum(pieces[6].astype(jnp.bfloat16), "dp").astype(jnp.float32),
    )
    return (
        output,
        tokens_grad,
        pieces[0],
        pieces[1],
        pieces[2],
        pieces[3],
        pieces[4],
        pieces[5],
        pieces[6],
        expert_sums[0],
        expert_sums[1],
    )


def solution(mesh):
    return jax.shard_map(
        on_device,
        mesh=mesh,
        in_specs=(
            P(("dp", "expert"), None),
            P(("dp", "expert"), None),
            P(("dp", "expert"), None),
            P(None, "expert"),
            P(None, "expert"),
            P(None, "expert"),
            P(None, "expert"),
            P(None, "expert"),
            P(None, "expert"),
            P(None, "expert"),
            P("expert", None, "dp"),
            P("expert", None, "dp"),
            P(("dp", "expert"), None),
        ),
        out_specs=(
            P(("dp", "expert"), None),
            P(("dp", "expert"), None),
            P(None, "expert"),
            P(None, "expert"),
            P(None, "expert"),
            P(None, "expert"),
            P(None, "expert"),
            P(None, "expert"),
            P(None, "expert"),
            P("expert", None, "dp"),
            P("expert", None, "dp"),
        ),
        check_vma=False,
    )
```

profile of v0, /device:TPU:0, one launch (start us, length us, event | category | flops | bytes accessed | tf_op | source)
XLA Modules:
  0.0 1052.3 jit_solution(939049423359914430)
XLA Ops:
  12.3 10.3 all-gather
  22.8 8.9 all-gather.1
  34.3 12.3 %all-gather.10.cloned.1.call-done = bf16[768,2304]{0,1:T(8,128)(2,1)} async-done(((bf16[768,288]{0,1:T(8,128)(2,1)}), bf16[768,2304]{0,1:T(8,128)(2,1)}) %all-gather.10.cloned.1.call-update) | async-done | bytes 3538960 | tf_op jit(solution)/shard_map/all_gather | solution.py:53
  46.6 4.9 convolution_convert_fusion.5
  51.5 2.8 copy.53
  56.6 1.8 copy-done
  58.5 2.2 fusion.46
  60.7 11.9 %all-gather.12.cloned.1.call-done = bf16[768,768]{0,1:T(8,128)(2,1)} async-done(((bf16[768,96]{0,1:T(8,128)(2,1)}), bf16[768,768]{0,1:T(8,128)(2,1)}) %all-gather.12.cloned.1.call-update) | async-done | bytes 1179664 | tf_op jit(solution)/shard_map/all_gather | solution.py:54
  72.6 2.2 fusion.113
  75.1 39.1 %all-gather.14.cloned.1.call-done = bf16[768,3072]{1,0:T(8,128)(2,1)} async-done(((bf16[768,384]{1,0:T(8,128)(2,1)}), bf16[768,3072]{1,0:T(8,128)(2,1)}) %all-gather.14.cloned.1.call-update) | async-done | bytes 4718608 | tf_op jit(solution)/shard_map/all_gather | solution.py:55
  114.2 6.6 fusion.107
  120.9 34.1 %all-gather.16.cloned.1.call-done = bf16[3072,768]{0,1:T(8,128)(2,1)} async-done(((bf16[3072,96]{0,1:T(8,128)(2,1)}), bf16[3072,768]{0,1:T(8,128)(2,1)}) %all-gather.16.cloned.1.call-update) | async-done | bytes 4718608 | tf_op jit(solution)/shard_map/all_gather | solution.py:56
  154.9 6.8 fusion.114
  162.0 3.7 scatter_custom_fusion
  165.7 3.6 all-to-all-start
  169.2 76.6 %all-gather.18.cloned.1.call-done = bf16[1,768,3072]{2,1,0:T(8,128)(2,1)} async-done(((bf16[1,768,768]{2,1,0:T(8,128)(2,1)}), bf16[1,768,3072]{2,1,0:T(8,128)(2,1)}) %all-gather.18.cloned.1.call-update) | async-done | bytes 4718608 | tf_op jit(solution)/shard_map/all_gather | solution.py:69
  245.8 8.9 fusion.22
  254.7 80.3 %all-gather.20.cloned.1.call-done = bf16[1,768,3072]{2,1,0:T(8,128)(2,1)} async-done(((bf16[1,768,768]{2,1,0:T(8,128)(2,1)}), bf16[1,768,3072]{2,1,0:T(8,128)(2,1)}) %all-gather.20.cloned.1.call-update) | async-done | bytes 4718608 | tf_op jit(solution)/shard_map/all_gather | solution.py:70
  335.1 11.6 %fusion.39 = bf16[768,768]{1,0:T(8,128)(2,1)} fusion(bf16[1,768,3072]{2,1,0:T(8,128)(2,1)} %all-gather.20.cloned.1.call-done, f32[768,3072]{1,0:T(8,128)} %fusion.22), kind=kOutput, calls=%fused_computation.66 | convolution fusion | flops 3645702144 | bytes 15335424 | tf_op jit(solution)/shard_map/dot_general | solution.py:27
  346.7 3.7 all-to-all-start.1
  350.4 19.8 %all-gather.2 = bf16[8,96,8]{1,2,0:T(8,128)(2,1)S(1)} all-gather(bf16[1,96,8]{1,2,0:T(8,128)(2,1)} %bitcast.160), channel_id=1, replica_groups=mesh['dp'=4,'expert'=8] {'expert'}, dimensions={0}, use_global_device_ids=true | all-gather | bytes 13824 | tf_op jit(solution)/shard_map/all_gather | solution.py:57
  370.9 1.4 reshape.300
  373.5 3.1 multiply_reduce_fusion.5
  376.7 3.2 gather_fusion
  379.8 1.5 fusion.63
  382.6 3.0 scatter_custom_fusion.1
  385.6 19.6 %all_to_all.20 = bf16[8,96,768]{2,1,0:T(8,128)(2,1)S(1)} all-to-all(bf16[8,96,768]{2,1,0:T(8,128)(2,1)S(1)} %bitcast.138), channel_id=1, replica_groups=mesh['dp'=4,'expert'=8] {'expert'}, dimensions={0} | all-to-all | bytes 2359296 | tf_op jit(solution)/shard_map/all_to_all | solution.py:147
  405.2 13.3 %fusion.6 = bf16[768,3072]{1,0:T(8,128)(2,1)S(1)} fusion(f32[768,3072]{1,0:T(8,128)} %fusion.22, bf16[768,768]{1,0:T(8,128)(2,1)S(1)} %bitcast.145, bf16[1,768,3072]{2,1,0:T(8,128)(2,1)} %all-gather.20.cloned.1.call-done), kind=kOutput, calls=%fused_computation.12 | convolution fusion | flops 3671064576 | bytes 20054016 | tf_op jit(solution)/shard_map/dot_general | solution.py:154
  418.5 3.9 fusion.36
  422.4 19.4 %all_to_all.21 = bf16[8,96,768]{2,1,0:T(8,128)(2,1)S(1)} all-to-all(bf16[8,96,768]{2,1,0:T(8,128)(2,1)S(1)} %bitcast.148), channel_id=1, replica_groups=mesh['dp'=4,'expert'=8] {'expert'}, dimensions={0} | all-to-all | bytes 2359296 | tf_op jit(solution)/shard_map/all_to_all | solution.py:168
  441.8 2.8 gather_fusion.1
  444.6 2.8 multiply_reduce_fusion.1
  447.5 1.6 fusion.111
  450.7 7.9 fusion.15
  458.7 1.4 copy-done.65
  460.1 4.8 convolution_convert_fusion.4
  464.8 6.7 copy.68
  473.0 6.5 multiply_reduce_fusion.2
  483.0 3.1 convolution_convert_fusion.6
  486.5 7.5 multiply_reduce_fusion
  494.0 4.4 multiply_convert_fusion.1
  498.5 2.4 fusion.53
  500.9 1.8 fusion.54
  505.7 4.0 convolution_convert_fusion
  510.7 7.7 convolution_convert_fusion.3
  521.3 4.3 fusion.109
  528.3 8.5 fusion.25
  536.9 8.8 fusion.24
  545.8 2.2 copy.69
  547.9 15.2 %reduce-scatter.20.cloned.1.call-done = bf16[768,96]{0,1:T(8,128)(2,1)} async-done(((bf16[768,768]{0,1:T(8,128)(2,1)}), bf16[768,96]{0,1:T(8,128)(2,1)}) %reduce-scatter.20.cloned.1.call-update) | async-done | bytes 147472 | tf_op jit(solution)/shard_map/reduce_scatter | solution.py:234
  563.1 51.6 %reduce-scatter.18.cloned.1.call-done = bf16[768,288]{0,1:T(8,128)(2,1)} async-done(((bf16[768,2304]{0,1:T(8,128)(2,1)}), bf16[768,288]{0,1:T(8,128)(2,1)}) %reduce-scatter.18.cloned.1.call-update) | async-done | bytes 442384 | tf_op jit(solution)/shard_map/reduce_scatter | solution.py:231
  614.7 57.2 %reduce-scatter.22.cloned.1.call-done = bf16[3072,96]{0,1:T(8,128)(2,1)} async-done(((bf16[3072,768]{0,1:T(8,128)(2,1)}), bf16[3072,96]{0,1:T(8,128)(2,1)}) %reduce-scatter.22.cloned.1.call-update) | async-done | bytes 589840 | tf_op jit(solution)/shard_map/reduce_scatter | solution.py:240
  671.9 37.4 %reduce-scatter.34.cloned.1.call-done = bf16[96,8]{1,0:T(8,128)(2,1)} async-done(((bf16[768,8]{1,0:T(8,128)(2,1)}), bf16[96,8]{1,0:T(8,128)(2,1)}) %reduce-scatter.34.cloned.1.call-update) | async-done | bytes 1552
  710.1 1.5 add_add_fusion.3
  711.6 34.7 %reduce-scatter.28.cloned.1.call-done = bf16[96,3]{1,0:T(8,128)(2,1)} async-done(((bf16[768,3]{1,0:T(8,128)(2,1)}), bf16[96,3]{1,0:T(8,128)(2,1)}) %reduce-scatter.28.cloned.1.call-update) | async-done | bytes 592
  747.1 36.6 %reduce-scatter.30.cloned.1.call-done = bf16[96,3]{1,0:T(8,128)(2,1)} async-done(((bf16[768,3]{1,0:T(8,128)(2,1)}), bf16[96,3]{1,0:T(8,128)(2,1)}) %reduce-scatter.30.cloned.1.call-update) | async-done | bytes 592
  784.6 11.9 %all-reduce = (bf16[3,96]{1,0:T(4,128)(2,1)S(1)}, bf16[3,96]{1,0:T(4,128)(2,1)S(1)}, bf16[8,96]{1,0:T(8,128)(2,1)S(1)}) all-reduce(bf16[3,96]{1,0:T(4,128)(2,1)S(1)} %copy.65, bf16[3,96]{1,0:T(4,128)(2,1)S(1)} %copy.67, bf16[8,96]{1,0:T(8,128)(2,1)S(1)} %copy.71), channel_id=1, replica_groups=mesh['dp'=4,'expert'=8] {'dp'}, use_global_device_ids=true, to_apply=%region_26.27 | all-reduce | flops 1344 | bytes 5376 | tf_op jit(solution)/shard_map/psum | solution.py:248
  798.2 73.1 %reduce-scatter.26.cloned.1.call-done = bf16[1,768,768]{2,1,0:T(8,128)(2,1)} async-done(((bf16[1,768,3072]{2,1,0:T(8,128)(2,1)}), bf16[1,768,768]{2,1,0:T(8,128)(2,1)}) %reduce-scatter.26.cloned.1.call-update) | async-done | bytes 1179664 | tf_op jit(solution)/shard_map/reduce_scatter | solution.py:164
  871.3 2.8 convert_element_type.214
  874.1 85.0 %reduce-scatter.24.cloned.1.call-done = bf16[1,768,768]{2,1,0:T(8,128)(2,1)} async-done(((bf16[1,768,3072]{2,1,0:T(8,128)(2,1)}), bf16[1,768,768]{2,1,0:T(8,128)(2,1)}) %reduce-scatter.24.cloned.1.call-update) | async-done | bytes 1179664 | tf_op jit(solution)/shard_map/reduce_scatter | solution.py:161
  959.1 2.8 convert_element_type.211
  962.0 77.4 %all-reduce.4.cloned.1.call-done = (bf16[768,288]{0,1:T(8,128)(2,1)}, bf16[768,96]{0,1:T(8,128)(2,1)}, bf16[768,384]{1,0:T(8,128)(2,1)}, bf16[3072,96]{0,1:T(8,128)(2,1)}) async-done(((bf16[768,288]{0,1:T(8,128)(2,1)}, bf16[768,96]{0,1:T(8,128)(2,1)}, bf16[768,384]{1,0:T(8,128)(2,1)}, bf16[3072,96]{0,1:T(8,128)(2,1)}), (bf16[768,288]{0,1:T(8,128)(2,1)}, bf16[768,96]{0,1:T(8,128)(2,1)}, ...) | async-done | bytes 1769488 | tf_op jit(solution)/shard_map/psum | solution.py:250
  1039.4 1.7 convert_element_type.202
  1041.1 2.0 convert_element_type.200
  (241 shorter events, 36.5 us)
Async XLA Ops:
  7.2 39.4 %all-gather.10.cloned.1.call-start = ((), (), s32[]{:S(2)}) async-start(), calls=%async_computation.13 | async-start | bytes 3981312 | tf_op jit(solution)/shard_map/all_gather | solution.py:53
  7.9 64.7 %all-gather.12.cloned.1.call-start = ((), (), s32[]{:S(2)}) async-start(), calls=%async_computation.14 | async-start | bytes 1327104 | tf_op jit(solution)/shard_map/all_gather | solution.py:54
  8.7 2.5 copy-start.62
  8.7 2.6 copy-start.1
  8.7 105.5 %all-gather.14.cloned.1.call-start = ((), (), s32[]{:S(2)}) async-start(), calls=%async_computation.15 | async-start | bytes 5308416 | tf_op jit(solution)/shard_map/all_gather | solution.py:55
  9.4 145.5 %all-gather.16.cloned.1.call-start = ((), (), s32[]{:S(2)}) async-start(), calls=%async_computation.16 | async-start | bytes 5308416 | tf_op jit(solution)/shard_map/all_gather | solution.py:56
  10.0 12.7 %copy-start.64 = (bf16[3,96]{1,0:T(4,128)(2,1)S(1)}, bf16[3,96]{1,0:T(4,128)(2,1)}, u32[]{:S(2)}) copy-start(bf16[3,96]{1,0:T(4,128)(2,1)} %param.17) | copy-start | bytes 1732
  10.0 235.8 %all-gather.18.cloned.1.call-start = ((), (), s32[]{:S(2)}) async-start(), calls=%async_computation.17 | async-start | bytes 5898240 | tf_op jit(solution)/shard_map/all_gather | solution.py:69
  10.6 324.5 %all-gather.20.cloned.1.call-start = ((), (), s32[]{:S(2)}) async-start(), calls=%async_computation.18 | async-start | bytes 5898240 | tf_op jit(solution)/shard_map/all_gather | solution.py:70
  11.2 35.4 %copy-start.25 = (s32[384]{0:T(512)}, s32[384]{0:T(512)S(1)}, u32[]{:S(2)}) copy-start(s32[384]{0:T(512)S(1)} %reduce.7) | copy-start | bytes 4612
  11.4 40.1 %copy-start.27 = (f32[384]{0:T(512)}, f32[384]{0:T(512)S(1)}, u32[]{:S(2)}) copy-start(f32[384]{0:T(512)S(1)} %broadcast_multiply_fusion.2) | copy-start | bytes 4612
  11.8 39.7 %copy-start.40 = (f32[384]{0:T(512)}, f32[384]{0:T(512)S(1)}, u32[]{:S(2)}) copy-start(f32[384]{0:T(512)S(1)} %fusion.100) | copy-start | bytes 4612
  34.3 12.3 %copy-start.56 = (f32[768]{0:T(1024)}, f32[768]{0:T(1024)S(1)}, u32[]{:S(2)}) copy-start(f32[768]{0:T(1024)S(1)} %get-tuple-element.26) | copy-start | bytes 9220
  55.6 2.8 copy-start
  55.6 2.9 copy-start.21
  72.6 41.7 %copy-start.47 = (f32[768]{0:T(1024)S(1)}, f32[768]{0:T(1024)}, u32[]{:S(2)}) copy-start(f32[768]{0:T(1024)} %get-tuple-element.54) | copy-start | bytes 9220
  72.6 41.7 %copy-start.58 = (f32[768]{0:T(1024)S(1)}, f32[768]{0:T(1024)}, u32[]{:S(2)}) copy-start(f32[768]{0:T(1024)} %get-tuple-element.25) | copy-start | bytes 9220
  74.8 46.0 %copy-start.30 = (f32[384]{0:T(512)}, f32[384]{0:T(512)S(1)}, u32[]{:S(2)}) copy-start(f32[384]{0:T(512)S(1)} %broadcast_multiply_fusion.1) | copy-start | bytes 4612
  75.1 45.8 %copy-start.36 = (f32[384]{0:T(512)}, f32[384]{0:T(512)S(1)}, u32[]{:S(2)}) copy-start(f32[384]{0:T(512)S(1)} %multiply_reduce_fusion.7) | copy-start | bytes 4612
  75.1 39.1 %copy-start.50 = (f32[384]{0:T(512)}, f32[384]{0:T(512)S(1)}, u32[]{:S(2)}) copy-start(f32[384]{0:T(512)S(1)} %fusion.101) | copy-start | bytes 4612
  120.9 41.1 %copy-start.23 = (f32[768]{0:T(1024)S(1)}, f32[768]{0:T(1024)}, u32[]{:S(2)}) copy-start(f32[768]{0:T(1024)} %get-tuple-element.24) | copy-start | bytes 9220
  162.0 3.7 copy-start.38
  165.7 80.1 %all-to-all-start = ((bf16[8,96,768]{2,1,0:T(8,128)(2,1)}), bf16[8,96,768]{2,1,0:T(8,128)(2,1)S(1)}, u32[]{:S(2)}, u32[]{:S(2)}) async-start(bf16[8,96,768]{2,1,0:T(8,128)(2,1)} %bitcast.16), calls=%async_computation | async-start | bytes 2359296 | tf_op jit(solution)/shard_map/all_to_all | solution.py:116
  245.8 8.9 copy-start.13
  346.7 29.9 %all-to-all-start.1 = ((bf16[8,96,768]{2,1,0:T(8,128)(2,1)}), bf16[8,96,768]{2,1,0:T(8,128)(2,1)S(1)}, u32[]{:S(2)}, u32[]{:S(2)}) async-start(bf16[8,96,768]{2,1,0:T(8,128)(2,1)} %bitcast.147), calls=%async_computation.1 | async-start | bytes 2359296 | tf_op jit(solution)/shard_map/all_to_all | solution.py:126
  350.4 195.4 %reduce-scatter.32.cloned.1.call-start = ((), (), s32[]{:S(2)}) async-start(), calls=%async_computation.26 | async-start | bytes 5308416
  385.6 32.9 %slice-start.2 = ((s8[4718592]{0:T(1024)(128)(4,1)}), s8[4194304]{0:T(1024)(128)(4,1)S(1)}, s32[]{:S(2)}) async-start(s8[4718592]{0:T(1024)(128)(4,1)} %bitcast.163), calls=%async_computation.31 | async-start | bytes 8388608
  405.2 13.3 %copy-start.14 = (bf16[8,96,768]{2,1,0:T(8,128)(2,1)}, bf16[8,96,768]{2,1,0:T(8,128)(2,1)S(1)}, u32[]{:S(2)}) copy-start(bf16[8,96,768]{2,1,0:T(8,128)(2,1)S(1)} %all_to_all.20) | copy-start | bytes 3538948
  405.2 13.3 %slice-start.3 = ((s8[4718592]{0:T(1024)(128)(4,1)}), s8[524288]{0:T(1024)(128)(4,1)S(1)}, s32[]{:S(2)}) async-start(s8[4718592]{0:T(1024)(128)(4,1)} %bitcast.163), calls=%async_computation.32 | async-start | bytes 1048576
  418.5 3.9 copy-start.66
  444.5 2.8 copy-start.39
  444.5 2.9 copy-start.4
  444.6 2.9 copy-start.9
  444.6 2.9 copy-start.10
  444.6 2.9 copy-start.33
  444.6 2.9 copy-start.45
  450.7 9.4 copy-start.31
  450.7 9.4 copy-start.48
  450.7 9.4 copy-start.51
  450.7 9.4 copy-start.59
  471.6 91.6 %reduce-scatter.20.cloned.1.call-start = ((), (), s32[]{:S(2)}) async-start(), calls=%async_computation.20 | async-start | bytes 1327104 | tf_op jit(solution)/shard_map/reduce_scatter | solution.py:234
  473.0 6.5 copy-start.37
  473.0 6.5 copy-start.32
  473.0 6.5 copy-start.49
  473.0 6.5 copy-start.52
  483.0 3.4 copy-start.7
  483.0 3.4 copy-start.19
  486.2 128.6 %reduce-scatter.18.cloned.1.call-start = ((), (), s32[]{:S(2)}) async-start(), calls=%async_computation.19 | async-start | bytes 3981312 | tf_op jit(solution)/shard_map/reduce_scatter | solution.py:231
  486.4 7.6 slice-start
  486.5 7.6 slice-start.1
  509.7 162.3 %reduce-scatter.22.cloned.1.call-start = ((), (), s32[]{:S(2)}) async-start(), calls=%async_computation.21 | async-start | bytes 5308416 | tf_op jit(solution)/shard_map/reduce_scatter | solution.py:240
  518.5 2.8 copy-start.54
  518.5 2.8 copy-start.61
  518.5 190.9 %reduce-scatter.34.cloned.1.call-start = ((), (), s32[]{:S(2)}) async-start(), calls=%async_computation.27 | async-start | bytes 221184
  520.9 225.4 %reduce-scatter.28.cloned.1.call-start = ((), (), s32[]{:S(2)}) async-start(), calls=%async_computation.24 | async-start | bytes 221184
  521.3 4.4 copy-start.35
  521.3 4.4 copy-start.29
  521.3 4.4 copy-start.42
  527.3 256.5 %reduce-scatter.30.cloned.1.call-start = ((), (), s32[]{:S(2)}) async-start(), calls=%async_computation.25 | async-start | bytes 221184
  528.2 343.1 %reduce-scatter.26.cloned.1.call-start = ((), (), s32[]{:S(2)}) async-start(), calls=%async_computation.23 | async-start | bytes 5898240 | tf_op jit(solution)/shard_map/reduce_scatter | solution.py:164
  536.8 422.3 %reduce-scatter.24.cloned.1.call-start = ((), (), s32[]{:S(2)}) async-start(), calls=%async_computation.22 | async-start | bytes 5898240 | tf_op jit(solution)/shard_map/reduce_scatter | solution.py:161
  545.7 493.7 %all-reduce.4.cloned.1.call-start = ((), (), s32[]{:S(2)}) async-start(), calls=%async_computation.28 | async-start | bytes 3538944 | tf_op jit(solution)/shard_map/psum | solution.py:250
  1039.4 3.7 copy-start.16
  1039.4 4.8 copy-start.15
  (25 other events, 34.0 us)
Sparse Core Ops, SparseCore 0:
  9.9 36.6 all-gather.9
  48.5 24.0 all-gather.11
  74.5 39.7 all-gather.13
  116.0 38.9 all-gather.15
  156.3 89.4 all-gather.17
  247.2 87.8 all-gather.19
  471.7 50.4 reduce-scatter.31
  526.3 36.7 reduce-scatter.19
  566.6 48.0 reduce-scatter.17
  618.0 53.8 reduce-scatter.21
  675.8 33.4 reduce-scatter.33
  712.8 33.4 reduce-scatter.27
  750.2 33.5 reduce-scatter.29
  785.9 85.2 reduce-scatter.25
  873.4 85.6 reduce-scatter.23
  962.2 77.1 all-reduce.3
where the time goes:
time: 1060 us; the launch traced here: 1050 us
  waiting for transfers between devices  726 us (68%)
  matrix products  135 us (13%)
  blocking collectives  89.8 us (8%)
  other arithmetic  41.4 us (4%)
  local copies, waits for them, and re-layouts  35.9 us (3%)
  between operations  15.3 us (1%)
    unnamed x20, waiting for transfers between devices  113 us
    reduce_scatter x1, waiting for transfers between devices, on_device(): lax.psum_scatter(up_grad_own[None].astype(jnp.bfloat16), 'dp', scatter_di...  85 us
    all_gather x1, waiting for transfers between devices, on_device(): lax.all_gather(expert_down, 'dp', axis=2, tiled=True)  80.3 us
    psum x1, waiting for transfers between devices, on_device(): lax.psum(pieces[2].astype(jnp.bfloat16), 'dp').astype(jnp.float32)  77.4 us
    all_gather x1, waiting for transfers between devices, on_device(): lax.all_gather(expert_up, 'dp', axis=2, tiled=True)  76.6 us
    reduce_scatter x1, waiting for transfers between devices, on_device(): lax.psum_scatter(down_grad_own[None].astype(jnp.bfloat16), 'dp', scatter_...  73.1 us
    reduce_scatter x1, waiting for transfers between devices, on_device(): lax.psum_scatter(dense_down_full.astype(jnp.bfloat16), 'expert', scatter_...  57.2 us
    reduce_scatter x1, waiting for transfers between devices, on_device(): lax.psum_scatter(project_in_full.astype(jnp.bfloat16), 'expert', scatter_...  51.6 us
  transfers between devices with their start and end apart: 18, of which 15 were waited for; matrix products, arithmetic and copies ran while one was open for 13% of the time, Pallas kernels for 0%

commit v1 on v0

v1 whole, which is shorter than its diff:
```python
import functools

import jax
import jax.numpy as jnp
from jax import lax
from jax.experimental import pallas as pl
from jax.experimental.pallas import tpu as pltpu
from jax.sharding import PartitionSpec as P

HEAD_DIM = 64
EXTRA = 128
BF = jnp.bfloat16
F32 = jnp.float32
I32 = jnp.int32
ROOT = 0.7978845608028654
COST = dict(
    prepare=3, attend=16, widen=9, dispatch=10, expert_rows=4, expert=20, gate_back=10, widen_back=12, fold=1,
    second_back=14, attend_back=5, fold_again=1, project_back=2, tokens_back=2, fold_last=1, joined=1,
    combine=1, finish=1, settle=1,
)
WIDE = ("attend", "widen", "dispatch", "expert", "widen_back")
VMEM_LIMIT = 60 * 1024 * 1024


def mm(left, right):
    return lax.dot_general(left, right, (((1,), (0,)), ((), ())), preferred_element_type=F32)


def mm_t(left, right):
    return lax.dot_general(left, right, (((1,), (1,)), ((), ())), preferred_element_type=F32)


def t_mm(left, right):
    return lax.dot_general(left, right, (((0,), (0,)), ((), ())), preferred_element_type=F32)


def normalize(rows):
    share = 1.0 / rows.shape[-1]
    centred = rows - jnp.sum(rows, axis=-1, keepdims=True) * share
    spread = jnp.sum(centred * centred, axis=-1, keepdims=True) * share
    inverse = lax.rsqrt(spread + 1e-05)
    return centred * inverse, inverse


def normalize_back(grad, normal, inverse, gain):
    share = 1.0 / grad.shape[-1]
    scaled = grad * gain
    first = jnp.sum(scaled, axis=-1, keepdims=True) * share
    second = jnp.sum(scaled * normal, axis=-1, keepdims=True) * share
    rows = inverse * (scaled - first - normal * second)
    return rows, jnp.sum(grad * normal, axis=0, keepdims=True), jnp.sum(grad, axis=0, keepdims=True)


def smooth_and_slope(v):
    square = v * v
    bend = jnp.tanh(v * (ROOT + ROOT * 0.044715 * square))
    half = 0.5 + 0.5 * bend
    slope = half + 0.5 * v * (1.0 - bend * bend) * (ROOT + 3.0 * ROOT * 0.044715 * square)
    return v * half, slope


def split3(v):
    hi = v.astype(BF)
    rest = v - hi.astype(F32)
    mid = rest.astype(BF)
    return hi, mid, (rest - mid.astype(F32)).astype(BF)


def scalar_columns(v):
    hi, mid, low = split3(v)
    lane = lax.broadcasted_iota(I32, (v.shape[0], EXTRA), 1)
    out = jnp.where(lane == 0, hi.astype(F32), 0.0)
    out = jnp.where(lane == 1, mid.astype(F32), out)
    return jnp.where(lane == 2, low.astype(F32), out).astype(BF)


def columns_scalar(columns):
    return jnp.sum(columns.astype(F32), axis=-1, keepdims=True)


def bias_of(by_row, by_column):
    count = by_row.shape[0]
    row = lax.broadcasted_iota(I32, (count, count), 0)
    column = lax.broadcasted_iota(I32, (count, count), 1)
    allowed = (by_row == by_column) & (row >= column)
    return jnp.where(allowed, 0.0, -1000000000.0)


def half_masks():
    lane = lax.broadcasted_iota(I32, (1, 2 * HEAD_DIM), 1)
    first = jnp.where(lane < HEAD_DIM, 1.0, 0.0)
    return first.astype(BF), (1.0 - first).astype(BF)


BEFORE = []


def smallest(outs):
    return min(outs, key=lambda a: a.size * a.dtype.itemsize)


def call(kernel, outs, args, spaces, scratch, name, flops, moved, after=(), results=None):
    where = {"v": pltpu.VMEM, "a": pl.ANY}
    after = list(after) + BEFORE
    read, waited = len(args), len(after)
    args, spaces = list(args) + list(after), spaces + "a" * waited

    def body(*refs):
        kernel(*refs[:read], *refs[read + waited :])

    got = pl.pallas_call(
        body,
        out_shape=outs,
        in_specs=[pl.BlockSpec(memory_space=where[s]) for s in spaces],
        out_specs=[pl.BlockSpec(memory_space=where[s]) for s in results or "v" * len(outs)],
        scratch_shapes=scratch,
        compiler_params=pltpu.CompilerParams(vmem_limit_bytes=VMEM_LIMIT if name in WIDE else VMEM_LIMIT // 2),
        cost_estimate=pl.CostEstimate(flops=COST[name] * 1150000000, bytes_accessed=1000, transcendentals=0),
        name=name,
    )(*args)
    BEFORE[:] = [smallest(got)]
    return got


class Weight:
    def __init__(self, arrays, copies, shape):
        self.arrays, self.copies, self.shape = arrays, copies, shape

    def scratch(self):
        return [pltpu.VMEM(self.shape, BF), pltpu.SemaphoreType.DMA((len(self.copies),))]

    def start(self, refs, whole, sems):
        me = lax.axis_index("expert")
        running = []
        for i, (index, source, place) in enumerate(self.copies):
            copy = pltpu.make_async_copy(
                refs[index].at[source], whole.at[place(me)], sems.at[i]
            )
            copy.start()
            running.append(copy)
        return running


def row_place(k, size, offset, rows, step):
    def place(me):
        if k is None:
            return (pl.ds(offset, rows),)
        return (pl.ds(pl.multiple_of((me ^ k) * size + offset, step), rows),)

    return place


def column_place(k, size, offset, rows):
    def place(me):
        if k is None:
            return (pl.ds(0, rows),)
        start = pl.multiple_of((me ^ k) * size, 128)
        return (pl.ds(offset, rows), pl.ds(start, size))

    return place


class Links:
    def __init__(self, n, m):
        self.n, self.m = n, m
        self.cube = n == 8
        self.line = m == 4
        self.second = ()

    def hop(self, value, bit):
        return lax.ppermute(value, "expert", [(i, i ^ bit) for i in range(self.n)])

    def gated(self, value, gate):
        return lax.optimization_barrier((value, *gate))[0] if gate else value

    def start(self, shard, gate=()):
        if not self.cube:
            return [shard]
        shard = self.gated(shard, gate)
        return [shard, self.hop(shard, 2), self.hop(shard, 4)]

    def pieces(self, started, gate=()):
        shard, by_x, by_y = lax.optimization_barrier((*started, *gate))[:3] if gate else started
        half = shard.shape[0] // 2 // 16 * 16
        far_a = self.hop(by_y[:half], 2)
        far_b = self.hop(by_x[half:], 4)
        self.second = (far_a, far_b)
        return [
            (0, 0, shard), (1, 0, self.hop(shard, 1)), (2, 0, by_x), (3, 0, self.hop(by_x, 1)),
            (4, 0, by_y), (5, 0, self.hop(by_y, 1)), (6, 0, far_a), (6, half, far_b),
            (7, 0, self.hop(far_a, 1)), (7, half, self.hop(far_b, 1)),
        ]

    def by_rows(self, sizes, started, gate=()):
        group = started[0]
        weights, first = [], 0
        if not self.cube:
            whole = lax.all_gather(group, "expert", axis=0, tiled=False)
            for size in sizes:
                part = whole[:, first : first + size].reshape(-1, group.shape[1])
                copies = [(0, (pl.ds(0, part.shape[0]),), row_place(None, 0, 0, part.shape[0], 8))]
                weights.append(Weight([part], copies, part.shape))
                first += size
            return weights
        pieces = self.pieces(started, gate)
        for size in sizes:
            arrays, copies = [], []
            for k, row, array in pieces:
                low, high = max(first, row), min(first + size, row + array.shape[0])
                if low < high:
                    source = (pl.ds(low - row, high - low),)
                    place = row_place(k, size, low - first, high - low, 16 if size % 16 == 0 else 8)
                    copies.append((len(arrays), source, place))
                    arrays.append(array)
            weights.append(Weight(arrays, copies, (self.n * size, group.shape[1])))
            first += size
        return weights

    def by_columns(self, started, gate=()):
        shard = started[0]
        rows, size = shard.shape
        if not self.cube:
            whole = lax.all_gather(shard, "expert", axis=1, tiled=True)
            return Weight([whole], [(0, (pl.ds(0, rows),), column_place(None, 0, 0, rows))], whole.shape)
        arrays, copies = [], []
        for k, row, array in self.pieces(started, gate):
            source = (pl.ds(0, array.shape[0]),)
            copies.append((len(arrays), source, column_place(k, size, row, array.shape[0])))
            arrays.append(array)
        return Weight(arrays, copies, (rows, self.n * size))

    def exchange(self, rows, gate=()):
        blocks = self.gated(rows, gate).reshape(self.n, -1, rows.shape[1])
        got = lax.all_to_all(blocks, "expert", split_axis=0, concat_axis=0, tiled=True)
        return got.reshape(rows.shape)

    def sum_shapes(self, rows, width):
        if not self.cube:
            return [jax.ShapeDtypeStruct((self.n, rows, width), BF)]
        return [jax.ShapeDtypeStruct((self.n // 2, rows, width), BF)] * 2

    def write_sum(self, refs, whole, first, size):
        for k in range(self.n):
            if self.cube:
                me = lax.axis_index("expert")
                step = 16 if size % 16 == 0 else 8
                start = pl.multiple_of((me ^ k) * size, step)
                refs[k % 2][k // 2, first : first + size] = whole[pl.ds(start, size)]
            else:
                refs[0][k, first : first + size] = whole[k * size : (k + 1) * size]

    def twins(self, blocks):
        return [self.hop(blocks[1], 1)] if self.cube else []

    def fold(self, groups, twins, after=()):
        if not self.cube:
            return [jnp.concatenate([g[0] for g in groups], axis=1)]
        rows = [g[0].shape[1] for g in groups]
        total, columns = sum(rows), groups[0][0].shape[2]
        half = total // 2 // 16 * 16

        def kernel(*refs):
            count = len(groups)
            outs = refs[2 * count :]
            first = 0
            for even, odd in zip(refs[:count], refs[count : 2 * count]):
                for m in range(4):
                    value = (even[m].astype(F32) + odd[m].astype(F32)).astype(BF)
                    low, high = first, first + even.shape[1]
                    cut = min(max(half, low), high)
                    if low < cut:
                        outs[m % 2][m // 2, low:cut] = value[: cut - low]
                    if cut < high:
                        outs[2 + m // 2][m % 2, cut - half : high - half] = value[cut - low :]
                first += even.shape[1]

        outs = [jax.ShapeDtypeStruct((2, half, columns), BF)] * 2
        outs += [jax.ShapeDtypeStruct((2, total - half, columns), BF)] * 2
        args = [g[0] for g in groups] + list(twins)
        return list(call(kernel, outs, args, "v" * len(args), [], "fold", 0, 0, after))

    def across(self, kept):
        return [self.hop(kept[1], 2), self.hop(kept[3], 4)] if self.cube else []

    def fold_again(self, kept, got):
        if not self.cube:
            return kept

        def kernel(first, got_first, second, got_second, *outs):
            for i, (mine, other) in enumerate(((first, got_first), (second, got_second))):
                for j in range(2):
                    outs[2 * i + j][...] = (mine[j].astype(F32) + other[j].astype(F32)).astype(BF)

        outs = [jax.ShapeDtypeStruct(a.shape[1:], BF) for a in (kept[0], kept[0], kept[2], kept[2])]
        args = [kept[0], got[0], kept[2], got[1]]
        return list(call(kernel, outs, args, "vvvv", [], "fold_again", 0, 0))

    def across_again(self, kept):
        return [self.hop(kept[1], 4), self.hop(kept[3], 2)] if self.cube else []

    def fold_last(self, kept, got):
        if not self.cube:
            return lax.psum_scatter(kept[0], "expert", scatter_dimension=0, tiled=True)[0]
        half = kept[0].shape[0]

        def kernel(first, got_first, second, got_second, out):
            out[:half] = (first[...].astype(F32) + got_first[...].astype(F32)).astype(BF)
            out[half:] = (second[...].astype(F32) + got_second[...].astype(F32)).astype(BF)

        rows = half + kept[2].shape[0]
        outs = [jax.ShapeDtypeStruct((rows, kept[0].shape[1]), BF)]
        return call(kernel, outs, [kept[0], got[0], kept[2], got[1]], "vvvv", [], "fold_last", 0, 0)[0]

    def along(self, value, pairs):
        return lax.ppermute(value, "dp", pairs)

    def inward(self, value):
        return [self.along(value, [(0, 1), (3, 2)])] if self.line else []

    def middle(self, value):
        return [self.along(value, [(1, 2), (2, 1)])] if self.line else []

    def outward(self, value):
        return [self.along(value, [(1, 0), (2, 3)])] if self.line else []

    def joined(self, value, got):
        if not self.line:
            return value

        def kernel(mine, other, out):
            out[...] = (mine[...].astype(F32) + other[...].astype(F32)).astype(BF)

        outs = [jax.ShapeDtypeStruct(value.shape, BF)]
        return call(kernel, outs, [value, got[0]], "vv", [], "joined", 0, 0)[0]

    def settled(self, value, got):
        if not self.line:
            return lax.psum(value, "dp").astype(F32)
        place = lax.axis_index("dp")
        return jnp.where((place == 1) | (place == 2), value, got[0]).astype(F32)


    def settled_across(self, value, got, units):
        if not self.line:
            value = lax.psum(value, "dp").astype(F32)
            return value[:units].T, value[units:]

        def kernel(mine, other, up, out):
            place = lax.axis_index("dp")

            def write(ref):
                up[...] = ref[:units].astype(F32).T
                out[...] = ref[units:].astype(F32)

            middle = (place == 1) | (place == 2)
            pl.when(middle)(lambda: write(mine))
            pl.when(jnp.logical_not(middle))(lambda: write(other))

        rows, width = value.shape
        outs = [jax.ShapeDtypeStruct((width, units), F32), jax.ShapeDtypeStruct((rows - units, width), F32)]
        return call(kernel, outs, [value, got[0]], "vv", [], "settle", 0, 0)


def finish(parts):
    width = parts[0].shape[1]

    def kernel(*refs):
        ups, downs = refs[-2:]
        first = 0
        for ref in refs[:-2]:
            for i, out in enumerate((ups, downs)):
                out[:, first : first + ref.shape[2]] = ref[i].astype(F32)
            first += ref.shape[2]

    outs = [jax.ShapeDtypeStruct((width, sum(p.shape[2] for p in parts)), F32)] * 2
    return call(kernel, outs, parts, "v" * len(parts), [], "finish", 0, 0)


def prepare(links, routes, cotangent, capacity):
    count, width = cotangent.shape
    n = links.n
    total = n * capacity

    def kernel(by_row, by_column, cot, row_out, column_out, out):
        route_c, route_r = by_row[...], by_column[...]
        token = lax.broadcasted_iota(I32, (count, count), 0)
        other = lax.broadcasted_iota(I32, (count, count), 1)
        same = route_c == route_r
        rank_c = jnp.sum(jnp.where(same & (other < token), 1.0, 0.0), axis=1, keepdims=True)
        rank_r = jnp.sum(jnp.where(same & (token < other), 1.0, 0.0), axis=0, keepdims=True)
        slot_c = route_c * capacity + rank_c.astype(I32)
        slot_r = route_r * capacity + rank_r.astype(I32)
        column_out[...] = slot_c
        row_out[...] = slot_r
        place = lax.broadcasted_iota(I32, (total, count), 0)
        to_slots = jnp.where(place == slot_r, 1.0, 0.0).astype(BF)
        out[...] = mm(to_slots, cot[...]).astype(BF)

    outs = [jax.ShapeDtypeStruct((1, count), I32), jax.ShapeDtypeStruct((count, 1), I32)]
    outs.append(jax.ShapeDtypeStruct((total, width), BF))
    args = [routes, routes.reshape(1, count), cotangent]
    return call(
        kernel, outs, args, "vvv", [], "prepare", 2 * total * count * width, 4 * total * width
    )


def attend(n, tokens, segments, weight_small, weight_in, weight_out, after):
    count, width = tokens.shape
    pairs = width // (2 * HEAD_DIM)
    block = 128
    n_small, n_in, n_out = len(weight_small.arrays), len(weight_in.arrays), len(weight_out.arrays)
    small_rows, cols = weight_small.shape[0] // n, width // n

    def kernel(tok, seg_c, seg_r, *refs):
        small_refs, refs = refs[:n_small], refs[n_small:]
        in_refs, refs = refs[:n_in], refs[n_in:]
        out_refs, refs = refs[:n_out], refs[n_out:]
        first_ref, proj, mixed, lse, after_ref, second_ref, small_ref = refs[:7]
        w_small, small_sems, w_in, in_sems, w_out, out_sems, bias = refs[7:]
        small_copies = weight_small.start(small_refs, w_small, small_sems)
        in_copies = weight_in.start(in_refs, w_in, in_sems)
        out_copies = weight_out.start(out_refs, w_out, out_sems)
        rows = tok[...].astype(F32)
        normal, _ = normalize(rows)
        source = lax.broadcasted_iota(I32, (cols, width), 0)
        place = lax.broadcasted_iota(I32, (cols, width), 1)
        for copy in small_copies:
            copy.wait()
        small = jnp.zeros((small_rows, width), F32)
        for j in range(n):
            spread = jnp.where(place == source + j * cols, 1.0, 0.0).astype(BF)
            small += mm(w_small[j * small_rows : (j + 1) * small_rows, :cols], spread)
        small_ref[...] = small
        first = (normal * small_ref[0:1] + small_ref[3:4]).astype(BF)
        first_ref[...] = first
        bias[...] = bias_of(seg_c[...], seg_r[...])
        lse[...] = jnp.zeros_like(lse)
        for copy in in_copies:
            copy.wait()
        proj[...] = mm_t(first, w_in[...]).astype(BF)
        masks = half_masks()
        lane = lax.broadcasted_iota(I32, (block, 128), 1)

        def pair(i, carry):
            at = [pl.ds(pl.multiple_of(part * width + 128 * i, 128), 128) for part in range(3)]
            for b in range(count // block):
                mine, keys = pl.ds(b * block, block), pl.ds(0, (b + 1) * block)
                q, k, v = proj[mine, at[0]] * 0.125, proj[keys, at[1]], proj[keys, at[2]]
                got = jnp.zeros((block, 128), F32)
                kept = lse[mine]
                for h in range(2):
                    scores = mm_t(q * masks[h], k) + bias[mine, keys]
                    top = jnp.max(scores, axis=1, keepdims=True)
                    lifted = jnp.exp(scores - top)
                    totals = jnp.sum(lifted, axis=1, keepdims=True)
                    probs = (lifted * (1.0 / totals)).astype(BF)
                    got += mm(probs, v * masks[h])
                    kept = jnp.where(lane == 2 * i + h, top + jnp.log(totals), kept)
                lse[mine] = kept
                mixed[mine, at[0]] = got.astype(BF)
            return carry

        lax.fori_loop(0, pairs, pair, 0)
        for copy in out_copies:
            copy.wait()
        after = rows + mm_t(mixed[...], w_out[...])
        after_ref[...] = after
        normal, _ = normalize(after)
        second_ref[...] = (normal * small_ref[1:2] + small_ref[4:5]).astype(BF)

    shape = jax.ShapeDtypeStruct
    outs = [
        shape((count, width), BF), shape((count, 3 * width), BF), shape((count, width), BF),
        shape((count, 128), F32), shape((count, width), F32), shape((count, width), BF),
        shape((small_rows, width), F32),
    ]
    args = [tokens, segments.reshape(count, 1), segments]
    args += weight_small.arrays + weight_in.arrays + weight_out.arrays
    spaces = "vvv" + "a" * (n_small + n_in + n_out)
    scratch = weight_small.scratch() + weight_in.scratch() + weight_out.scratch() + [pltpu.VMEM((count, count), F32)]
    flops = 2 * count * width * (4 * width + 2 * count) * 2
    return call(kernel, outs, args, spaces, scratch, "attend", flops, 12 * count * width * 4, after)


def widen(second_in, weight_up, after):
    count = second_in.shape[0]
    hidden = weight_up.shape[1]
    pieces = len(weight_up.arrays)
    part = hidden // 4

    def kernel(second, *refs):
        up_refs, (act_ref, slope_ref, up, sems) = refs[:pieces], refs[pieces:]
        for copy in weight_up.start(up_refs, up, sems):
            copy.wait()
        rows = second[...]
        for i in range(4):
            at = pl.ds(i * part, part)
            value, slope = smooth_and_slope(mm(rows, up[:, at]))
            act_ref[:, at] = value.astype(BF)
            slope_ref[:, at] = slope.astype(BF)

    outs = [jax.ShapeDtypeStruct((count, hidden), BF)] * 2
    args = [second_in] + weight_up.arrays
    return call(
        kernel, outs, args, "v" + "a" * pieces, weight_up.scratch(), "widen",
        4 * count * hidden * second_in.shape[1], 8 * count * hidden, after,
    )


def dispatch(links, activated, after_attn, small, row_slots, routes, weight_down, total, after):
    count, width = after_attn.shape
    n = links.n
    pieces = len(weight_down.arrays)

    def kernel(act, after, small_ref, slot_r, route_c, *refs):
        down_refs, refs = refs[:pieces], refs[pieces:]
        hidden_ref, gates_ref, sent_ref = refs[:-2]
        down, sems = refs[-2:]
        for copy in weight_down.start(down_refs, down, sems):
            copy.wait()
        hidden = after[...] + mm_t(act[...], down[...])
        hidden_ref[...] = hidden
        normal, _ = normalize(hidden)
        moe_in = normal * small_ref[2:3] + small_ref[5:6]
        lane = lax.broadcasted_iota(I32, (count, n), 1)
        onehot = jnp.where(lane == route_c[...], 1.0, 0.0).astype(BF)
        chosen = mm(onehot, small_ref[6 : 6 + n].astype(BF))
        logit = jnp.sum(moe_in * chosen, axis=1, keepdims=True)
        gates = 1.0 / (1.0 + jnp.exp(-logit))
        gates_ref[...] = gates
        sent = jnp.concatenate([moe_in.astype(BF), scalar_columns(gates)], axis=1)
        place = lax.broadcasted_iota(I32, (total, count), 0)
        to_slots = jnp.where(place == slot_r[...], 1.0, 0.0).astype(BF)
        sent_ref[...] = mm(to_slots, sent).astype(BF)

    shape = jax.ShapeDtypeStruct
    outs = [shape((count, width), F32), shape((count, 1), F32)]
    outs.append(shape((total, width + EXTRA), BF))
    args = [activated, after_attn, small, row_slots, routes] + weight_down.arrays
    return call(
        kernel, outs, args, "vvvvv" + "a" * pieces, weight_down.scratch(), "dispatch",
        4 * count * width * 4 * width, 16 * count * width, after,
    )


def expert_rows(arrived, cots, width, after):
    total = arrived.shape[0]

    def kernel(arrived_ref, cot_ref, rows_ref, grads_ref, rows_across, grads_across):
        rows = arrived_ref[:, :width]
        rows_ref[...] = rows
        rows_across[...] = rows.T
        gates = columns_scalar(arrived_ref[:, width:])
        grads = (gates * cot_ref[...].astype(F32)).astype(BF)
        grads_ref[...] = grads
        grads_across[...] = grads.T

    outs = [jax.ShapeDtypeStruct((total, width), BF)] * 2 + [jax.ShapeDtypeStruct((width, total), BF)] * 2
    return call(kernel, outs, [arrived, cots], "vv", [], "expert_rows", 0, 0, after)


def expert(rows, grads, across, weights, sums, cot):
    total, width = rows.shape
    m, _, _, wide = weights.shape
    last, started = cot is not None, sums is not None

    def kernel(rows_ref, grads_ref, rows_across, grads_across, *refs):
        refs = list(refs)
        take = lambda k: [refs.pop(0) for _ in range(k)]
        carried = take(2) if started else None
        (cot_ref,) = take(1) if last else (None,)
        (weight_ref,) = take(1)
        (w_grads,) = take(1)
        outs = take(2)
        held, grad_held, sems, out_sems, out_sum, row_sum = refs
        entering = [pltpu.make_async_copy(weight_ref.at[i], held.at[i], sems.at[i]) for i in range(m)]
        for copy in entering:
            copy.start()
        r, g = rows_ref[...], grads_ref[...]
        leaving = []
        for i in range(m):
            entering[i].wait()
            up, down = held[i, 0], held[i, 1]
            value, slope = smooth_and_slope(mm(r, up))
            act = value.astype(BF)
            pre_grad = (mm(g, down) * slope).astype(BF)
            row_part, out_part = mm_t(pre_grad, up), mm_t(act, down)
            if i == 0 and started:
                row_part, out_part = row_part + carried[0][...], out_part + carried[1][...]
            if i > 0:
                row_part, out_part = row_part + row_sum[...], out_part + out_sum[...]
            row_sum[...] = row_part
            out_sum[...] = out_part
            grad_held[i, 0] = mm(rows_across[...], pre_grad).astype(BF)
            grad_held[i, 1] = mm(grads_across[...], act).astype(BF)
            copy = pltpu.make_async_copy(grad_held.at[i], w_grads.at[i], out_sems.at[i])
            copy.start()
            leaving.append(copy)
        if last:
            result = out_sum[...].astype(BF)
            gate_grad = jnp.sum(cot_ref[...].astype(F32) * result.astype(F32), axis=1, keepdims=True)
            outs[0][...] = jnp.concatenate([row_sum[...].astype(BF), scalar_columns(gate_grad)], axis=1)
            outs[1][...] = result
        else:
            outs[0][...] = row_sum[...]
            outs[1][...] = out_sum[...]
        for copy in leaving:
            copy.wait()

    shape = jax.ShapeDtypeStruct
    args = [rows, grads, *across] + (sums if started else []) + ([cot] if last else [])
    spaces = "v" * len(args) + "a"
    outs = [shape((m, 2, width, wide), BF)]
    if last:
        outs += [shape((total, width + EXTRA), BF), shape((total, width), BF)]
    else:
        outs += [shape((total, width), F32)] * 2
    scratch = [
        pltpu.VMEM((m, 2, width, wide), BF), pltpu.VMEM((m, 2, width, wide), BF),
        pltpu.SemaphoreType.DMA((m,)), pltpu.SemaphoreType.DMA((m,)),
        pltpu.VMEM((total, width), F32), pltpu.VMEM((total, width), F32),
    ]
    return call(kernel, outs, args + [weights], spaces, scratch, "expert", 0, 0, [], "avv")


def combine(returned, slots, hidden, gates):
    count, width = hidden.shape

    def kernel(slot_c, hidden_ref, gates_ref, got_ref, out):
        got = got_ref[...]
        place = lax.broadcasted_iota(I32, (count, got.shape[0]), 1)
        pick = jnp.where(place == slot_c[...], 1.0, 0.0).astype(BF)
        out[...] = (hidden_ref[...] + gates_ref[...] * mm(pick, got)).astype(BF)

    return call(
        kernel, [jax.ShapeDtypeStruct((count, width), BF)], [slots, hidden, gates, returned],
        "vvvv", [], "combine", 4 * count * count * width, 10 * count * width,
    )[0]


def gate_back(links, back, slots, routes, hidden, gates, small, cotangent, activated):
    count, width = hidden.shape
    n = links.n
    size = width // n
    units = activated.shape[1]

    def kernel(slot_c, route_c, hidden_ref, gates_ref, small_ref, cot, act, back_ref, *refs):
        got = back_ref[...]
        hidden_grad_ref, down_in_ref, small_out, centroid_out, *sums = refs[:-1]
        whole = refs[-1]
        place = lax.broadcasted_iota(I32, (count, got.shape[0]), 1)
        pick = jnp.where(place == slot_c[...], 1.0, 0.0).astype(BF)
        got = mm(pick, got)
        gates = gates_ref[...]
        logit_grad = columns_scalar(got[:, width:]) * gates * (1.0 - gates)
        lane = lax.broadcasted_iota(I32, (count, n), 1)
        onehot = jnp.where(lane == route_c[...], 1.0, 0.0).astype(BF)
        chosen = mm(onehot, small_ref[6 : 6 + n].astype(BF))
        normal, inverse = normalize(hidden_ref[...])
        gain = small_ref[2:3]
        moe_in = normal * gain + small_ref[5:6]
        terms = split3(logit_grad * moe_in)
        centroid_out[...] = t_mm(onehot, terms[0]) + t_mm(onehot, terms[1]) + t_mm(onehot, terms[2])
        moe_grad = got[:, :width] + logit_grad * chosen
        part, gain_grad, shift_grad = normalize_back(moe_grad, normal, inverse, gain)
        small_out[...] = jnp.concatenate([gain_grad, shift_grad], axis=0)
        hidden_grad = cot[...].astype(F32) + part
        hidden_grad_ref[...] = hidden_grad
        down_in = hidden_grad.astype(BF)
        down_in_ref[...] = down_in
        whole[...] = t_mm(down_in, act[...]).astype(BF)
        links.write_sum(sums, whole, 0, size)

    shape = jax.ShapeDtypeStruct
    outs = [
        shape((count, width), F32), shape((count, width), BF), shape((2, width), F32), shape((n, width), F32),
    ] + links.sum_shapes(size, units)
    args = [slots, routes, hidden, gates, small, cotangent, activated, back]
    hidden_grad, down_in, small_out, centroid_out, *sums = call(
        kernel, outs, args, "v" * len(args), [pltpu.VMEM((width, units), BF)], "gate_back",
        2 * count * width * units * 2, 8 * count * units,
    )
    return hidden_grad, down_in, small_out, centroid_out, sums


def widen_back(links, down_in, slope, second_in, weight_down):
    count, width = down_in.shape
    units = slope.shape[1]
    size = units // links.n
    pieces = len(weight_down.arrays)

    def kernel(down_in_ref, slope_ref, second, *refs):
        down_refs, refs = refs[:pieces], refs[pieces:]
        grad, *sums = refs[:-3]
        down, sems, whole = refs[-3:]
        for copy in weight_down.start(down_refs, down, sems):
            copy.wait()
        rows = down_in_ref[...]
        part = units // 4
        for i in range(4):
            at = pl.ds(i * part, part)
            piece = (mm(rows, down[:, at]) * slope_ref[:, at].astype(F32)).astype(BF)
            grad[:, at] = piece
            whole[at] = t_mm(piece, second[...]).astype(BF)
        links.write_sum(sums, whole, 0, size)

    outs = [jax.ShapeDtypeStruct((count, units), BF)] + links.sum_shapes(size, width)
    args = [down_in, slope, second_in]
    spaces = "vvv" + "a" * pieces
    scratch = weight_down.scratch() + [pltpu.VMEM((units, width), BF)]
    grad, *sums = call(
        kernel, outs, args + weight_down.arrays, spaces, scratch, "widen_back",
        4 * count * width * units, 8 * width * units,
    )
    return grad, sums


def second_back(links, widened_grad, after_attn, hidden_grad, mixed, small, weight_up, after):
    count, width = after_attn.shape
    n = links.n
    size = width // n
    pieces = len(weight_up.arrays)

    def kernel(grad, after_ref, hidden_grad_ref, mixed_ref, small_ref, *refs):
        up_refs, refs = refs[:pieces], refs[pieces:]
        after_grad_ref, attn_grad_ref, small_out, *sums = refs[:-3]
        up, sems, whole = refs[-3:]
        copies = weight_up.start(up_refs, up, sems)
        normal, inverse = normalize(after_ref[...])
        for copy in copies:
            copy.wait()
        second_grad = mm_t(grad[...], up[...])
        back, gain_grad, shift_grad = normalize_back(second_grad, normal, inverse, small_ref[1:2])
        small_out[...] = jnp.concatenate([gain_grad, shift_grad], axis=0)
        after_grad = hidden_grad_ref[...] + back
        after_grad_ref[...] = after_grad
        attn_grad = after_grad.astype(BF)
        attn_grad_ref[...] = attn_grad
        whole[...] = t_mm(attn_grad, mixed_ref[...]).astype(BF)
        links.write_sum(sums, whole, 0, size)

    shape = jax.ShapeDtypeStruct
    outs = [shape((count, width), F32), shape((count, width), BF), shape((2, width), F32)]
    outs += links.sum_shapes(size, width)
    args = [widened_grad, after_attn, hidden_grad, mixed, small]
    spaces = "vvvvv" + "a" * pieces
    scratch = weight_up.scratch() + [pltpu.VMEM((width, width), BF)]
    after_grad, attn_grad, small_out, *sums = call(
        kernel, outs, args + weight_up.arrays, spaces, scratch, "second_back",
        2 * count * width * 4 * width, 8 * width * 4 * width, after,
    )
    return after_grad, attn_grad, small_out, sums


def attend_back(attn_grad, projected, lse, segments, weight_out, after):
    count, width = attn_grad.shape
    pairs = width // (2 * HEAD_DIM)
    block = 128
    blocks = count // block
    n_out = len(weight_out.arrays)

    def kernel(attn_ref, proj, lse, seg_c, seg_r, *refs):
        out_refs, refs = refs[:n_out], refs[n_out:]
        grad, w_out, out_sems, bias, mixed_grad = refs
        copies = weight_out.start(out_refs, w_out, out_sems)
        bias[...] = bias_of(seg_c[...], seg_r[...])
        for copy in copies:
            copy.wait()
        mixed_grad[...] = mm(attn_ref[...], w_out[...]).astype(BF)
        masks = half_masks()
        lane = lax.broadcasted_iota(I32, (block, 128), 1)

        def pair(i, carry):
            at = [pl.ds(pl.multiple_of(part * width + 128 * i, 128), 128) for part in range(3)]
            k_grad = [jnp.zeros((block, 128), F32) for _ in range(blocks)]
            v_grad = [jnp.zeros((block, 128), F32) for _ in range(blocks)]
            for b in range(blocks):
                mine, keys = pl.ds(b * block, block), pl.ds(0, (b + 1) * block)
                q, k, v = proj[mine, at[0]] * 0.125, proj[keys, at[1]], proj[keys, at[2]]
                upper = mixed_grad[mine, at[0]]
                kept = lse[mine]
                q_grad = jnp.zeros((block, 128), F32)
                for h in range(2):
                    q_h, upper_h = q * masks[h], upper * masks[h]
                    log_total = jnp.sum(jnp.where(lane == 2 * i + h, kept, 0.0), axis=1, keepdims=True)
                    probs = jnp.exp(mm_t(q_h, k) + bias[mine, keys] - log_total)
                    probs_grad = mm_t(upper_h, v)
                    mean = jnp.sum(probs * probs_grad, axis=1, keepdims=True)
                    scores_grad = (probs * (probs_grad - mean)).astype(BF)
                    q_grad += mm(scores_grad, k * masks[h])
                    dv = t_mm(probs.astype(BF), upper_h)
                    dk = t_mm(scores_grad, q_h)
                    for c in range(b + 1):
                        v_grad[c] += dv[c * block : (c + 1) * block]
                        k_grad[c] += dk[c * block : (c + 1) * block]
                grad[mine, at[0]] = (q_grad * 0.125).astype(BF)
            for c in range(blocks):
                mine = pl.ds(c * block, block)
                grad[mine, at[1]] = k_grad[c].astype(BF)
                grad[mine, at[2]] = v_grad[c].astype(BF)
            return carry

        lax.fori_loop(0, pairs, pair, 0)

    args = [attn_grad, projected, lse, segments.reshape(count, 1), segments]
    spaces = "v" * len(args) + "a" * n_out
    scratch = weight_out.scratch() + [pltpu.VMEM((count, count), F32), pltpu.VMEM((count, width), BF)]
    return call(
        kernel, [jax.ShapeDtypeStruct((count, 3 * width), BF)], args + weight_out.arrays, spaces, scratch,
        "attend_back", 2 * count * width * (width + 5 * count) * 2, 12 * count * width * 4, after,
    )[0]


def project_back(links, projected_grad, first_in, after):
    width = first_in.shape[1]
    size = 3 * width // links.n

    def kernel(grad, first, *refs):
        whole = refs[-1]
        whole[...] = t_mm(grad[...], first[...]).astype(BF)
        links.write_sum(refs[:-1], whole, 0, size)

    return call(
        kernel, links.sum_shapes(size, width), [projected_grad, first_in], "vv",
        [pltpu.VMEM((3 * width, width), BF)], "project_back", 6 * width**3, 12 * width * width, after,
    )


def tokens_back(links, projected_grad, tokens, after_grad, small, smalls, centroid_grad, weight_in, after):
    count, width = tokens.shape
    n, n_in = links.n, len(weight_in.arrays)
    cols, rows = width // n, small.shape[0]

    def kernel(grad, tok, after_ref, small_ref, small_2, small_3, centroids, *refs):
        in_refs, refs = refs[:n_in], refs[n_in:]
        out, *sums = refs[:-2]
        w_in, sems = refs[-2:]
        copies = weight_in.start(in_refs, w_in, sems)
        normal, inverse = normalize(tok[...].astype(F32))
        for copy in copies:
            copy.wait()
        first_grad = mm(grad[...], w_in[...])
        back, gain_grad, shift_grad = normalize_back(first_grad, normal, inverse, small_ref[0:1])
        out[...] = after_ref[...] + back
        parts = [gain_grad, small_2[0:1], small_3[0:1], shift_grad, small_2[1:2], small_3[1:2]]
        parts += [centroids[...], jnp.zeros((rows - 6 - n, width), F32)]
        both = jnp.concatenate(parts, axis=0).astype(BF)
        me = lax.axis_index("expert") if links.cube else 0
        source = lax.broadcasted_iota(I32, (128, width), 0)
        place = lax.broadcasted_iota(I32, (128, width), 1)
        for k in range(n):
            mine = (place == source + (me ^ k) * cols) & (source < cols)
            block = mm_t(both, jnp.where(mine, 1.0, 0.0).astype(BF)).astype(BF)
            ref, i = (sums[k % 2], k // 2) if links.cube else (sums[0], k)
            ref[i] = jnp.zeros((rows, width), BF)
            ref[i, :, :128] = block

    outs = [jax.ShapeDtypeStruct((count, width), F32)] + links.sum_shapes(rows, width)
    args = [projected_grad, tokens, after_grad, small, *smalls, centroid_grad]
    out, *sums = call(
        kernel, outs, args + weight_in.arrays, "v" * len(args) + "a" * n_in, weight_in.scratch(),
        "tokens_back", 6 * count * width * width, 20 * count * width, after,
    )
    return out, sums


def on_device(
    n, m, tokens, segments, routes, norm_gains, norm_shifts, project_in, project_out,
    dense_up, dense_down, centroids, expert_up, expert_down, cotangent,
):
    count, width = tokens.shape
    BEFORE.clear()
    capacity = 2 * count // n
    total = n * capacity
    own_hidden = expert_up.shape[2]
    links = Links(n, m)
    cols = width // n

    def chunk(start, wide):
        part = slice(start, start + wide)
        return jnp.concatenate([expert_up[0][:, part], expert_down[0][:, part]], axis=0)

    chunks = [512, 256] if own_hidden == 768 and m == 4 else [own_hidden]
    gathered, start = [], 0
    for wide in chunks:
        whole = lax.all_gather(chunk(start, wide), "dp", axis=0, tiled=True)
        gathered.append(whole.reshape(m, 2, width, wide))
        start += wide

    pad = -(6 + n) % 16
    small = jnp.concatenate([norm_gains, norm_shifts, centroids], axis=0)
    small = jnp.pad(small, ((0, pad), (0, width - cols)))
    group = [project_in.T, project_out.T, small]
    started = links.start(jnp.concatenate(group, axis=0))
    weight_in, weight_out, weight_small = links.by_rows([a.shape[0] for a in group], started)
    started_up = links.start(dense_up, links.second)
    started_down = links.start(dense_down.T, links.second)

    row_slots, slots, cots = prepare(links, routes, cotangent, capacity)
    first_in, projected, mixed, lse, after_attn, second_in, small = attend(
        n, tokens, segments, weight_small, weight_in, weight_out, []
    )
    weight_up = links.by_columns(started_up, [small])
    (weight_down,) = links.by_rows([cols], started_down, [small])
    cots = links.exchange(cots, links.second)
    activated, slope = widen(second_in, weight_up, [])
    hidden, gates, sent = dispatch(
        links, activated, after_attn, small, row_slots, routes, weight_down, total, [cots]
    )
    rows, grads, *across = expert_rows(links.exchange(sent), cots, width, [])

    sums, expert_sums = None, []
    for c, whole in enumerate(gathered):
        last = c == len(chunks) - 1
        w_grads, *sums = expert(rows, grads, across, whole, sums, cots if last else None)
        expert_sums.append(w_grads)
    back, results = sums

    def own_sum(grads):
        sums = lax.psum_scatter(grads.reshape(-1, grads.shape[-1]), "dp", scatter_dimension=0, tiled=True)
        return sums.reshape(grads.shape[1:])

    summed = [own_sum(expert_sums[0])]
    back = links.exchange(back)
    returned = links.exchange(results, [back])

    hidden_grad, down_in, small_3, centroid_grad, sums_down = gate_back(
        links, back, slots, routes, hidden, gates, small, cotangent, activated
    )
    twin_down = links.twins(sums_down)
    widened_grad, sums_up = widen_back(links, down_in, slope, second_in, weight_down)
    twin_up = links.twins(sums_up)
    down = links.fold([sums_down], twin_down, [returned])
    down_got = links.across(down)
    after_grad, attn_grad, small_2, sums_out = second_back(
        links, widened_grad, after_attn, hidden_grad, mixed, small, weight_up, []
    )
    twin_out = links.twins(sums_out)
    projected_grad = attend_back(attn_grad, projected, lse, segments, weight_out, [])
    up = links.fold([sums_up, sums_out], twin_up + twin_out)
    up_got = links.across(up)
    down = links.fold_again(down, down_got)
    down_got = links.across_again(down)
    tokens_grad, sums_small = tokens_back(
        links, projected_grad, tokens, after_grad, small, [small_2, small_3], centroid_grad, weight_in, []
    )
    twin_small = links.twins(sums_small)
    for grads in expert_sums[1:]:
        summed.append(own_sum(links.gated(grads, summed + [sums_small[0]])))
    sums_in = project_back(links, projected_grad, first_in, [])
    twin_in = links.twins(sums_in)
    inner = links.fold([sums_in, sums_small], twin_in + twin_small)
    inner_got = links.across(inner)
    down = links.fold_last(down, down_got)
    down_got = links.inward(down)
    up = links.fold_again(up, up_got)
    up_got = links.across_again(up)
    inner = links.fold_again(inner, inner_got)
    inner_got = links.across_again(inner)
    up = links.fold_last(up, up_got)
    up_got = links.inward(up)
    inner = links.fold_last(inner, inner_got)
    inner_got = links.inward(inner)
    output = combine(returned, slots, hidden, gates)
    down = links.joined(down, down_got)
    down_got = links.middle(down)
    down = links.joined(down, down_got)
    down_got = links.outward(down)
    up = links.joined(up, up_got)
    up_got = links.middle(up)
    inner = links.joined(inner, inner_got)
    inner_got = links.middle(inner)
    up = links.joined(up, up_got)
    up_got = links.outward(up)
    inner = links.joined(inner, inner_got)
    inner_got = links.outward(inner)
    expert_sums = finish(summed)
    units, columns = dense_up.shape[1], project_in.shape[1]
    down_sum = links.settled(down, down_got)
    up_sum, out_sum = links.settled_across(up, up_got, units)
    inner_sum = links.settled(inner, inner_got)
    small_sum = inner_sum[columns:, :cols]

    return (
        output, tokens_grad, small_sum[:3], small_sum[3:6], inner_sum[:columns].T, out_sum.T, up_sum,
        down_sum.T, small_sum[6 : 6 + n], expert_sums[0][None], expert_sums[1][None],
    )


def solution(mesh):
    sizes = dict(mesh.shape)
    both, over = P(("dp", "expert"), None), P(None, "expert")
    expert_place = P("expert", None, "dp")
    return jax.shard_map(
        functools.partial(on_device, sizes["expert"], sizes["dp"]),
        mesh=mesh,
        in_specs=(both,) * 3 + (over,) * 7 + (expert_place,) * 2 + (both,),
        out_specs=(both,) * 2 + (over,) * 7 + (expert_place,) * 2,
        check_vma=False,
    )
```

time: 1060 us -> 469 us (0.44)
  waiting for transfers between devices: 726 us -> 156 us
  Pallas kernels: 0 us -> 142 us
  matrix products: 135 us -> 0 us
  starting transfers between devices: 8.33 us -> 56 us
  blocking collectives: 89.8 us -> 45.4 us
  other arithmetic: 41.4 us -> 5.58 us
    reduce_scatter x5 -> x2, waiting for transfers between devices: 282 us -> 0.01 us  [own_sum(): lax.psum_scatter(grads.reshape(-1, grads.shape[-1]), 'dp', scatter_dimens...]
    all_gather x6 -> x2, waiting for transfers between devices: 254 us -> 19.3 us  [on_device(): whole = lax.all_gather(chunk(start, wide), 'dp', axis=0, tiled=True)]
    pallas_call x0 -> x31, Pallas kernels: none -> 142 us  [call(): pl.pallas_call(body, out_shape=outs, in_specs=[pl.BlockSpec(memory_space=...]
    dot_general x26 -> x0, matrix products: 135 us -> none  [the longest x6 37 us: contract_rows(): lax.dot_general(left, right, (((0,), (0,)), ((), ())), preferred_element_...]
    ppermute x0 -> x53, waiting for transfers between devices: none -> 131 us  [the longest x9 65.4 us: along(): return lax.ppermute(value, 'dp', pairs)]
    unnamed x20 -> x4, waiting for transfers between devices: 113 us -> 0.07 us
    psum x1 -> x0, waiting for transfers between devices: 77.4 us -> none  [on_device(): lax.psum(pieces[2].astype(jnp.bfloat16), 'dp').astype(jnp.float32)]
    ppermute x0 -> x53, starting transfers between devices: none -> 48.6 us  [the longest x44 30.9 us: hop(): return lax.ppermute(value, 'expert', [(i, i ^ bit) for i in range(self.n)])]
  transfers between devices with their start and end apart: 18 -> 59, of which waited for: 15 -> 23; matrix products, arithmetic and copies ran while one was open for 13% -> 3% of each run, Pallas kernels for 0% -> 30%
where the time goes in v1:
time: 469 us; the launch traced here: 461 us
  waiting for transfers between devices  156 us (33%)
  Pallas kernels  142 us (30%)
  starting transfers between devices  56 us (12%)
  blocking collectives  45.4 us (10%)
  local copies, waits for them, and re-layouts  41.6 us (9%)
  between operations  15 us (3%)
  other arithmetic  5.58 us (1%)
    pallas_call x31, Pallas kernels, call(): pl.pallas_call(body, out_shape=outs, in_specs=[pl.BlockSpec(memory_space=...  142 us
    ppermute x9, waiting for transfers between devices, along(): return lax.ppermute(value, 'dp', pairs)  65.4 us
    ppermute x44, waiting for transfers between devices, hop(): return lax.ppermute(value, 'expert', [(i, i ^ bit) for i in range(self.n)])  65.2 us
    all_to_all x2, blocking collectives, exchange(): lax.all_to_all(blocks, 'expert', split_axis=0, concat_axis=0, tiled=True)  45.4 us
    ppermute x44, starting transfers between devices, hop(): return lax.ppermute(value, 'expert', [(i, i ^ bit) for i in range(self.n)])  30.9 us
    unnamed x177, local copies, waits for them, and re-layouts  30.1 us
    all_gather x2, waiting for transfers between devices, on_device(): whole = lax.all_gather(chunk(start, wide), 'dp', axis=0, tiled=True)  19.3 us
    ppermute x9, starting transfers between devices, along(): return lax.ppermute(value, 'dp', pairs)  17.7 us
  transfers between devices with their start and end apart: 59, of which 23 were waited for; matrix products, arithmetic and copies ran while one was open for 3% of the time, Pallas kernels for 30%

profile of v1, /device:TPU:0, one launch (start us, length us, event | category | flops | bytes accessed | tf_op | source)
XLA Modules:
  0.0 461.5 jit_solution(11377945604449615979)
XLA Ops:
  11.2 3.0 collective-permute-start.1
  14.2 1.5 collective-permute-start.3
  15.7 12.3 %collective-permute-done.1.refs_5_.refs_13_.refs_23_.refs_7_.refs_9_ = bf16[400,768]{1,0:T(8,128)(2,1)S(1)} collective-permute-done((bf16[400,768]{1,0:T(8,128)(2,1)S(1)}, bf16[400,768]{1,0:T(8,128)(2,1)S(1)}, u32[]{:S(2)}, u32[]{:S(2)}) %collective-permute-start.1) | collective-permute-done | bytes 614432 | tf_op jit(solution)/shard_map/ppermute | solution.py:171
  28.8 1.8 collective-permute-start.5
  31.4 1.5 collective-permute-start.7
  35.0 4.3 collective-permute-done.7.refs_17_.refs_13_
  41.9 1.9 prepare.1
  44.5 1.5 collective-permute-start.9
  49.3 15.8 %attend.1 = (bf16[384,768]{1,0:T(8,128)(2,1)}, bf16[384,2304]{1,0:T(8,128)(2,1)}, bf16[384,768]{1,0:T(8,128)(2,1)}, f32[384,128]{1,0:T(8,128)}, f32[384,768]{1,0...) custom-call(bf16[384,768]{1,0:T(8,128)(2,1)} %refs_1_.3, s32[384,1]{1,0:T(8,128)} %copy.28.refs_1_.refs_3_, ...), custom_call_target="tpu_custom_call" | custom-call | flops 18400000000 | bytes 1000 | tf_op jit(solution)/shard_map/attend/pallas_call | solution.py:111
  66.2 1.5 collective-permute-start.14
  69.3 4.2 collective-permute-done.18.refs_7_.refs_5_
  73.6 1.5 collective-permute-done.19.refs_9_.refs_7_
  76.5 3.4 collective-permute-done.14.refs_7_.refs_11_
  79.9 1.6 collective-permute-done.15.refs_8_.refs_12_
  81.5 3.9 collective-permute-done.23.refs_11_.refs_9_
  86.6 1.9 slice.65
  88.5 1.8 slice.64
  90.3 3.6 all-to-all-start
  93.9 2.0 pad_maximum_fusion.1
  98.2 9.5 %widen.1 = (bf16[384,3072]{1,0:T(8,128)(2,1)}, bf16[384,3072]{1,0:T(8,128)(2,1)}) custom-call(bf16[384,768]{1,0:T(8,128)(2,1)} %get-tuple-element.96.refs_0_.refs_2_, bf16[768,384]{1,0:T(8,128)(2,1)} %refs_5_.2, bf16[768,384]{1,0:T(8,128)(2,1)} %copy-done.43, bf16[768,384]{1,0:T(8,128)(2,1)} %collective-permute-done.9.refs_3_.refs_7_, ...), custom_call_target="tpu_custom_call" | custom-call | flops 10350000128 | bytes 1000 | tf_op jit(solution)/shard_map/widen/pallas_call | solution.py:111
  108.5 2.1 all-to-all-done
  111.6 9.9 %dispatch.1 = (f32[384,768]{1,0:T(8,128)}, f32[384,1]{1,0:T(8,128)}, bf16[768,896]{1,0:T(8,128)(2,1)}) custom-call(bf16[384,3072]{1,0:T(8,128)(2,1)} %get-tuple-element.102.refs_0_.refs_16_.refs_6_, f32[384,768]{1,0:T(8,128)} %get-tuple-element.103.refs_1_, f32[16,768]{1,0:T(8,128)} %get-tuple-element.98.refs_11_.refs_2_.refs_4_.refs_3_, ...), custom_call_target="tpu_custom_call" | custom-call | flops 11500000256 | bytes 1000 | tf_op jit(solution)/shard_map/dispatch/pallas_call | solution.py:111
  121.5 22.5 %all_to_all.20 = bf16[8,96,896]{2,1,0:T(8,128)(2,1)S(1)} all-to-all(bf16[8,96,896]{2,1,0:T(8,128)(2,1)} %bitcast.43), channel_id=1, replica_groups=mesh['dp'=4,'expert'=8] {'expert'}, dimensions={0} | all-to-all | bytes 2752512 | tf_op jit(solution)/shard_map/all_to_all | solution.py:234
  149.1 23.7 %expert.2 = (bf16[4,2,768,512]{3,2,1,0:T(8,128)(2,1)}, f32[768,768]{1,0:T(8,128)}, f32[768,768]{1,0:T(8,128)}) custom-call(bf16[768,768]{1,0:T(8,128)(2,1)} %copy-done.66, bf16[768,768]{1,0:T(8,128)(2,1)} %copy-done.67, bf16[768,768]{1,0:T(8,128)(2,1)} %copy-done.68, bf16[768,768]{1,0:T(8,128)(2,1)} %copy-done.69, bf16[4,2,768,512]{3,2,1,0:T(8,128)(2,1)} %bitcast.50, ...), custom_call_target="tpu_custom_call" | custom-call | flops 23000000512 | bytes 1000 | tf_op jit(solution)/shard_map/expert/pallas_call | solution.py:111
  172.9 19.3 %all-gather.5.cloned.1.call-done = bf16[6144,256]{1,0:T(8,128)(2,1)} async-done(((bf16[1536,256]{1,0:T(8,128)(2,1)}), bf16[6144,256]{1,0:T(8,128)(2,1)}) %all-gather.5.cloned.1.call-update) | async-done | bytes 3145744 | tf_op jit(solution)/shard_map/all_gather | solution.py:886
  192.2 16.7 %expert.3 = (bf16[4,2,768,256]{3,2,1,0:T(8,128)(2,1)}, bf16[768,896]{1,0:T(8,128)(2,1)}, bf16[768,768]{1,0:T(8,128)(2,1)}) custom-call(bf16[768,768]{1,0:T(8,128)(2,1)} %copy-done.66, bf16[768,768]{1,0:T(8,128)(2,1)} %copy-done.67, bf16[768,768]{1,0:T(8,128)(2,1)} %copy-done.68, bf16[768,768]{1,0:T(8,128)(2,1)} %copy-done.69, ...), custom_call_target="tpu_custom_call" | custom-call | flops 23000000512 | bytes 1000 | tf_op jit(solution)/shard_map/expert/pallas_call | solution.py:111
  209.0 22.9 %all_to_all.21 = bf16[8,96,896]{2,1,0:T(8,128)(2,1)S(1)} all-to-all(bf16[8,96,896]{2,1,0:T(8,128)(2,1)} %bitcast.42), channel_id=1, replica_groups=mesh['dp'=4,'expert'=8] {'expert'}, dimensions={0} | all-to-all | bytes 2752512 | tf_op jit(solution)/shard_map/all_to_all | solution.py:234
  231.9 1.7 copy-done.70
  233.5 6.3 %gate_back.1 = (f32[384,768]{1,0:T(8,128)S(1)}, bf16[384,768]{1,0:T(8,128)(2,1)S(1)}, f32[2,768]{1,0:T(2,128)S(1)}, f32[8,768]{1,0:T(8,128)S(1)}, bf16[4,96,3072...) custom-call(s32[384,1]{1,0:T(8,128)S(1)} %copy-done.58, s32[384,1]{1,0:T(8,128)S(1)} %copy-done.26, ...), custom_call_target="tpu_custom_call" | custom-call | flops 11500000256 | bytes 1000 | tf_op jit(solution)/shard_map/gate_back/pallas_call | solution.py:111
  242.7 3.6 all-to-all-start.3
  246.3 11.9 %widen_back.1 = (bf16[384,3072]{1,0:T(8,128)(2,1)}, bf16[4,384,768]{2,1,0:T(8,128)(2,1)}, bf16[4,384,768]{2,1,0:T(8,128)(2,1)}) custom-call(bf16[384,768]{1,0:T(8,128)(2,1)} %copy-done.73, bf16[384,3072]{1,0:T(8,128)(2,1)} %get-tuple-element.123.refs_1_, bf16[384,768]{1,0:T(8,128)(2,1)} %get-tuple-element.96.refs_0_.refs_2_, ...), custom_call_target="tpu_custom_call" | custom-call | flops 13799999488 | bytes 1000 | tf_op jit(solution)/shard_map/widen_back/pallas_call | solution.py:111
  258.7 4.3 all-to-all-done.3
  263.0 1.7 copy-done.4
  264.7 1.7 copy-done.5
  266.4 2.4 fold.3
  270.0 6.9 %second_back.1 = (f32[384,768]{1,0:T(8,128)S(1)}, bf16[384,768]{1,0:T(8,128)(2,1)S(1)}, f32[2,768]{1,0:T(2,128)S(1)}, bf16[4,96,768]{2,1,0:T(8,128)(2,1)S(1)}, bf16[4,96,768]{2,1,0:T(8,128)(2,1)S(1)}) custom-call(bf16[384,3072]{1,0:T(8,128)(2,1)S(1)} %copy-done.6, f32[384,768]{1,0:T(8,128)S(1)} %copy-done.72, f32[384,768]{1,0:T(8,128)S(1)} %get-tuple-element.126.refs_2_, ...), custom_call_target="tpu_custom_call" | custom-call | flops 16099999744 | bytes 1000 | tf_op jit(solution)/shard_map/second_back/pallas_call | solution.py:111
  278.2 12.6 %attend_back.1.refs_4_.refs_0_ = bf16[384,2304]{1,0:T(8,128)(2,1)S(1)} custom-call(bf16[384,768]{1,0:T(8,128)(2,1)S(1)} %get-tuple-element.131.refs_0_, bf16[384,2304]{1,0:T(8,128)(2,1)S(1)} %copy-done.65, f32[384,128]{1,0:T(8,128)S(1)} %copy-done.71, s32[384,1]{1,0:T(8,128)S(1)} %copy-done.24, s32[1,384]{1,0:T(1,128)S(1)} %copy-done.32, ...), custom_call_target="tpu_custom_call" | custom-call | flops 5750000128 | bytes 1000 | tf_op jit(solution)/shard_map/attend_back/pallas_call | solution.py:111
  290.8 2.3 fold.4
  296.2 5.7 %tokens_back.1 = (f32[384,768]{1,0:T(8,128)}, bf16[4,16,768]{2,1,0:T(8,128)(2,1)S(1)}, bf16[4,16,768]{2,1,0:T(8,128)(2,1)S(1)}) custom-call(bf16[384,2304]{1,0:T(8,128)(2,1)S(1)} %attend_back.1.refs_4_.refs_0_, bf16[384,768]{1,0:T(8,128)(2,1)S(1)} %copy-done.17, f32[384,768]{1,0:T(8,128)S(1)} %get-tuple-element.136.refs_2_, f32[16,768]{1,0:T(8,128)S(1)} %copy-done.27, ...), custom_call_target="tpu_custom_call" | custom-call | flops 2300000000 | bytes 1000 | tf_op jit(solution)/shard_map/tokens_back/pallas_call | solution.py:111
  302.0 3.5 project_back.1
  305.5 1.6 collective-permute-start.36
  307.0 1.5 collective-permute-start.37
  310.9 2.0 fold.5
  312.8 1.6 collective-permute-start.35
  314.5 18.4 %collective-permute-done.38.refs_1_ = bf16[48,3072]{1,0:T(8,128)(2,1)S(1)} collective-permute-done((bf16[48,3072]{1,0:T(8,128)(2,1)}, bf16[48,3072]{1,0:T(8,128)(2,1)S(1)}, u32[]{:S(2)}, u32[]{:S(2)}) %collective-permute-start.38) | collective-permute-done | bytes 294944 | tf_op jit(solution)/shard_map/ppermute | solution.py:171
  335.1 1.6 collective-permute-start.42
  338.2 1.9 collective-permute-start.46
  340.1 5.9 %collective-permute-done.34.refs_1_ = bf16[2,144,768]{2,1,0:T(8,128)(2,1)S(1)} collective-permute-done((bf16[2,144,768]{2,1,0:T(8,128)(2,1)S(1)}, bf16[2,144,768]{2,1,0:T(8,128)(2,1)S(1)}, u32[]{:S(2)}, u32[]{:S(2)}) %collective-permute-start.34) | collective-permute-done | bytes 442400 | tf_op jit(solution)/shard_map/ppermute | solution.py:171
  346.8 1.6 collective-permute-start.40
  348.4 2.9 collective-permute-done.42.refs_1_
  351.3 2.6 collective-permute-done.43.refs_3_
  355.4 1.5 collective-permute-done.41.refs_3_
  358.3 1.5 combine.1.refs_2_
  359.8 6.8 %collective-permute-done.46.refs_1_ = bf16[96,3072]{1,0:T(8,128)(2,1)S(1)} collective-permute-done((bf16[96,3072]{1,0:T(8,128)(2,1)S(1)}, bf16[96,3072]{1,0:T(8,128)(2,1)S(1)}, u32[]{:S(2)}, u32[]{:S(2)}) %collective-permute-start.46) | collective-permute-done | bytes 589856 | tf_op jit(solution)/shard_map/ppermute | solution.py:315
  368.5 7.6 %collective-permute-start.44 = (bf16[304,768]{1,0:T(8,128)(2,1)S(1)}, bf16[304,768]{1,0:T(8,128)(2,1)S(1)}, u32[]{:S(2)}, u32[]{:S(2)}) collective-permute-start(bf16[304,768]{1,0:T(8,128)(2,1)S(1)} %fold_last.5.refs_4_.refs_0_), channel_id=1, source_target_pairs={{0,8},{24,16},{1,9},{25,17},{2,10},{26,18},{3,11},{27,19},{4,12},{... | collective-permute-start | bytes 1400840 | tf_op jit(solution)/shard_map/ppermute | solution.py:315
  376.3 16.5 %collective-permute-done.45.refs_1_ = bf16[480,768]{1,0:T(8,128)(2,1)S(1)} collective-permute-done((bf16[480,768]{1,0:T(8,128)(2,1)S(1)}, bf16[480,768]{1,0:T(8,128)(2,1)S(1)}, u32[]{:S(2)}, u32[]{:S(2)}) %collective-permute-start.45) | collective-permute-done | bytes 737312 | tf_op jit(solution)/shard_map/ppermute | solution.py:315
  395.0 6.7 %collective-permute-done.44.refs_1_ = bf16[304,768]{1,0:T(8,128)(2,1)S(1)} collective-permute-done((bf16[304,768]{1,0:T(8,128)(2,1)S(1)}, bf16[304,768]{1,0:T(8,128)(2,1)S(1)}, u32[]{:S(2)}, u32[]{:S(2)}) %collective-permute-start.44) | collective-permute-done | bytes 466976 | tf_op jit(solution)/shard_map/ppermute | solution.py:315
  405.9 6.5 %collective-permute-done.52 = bf16[96,3072]{1,0:T(8,128)(2,1)} collective-permute-done((bf16[96,3072]{1,0:T(8,128)(2,1)S(1)}, bf16[96,3072]{1,0:T(8,128)(2,1)}, u32[]{:S(2)}, u32[]{:S(2)}) %collective-permute-start.52) | collective-permute-done | bytes 589856 | tf_op jit(solution)/shard_map/ppermute | solution.py:315
  412.3 2.2 convert_bitcast_fusion
  415.9 22.6 %collective-permute-done.50 = bf16[304,768]{1,0:T(8,128)(2,1)S(1)} collective-permute-done((bf16[304,768]{1,0:T(8,128)(2,1)S(1)}, bf16[304,768]{1,0:T(8,128)(2,1)S(1)}, u32[]{:S(2)}, u32[]{:S(2)}) %collective-permute-start.50) | collective-permute-done | bytes 466976 | tf_op jit(solution)/shard_map/ppermute | solution.py:315
  441.9 2.4 finish.1
  444.3 6.3 %collective-permute-done.51.refs_1_ = bf16[480,768]{1,0:T(8,128)(2,1)} collective-permute-done((bf16[480,768]{1,0:T(8,128)(2,1)S(1)}, bf16[480,768]{1,0:T(8,128)(2,1)}, u32[]{:S(2)}, u32[]{:S(2)}) %collective-permute-start.51) | collective-permute-done | bytes 737312 | tf_op jit(solution)/shard_map/ppermute | solution.py:315
  450.6 1.7 copy-done.53
  452.2 2.5 settle.1
  (288 shorter events, 60.1 us)
Async XLA Ops:
  7.2 141.9 %all-gather.3.cloned.1.call-start = ((), (), s32[]{:S(2)}) async-start(), calls=%async_computation.6 | async-start | bytes 7864320 | tf_op jit(solution)/shard_map/all_gather | solution.py:886
  10.7 23.5 %copy-start.31 = (s32[1,384]{1,0:T(1,128)S(1)}, s32[1,384]{1,0:T(1,128)}, u32[]{:S(2)}) copy-start(s32[1,384]{1,0:T(1,128)} %refs_4_.2) | copy-start | bytes 4612
  11.1 32.7 %copy-start = (bf16[400,768]{1,0:T(8,128)(2,1)}, bf16[400,768]{1,0:T(8,128)(2,1)S(1)}, u32[]{:S(2)}) copy-start(bf16[400,768]{1,0:T(8,128)(2,1)S(1)} %pad_maximum_fusion.2.refs_3_.refs_11_.refs_21_.refs_5_.refs_7_) | copy-start | bytes 1843204
  11.2 16.9 %collective-permute-start.1 = (bf16[400,768]{1,0:T(8,128)(2,1)S(1)}, bf16[400,768]{1,0:T(8,128)(2,1)S(1)}, u32[]{:S(2)}, u32[]{:S(2)}) collective-permute-start(bf16[400,768]{1,0:T(8,128)(2,1)S(1)} %pad_maximum_fusion.2.refs_3_.refs_11_.refs_21_.refs_5_.refs_7_), channel_id=1, source_target_pairs={{0,2},{1,3},{2,0},{3,1},{4,6},{5,7},{6,4},{7,5},{8,10},{9,11},{10,... | collective-permute-start | bytes 1843208 | tf_op jit(solution)/shard_map/ppermute | solution.py:171
  14.2 16.4 %collective-permute-start.3 = (bf16[400,768]{1,0:T(8,128)(2,1)S(1)}, bf16[400,768]{1,0:T(8,128)(2,1)S(1)}, u32[]{:S(2)}, u32[]{:S(2)}) collective-permute-start(bf16[400,768]{1,0:T(8,128)(2,1)S(1)} %pad_maximum_fusion.2.refs_3_.refs_11_.refs_21_.refs_5_.refs_7_), channel_id=1, source_target_pairs={{0,4},{1,5},{2,6},{3,7},{4,0},{5,1},{6,2},{7,3},{8,12},{9,13},{10,... | collective-permute-start | bytes 1843208 | tf_op jit(solution)/shard_map/ppermute | solution.py:171
  28.8 10.6 %collective-permute-start.5 = (bf16[208,768]{1,0:T(8,128)(2,1)}, bf16[208,768]{1,0:T(8,128)(2,1)S(1)}, u32[]{:S(2)}, u32[]{:S(2)}) collective-permute-start(bf16[208,768]{1,0:T(8,128)(2,1)} %slice.60), channel_id=1, source_target_pairs={{0,4},{1,5},{2,6},{3,7},{4,0},{5,1},{6,2},{7,3},{8,12},{9,13},{10,... | collective-permute-start | bytes 958472 | tf_op jit(solution)/shard_map/ppermute | solution.py:171
  31.4 8.0 %collective-permute-start.7 = (bf16[192,768]{1,0:T(8,128)(2,1)}, bf16[192,768]{1,0:T(8,128)(2,1)}, u32[]{:S(2)}, u32[]{:S(2)}) collective-permute-start(bf16[192,768]{1,0:T(8,128)(2,1)} %slice.61), channel_id=1, source_target_pairs={{0,2},{1,3},{2,0},{3,1},{4,6},{5,7},{6,4},{7,5},{8,10},{9,11},{10,... | collective-permute-start | bytes 884744 | tf_op jit(solution)/shard_map/ppermute | solution.py:171
  32.8 11.7 %collective-permute-start = (bf16[400,768]{1,0:T(8,128)(2,1)S(1)}, bf16[400,768]{1,0:T(8,128)(2,1)S(1)}, u32[]{:S(2)}, u32[]{:S(2)}) collective-permute-start(bf16[400,768]{1,0:T(8,128)(2,1)S(1)} %pad_maximum_fusion.2.refs_3_.refs_11_.refs_21_.refs_5_.refs_7_), channel_id=1, source_target_pairs={{0,1},{1,0},{2,3},{3,2},{4,5},{5,4},{6,7},{7,6},{8,9},{9,8},{10,11... | collective-permute-start | bytes 1843208 | tf_op jit(solution)/shard_map/ppermute | solution.py:171
  32.8 13.7 %collective-permute-start.2 = (bf16[400,768]{1,0:T(8,128)(2,1)S(1)}, bf16[400,768]{1,0:T(8,128)(2,1)S(1)}, u32[]{:S(2)}, u32[]{:S(2)}) collective-permute-start(bf16[400,768]{1,0:T(8,128)(2,1)S(1)} %collective-permute-done.1.refs_5_.refs_13_.refs_23_.refs_7_.refs_9_), channel_id=1, source_target_pairs={{0,1},{1,0},{2,3},{3,2},{4,5},{5,4},{6,7},{7,6},{8,9},{9,8},{10,11... | collective-permute-start | bytes 1843208 | tf_op jit(solution)/shard_map/ppermute | solution.py:171
  33.4 13.8 %collective-permute-start.4 = (bf16[400,768]{1,0:T(8,128)(2,1)S(1)}, bf16[400,768]{1,0:T(8,128)(2,1)}, u32[]{:S(2)}, u32[]{:S(2)}) collective-permute-start(bf16[400,768]{1,0:T(8,128)(2,1)S(1)} %collective-permute-done.3.refs_7_.refs_15_.refs_25_.refs_9_.refs_11_), channel_id=1, source_target_pairs={{0,1},{1,0},{2,3},{3,2},{4,5},{5,4},{6,7},{7,6},{8,9},{9,8},{10,11... | collective-permute-start | bytes 1843208 | tf_op jit(solution)/shard_map/ppermute | solution.py:171
  39.4 6.6 %collective-permute-start.8 = (bf16[192,768]{1,0:T(8,128)(2,1)}, bf16[192,768]{1,0:T(8,128)(2,1)S(1)}, u32[]{:S(2)}, u32[]{:S(2)}) collective-permute-start(bf16[192,768]{1,0:T(8,128)(2,1)} %collective-permute-done.7.refs_17_.refs_13_), channel_id=1, source_target_pairs={{0,1},{1,0},{2,3},{3,2},{4,5},{5,4},{6,7},{7,6},{8,9},{9,8},{10,11... | collective-permute-start | bytes 884744 | tf_op jit(solution)/shard_map/ppermute | solution.py:171
  39.4 9.2 %collective-permute-start.6 = (bf16[208,768]{1,0:T(8,128)(2,1)S(1)}, bf16[208,768]{1,0:T(8,128)(2,1)S(1)}, u32[]{:S(2)}, u32[]{:S(2)}) collective-permute-start(bf16[208,768]{1,0:T(8,128)(2,1)S(1)} %collective-permute-done.5.refs_9_.refs_18_.refs_27_.refs_11_.refs_14_), channel_id=1, source_target_pairs={{0,1},{1,0},{2,3},{3,2},{4,5},{5,4},{6,7},{7,6},{8,9},{9,8},{10,11... | collective-permute-start | bytes 958472 | tf_op jit(solution)/shard_map/ppermute | solution.py:171
  44.5 20.7 %collective-permute-start.9 = (bf16[768,384]{1,0:T(8,128)(2,1)}, bf16[768,384]{1,0:T(8,128)(2,1)}, u32[]{:S(2)}, u32[]{:S(2)}) collective-permute-start(bf16[768,384]{1,0:T(8,128)(2,1)} %refs_5_.2), channel_id=1, source_target_pairs={{0,2},{1,3},{2,0},{3,1},{4,6},{5,7},{6,4},{7,5},{8,10},{9,11},{10,... | collective-permute-start | bytes 1769480 | tf_op jit(solution)/shard_map/ppermute | solution.py:171
  46.0 19.2 %collective-permute-start.10 = (bf16[768,384]{1,0:T(8,128)(2,1)}, bf16[768,384]{1,0:T(8,128)(2,1)}, u32[]{:S(2)}, u32[]{:S(2)}) collective-permute-start(bf16[768,384]{1,0:T(8,128)(2,1)} %refs_5_.2), channel_id=1, source_target_pairs={{0,4},{1,5},{2,6},{3,7},{4,0},{5,1},{6,2},{7,3},{8,12},{9,13},{10,... | collective-permute-start | bytes 1769480 | tf_op jit(solution)/shard_map/ppermute | solution.py:171
  46.5 27.0 %collective-permute-start.18 = (bf16[96,3072]{1,0:T(8,128)(2,1)}, bf16[96,3072]{1,0:T(8,128)(2,1)S(1)}, u32[]{:S(2)}, u32[]{:S(2)}) collective-permute-start(bf16[96,3072]{1,0:T(8,128)(2,1)} %bitcast.4.refs_5_.refs_3_), channel_id=1, source_target_pairs={{0,2},{1,3},{2,0},{3,1},{4,6},{5,7},{6,4},{7,5},{8,10},{9,11},{10,... | collective-permute-start | bytes 1769480 | tf_op jit(solution)/shard_map/ppermute | solution.py:171
  47.1 27.9 %collective-permute-start.19 = (bf16[96,3072]{1,0:T(8,128)(2,1)}, bf16[96,3072]{1,0:T(8,128)(2,1)S(1)}, u32[]{:S(2)}, u32[]{:S(2)}) collective-permute-start(bf16[96,3072]{1,0:T(8,128)(2,1)} %bitcast.4.refs_5_.refs_3_), channel_id=1, source_target_pairs={{0,4},{1,5},{2,6},{3,7},{4,0},{5,1},{6,2},{7,3},{8,12},{9,13},{10,... | collective-permute-start | bytes 1769480 | tf_op jit(solution)/shard_map/ppermute | solution.py:171
  66.2 13.7 %collective-permute-start.14 = (bf16[384,384]{1,0:T(8,128)(2,1)S(1)}, bf16[384,384]{1,0:T(8,128)(2,1)S(1)}, u32[]{:S(2)}, u32[]{:S(2)}) collective-permute-start(bf16[384,384]{1,0:T(8,128)(2,1)S(1)} %slice.48), channel_id=1, source_target_pairs={{0,2},{1,3},{2,0},{3,1},{4,6},{5,7},{6,4},{7,5},{8,10},{9,11},{10,... | collective-permute-start | bytes 884744 | tf_op jit(solution)/shard_map/ppermute | solution.py:171
  68.7 12.8 %collective-permute-start.15 = (bf16[384,384]{1,0:T(8,128)(2,1)S(1)}, bf16[384,384]{1,0:T(8,128)(2,1)}, u32[]{:S(2)}, u32[]{:S(2)}) collective-permute-start(bf16[384,384]{1,0:T(8,128)(2,1)S(1)} %slice.49), channel_id=1, source_target_pairs={{0,4},{1,5},{2,6},{3,7},{4,0},{5,1},{6,2},{7,3},{8,12},{9,13},{10,... | collective-permute-start | bytes 884744 | tf_op jit(solution)/shard_map/ppermute | solution.py:171
  75.1 10.3 %collective-permute-start.23 = (bf16[48,3072]{1,0:T(8,128)(2,1)S(1)}, bf16[48,3072]{1,0:T(8,128)(2,1)S(1)}, u32[]{:S(2)}, u32[]{:S(2)}) collective-permute-start(bf16[48,3072]{1,0:T(8,128)(2,1)S(1)} %slice.50), channel_id=1, source_target_pairs={{0,2},{1,3},{2,0},{3,1},{4,6},{5,7},{6,4},{7,5},{8,10},{9,11},{10,... | collective-permute-start | bytes 884744 | tf_op jit(solution)/shard_map/ppermute | solution.py:171
  75.9 10.6 %collective-permute-start.24 = (bf16[48,3072]{1,0:T(8,128)(2,1)S(1)}, bf16[48,3072]{1,0:T(8,128)(2,1)S(1)}, u32[]{:S(2)}, u32[]{:S(2)}) collective-permute-start(bf16[48,3072]{1,0:T(8,128)(2,1)S(1)} %slice.51), channel_id=1, source_target_pairs={{0,4},{1,5},{2,6},{3,7},{4,0},{5,1},{6,2},{7,3},{8,12},{9,13},{10,... | collective-permute-start | bytes 884744 | tf_op jit(solution)/shard_map/ppermute | solution.py:171
  76.5 20.3 %collective-permute-start.11 = (bf16[768,384]{1,0:T(8,128)(2,1)}, bf16[768,384]{1,0:T(8,128)(2,1)S(1)}, u32[]{:S(2)}, u32[]{:S(2)}) collective-permute-start(bf16[768,384]{1,0:T(8,128)(2,1)} %refs_5_.2), channel_id=1, source_target_pairs={{0,1},{1,0},{2,3},{3,2},{4,5},{5,4},{6,7},{7,6},{8,9},{9,8},{10,11... | collective-permute-start | bytes 1769480 | tf_op jit(solution)/shard_map/ppermute | solution.py:171
  79.9 17.3 %collective-permute-start.12 = (bf16[768,384]{1,0:T(8,128)(2,1)}, bf16[768,384]{1,0:T(8,128)(2,1)S(1)}, u32[]{:S(2)}, u32[]{:S(2)}) collective-permute-start(bf16[768,384]{1,0:T(8,128)(2,1)} %collective-permute-done.9.refs_3_.refs_7_), channel_id=1, source_target_pairs={{0,1},{1,0},{2,3},{3,2},{4,5},{5,4},{6,7},{7,6},{8,9},{9,8},{10,11... | collective-permute-start | bytes 1769480 | tf_op jit(solution)/shard_map/ppermute | solution.py:171
  81.5 15.8 %collective-permute-start.13 = (bf16[768,384]{1,0:T(8,128)(2,1)}, bf16[768,384]{1,0:T(8,128)(2,1)S(1)}, u32[]{:S(2)}, u32[]{:S(2)}) collective-permute-start(bf16[768,384]{1,0:T(8,128)(2,1)} %collective-permute-done.10.refs_5_.refs_9_), channel_id=1, source_target_pairs={{0,1},{1,0},{2,3},{3,2},{4,5},{5,4},{6,7},{7,6},{8,9},{9,8},{10,11... | collective-permute-start | bytes 1769480 | tf_op jit(solution)/shard_map/ppermute | solution.py:171
  85.4 10.8 %collective-permute-start.16 = (bf16[384,384]{1,0:T(8,128)(2,1)S(1)}, bf16[384,384]{1,0:T(8,128)(2,1)}, u32[]{:S(2)}, u32[]{:S(2)}) collective-permute-start(bf16[384,384]{1,0:T(8,128)(2,1)S(1)} %collective-permute-done.14.refs_7_.refs_11_), channel_id=1, source_target_pairs={{0,1},{1,0},{2,3},{3,2},{4,5},{5,4},{6,7},{7,6},{8,9},{9,8},{10,11... | collective-permute-start | bytes 884744 | tf_op jit(solution)/shard_map/ppermute | solution.py:171
  86.6 10.0 %collective-permute-start.17 = (bf16[384,384]{1,0:T(8,128)(2,1)}, bf16[384,384]{1,0:T(8,128)(2,1)}, u32[]{:S(2)}, u32[]{:S(2)}) collective-permute-start(bf16[384,384]{1,0:T(8,128)(2,1)} %collective-permute-done.15.refs_8_.refs_12_), channel_id=1, source_target_pairs={{0,1},{1,0},{2,3},{3,2},{4,5},{5,4},{6,7},{7,6},{8,9},{9,8},{10,11... | collective-permute-start | bytes 884744 | tf_op jit(solution)/shard_map/ppermute | solution.py:171
  90.3 20.3 %all-to-all-start = ((bf16[8,96,768]{2,1,0:T(8,128)(2,1)}), bf16[8,96,768]{2,1,0:T(8,128)(2,1)S(1)}, u32[]{:S(2)}, u32[]{:S(2)}) async-start(bf16[8,96,768]{2,1,0:T(8,128)(2,1)} %bitcast.5), calls=%async_computation | async-start | bytes 2359296 | tf_op jit(solution)/shard_map/all_to_all | solution.py:234
  93.8 98.3 %all-gather.5.cloned.1.call-start = ((), (), s32[]{:S(2)}) async-start(), calls=%async_computation.7 | async-start | bytes 3932160 | tf_op jit(solution)/shard_map/all_gather | solution.py:886
  96.0 209.5 %reduce-scatter.3.cloned.1.call-start = ((), (), s32[]{:S(2)}) async-start(), calls=%async_computation.8 | async-start | bytes 7864320 | tf_op jit(solution)/shard_map/reduce_scatter | solution.py:920
  96.2 11.6 %collective-permute-start.21 = (bf16[96,3072]{1,0:T(8,128)(2,1)}, bf16[96,3072]{1,0:T(8,128)(2,1)}, u32[]{:S(2)}, u32[]{:S(2)}) collective-permute-start(bf16[96,3072]{1,0:T(8,128)(2,1)} %copy-done.79), channel_id=1, source_target_pairs={{0,1},{1,0},{2,3},{3,2},{4,5},{5,4},{6,7},{7,6},{8,9},{9,8},{10,11... | collective-permute-start | bytes 1769480 | tf_op jit(solution)/shard_map/ppermute | solution.py:171
  96.6 11.9 %collective-permute-start.22 = (bf16[96,3072]{1,0:T(8,128)(2,1)}, bf16[96,3072]{1,0:T(8,128)(2,1)}, u32[]{:S(2)}, u32[]{:S(2)}) collective-permute-start(bf16[96,3072]{1,0:T(8,128)(2,1)} %copy-done.80), channel_id=1, source_target_pairs={{0,1},{1,0},{2,3},{3,2},{4,5},{5,4},{6,7},{7,6},{8,9},{9,8},{10,11... | collective-permute-start | bytes 1769480 | tf_op jit(solution)/shard_map/ppermute | solution.py:171
  96.8 11.0 %collective-permute-start.20 = (bf16[96,3072]{1,0:T(8,128)(2,1)}, bf16[96,3072]{1,0:T(8,128)(2,1)}, u32[]{:S(2)}, u32[]{:S(2)}) collective-permute-start(bf16[96,3072]{1,0:T(8,128)(2,1)} %bitcast.4.refs_5_.refs_3_), channel_id=1, source_target_pairs={{0,1},{1,0},{2,3},{3,2},{4,5},{5,4},{6,7},{7,6},{8,9},{9,8},{10,11... | collective-permute-start | bytes 1769480 | tf_op jit(solution)/shard_map/ppermute | solution.py:171
  97.1 10.6 %collective-permute-start.25 = (bf16[48,3072]{1,0:T(8,128)(2,1)S(1)}, bf16[48,3072]{1,0:T(8,128)(2,1)S(1)}, u32[]{:S(2)}, u32[]{:S(2)}) collective-permute-start(bf16[48,3072]{1,0:T(8,128)(2,1)S(1)} %collective-permute-done.23.refs_11_.refs_9_), channel_id=1, source_target_pairs={{0,1},{1,0},{2,3},{3,2},{4,5},{5,4},{6,7},{7,6},{8,9},{9,8},{10,11... | collective-permute-start | bytes 884744 | tf_op jit(solution)/shard_map/ppermute | solution.py:171
  97.4 10.4 %collective-permute-start.26 = (bf16[48,3072]{1,0:T(8,128)(2,1)}, bf16[48,3072]{1,0:T(8,128)(2,1)S(1)}, u32[]{:S(2)}, u32[]{:S(2)}) collective-permute-start(bf16[48,3072]{1,0:T(8,128)(2,1)} %copy-done.85), channel_id=1, source_target_pairs={{0,1},{1,0},{2,3},{3,2},{4,5},{5,4},{6,7},{7,6},{8,9},{9,8},{10,11... | collective-permute-start | bytes 884744 | tf_op jit(solution)/shard_map/ppermute | solution.py:171
  208.9 22.9 %copy-start.26 = (s32[384,1]{1,0:T(8,128)S(1)}, s32[384,1]{1,0:T(8,128)}, u32[]{:S(2)}) copy-start(s32[384,1]{1,0:T(8,128)} %copy.27.refs_0_.refs_4_.refs_1_) | copy-start | bytes 4612
  208.9 22.9 %copy-start.27 = (f32[16,768]{1,0:T(8,128)S(1)}, f32[16,768]{1,0:T(8,128)}, u32[]{:S(2)}) copy-start(f32[16,768]{1,0:T(8,128)} %get-tuple-element.98.refs_11_.refs_2_.refs_4_.refs_3_) | copy-start | bytes 147460
  242.6 20.4 %collective-permute-start.27 = (bf16[4,96,3072]{2,1,0:T(8,128)(2,1)}, bf16[4,96,3072]{2,1,0:T(8,128)(2,1)}, u32[]{:S(2)}, u32[]{:S(2)}) collective-permute-start(bf16[4,96,3072]{2,1,0:T(8,128)(2,1)} %get-tuple-element.129), channel_id=1, source_target_pairs={{0,1},{1,0},{2,3},{3,2},{4,5},{5,4},{6,7},{7,6},{8,9},{9,8},{10,11... | collective-permute-start | bytes 7077896 | tf_op jit(solution)/shard_map/ppermute | solution.py:171
  242.7 20.3 %all-to-all-start.3 = ((bf16[8,96,768]{2,1,0:T(8,128)(2,1)}), bf16[8,96,768]{2,1,0:T(8,128)(2,1)S(1)}, u32[]{:S(2)}, u32[]{:S(2)}) async-start(bf16[8,96,768]{2,1,0:T(8,128)(2,1)} %bitcast.15), calls=%async_computation.3 | async-start | bytes 2359296 | tf_op jit(solution)/shard_map/all_to_all | solution.py:234
  246.2 194.5 %reduce-scatter.5.cloned.1.call-start = ((), (), s32[]{:S(2)}) async-start(), calls=%async_computation.9 | async-start | bytes 3932160 | tf_op jit(solution)/shard_map/reduce_scatter | solution.py:920
  258.2 32.6 %collective-permute-start.30 = (bf16[4,384,768]{2,1,0:T(8,128)(2,1)}, bf16[4,384,768]{2,1,0:T(8,128)(2,1)}, u32[]{:S(2)}, u32[]{:S(2)}) collective-permute-start(bf16[4,384,768]{2,1,0:T(8,128)(2,1)} %get-tuple-element.143), channel_id=1, source_target_pairs={{0,1},{1,0},{2,3},{3,2},{4,5},{5,4},{6,7},{7,6},{8,9},{9,8},{10,11... | collective-permute-start | bytes 7077896 | tf_op jit(solution)/shard_map/ppermute | solution.py:171
  276.9 13.9 %collective-permute-start.31 = (bf16[4,96,768]{2,1,0:T(8,128)(2,1)S(1)}, bf16[4,96,768]{2,1,0:T(8,128)(2,1)S(1)}, u32[]{:S(2)}, u32[]{:S(2)}) collective-permute-start(bf16[4,96,768]{2,1,0:T(8,128)(2,1)S(1)} %get-tuple-element.144), channel_id=1, source_target_pairs={{0,1},{1,0},{2,3},{3,2},{4,5},{5,4},{6,7},{7,6},{8,9},{9,8},{10,11... | collective-permute-start | bytes 1769480 | tf_op jit(solution)/shard_map/ppermute | solution.py:171
  277.0 16.2 %collective-permute-start.28 = (bf16[2,48,3072]{2,1,0:T(8,128)(2,1)S(1)}, bf16[2,48,3072]{2,1,0:T(8,128)(2,1)S(1)}, u32[]{:S(2)}, u32[]{:S(2)}) collective-permute-start(bf16[2,48,3072]{2,1,0:T(8,128)(2,1)S(1)} %get-tuple-element.138), channel_id=1, source_target_pairs={{0,2},{1,3},{2,0},{3,1},{4,6},{5,7},{6,4},{7,5},{8,10},{9,11},{10,... | collective-permute-start | bytes 1769480 | tf_op jit(solution)/shard_map/ppermute | solution.py:171
  277.7 15.6 %collective-permute-start.29 = (bf16[2,48,3072]{2,1,0:T(8,128)(2,1)S(1)}, bf16[2,48,3072]{2,1,0:T(8,128)(2,1)S(1)}, u32[]{:S(2)}, u32[]{:S(2)}) collective-permute-start(bf16[2,48,3072]{2,1,0:T(8,128)(2,1)S(1)} %get-tuple-element.140), channel_id=1, source_target_pairs={{0,4},{1,5},{2,6},{3,7},{4,0},{5,1},{6,2},{7,3},{8,12},{9,13},{10,... | collective-permute-start | bytes 1769480 | tf_op jit(solution)/shard_map/ppermute | solution.py:171
  305.4 5.5 %collective-permute-start.32 = (bf16[4,288,768]{2,1,0:T(8,128)(2,1)}, bf16[4,288,768]{2,1,0:T(8,128)(2,1)}, u32[]{:S(2)}, u32[]{:S(2)}) collective-permute-start(bf16[4,288,768]{2,1,0:T(8,128)(2,1)} %get-tuple-element.149), channel_id=1, source_target_pairs={{0,1},{1,0},{2,3},{3,2},{4,5},{5,4},{6,7},{7,6},{8,9},{9,8},{10,11... | collective-permute-start | bytes 5308424 | tf_op jit(solution)/shard_map/ppermute | solution.py:171
  305.5 28.1 %collective-permute-start.36 = (bf16[2,240,768]{2,1,0:T(8,128)(2,1)}, bf16[2,240,768]{2,1,0:T(8,128)(2,1)S(1)}, u32[]{:S(2)}, u32[]{:S(2)}) collective-permute-start(bf16[2,240,768]{2,1,0:T(8,128)(2,1)} %copy-done.40), channel_id=1, source_target_pairs={{0,2},{1,3},{2,0},{3,1},{4,6},{5,7},{6,4},{7,5},{8,10},{9,11},{10,... | collective-permute-start | bytes 2211848 | tf_op jit(solution)/shard_map/ppermute | solution.py:171
  307.0 26.6 %collective-permute-start.37 = (bf16[2,240,768]{2,1,0:T(8,128)(2,1)}, bf16[2,240,768]{2,1,0:T(8,128)(2,1)S(1)}, u32[]{:S(2)}, u32[]{:S(2)}) collective-permute-start(bf16[2,240,768]{2,1,0:T(8,128)(2,1)} %copy-done.39), channel_id=1, source_target_pairs={{0,4},{1,5},{2,6},{3,7},{4,0},{5,1},{6,2},{7,3},{8,12},{9,13},{10,... | collective-permute-start | bytes 2211848 | tf_op jit(solution)/shard_map/ppermute | solution.py:171
  308.5 24.3 %collective-permute-start.38 = (bf16[48,3072]{1,0:T(8,128)(2,1)}, bf16[48,3072]{1,0:T(8,128)(2,1)S(1)}, u32[]{:S(2)}, u32[]{:S(2)}) collective-permute-start(bf16[48,3072]{1,0:T(8,128)(2,1)} %copy-done.52), channel_id=1, source_target_pairs={{0,4},{1,5},{2,6},{3,7},{4,0},{5,1},{6,2},{7,3},{8,12},{9,13},{10,... | collective-permute-start | bytes 884744 | tf_op jit(solution)/shard_map/ppermute | solution.py:171
  309.1 1.3 collective-permute-start.33
  310.4 23.1 %collective-permute-start.39 = (bf16[48,3072]{1,0:T(8,128)(2,1)}, bf16[48,3072]{1,0:T(8,128)(2,1)S(1)}, u32[]{:S(2)}, u32[]{:S(2)}) collective-permute-start(bf16[48,3072]{1,0:T(8,128)(2,1)} %copy-done.51), channel_id=1, source_target_pairs={{0,2},{1,3},{2,0},{3,1},{4,6},{5,7},{6,4},{7,5},{8,10},{9,11},{10,... | collective-permute-start | bytes 884744 | tf_op jit(solution)/shard_map/ppermute | solution.py:171
  312.8 33.1 %collective-permute-start.35 = (bf16[2,160,768]{2,1,0:T(8,128)(2,1)S(1)}, bf16[2,160,768]{2,1,0:T(8,128)(2,1)S(1)}, u32[]{:S(2)}, u32[]{:S(2)}) collective-permute-start(bf16[2,160,768]{2,1,0:T(8,128)(2,1)S(1)} %get-tuple-element.154), channel_id=1, source_target_pairs={{0,4},{1,5},{2,6},{3,7},{4,0},{5,1},{6,2},{7,3},{8,12},{9,13},{10,... | collective-permute-start | bytes 1474568 | tf_op jit(solution)/shard_map/ppermute | solution.py:171
  332.9 13.1 %collective-permute-start.34 = (bf16[2,144,768]{2,1,0:T(8,128)(2,1)S(1)}, bf16[2,144,768]{2,1,0:T(8,128)(2,1)S(1)}, u32[]{:S(2)}, u32[]{:S(2)}) collective-permute-start(bf16[2,144,768]{2,1,0:T(8,128)(2,1)S(1)} %get-tuple-element.152), channel_id=1, source_target_pairs={{0,2},{1,3},{2,0},{3,1},{4,6},{5,7},{6,4},{7,5},{8,10},{9,11},{10,... | collective-permute-start | bytes 1327112 | tf_op jit(solution)/shard_map/ppermute | solution.py:171
  335.1 16.2 %collective-permute-start.42 = (bf16[240,768]{1,0:T(8,128)(2,1)S(1)}, bf16[240,768]{1,0:T(8,128)(2,1)S(1)}, u32[]{:S(2)}, u32[]{:S(2)}) collective-permute-start(bf16[240,768]{1,0:T(8,128)(2,1)S(1)} %get-tuple-element.166), channel_id=1, source_target_pairs={{0,4},{1,5},{2,6},{3,7},{4,0},{5,1},{6,2},{7,3},{8,12},{9,13},{10,... | collective-permute-start | bytes 1105928 | tf_op jit(solution)/shard_map/ppermute | solution.py:171
  336.7 17.2 %collective-permute-start.43 = (bf16[240,768]{1,0:T(8,128)(2,1)S(1)}, bf16[240,768]{1,0:T(8,128)(2,1)S(1)}, u32[]{:S(2)}, u32[]{:S(2)}) collective-permute-start(bf16[240,768]{1,0:T(8,128)(2,1)S(1)} %get-tuple-element.168), channel_id=1, source_target_pairs={{0,2},{1,3},{2,0},{3,1},{4,6},{5,7},{6,4},{7,5},{8,10},{9,11},{10,... | collective-permute-start | bytes 1105928 | tf_op jit(solution)/shard_map/ppermute | solution.py:171
  338.2 28.4 %collective-permute-start.46 = (bf16[96,3072]{1,0:T(8,128)(2,1)S(1)}, bf16[96,3072]{1,0:T(8,128)(2,1)S(1)}, u32[]{:S(2)}, u32[]{:S(2)}) collective-permute-start(bf16[96,3072]{1,0:T(8,128)(2,1)S(1)} %fold_last.3.refs_4_.refs_0_), channel_id=1, source_target_pairs={{0,8},{24,16},{1,9},{25,17},{2,10},{26,18},{3,11},{27,19},{4,12},{... | collective-permute-start | bytes 1769480 | tf_op jit(solution)/shard_map/ppermute | solution.py:315
  346.2 10.7 %collective-permute-start.41 = (bf16[160,768]{1,0:T(8,128)(2,1)S(1)}, bf16[160,768]{1,0:T(8,128)(2,1)S(1)}, u32[]{:S(2)}, u32[]{:S(2)}) collective-permute-start(bf16[160,768]{1,0:T(8,128)(2,1)S(1)} %get-tuple-element.165), channel_id=1, source_target_pairs={{0,2},{1,3},{2,0},{3,1},{4,6},{5,7},{6,4},{7,5},{8,10},{9,11},{10,... | collective-permute-start | bytes 737288 | tf_op jit(solution)/shard_map/ppermute | solution.py:171
  346.8 8.6 %collective-permute-start.40 = (bf16[144,768]{1,0:T(8,128)(2,1)S(1)}, bf16[144,768]{1,0:T(8,128)(2,1)S(1)}, u32[]{:S(2)}, u32[]{:S(2)}) collective-permute-start(bf16[144,768]{1,0:T(8,128)(2,1)S(1)} %get-tuple-element.163), channel_id=1, source_target_pairs={{0,4},{1,5},{2,6},{3,7},{4,0},{5,1},{6,2},{7,3},{8,12},{9,13},{10,... | collective-permute-start | bytes 663560 | tf_op jit(solution)/shard_map/ppermute | solution.py:171
  354.1 38.7 %collective-permute-start.45 = (bf16[480,768]{1,0:T(8,128)(2,1)S(1)}, bf16[480,768]{1,0:T(8,128)(2,1)S(1)}, u32[]{:S(2)}, u32[]{:S(2)}) collective-permute-start(bf16[480,768]{1,0:T(8,128)(2,1)S(1)} %fold_last.4.refs_4_.refs_0_), channel_id=1, source_target_pairs={{0,8},{24,16},{1,9},{25,17},{2,10},{26,18},{3,11},{27,19},{4,12},{... | collective-permute-start | bytes 2211848 | tf_op jit(solution)/shard_map/ppermute | solution.py:315
  367.8 8.3 %collective-permute-start.47 = (bf16[96,3072]{1,0:T(8,128)(2,1)S(1)}, bf16[96,3072]{1,0:T(8,128)(2,1)S(1)}, u32[]{:S(2)}, u32[]{:S(2)}) collective-permute-start(bf16[96,3072]{1,0:T(8,128)(2,1)S(1)} %joined.6.refs_0_.refs_2_), channel_id=1, source_target_pairs={{8,16},{16,8},{9,17},{17,9},{10,18},{18,10},{11,19},{19,11},{12,20... | collective-permute-start | bytes 1769480 | tf_op jit(solution)/shard_map/ppermute | solution.py:315
  368.5 33.2 %collective-permute-start.44 = (bf16[304,768]{1,0:T(8,128)(2,1)S(1)}, bf16[304,768]{1,0:T(8,128)(2,1)S(1)}, u32[]{:S(2)}, u32[]{:S(2)}) collective-permute-start(bf16[304,768]{1,0:T(8,128)(2,1)S(1)} %fold_last.5.refs_4_.refs_0_), channel_id=1, source_target_pairs={{0,8},{24,16},{1,9},{25,17},{2,10},{26,18},{3,11},{27,19},{4,12},{... | collective-permute-start | bytes 1400840 | tf_op jit(solution)/shard_map/ppermute | solution.py:315
  393.0 10.3 %collective-permute-start.49 = (bf16[480,768]{1,0:T(8,128)(2,1)S(1)}, bf16[480,768]{1,0:T(8,128)(2,1)S(1)}, u32[]{:S(2)}, u32[]{:S(2)}) collective-permute-start(bf16[480,768]{1,0:T(8,128)(2,1)S(1)} %joined.8.refs_2_.refs_0_), channel_id=1, source_target_pairs={{8,16},{16,8},{9,17},{17,9},{10,18},{18,10},{11,19},{19,11},{12,20... | collective-permute-start | bytes 2211848 | tf_op jit(solution)/shard_map/ppermute | solution.py:315
  393.7 18.7 %collective-permute-start.52 = (bf16[96,3072]{1,0:T(8,128)(2,1)S(1)}, bf16[96,3072]{1,0:T(8,128)(2,1)}, u32[]{:S(2)}, u32[]{:S(2)}) collective-permute-start(bf16[96,3072]{1,0:T(8,128)(2,1)S(1)} %joined.7.refs_2_), channel_id=1, source_target_pairs={{8,0},{16,24},{9,1},{17,25},{10,2},{18,26},{11,3},{19,27},{12,4},{... | collective-permute-start | bytes 1769480 | tf_op jit(solution)/shard_map/ppermute | solution.py:315
  401.8 1.6 collective-permute-start.48
  404.6 34.0 %collective-permute-start.50 = (bf16[304,768]{1,0:T(8,128)(2,1)S(1)}, bf16[304,768]{1,0:T(8,128)(2,1)S(1)}, u32[]{:S(2)}, u32[]{:S(2)}) collective-permute-start(bf16[304,768]{1,0:T(8,128)(2,1)S(1)} %joined.11.refs_2_), channel_id=1, source_target_pairs={{8,0},{16,24},{9,1},{17,25},{10,2},{18,26},{11,3},{19,27},{12,4},{... | collective-permute-start | bytes 1400840 | tf_op jit(solution)/shard_map/ppermute | solution.py:315
  414.5 26.2 %copy-start.33 = (bf16[1536,512]{1,0:T(8,128)(2,1)S(1)}, bf16[1536,512]{1,0:T(8,128)(2,1)}, u32[]{:S(2)}) copy-start(bf16[1536,512]{1,0:T(8,128)(2,1)} %reduce-scatter.3.cloned.1.call-done) | copy-start | bytes 4718596
  414.5 36.1 %collective-permute-start.51 = (bf16[480,768]{1,0:T(8,128)(2,1)S(1)}, bf16[480,768]{1,0:T(8,128)(2,1)}, u32[]{:S(2)}, u32[]{:S(2)}) collective-permute-start(bf16[480,768]{1,0:T(8,128)(2,1)S(1)} %joined.10.refs_2_.refs_0_), channel_id=1, source_target_pairs={{8,0},{16,24},{9,1},{17,25},{10,2},{18,26},{11,3},{19,27},{12,4},{... | collective-permute-start | bytes 2211848 | tf_op jit(solution)/shard_map/ppermute | solution.py:315
  (83 other events, 437.5 us)
Sparse Core Ops, SparseCore 0:
  10.2 118.0 all-gather.2
  130.4 61.7 all-gather.4
  194.5 109.3 reduce-scatter.2
  306.1 83.7 reduce-scatter.4

commit v2 on v1

--- a/solution.py
+++ b/solution.py
@@ -14,11 +14,11 @@
 I32 = jnp.int32
 ROOT = 0.7978845608028654
 COST = dict(
-    prepare=3, attend=16, widen=9, dispatch=10, expert_rows=4, expert=20, gate_back=10, widen_back=12, fold=1,
-    second_back=14, attend_back=5, fold_again=1, project_back=2, tokens_back=2, fold_last=1, joined=1,
+    prepare=3, attend=16, widen=9, dispatch=10, expert_rows=4, expert=20, expert_last=10, expert_grads=6, gate_back=10, widen_back=12, fold=1,
+    second_back=17, attend_back=2, fold_again=1, fold_wait=12, project_back=2, tokens_back=2, fold_last=1, joined=1,
     combine=1, finish=1, settle=1,
 )
-WIDE = ("attend", "widen", "dispatch", "expert", "widen_back")
+WIDE = ("attend", "widen", "dispatch", "expert", "expert_last", "widen_back", "settle")
 VMEM_LIMIT = 60 * 1024 * 1024
 
 
@@ -282,7 +282,7 @@
     def across(self, kept):
         return [self.hop(kept[1], 2), self.hop(kept[3], 4)] if self.cube else []
 
-    def fold_again(self, kept, got):
+    def fold_again(self, kept, got, name="fold_again"):
         if not self.cube:
             return kept
 
@@ -293,7 +293,7 @@
 
         outs = [jax.ShapeDtypeStruct(a.shape[1:], BF) for a in (kept[0], kept[0], kept[2], kept[2])]
         args = [kept[0], got[0], kept[2], got[1]]
-        return list(call(kernel, outs, args, "vvvv", [], "fold_again", 0, 0))
+        return list(call(kernel, outs, args, "vvvv", [], name, 0, 0))
 
     def across_again(self, kept):
         return [self.hop(kept[1], 4), self.hop(kept[3], 2)] if self.cube else []
@@ -336,9 +336,19 @@
     def settled(self, value, got):
         if not self.line:
             return lax.psum(value, "dp").astype(F32)
-        place = lax.axis_index("dp")
-        return jnp.where((place == 1) | (place == 2), value, got[0]).astype(F32)
-
+
+        def kernel(mine, other, out):
+            place = lax.axis_index("dp")
+
+            def write(ref):
+                out[...] = ref[...].astype(F32)
+
+            middle = (place == 1) | (place == 2)
+            pl.when(middle)(lambda: write(mine))
+            pl.when(jnp.logical_not(middle))(lambda: write(other))
+
+        outs = [jax.ShapeDtypeStruct(value.shape, F32)]
+        return call(kernel, outs, [value, got[0]], "vv", [], "settle", 0, 0)[0]
 
     def settled_across(self, value, got, units):
         if not self.line:
@@ -570,9 +580,12 @@
         carried = take(2) if started else None
         (cot_ref,) = take(1) if last else (None,)
         (weight_ref,) = take(1)
-        (w_grads,) = take(1)
-        outs = take(2)
-        held, grad_held, sems, out_sems, out_sum, row_sum = refs
+        if last:
+            outs, (acts, pre_grads) = take(2), take(2)
+            held, sems, out_sum, row_sum = refs
+        else:
+            (w_grads,), outs = take(1), take(2)
+            held, sems, out_sum, row_sum, grad_held, out_sems = refs
         entering = [pltpu.make_async_copy(weight_ref.at[i], held.at[i], sems.at[i]) for i in range(m)]
         for copy in entering:
             copy.start()
@@ -591,11 +604,15 @@
                 row_part, out_part = row_part + row_sum[...], out_part + out_sum[...]
             row_sum[...] = row_part
             out_sum[...] = out_part
-            grad_held[i, 0] = mm(rows_across[...], pre_grad).astype(BF)
-            grad_held[i, 1] = mm(grads_across[...], act).astype(BF)
-            copy = pltpu.make_async_copy(grad_held.at[i], w_grads.at[i], out_sems.at[i])
-            copy.start()
-            leaving.append(copy)
+            if last:
+                acts[i] = act
+                pre_grads[i] = pre_grad
+            else:
+                grad_held[i, 0] = mm(rows_across[...], pre_grad).astype(BF)
+                grad_held[i, 1] = mm(grads_across[...], act).astype(BF)
+                copy = pltpu.make_async_copy(grad_held.at[i], w_grads.at[i], out_sems.at[i])
+                copy.start()
+                leaving.append(copy)
         if last:
             result = out_sum[...].astype(BF)
             gate_grad = jnp.sum(cot_ref[...].astype(F32) * result.astype(F32), axis=1, keepdims=True)
@@ -610,17 +627,29 @@
     shape = jax.ShapeDtypeStruct
     args = [rows, grads, *across] + (sums if started else []) + ([cot] if last else [])
     spaces = "v" * len(args) + "a"
-    outs = [shape((m, 2, width, wide), BF)]
-    if last:
-        outs += [shape((total, width + EXTRA), BF), shape((total, width), BF)]
-    else:
-        outs += [shape((total, width), F32)] * 2
     scratch = [
-        pltpu.VMEM((m, 2, width, wide), BF), pltpu.VMEM((m, 2, width, wide), BF),
-        pltpu.SemaphoreType.DMA((m,)), pltpu.SemaphoreType.DMA((m,)),
+        pltpu.VMEM((m, 2, width, wide), BF), pltpu.SemaphoreType.DMA((m,)),
         pltpu.VMEM((total, width), F32), pltpu.VMEM((total, width), F32),
     ]
+    if last:
+        outs = [shape((total, width + EXTRA), BF), shape((total, width), BF)] + [shape((m, total, wide), BF)] * 2
+        return call(kernel, outs, args + [weights], spaces, scratch, "expert_last", 0, 0)
+    outs = [shape((m, 2, width, wide), BF)] + [shape((total, width), F32)] * 2
+    scratch += [pltpu.VMEM((m, 2, width, wide), BF), pltpu.SemaphoreType.DMA((m,))]
     return call(kernel, outs, args + [weights], spaces, scratch, "expert", 0, 0, [], "avv")
+
+
+def expert_grads(across, acts, pre_grads):
+    m, _, wide = acts.shape
+    width = across[0].shape[0]
+
+    def kernel(rows_across, grads_across, acts_ref, pre_ref, out):
+        for i in range(m):
+            out[i, 0] = mm(rows_across[...], pre_ref[i]).astype(BF)
+            out[i, 1] = mm(grads_across[...], acts_ref[i]).astype(BF)
+
+    outs = [jax.ShapeDtypeStruct((m, 2, width, wide), BF)]
+    return call(kernel, outs, [*across, acts, pre_grads], "vvvv", [], "expert_grads", 0, 0)[0]
 
 
 def combine(returned, slots, hidden, gates):
@@ -911,17 +940,19 @@
 
     sums, expert_sums = None, []
     for c, whole in enumerate(gathered):
-        last = c == len(chunks) - 1
-        w_grads, *sums = expert(rows, grads, across, whole, sums, cots if last else None)
-        expert_sums.append(w_grads)
-    back, results = sums
+        if c < len(chunks) - 1:
+            w_grads, *sums = expert(rows, grads, across, whole, sums, None)
+            expert_sums.append(w_grads)
+        else:
+            back, results, acts, pre_grads = expert(rows, grads, across, whole, sums, cots)
+    back = links.exchange(back)
+    expert_sums.append(expert_grads(across, acts, pre_grads))
 
     def own_sum(grads):
         sums = lax.psum_scatter(grads.reshape(-1, grads.shape[-1]), "dp", scatter_dimension=0, tiled=True)
         return sums.reshape(grads.shape[1:])
 
     summed = [own_sum(expert_sums[0])]
-    back = links.exchange(back)
     returned = links.exchange(results, [back])
 
     hidden_grad, down_in, small_3, centroid_grad, sums_down = gate_back(
@@ -949,12 +980,12 @@
         summed.append(own_sum(links.gated(grads, summed + [sums_small[0]])))
     sums_in = project_back(links, projected_grad, first_in, [])
     twin_in = links.twins(sums_in)
+    up = links.fold_again(up, up_got, "fold_wait")
+    up_got = links.across_again(up)
     inner = links.fold([sums_in, sums_small], twin_in + twin_small)
     inner_got = links.across(inner)
     down = links.fold_last(down, down_got)
     down_got = links.inward(down)
-    up = links.fold_again(up, up_got)
-    up_got = links.across_again(up)
     inner = links.fold_again(inner, inner_got)
     inner_got = links.across_again(inner)
     up = links.fold_last(up, up_got)

time: 469 us -> 474 us (1.011)
  blocking collectives: 45.4 us -> 22.5 us
  local copies, waits for them, and re-layouts: 41.6 us -> 54.2 us
  waiting for transfers between devices: 156 us -> 166 us
  starting transfers between devices: 56 us -> 61.2 us
    all_to_all x2 -> x1, blocking collectives: 45.4 us -> 22.5 us  [exchange(): lax.all_to_all(blocks, 'expert', split_axis=0, concat_axis=0, tiled=True)]
    unnamed x177 -> x213, local copies, waits for them, and re-layouts: 30.1 us -> 40.9 us
    all_to_all x2 -> x3, waiting for transfers between devices: 6.37 us -> 16.6 us  [exchange(): lax.all_to_all(blocks, 'expert', split_axis=0, concat_axis=0, tiled=True)]
    all_to_all x2 -> x3, starting transfers between devices: 7.14 us -> 11.6 us  [exchange(): lax.all_to_all(blocks, 'expert', split_axis=0, concat_axis=0, tiled=True)]
    pallas_call x31 -> x34, Pallas kernels: 142 us -> 144 us  [call(): pl.pallas_call(body, out_shape=outs, in_specs=[pl.BlockSpec(memory_space=...]
  transfers between devices with their start and end apart: 59 -> 60, of which waited for: 23 -> 24; matrix products, arithmetic and copies ran while one was open for 3% -> 2% of each run, Pallas kernels for 30% -> 30%
where the time goes in v2:
time: 474 us; the launch traced here: 467 us
  waiting for transfers between devices  166 us (35%)
  Pallas kernels  144 us (30%)
  starting transfers between devices  61.2 us (13%)
  local copies, waits for them, and re-layouts  54.2 us (11%)
  blocking collectives  22.5 us (5%)
  between operations  15.3 us (3%)
    pallas_call x34, Pallas kernels, call(): pl.pallas_call(body, out_shape=outs, in_specs=[pl.BlockSpec(memory_space=...  144 us
    ppermute x44, waiting for transfers between devices, hop(): return lax.ppermute(value, 'expert', [(i, i ^ bit) for i in range(self.n)])  65.1 us
    ppermute x9, waiting for transfers between devices, along(): return lax.ppermute(value, 'dp', pairs)  65 us
    unnamed x213, local copies, waits for them, and re-layouts  40.9 us
    ppermute x44, starting transfers between devices, hop(): return lax.ppermute(value, 'expert', [(i, i ^ bit) for i in range(self.n)])  32.2 us
    all_to_all x1, blocking collectives, exchange(): lax.all_to_all(blocks, 'expert', split_axis=0, concat_axis=0, tiled=True)  22.5 us
    all_gather x2, waiting for transfers between devices, on_device(): whole = lax.all_gather(chunk(start, wide), 'dp', axis=0, tiled=True)  18.7 us
    ppermute x9, starting transfers between devices, along(): return lax.ppermute(value, 'dp', pairs)  17 us
  transfers between devices with their start and end apart: 60, of which 24 were waited for; matrix products, arithmetic and copies ran while one was open for 2% of the time, Pallas kernels for 30%

profile of v2, /device:TPU:0, one launch (start us, length us, event | category | flops | bytes accessed | tf_op | source)
XLA Modules:
  0.0 466.5 jit_solution(12027450128127401154)
XLA Ops:
  11.2 3.0 collective-permute-start.1
  14.2 1.5 collective-permute-start.3
  15.7 12.3 %collective-permute-done.1.refs_5_.refs_13_.refs_23_.refs_7_.refs_9_ = bf16[400,768]{1,0:T(8,128)(2,1)S(1)} collective-permute-done((bf16[400,768]{1,0:T(8,128)(2,1)S(1)}, bf16[400,768]{1,0:T(8,128)(2,1)S(1)}, u32[]{:S(2)}, u32[]{:S(2)}) %collective-permute-start.1) | collective-permute-done | bytes 614432 | tf_op jit(solution)/shard_map/ppermute | solution.py:171
  28.9 1.8 collective-permute-start.5
  31.4 1.5 collective-permute-start.7
  35.1 4.4 collective-permute-done.7.refs_17_.refs_13_
  42.0 1.9 prepare.1
  44.6 1.5 collective-permute-start.9
  47.2 1.4 collective-permute-start.19
  49.4 15.9 %attend.1 = (bf16[384,768]{1,0:T(8,128)(2,1)}, bf16[384,2304]{1,0:T(8,128)(2,1)}, bf16[384,768]{1,0:T(8,128)(2,1)}, f32[384,128]{1,0:T(8,128)}, f32[384,768]{1,0...) custom-call(bf16[384,768]{1,0:T(8,128)(2,1)} %refs_1_.3, s32[384,1]{1,0:T(8,128)} %copy.28.refs_1_.refs_3_, ...), custom_call_target="tpu_custom_call" | custom-call | flops 18400000000 | bytes 1000 | tf_op jit(solution)/shard_map/attend/pallas_call | solution.py:111
  66.5 1.6 collective-permute-start.14
  68.7 5.0 %collective-permute-done.18.refs_7_.refs_5_ = bf16[96,3072]{1,0:T(8,128)(2,1)S(1)} collective-permute-done((bf16[96,3072]{1,0:T(8,128)(2,1)}, bf16[96,3072]{1,0:T(8,128)(2,1)S(1)}, u32[]{:S(2)}, u32[]{:S(2)}) %collective-permute-start.18) | collective-permute-done | bytes 589856 | tf_op jit(solution)/shard_map/ppermute | solution.py:171
  73.6 1.5 collective-permute-done.19.refs_9_.refs_7_
  76.5 3.5 collective-permute-done.14.refs_7_.refs_11_
  80.0 1.6 collective-permute-done.15.refs_8_.refs_12_
  81.6 3.9 collective-permute-done.23.refs_11_.refs_9_
  87.4 1.8 slice.65
  89.2 1.8 slice.64
  91.0 3.6 all-to-all-start
  94.6 2.0 pad_maximum_fusion.1
  98.8 9.5 %widen.1 = (bf16[384,3072]{1,0:T(8,128)(2,1)}, bf16[384,3072]{1,0:T(8,128)(2,1)}) custom-call(bf16[384,768]{1,0:T(8,128)(2,1)} %get-tuple-element.97.refs_0_.refs_2_, bf16[768,384]{1,0:T(8,128)(2,1)} %refs_5_.2, bf16[768,384]{1,0:T(8,128)(2,1)} %copy-done.54, bf16[768,384]{1,0:T(8,128)(2,1)} %copy-done.32, bf16[768,384]{1,0:T(8,128)(2,1)} %copy-done.56, ...), custom_call_target="tpu_custom_call" | custom-call | flops 10350000128 | bytes 1000 | tf_op jit(solution)/shard_map/widen/pallas_call | solution.py:111
  108.4 2.9 all-to-all-done
  112.3 9.8 %dispatch.1 = (f32[384,768]{1,0:T(8,128)}, f32[384,1]{1,0:T(8,128)}, bf16[768,896]{1,0:T(8,128)(2,1)}) custom-call(bf16[384,3072]{1,0:T(8,128)(2,1)} %get-tuple-element.103.refs_0_.refs_16_.refs_6_, f32[384,768]{1,0:T(8,128)} %get-tuple-element.104.refs_1_, f32[16,768]{1,0:T(8,128)} %get-tuple-element.99.refs_11_.refs_2_.refs_4_.refs_3_, ...), custom_call_target="tpu_custom_call" | custom-call | flops 11500000256 | bytes 1000 | tf_op jit(solution)/shard_map/dispatch/pallas_call | solution.py:111
  122.2 22.5 %all_to_all.20 = bf16[8,96,896]{2,1,0:T(8,128)(2,1)S(1)} all-to-all(bf16[8,96,896]{2,1,0:T(8,128)(2,1)} %bitcast.42), channel_id=1, replica_groups=mesh['dp'=4,'expert'=8] {'expert'}, dimensions={0} | all-to-all | bytes 2752512 | tf_op jit(solution)/shard_map/all_to_all | solution.py:234
  149.7 23.7 %expert.1 = (bf16[4,2,768,512]{3,2,1,0:T(8,128)(2,1)}, f32[768,768]{1,0:T(8,128)}, f32[768,768]{1,0:T(8,128)}) custom-call(bf16[768,768]{1,0:T(8,128)(2,1)} %copy-done.85, bf16[768,768]{1,0:T(8,128)(2,1)} %copy-done.86, bf16[768,768]{1,0:T(8,128)(2,1)} %copy-done.81, bf16[768,768]{1,0:T(8,128)(2,1)} %copy-done.83, bf16[4,2,768,512]{3,2,1,0:T(8,128)(2,1)} %bitcast.50, ...), custom_call_target="tpu_custom_call" | custom-call | flops 23000000512 | bytes 1000 | tf_op jit(solution)/shard_map/expert/pallas_call | solution.py:111
  173.5 18.7 %all-gather.5.cloned.1.call-done = bf16[6144,256]{1,0:T(8,128)(2,1)} async-done(((bf16[1536,256]{1,0:T(8,128)(2,1)}), bf16[6144,256]{1,0:T(8,128)(2,1)}) %all-gather.5.cloned.1.call-update) | async-done | bytes 3145744 | tf_op jit(solution)/shard_map/all_gather | solution.py:915
  192.2 14.6 %expert_last.1 = (bf16[768,896]{1,0:T(8,128)(2,1)}, bf16[768,768]{1,0:T(8,128)(2,1)}, bf16[4,768,256]{2,1,0:T(8,128)(2,1)}, bf16[4,768,256]{2,1,0:T(8,128)(2,1)}) custom-call(bf16[768,768]{1,0:T(8,128)(2,1)} %copy-done.85, bf16[768,768]{1,0:T(8,128)(2,1)} %copy-done.86, bf16[768,768]{1,0:T(8,128)(2,1)} %copy-done.81, bf16[768,768]{1,0:T(8,128)(2,1)} %copy-done.83, ...), custom_call_target="tpu_custom_call" | custom-call | flops 11500000256 | bytes 1000 | tf_op jit(solution)/shard_map/expert_last/pallas_call | solution.py:111
  206.8 4.5 all-to-all-start.2
  218.0 2.6 expert_grads.1.refs_8_
  220.6 9.6 %all-to-all-done.2 = bf16[8,96,896]{2,1,0:T(8,128)(2,1)} async-done(((bf16[8,96,896]{2,1,0:T(8,128)(2,1)}), bf16[8,96,896]{2,1,0:T(8,128)(2,1)}, u32[]{:S(2)}, u32[]{:S(2)}) %all-to-all-start.2) | async-done | bytes 1376288 | tf_op jit(solution)/shard_map/all_to_all | solution.py:234
  234.4 1.7 copy-done.87
  236.1 7.6 %gate_back.1 = (f32[384,768]{1,0:T(8,128)S(1)}, bf16[384,768]{1,0:T(8,128)(2,1)S(1)}, f32[2,768]{1,0:T(2,128)S(1)}, f32[8,768]{1,0:T(8,128)S(1)}, bf16[4,96,3072...) custom-call(s32[384,1]{1,0:T(8,128)S(1)} %copy-done.71, s32[384,1]{1,0:T(8,128)S(1)} %copy-done.30, ...), custom_call_target="tpu_custom_call" | custom-call | flops 11500000256 | bytes 1000 | tf_op jit(solution)/shard_map/gate_back/pallas_call | solution.py:111
  248.1 3.6 all-to-all-start.3
  251.7 12.1 %widen_back.1 = (bf16[384,3072]{1,0:T(8,128)(2,1)}, bf16[4,384,768]{2,1,0:T(8,128)(2,1)}, bf16[4,384,768]{2,1,0:T(8,128)(2,1)}) custom-call(bf16[384,768]{1,0:T(8,128)(2,1)} %copy-done.91, bf16[384,3072]{1,0:T(8,128)(2,1)} %get-tuple-element.126.refs_1_, bf16[384,768]{1,0:T(8,128)(2,1)} %get-tuple-element.97.refs_0_.refs_2_, ...), custom_call_target="tpu_custom_call" | custom-call | flops 13799999488 | bytes 1000 | tf_op jit(solution)/shard_map/widen_back/pallas_call | solution.py:111
  264.3 4.1 all-to-all-done.3
  268.4 1.7 copy-done.14
  270.2 2.4 fold.3
  274.0 6.9 %second_back.1 = (f32[384,768]{1,0:T(8,128)S(1)}, bf16[384,768]{1,0:T(8,128)(2,1)S(1)}, f32[2,768]{1,0:T(2,128)S(1)}, bf16[4,96,768]{2,1,0:T(8,128)(2,1)S(1)}, bf16[4,96,768]{2,1,0:T(8,128)(2,1)S(1)}) custom-call(bf16[384,3072]{1,0:T(8,128)(2,1)S(1)} %copy-done.15, f32[384,768]{1,0:T(8,128)S(1)} %copy-done.88, f32[384,768]{1,0:T(8,128)S(1)} %copy-done.90, ...), custom_call_target="tpu_custom_call" | custom-call | flops 19549999104 | bytes 1000 | tf_op jit(solution)/shard_map/second_back/pallas_call | solution.py:111
  282.3 12.6 %attend_back.1.refs_4_.refs_0_ = bf16[384,2304]{1,0:T(8,128)(2,1)S(1)} custom-call(bf16[384,768]{1,0:T(8,128)(2,1)S(1)} %get-tuple-element.134.refs_0_, bf16[384,2304]{1,0:T(8,128)(2,1)S(1)} %copy-done.16, f32[384,128]{1,0:T(8,128)S(1)} %copy-done.31, s32[384,1]{1,0:T(8,128)S(1)} %copy-done.24, s32[1,384]{1,0:T(1,128)S(1)} %copy-done.41, ...), custom_call_target="tpu_custom_call" | custom-call | flops 2300000000 | bytes 1000 | tf_op jit(solution)/shard_map/attend_back/pallas_call | solution.py:111
  294.9 2.4 fold.4
  300.2 5.7 %tokens_back.1 = (f32[384,768]{1,0:T(8,128)}, bf16[4,16,768]{2,1,0:T(8,128)(2,1)S(1)}, bf16[4,16,768]{2,1,0:T(8,128)(2,1)S(1)}) custom-call(bf16[384,2304]{1,0:T(8,128)(2,1)S(1)} %attend_back.1.refs_4_.refs_0_, bf16[384,768]{1,0:T(8,128)(2,1)S(1)} %copy-done.26, f32[384,768]{1,0:T(8,128)S(1)} %get-tuple-element.139.refs_2_, f32[16,768]{1,0:T(8,128)S(1)} %copy-done.35, ...), custom_call_target="tpu_custom_call" | custom-call | flops 2300000000 | bytes 1000 | tf_op jit(solution)/shard_map/tokens_back/pallas_call | solution.py:111
  307.2 1.5 collective-permute-start.34
  308.7 1.4 collective-permute-start.35
  312.1 2.3 project_back.1
  314.9 10.8 %collective-permute-done.34.refs_1_ = bf16[2,240,768]{2,1,0:T(8,128)(2,1)S(1)} collective-permute-done((bf16[2,240,768]{2,1,0:T(8,128)(2,1)}, bf16[2,240,768]{2,1,0:T(8,128)(2,1)S(1)}, u32[]{:S(2)}, u32[]{:S(2)}) %collective-permute-start.34) | collective-permute-done | bytes 737312 | tf_op jit(solution)/shard_map/ppermute | solution.py:171
  327.7 1.5 collective-permute-start.37
  330.4 1.5 collective-permute-start.39
  331.8 1.4 collective-permute-start.42
  333.2 15.0 %collective-permute-done.38.refs_1_ = bf16[48,3072]{1,0:T(8,128)(2,1)S(1)} collective-permute-done((bf16[48,3072]{1,0:T(8,128)(2,1)S(1)}, bf16[48,3072]{1,0:T(8,128)(2,1)S(1)}, u32[]{:S(2)}, u32[]{:S(2)}) %collective-permute-start.38) | collective-permute-done | bytes 294944 | tf_op jit(solution)/shard_map/ppermute | solution.py:171
  350.5 1.5 collective-permute-start.41
  352.1 1.4 collective-permute-start.40
  353.5 2.7 collective-permute-done.42.refs_1_
  361.0 1.5 combine.1.refs_2_
  362.5 14.2 %collective-permute-done.46.refs_1_ = bf16[96,3072]{1,0:T(8,128)(2,1)S(1)} collective-permute-done((bf16[96,3072]{1,0:T(8,128)(2,1)S(1)}, bf16[96,3072]{1,0:T(8,128)(2,1)S(1)}, u32[]{:S(2)}, u32[]{:S(2)}) %collective-permute-start.46) | collective-permute-done | bytes 589856 | tf_op jit(solution)/shard_map/ppermute | solution.py:315
  378.8 13.0 %collective-permute-done.45.refs_1_ = bf16[480,768]{1,0:T(8,128)(2,1)S(1)} collective-permute-done((bf16[480,768]{1,0:T(8,128)(2,1)S(1)}, bf16[480,768]{1,0:T(8,128)(2,1)S(1)}, u32[]{:S(2)}, u32[]{:S(2)}) %collective-permute-start.45) | collective-permute-done | bytes 737312 | tf_op jit(solution)/shard_map/ppermute | solution.py:315
  392.7 8.3 %collective-permute-start.44 = (bf16[304,768]{1,0:T(8,128)(2,1)S(1)}, bf16[304,768]{1,0:T(8,128)(2,1)S(1)}, u32[]{:S(2)}, u32[]{:S(2)}) collective-permute-start(bf16[304,768]{1,0:T(8,128)(2,1)S(1)} %fold_last.5.refs_4_.refs_0_), channel_id=1, source_target_pairs={{0,8},{24,16},{1,9},{25,17},{2,10},{26,18},{3,11},{27,19},{4,12},{... | collective-permute-start | bytes 1400840 | tf_op jit(solution)/shard_map/ppermute | solution.py:315
  401.0 8.1 %collective-permute-done.44.refs_1_ = bf16[304,768]{1,0:T(8,128)(2,1)S(1)} collective-permute-done((bf16[304,768]{1,0:T(8,128)(2,1)S(1)}, bf16[304,768]{1,0:T(8,128)(2,1)S(1)}, u32[]{:S(2)}, u32[]{:S(2)}) %collective-permute-start.44) | collective-permute-done | bytes 466976 | tf_op jit(solution)/shard_map/ppermute | solution.py:315
  410.1 1.4 collective-permute-start.51
  415.5 2.4 finish.1
  417.9 28.9 %collective-permute-done.52.refs_1_ = bf16[96,3072]{1,0:T(8,128)(2,1)} collective-permute-done((bf16[96,3072]{1,0:T(8,128)(2,1)S(1)}, bf16[96,3072]{1,0:T(8,128)(2,1)}, u32[]{:S(2)}, u32[]{:S(2)}) %collective-permute-start.52) | collective-permute-done | bytes 589856 | tf_op jit(solution)/shard_map/ppermute | solution.py:315
  446.8 2.3 settle.3.refs_2_
  449.2 2.7 settle.4
  452.6 2.2 settle.5
  456.1 2.1 slice_bitcast_fusion
  (326 shorter events, 72.7 us)
Async XLA Ops:
  7.2 142.6 %all-gather.3.cloned.1.call-start = ((), (), s32[]{:S(2)}) async-start(), calls=%async_computation.6 | async-start | bytes 7864320 | tf_op jit(solution)/shard_map/all_gather | solution.py:915
  10.8 23.5 %copy-start.40 = (s32[1,384]{1,0:T(1,128)S(1)}, s32[1,384]{1,0:T(1,128)}, u32[]{:S(2)}) copy-start(s32[1,384]{1,0:T(1,128)} %refs_4_.2) | copy-start | bytes 4612
  11.2 32.7 %copy-start = (bf16[400,768]{1,0:T(8,128)(2,1)}, bf16[400,768]{1,0:T(8,128)(2,1)S(1)}, u32[]{:S(2)}) copy-start(bf16[400,768]{1,0:T(8,128)(2,1)S(1)} %pad_maximum_fusion.2.refs_3_.refs_11_.refs_21_.refs_5_.refs_7_) | copy-start | bytes 1843204
  11.2 16.9 %collective-permute-start.1 = (bf16[400,768]{1,0:T(8,128)(2,1)S(1)}, bf16[400,768]{1,0:T(8,128)(2,1)S(1)}, u32[]{:S(2)}, u32[]{:S(2)}) collective-permute-start(bf16[400,768]{1,0:T(8,128)(2,1)S(1)} %pad_maximum_fusion.2.refs_3_.refs_11_.refs_21_.refs_5_.refs_7_), channel_id=1, source_target_pairs={{0,2},{1,3},{2,0},{3,1},{4,6},{5,7},{6,4},{7,5},{8,10},{9,11},{10,... | collective-permute-start | bytes 1843208 | tf_op jit(solution)/shard_map/ppermute | solution.py:171
  14.2 16.4 %collective-permute-start.3 = (bf16[400,768]{1,0:T(8,128)(2,1)S(1)}, bf16[400,768]{1,0:T(8,128)(2,1)S(1)}, u32[]{:S(2)}, u32[]{:S(2)}) collective-permute-start(bf16[400,768]{1,0:T(8,128)(2,1)S(1)} %pad_maximum_fusion.2.refs_3_.refs_11_.refs_21_.refs_5_.refs_7_), channel_id=1, source_target_pairs={{0,4},{1,5},{2,6},{3,7},{4,0},{5,1},{6,2},{7,3},{8,12},{9,13},{10,... | collective-permute-start | bytes 1843208 | tf_op jit(solution)/shard_map/ppermute | solution.py:171
  28.9 10.6 %collective-permute-start.5 = (bf16[208,768]{1,0:T(8,128)(2,1)}, bf16[208,768]{1,0:T(8,128)(2,1)S(1)}, u32[]{:S(2)}, u32[]{:S(2)}) collective-permute-start(bf16[208,768]{1,0:T(8,128)(2,1)} %slice.60), channel_id=1, source_target_pairs={{0,4},{1,5},{2,6},{3,7},{4,0},{5,1},{6,2},{7,3},{8,12},{9,13},{10,... | collective-permute-start | bytes 958472 | tf_op jit(solution)/shard_map/ppermute | solution.py:171
  31.4 8.0 %collective-permute-start.7 = (bf16[192,768]{1,0:T(8,128)(2,1)}, bf16[192,768]{1,0:T(8,128)(2,1)}, u32[]{:S(2)}, u32[]{:S(2)}) collective-permute-start(bf16[192,768]{1,0:T(8,128)(2,1)} %slice.61), channel_id=1, source_target_pairs={{0,2},{1,3},{2,0},{3,1},{4,6},{5,7},{6,4},{7,5},{8,10},{9,11},{10,... | collective-permute-start | bytes 884744 | tf_op jit(solution)/shard_map/ppermute | solution.py:171
  32.9 11.7 %collective-permute-start = (bf16[400,768]{1,0:T(8,128)(2,1)S(1)}, bf16[400,768]{1,0:T(8,128)(2,1)S(1)}, u32[]{:S(2)}, u32[]{:S(2)}) collective-permute-start(bf16[400,768]{1,0:T(8,128)(2,1)S(1)} %pad_maximum_fusion.2.refs_3_.refs_11_.refs_21_.refs_5_.refs_7_), channel_id=1, source_target_pairs={{0,1},{1,0},{2,3},{3,2},{4,5},{5,4},{6,7},{7,6},{8,9},{9,8},{10,11... | collective-permute-start | bytes 1843208 | tf_op jit(solution)/shard_map/ppermute | solution.py:171
  32.9 13.7 %collective-permute-start.2 = (bf16[400,768]{1,0:T(8,128)(2,1)S(1)}, bf16[400,768]{1,0:T(8,128)(2,1)S(1)}, u32[]{:S(2)}, u32[]{:S(2)}) collective-permute-start(bf16[400,768]{1,0:T(8,128)(2,1)S(1)} %collective-permute-done.1.refs_5_.refs_13_.refs_23_.refs_7_.refs_9_), channel_id=1, source_target_pairs={{0,1},{1,0},{2,3},{3,2},{4,5},{5,4},{6,7},{7,6},{8,9},{9,8},{10,11... | collective-permute-start | bytes 1843208 | tf_op jit(solution)/shard_map/ppermute | solution.py:171
  33.4 13.8 %collective-permute-start.4 = (bf16[400,768]{1,0:T(8,128)(2,1)S(1)}, bf16[400,768]{1,0:T(8,128)(2,1)}, u32[]{:S(2)}, u32[]{:S(2)}) collective-permute-start(bf16[400,768]{1,0:T(8,128)(2,1)S(1)} %collective-permute-done.3.refs_7_.refs_15_.refs_25_.refs_9_.refs_11_), channel_id=1, source_target_pairs={{0,1},{1,0},{2,3},{3,2},{4,5},{5,4},{6,7},{7,6},{8,9},{9,8},{10,11... | collective-permute-start | bytes 1843208 | tf_op jit(solution)/shard_map/ppermute | solution.py:171
  39.4 6.7 %collective-permute-start.8 = (bf16[192,768]{1,0:T(8,128)(2,1)}, bf16[192,768]{1,0:T(8,128)(2,1)S(1)}, u32[]{:S(2)}, u32[]{:S(2)}) collective-permute-start(bf16[192,768]{1,0:T(8,128)(2,1)} %collective-permute-done.7.refs_17_.refs_13_), channel_id=1, source_target_pairs={{0,1},{1,0},{2,3},{3,2},{4,5},{5,4},{6,7},{7,6},{8,9},{9,8},{10,11... | collective-permute-start | bytes 884744 | tf_op jit(solution)/shard_map/ppermute | solution.py:171
  39.5 9.2 %collective-permute-start.6 = (bf16[208,768]{1,0:T(8,128)(2,1)S(1)}, bf16[208,768]{1,0:T(8,128)(2,1)S(1)}, u32[]{:S(2)}, u32[]{:S(2)}) collective-permute-start(bf16[208,768]{1,0:T(8,128)(2,1)S(1)} %collective-permute-done.5.refs_9_.refs_18_.refs_27_.refs_11_.refs_14_), channel_id=1, source_target_pairs={{0,1},{1,0},{2,3},{3,2},{4,5},{5,4},{6,7},{7,6},{8,9},{9,8},{10,11... | collective-permute-start | bytes 958472 | tf_op jit(solution)/shard_map/ppermute | solution.py:171
  44.6 20.7 %collective-permute-start.9 = (bf16[768,384]{1,0:T(8,128)(2,1)}, bf16[768,384]{1,0:T(8,128)(2,1)S(1)}, u32[]{:S(2)}, u32[]{:S(2)}) collective-permute-start(bf16[768,384]{1,0:T(8,128)(2,1)} %refs_5_.2), channel_id=1, source_target_pairs={{0,2},{1,3},{2,0},{3,1},{4,6},{5,7},{6,4},{7,5},{8,10},{9,11},{10,... | collective-permute-start | bytes 1769480 | tf_op jit(solution)/shard_map/ppermute | solution.py:171
  46.1 19.2 %collective-permute-start.10 = (bf16[768,384]{1,0:T(8,128)(2,1)}, bf16[768,384]{1,0:T(8,128)(2,1)}, u32[]{:S(2)}, u32[]{:S(2)}) collective-permute-start(bf16[768,384]{1,0:T(8,128)(2,1)} %refs_5_.2), channel_id=1, source_target_pairs={{0,4},{1,5},{2,6},{3,7},{4,0},{5,1},{6,2},{7,3},{8,12},{9,13},{10,... | collective-permute-start | bytes 1769480 | tf_op jit(solution)/shard_map/ppermute | solution.py:171
  46.6 27.0 %collective-permute-start.18 = (bf16[96,3072]{1,0:T(8,128)(2,1)}, bf16[96,3072]{1,0:T(8,128)(2,1)S(1)}, u32[]{:S(2)}, u32[]{:S(2)}) collective-permute-start(bf16[96,3072]{1,0:T(8,128)(2,1)} %bitcast.4.refs_5_.refs_3_), channel_id=1, source_target_pairs={{0,2},{1,3},{2,0},{3,1},{4,6},{5,7},{6,4},{7,5},{8,10},{9,11},{10,... | collective-permute-start | bytes 1769480 | tf_op jit(solution)/shard_map/ppermute | solution.py:171
  47.2 27.9 %collective-permute-start.19 = (bf16[96,3072]{1,0:T(8,128)(2,1)}, bf16[96,3072]{1,0:T(8,128)(2,1)S(1)}, u32[]{:S(2)}, u32[]{:S(2)}) collective-permute-start(bf16[96,3072]{1,0:T(8,128)(2,1)} %bitcast.4.refs_5_.refs_3_), channel_id=1, source_target_pairs={{0,4},{1,5},{2,6},{3,7},{4,0},{5,1},{6,2},{7,3},{8,12},{9,13},{10,... | collective-permute-start | bytes 1769480 | tf_op jit(solution)/shard_map/ppermute | solution.py:171
  65.3 23.9 %copy-start.32 = (bf16[768,384]{1,0:T(8,128)(2,1)}, bf16[768,384]{1,0:T(8,128)(2,1)S(1)}, u32[]{:S(2)}) copy-start(bf16[768,384]{1,0:T(8,128)(2,1)S(1)} %collective-permute-done.9.refs_3_.refs_7_) | copy-start | bytes 1769476
  66.5 13.4 %collective-permute-start.14 = (bf16[384,384]{1,0:T(8,128)(2,1)S(1)}, bf16[384,384]{1,0:T(8,128)(2,1)S(1)}, u32[]{:S(2)}, u32[]{:S(2)}) collective-permute-start(bf16[384,384]{1,0:T(8,128)(2,1)S(1)} %slice.48), channel_id=1, source_target_pairs={{0,2},{1,3},{2,0},{3,1},{4,6},{5,7},{6,4},{7,5},{8,10},{9,11},{10,... | collective-permute-start | bytes 884744 | tf_op jit(solution)/shard_map/ppermute | solution.py:171
  68.1 13.5 %collective-permute-start.15 = (bf16[384,384]{1,0:T(8,128)(2,1)S(1)}, bf16[384,384]{1,0:T(8,128)(2,1)}, u32[]{:S(2)}, u32[]{:S(2)}) collective-permute-start(bf16[384,384]{1,0:T(8,128)(2,1)S(1)} %slice.49), channel_id=1, source_target_pairs={{0,4},{1,5},{2,6},{3,7},{4,0},{5,1},{6,2},{7,3},{8,12},{9,13},{10,... | collective-permute-start | bytes 884744 | tf_op jit(solution)/shard_map/ppermute | solution.py:171
  75.2 10.3 %collective-permute-start.23 = (bf16[48,3072]{1,0:T(8,128)(2,1)S(1)}, bf16[48,3072]{1,0:T(8,128)(2,1)S(1)}, u32[]{:S(2)}, u32[]{:S(2)}) collective-permute-start(bf16[48,3072]{1,0:T(8,128)(2,1)S(1)} %slice.50), channel_id=1, source_target_pairs={{0,2},{1,3},{2,0},{3,1},{4,6},{5,7},{6,4},{7,5},{8,10},{9,11},{10,... | collective-permute-start | bytes 884744 | tf_op jit(solution)/shard_map/ppermute | solution.py:171
  75.8 10.8 %collective-permute-start.24 = (bf16[48,3072]{1,0:T(8,128)(2,1)S(1)}, bf16[48,3072]{1,0:T(8,128)(2,1)S(1)}, u32[]{:S(2)}, u32[]{:S(2)}) collective-permute-start(bf16[48,3072]{1,0:T(8,128)(2,1)S(1)} %slice.51), channel_id=1, source_target_pairs={{0,4},{1,5},{2,6},{3,7},{4,0},{5,1},{6,2},{7,3},{8,12},{9,13},{10,... | collective-permute-start | bytes 884744 | tf_op jit(solution)/shard_map/ppermute | solution.py:171
  76.5 21.1 %collective-permute-start.11 = (bf16[768,384]{1,0:T(8,128)(2,1)}, bf16[768,384]{1,0:T(8,128)(2,1)S(1)}, u32[]{:S(2)}, u32[]{:S(2)}) collective-permute-start(bf16[768,384]{1,0:T(8,128)(2,1)} %refs_5_.2), channel_id=1, source_target_pairs={{0,1},{1,0},{2,3},{3,2},{4,5},{5,4},{6,7},{7,6},{8,9},{9,8},{10,11... | collective-permute-start | bytes 1769480 | tf_op jit(solution)/shard_map/ppermute | solution.py:171
  80.0 18.0 %collective-permute-start.12 = (bf16[768,384]{1,0:T(8,128)(2,1)S(1)}, bf16[768,384]{1,0:T(8,128)(2,1)S(1)}, u32[]{:S(2)}, u32[]{:S(2)}) collective-permute-start(bf16[768,384]{1,0:T(8,128)(2,1)S(1)} %collective-permute-done.9.refs_3_.refs_7_), channel_id=1, source_target_pairs={{0,1},{1,0},{2,3},{3,2},{4,5},{5,4},{6,7},{7,6},{8,9},{9,8},{10,11... | collective-permute-start | bytes 1769480 | tf_op jit(solution)/shard_map/ppermute | solution.py:171
  81.6 16.5 %collective-permute-start.13 = (bf16[768,384]{1,0:T(8,128)(2,1)}, bf16[768,384]{1,0:T(8,128)(2,1)}, u32[]{:S(2)}, u32[]{:S(2)}) collective-permute-start(bf16[768,384]{1,0:T(8,128)(2,1)} %collective-permute-done.10.refs_5_.refs_9_), channel_id=1, source_target_pairs={{0,1},{1,0},{2,3},{3,2},{4,5},{5,4},{6,7},{7,6},{8,9},{9,8},{10,11... | collective-permute-start | bytes 1769480 | tf_op jit(solution)/shard_map/ppermute | solution.py:171
  85.5 11.5 %collective-permute-start.16 = (bf16[384,384]{1,0:T(8,128)(2,1)S(1)}, bf16[384,384]{1,0:T(8,128)(2,1)}, u32[]{:S(2)}, u32[]{:S(2)}) collective-permute-start(bf16[384,384]{1,0:T(8,128)(2,1)S(1)} %collective-permute-done.14.refs_7_.refs_11_), channel_id=1, source_target_pairs={{0,1},{1,0},{2,3},{3,2},{4,5},{5,4},{6,7},{7,6},{8,9},{9,8},{10,11... | collective-permute-start | bytes 884744 | tf_op jit(solution)/shard_map/ppermute | solution.py:171
  87.4 10.1 %collective-permute-start.17 = (bf16[384,384]{1,0:T(8,128)(2,1)}, bf16[384,384]{1,0:T(8,128)(2,1)}, u32[]{:S(2)}, u32[]{:S(2)}) collective-permute-start(bf16[384,384]{1,0:T(8,128)(2,1)} %collective-permute-done.15.refs_8_.refs_12_), channel_id=1, source_target_pairs={{0,1},{1,0},{2,3},{3,2},{4,5},{5,4},{6,7},{7,6},{8,9},{9,8},{10,11... | collective-permute-start | bytes 884744 | tf_op jit(solution)/shard_map/ppermute | solution.py:171
  91.0 20.3 %all-to-all-start = ((bf16[8,96,768]{2,1,0:T(8,128)(2,1)}), bf16[8,96,768]{2,1,0:T(8,128)(2,1)S(1)}, u32[]{:S(2)}, u32[]{:S(2)}) async-start(bf16[8,96,768]{2,1,0:T(8,128)(2,1)} %bitcast.5), calls=%async_computation | async-start | bytes 2359296 | tf_op jit(solution)/shard_map/all_to_all | solution.py:234
  94.5 97.7 %all-gather.5.cloned.1.call-start = ((), (), s32[]{:S(2)}) async-start(), calls=%async_computation.7 | async-start | bytes 3932160 | tf_op jit(solution)/shard_map/all_gather | solution.py:915
  96.7 210.5 %reduce-scatter.3.cloned.1.call-start = ((), (), s32[]{:S(2)}) async-start(), calls=%async_computation.8 | async-start | bytes 7864320 | tf_op jit(solution)/shard_map/reduce_scatter | solution.py:952
  96.9 11.4 %collective-permute-start.21 = (bf16[96,3072]{1,0:T(8,128)(2,1)}, bf16[96,3072]{1,0:T(8,128)(2,1)}, u32[]{:S(2)}, u32[]{:S(2)}) collective-permute-start(bf16[96,3072]{1,0:T(8,128)(2,1)} %copy-done.97), channel_id=1, source_target_pairs={{0,1},{1,0},{2,3},{3,2},{4,5},{5,4},{6,7},{7,6},{8,9},{9,8},{10,11... | collective-permute-start | bytes 1769480 | tf_op jit(solution)/shard_map/ppermute | solution.py:171
  97.5 10.9 %collective-permute-start.22 = (bf16[96,3072]{1,0:T(8,128)(2,1)}, bf16[96,3072]{1,0:T(8,128)(2,1)}, u32[]{:S(2)}, u32[]{:S(2)}) collective-permute-start(bf16[96,3072]{1,0:T(8,128)(2,1)} %copy-done.98), channel_id=1, source_target_pairs={{0,1},{1,0},{2,3},{3,2},{4,5},{5,4},{6,7},{7,6},{8,9},{9,8},{10,11... | collective-permute-start | bytes 1769480 | tf_op jit(solution)/shard_map/ppermute | solution.py:171
  97.6 10.8 %collective-permute-start.20 = (bf16[96,3072]{1,0:T(8,128)(2,1)}, bf16[96,3072]{1,0:T(8,128)(2,1)}, u32[]{:S(2)}, u32[]{:S(2)}) collective-permute-start(bf16[96,3072]{1,0:T(8,128)(2,1)} %bitcast.4.refs_5_.refs_3_), channel_id=1, source_target_pairs={{0,1},{1,0},{2,3},{3,2},{4,5},{5,4},{6,7},{7,6},{8,9},{9,8},{10,11... | collective-permute-start | bytes 1769480 | tf_op jit(solution)/shard_map/ppermute | solution.py:171
  98.0 10.3 %collective-permute-start.25 = (bf16[48,3072]{1,0:T(8,128)(2,1)}, bf16[48,3072]{1,0:T(8,128)(2,1)S(1)}, u32[]{:S(2)}, u32[]{:S(2)}) collective-permute-start(bf16[48,3072]{1,0:T(8,128)(2,1)} %copy-done.102), channel_id=1, source_target_pairs={{0,1},{1,0},{2,3},{3,2},{4,5},{5,4},{6,7},{7,6},{8,9},{9,8},{10,11... | collective-permute-start | bytes 884744 | tf_op jit(solution)/shard_map/ppermute | solution.py:171
  98.1 10.3 %collective-permute-start.26 = (bf16[48,3072]{1,0:T(8,128)(2,1)}, bf16[48,3072]{1,0:T(8,128)(2,1)S(1)}, u32[]{:S(2)}, u32[]{:S(2)}) collective-permute-start(bf16[48,3072]{1,0:T(8,128)(2,1)} %copy-done.103), channel_id=1, source_target_pairs={{0,1},{1,0},{2,3},{3,2},{4,5},{5,4},{6,7},{7,6},{8,9},{9,8},{10,11... | collective-permute-start | bytes 884744 | tf_op jit(solution)/shard_map/ppermute | solution.py:171
  206.8 23.4 %all-to-all-start.2 = ((bf16[8,96,896]{2,1,0:T(8,128)(2,1)}), bf16[8,96,896]{2,1,0:T(8,128)(2,1)}, u32[]{:S(2)}, u32[]{:S(2)}) async-start(bf16[8,96,896]{2,1,0:T(8,128)(2,1)} %bitcast.41), calls=%async_computation.2 | async-start | bytes 2752512 | tf_op jit(solution)/shard_map/all_to_all | solution.py:234
  248.1 20.3 %collective-permute-start.27 = (bf16[4,96,3072]{2,1,0:T(8,128)(2,1)}, bf16[4,96,3072]{2,1,0:T(8,128)(2,1)}, u32[]{:S(2)}, u32[]{:S(2)}) collective-permute-start(bf16[4,96,3072]{2,1,0:T(8,128)(2,1)} %get-tuple-element.132), channel_id=1, source_target_pairs={{0,1},{1,0},{2,3},{3,2},{4,5},{5,4},{6,7},{7,6},{8,9},{9,8},{10,11... | collective-permute-start | bytes 7077896 | tf_op jit(solution)/shard_map/ppermute | solution.py:171
  248.1 20.3 %all-to-all-start.3 = ((bf16[8,96,768]{2,1,0:T(8,128)(2,1)}), bf16[8,96,768]{2,1,0:T(8,128)(2,1)S(1)}, u32[]{:S(2)}, u32[]{:S(2)}) async-start(bf16[8,96,768]{2,1,0:T(8,128)(2,1)} %bitcast.34), calls=%async_computation.3 | async-start | bytes 2359296 | tf_op jit(solution)/shard_map/all_to_all | solution.py:234
  251.7 162.6 %reduce-scatter.5.cloned.1.call-start = ((), (), s32[]{:S(2)}) async-start(), calls=%async_computation.9 | async-start | bytes 3932160 | tf_op jit(solution)/shard_map/reduce_scatter | solution.py:952
  263.8 31.1 %collective-permute-start.30 = (bf16[4,384,768]{2,1,0:T(8,128)(2,1)}, bf16[4,384,768]{2,1,0:T(8,128)(2,1)}, u32[]{:S(2)}, u32[]{:S(2)}) collective-permute-start(bf16[4,384,768]{2,1,0:T(8,128)(2,1)} %get-tuple-element.146), channel_id=1, source_target_pairs={{0,1},{1,0},{2,3},{3,2},{4,5},{5,4},{6,7},{7,6},{8,9},{9,8},{10,11... | collective-permute-start | bytes 7077896 | tf_op jit(solution)/shard_map/ppermute | solution.py:171
  280.9 14.0 %collective-permute-start.31 = (bf16[4,96,768]{2,1,0:T(8,128)(2,1)S(1)}, bf16[4,96,768]{2,1,0:T(8,128)(2,1)S(1)}, u32[]{:S(2)}, u32[]{:S(2)}) collective-permute-start(bf16[4,96,768]{2,1,0:T(8,128)(2,1)S(1)} %get-tuple-element.147), channel_id=1, source_target_pairs={{0,1},{1,0},{2,3},{3,2},{4,5},{5,4},{6,7},{7,6},{8,9},{9,8},{10,11... | collective-permute-start | bytes 1769480 | tf_op jit(solution)/shard_map/ppermute | solution.py:171
  281.0 16.4 %collective-permute-start.28 = (bf16[2,48,3072]{2,1,0:T(8,128)(2,1)S(1)}, bf16[2,48,3072]{2,1,0:T(8,128)(2,1)S(1)}, u32[]{:S(2)}, u32[]{:S(2)}) collective-permute-start(bf16[2,48,3072]{2,1,0:T(8,128)(2,1)S(1)} %get-tuple-element.141), channel_id=1, source_target_pairs={{0,2},{1,3},{2,0},{3,1},{4,6},{5,7},{6,4},{7,5},{8,10},{9,11},{10,... | collective-permute-start | bytes 1769480 | tf_op jit(solution)/shard_map/ppermute | solution.py:171
  281.7 15.7 %collective-permute-start.29 = (bf16[2,48,3072]{2,1,0:T(8,128)(2,1)S(1)}, bf16[2,48,3072]{2,1,0:T(8,128)(2,1)S(1)}, u32[]{:S(2)}, u32[]{:S(2)}) collective-permute-start(bf16[2,48,3072]{2,1,0:T(8,128)(2,1)S(1)} %get-tuple-element.143), channel_id=1, source_target_pairs={{0,4},{1,5},{2,6},{3,7},{4,0},{5,1},{6,2},{7,3},{8,12},{9,13},{10,... | collective-permute-start | bytes 1769480 | tf_op jit(solution)/shard_map/ppermute | solution.py:171
  307.2 18.5 %collective-permute-start.34 = (bf16[2,240,768]{2,1,0:T(8,128)(2,1)}, bf16[2,240,768]{2,1,0:T(8,128)(2,1)S(1)}, u32[]{:S(2)}, u32[]{:S(2)}) collective-permute-start(bf16[2,240,768]{2,1,0:T(8,128)(2,1)} %copy-done.50), channel_id=1, source_target_pairs={{0,2},{1,3},{2,0},{3,1},{4,6},{5,7},{6,4},{7,5},{8,10},{9,11},{10,... | collective-permute-start | bytes 2211848 | tf_op jit(solution)/shard_map/ppermute | solution.py:171
  308.7 18.2 %collective-permute-start.35 = (bf16[2,240,768]{2,1,0:T(8,128)(2,1)}, bf16[2,240,768]{2,1,0:T(8,128)(2,1)S(1)}, u32[]{:S(2)}, u32[]{:S(2)}) collective-permute-start(bf16[2,240,768]{2,1,0:T(8,128)(2,1)} %copy-done.49), channel_id=1, source_target_pairs={{0,4},{1,5},{2,6},{3,7},{4,0},{5,1},{6,2},{7,3},{8,12},{9,13},{10,... | collective-permute-start | bytes 2211848 | tf_op jit(solution)/shard_map/ppermute | solution.py:171
  314.4 12.9 %collective-permute-start.32 = (bf16[4,288,768]{2,1,0:T(8,128)(2,1)S(1)}, bf16[4,288,768]{2,1,0:T(8,128)(2,1)S(1)}, u32[]{:S(2)}, u32[]{:S(2)}) collective-permute-start(bf16[4,288,768]{2,1,0:T(8,128)(2,1)S(1)} %get-tuple-element.152), channel_id=1, source_target_pairs={{0,1},{1,0},{2,3},{3,2},{4,5},{5,4},{6,7},{7,6},{8,9},{9,8},{10,11... | collective-permute-start | bytes 5308424 | tf_op jit(solution)/shard_map/ppermute | solution.py:171
  314.4 12.8 %collective-permute-start.33 = (bf16[4,16,768]{2,1,0:T(8,128)(2,1)S(1)}, bf16[4,16,768]{2,1,0:T(8,128)(2,1)S(1)}, u32[]{:S(2)}, u32[]{:S(2)}) collective-permute-start(bf16[4,16,768]{2,1,0:T(8,128)(2,1)S(1)} %copy-done.66), channel_id=1, source_target_pairs={{0,1},{1,0},{2,3},{3,2},{4,5},{5,4},{6,7},{7,6},{8,9},{9,8},{10,11... | collective-permute-start | bytes 294920 | tf_op jit(solution)/shard_map/ppermute | solution.py:171
  327.7 22.6 %collective-permute-start.37 = (bf16[2,160,768]{2,1,0:T(8,128)(2,1)S(1)}, bf16[2,160,768]{2,1,0:T(8,128)(2,1)S(1)}, u32[]{:S(2)}, u32[]{:S(2)}) collective-permute-start(bf16[2,160,768]{2,1,0:T(8,128)(2,1)S(1)} %get-tuple-element.161), channel_id=1, source_target_pairs={{0,4},{1,5},{2,6},{3,7},{4,0},{5,1},{6,2},{7,3},{8,12},{9,13},{10,... | collective-permute-start | bytes 1474568 | tf_op jit(solution)/shard_map/ppermute | solution.py:171
  329.2 21.1 %collective-permute-start.36 = (bf16[2,144,768]{2,1,0:T(8,128)(2,1)S(1)}, bf16[2,144,768]{2,1,0:T(8,128)(2,1)S(1)}, u32[]{:S(2)}, u32[]{:S(2)}) collective-permute-start(bf16[2,144,768]{2,1,0:T(8,128)(2,1)S(1)} %get-tuple-element.159), channel_id=1, source_target_pairs={{0,2},{1,3},{2,0},{3,1},{4,6},{5,7},{6,4},{7,5},{8,10},{9,11},{10,... | collective-permute-start | bytes 1327112 | tf_op jit(solution)/shard_map/ppermute | solution.py:171
  329.8 18.5 %collective-permute-start.38 = (bf16[48,3072]{1,0:T(8,128)(2,1)S(1)}, bf16[48,3072]{1,0:T(8,128)(2,1)S(1)}, u32[]{:S(2)}, u32[]{:S(2)}) collective-permute-start(bf16[48,3072]{1,0:T(8,128)(2,1)S(1)} %copy-done.62), channel_id=1, source_target_pairs={{0,4},{1,5},{2,6},{3,7},{4,0},{5,1},{6,2},{7,3},{8,12},{9,13},{10,... | collective-permute-start | bytes 884744 | tf_op jit(solution)/shard_map/ppermute | solution.py:171
  330.4 18.5 %collective-permute-start.39 = (bf16[48,3072]{1,0:T(8,128)(2,1)S(1)}, bf16[48,3072]{1,0:T(8,128)(2,1)S(1)}, u32[]{:S(2)}, u32[]{:S(2)}) collective-permute-start(bf16[48,3072]{1,0:T(8,128)(2,1)S(1)} %get-tuple-element.164), channel_id=1, source_target_pairs={{0,2},{1,3},{2,0},{3,1},{4,6},{5,7},{6,4},{7,5},{8,10},{9,11},{10,... | collective-permute-start | bytes 884744 | tf_op jit(solution)/shard_map/ppermute | solution.py:171
  331.8 24.3 %collective-permute-start.42 = (bf16[240,768]{1,0:T(8,128)(2,1)S(1)}, bf16[240,768]{1,0:T(8,128)(2,1)S(1)}, u32[]{:S(2)}, u32[]{:S(2)}) collective-permute-start(bf16[240,768]{1,0:T(8,128)(2,1)S(1)} %get-tuple-element.169), channel_id=1, source_target_pairs={{0,4},{1,5},{2,6},{3,7},{4,0},{5,1},{6,2},{7,3},{8,12},{9,13},{10,... | collective-permute-start | bytes 1105928 | tf_op jit(solution)/shard_map/ppermute | solution.py:171
  348.2 8.8 %collective-permute-start.43 = (bf16[240,768]{1,0:T(8,128)(2,1)S(1)}, bf16[240,768]{1,0:T(8,128)(2,1)S(1)}, u32[]{:S(2)}, u32[]{:S(2)}) collective-permute-start(bf16[240,768]{1,0:T(8,128)(2,1)S(1)} %get-tuple-element.171), channel_id=1, source_target_pairs={{0,2},{1,3},{2,0},{3,1},{4,6},{5,7},{6,4},{7,5},{8,10},{9,11},{10,... | collective-permute-start | bytes 1105928 | tf_op jit(solution)/shard_map/ppermute | solution.py:171
  348.9 27.8 %collective-permute-start.46 = (bf16[96,3072]{1,0:T(8,128)(2,1)S(1)}, bf16[96,3072]{1,0:T(8,128)(2,1)S(1)}, u32[]{:S(2)}, u32[]{:S(2)}) collective-permute-start(bf16[96,3072]{1,0:T(8,128)(2,1)S(1)} %fold_last.3.refs_4_.refs_0_), channel_id=1, source_target_pairs={{0,8},{24,16},{1,9},{25,17},{2,10},{26,18},{3,11},{27,19},{4,12},{... | collective-permute-start | bytes 1769480 | tf_op jit(solution)/shard_map/ppermute | solution.py:315
  350.5 9.2 %collective-permute-start.41 = (bf16[160,768]{1,0:T(8,128)(2,1)S(1)}, bf16[160,768]{1,0:T(8,128)(2,1)S(1)}, u32[]{:S(2)}, u32[]{:S(2)}) collective-permute-start(bf16[160,768]{1,0:T(8,128)(2,1)S(1)} %get-tuple-element.168), channel_id=1, source_target_pairs={{0,2},{1,3},{2,0},{3,1},{4,6},{5,7},{6,4},{7,5},{8,10},{9,11},{10,... | collective-permute-start | bytes 737288 | tf_op jit(solution)/shard_map/ppermute | solution.py:171
  352.1 6.6 %collective-permute-start.40 = (bf16[144,768]{1,0:T(8,128)(2,1)S(1)}, bf16[144,768]{1,0:T(8,128)(2,1)S(1)}, u32[]{:S(2)}, u32[]{:S(2)}) collective-permute-start(bf16[144,768]{1,0:T(8,128)(2,1)S(1)} %get-tuple-element.166), channel_id=1, source_target_pairs={{0,4},{1,5},{2,6},{3,7},{4,0},{5,1},{6,2},{7,3},{8,12},{9,13},{10,... | collective-permute-start | bytes 663560 | tf_op jit(solution)/shard_map/ppermute | solution.py:171
  357.2 34.6 %collective-permute-start.45 = (bf16[480,768]{1,0:T(8,128)(2,1)S(1)}, bf16[480,768]{1,0:T(8,128)(2,1)S(1)}, u32[]{:S(2)}, u32[]{:S(2)}) collective-permute-start(bf16[480,768]{1,0:T(8,128)(2,1)S(1)} %fold_last.4.refs_4_.refs_0_), channel_id=1, source_target_pairs={{0,8},{24,16},{1,9},{25,17},{2,10},{26,18},{3,11},{27,19},{4,12},{... | collective-permute-start | bytes 2211848 | tf_op jit(solution)/shard_map/ppermute | solution.py:315
  378.0 0.7 collective-permute-start.47
  378.8 32.7 %copy-start.25 = (bf16[96,3072]{1,0:T(8,128)(2,1)}, bf16[96,3072]{1,0:T(8,128)(2,1)S(1)}, u32[]{:S(2)}) copy-start(bf16[96,3072]{1,0:T(8,128)(2,1)S(1)} %joined.7.refs_2_.refs_0_) | copy-start | bytes 1769476
  392.0 17.9 %collective-permute-start.49 = (bf16[480,768]{1,0:T(8,128)(2,1)S(1)}, bf16[480,768]{1,0:T(8,128)(2,1)S(1)}, u32[]{:S(2)}, u32[]{:S(2)}) collective-permute-start(bf16[480,768]{1,0:T(8,128)(2,1)S(1)} %joined.8.refs_2_.refs_0_), channel_id=1, source_target_pairs={{8,16},{16,8},{9,17},{17,9},{10,18},{18,10},{11,19},{19,11},{12,20... | collective-permute-start | bytes 2211848 | tf_op jit(solution)/shard_map/ppermute | solution.py:315
  392.7 16.4 %collective-permute-start.44 = (bf16[304,768]{1,0:T(8,128)(2,1)S(1)}, bf16[304,768]{1,0:T(8,128)(2,1)S(1)}, u32[]{:S(2)}, u32[]{:S(2)}) collective-permute-start(bf16[304,768]{1,0:T(8,128)(2,1)S(1)} %fold_last.5.refs_4_.refs_0_), channel_id=1, source_target_pairs={{0,8},{24,16},{1,9},{25,17},{2,10},{26,18},{3,11},{27,19},{4,12},{... | collective-permute-start | bytes 1400840 | tf_op jit(solution)/shard_map/ppermute | solution.py:315
  409.2 3.7 collective-permute-start.48
  410.1 39.1 %collective-permute-start.51 = (bf16[480,768]{1,0:T(8,128)(2,1)S(1)}, bf16[480,768]{1,0:T(8,128)(2,1)}, u32[]{:S(2)}, u32[]{:S(2)}) collective-permute-start(bf16[480,768]{1,0:T(8,128)(2,1)S(1)} %joined.10.refs_2_.refs_0_), channel_id=1, source_target_pairs={{8,0},{16,24},{9,1},{17,25},{10,2},{18,26},{11,3},{19,27},{12,4},{... | collective-permute-start | bytes 2211848 | tf_op jit(solution)/shard_map/ppermute | solution.py:315
  411.5 35.3 %collective-permute-start.52 = (bf16[96,3072]{1,0:T(8,128)(2,1)S(1)}, bf16[96,3072]{1,0:T(8,128)(2,1)}, u32[]{:S(2)}, u32[]{:S(2)}) collective-permute-start(bf16[96,3072]{1,0:T(8,128)(2,1)S(1)} %joined.7.refs_2_.refs_0_), channel_id=1, source_target_pairs={{8,0},{16,24},{9,1},{17,25},{10,2},{18,26},{11,3},{19,27},{12,4},{... | collective-permute-start | bytes 1769480 | tf_op jit(solution)/shard_map/ppermute | solution.py:315
  413.0 39.6 %collective-permute-start.50 = (bf16[304,768]{1,0:T(8,128)(2,1)S(1)}, bf16[304,768]{1,0:T(8,128)(2,1)}, u32[]{:S(2)}, u32[]{:S(2)}) collective-permute-start(bf16[304,768]{1,0:T(8,128)(2,1)S(1)} %joined.11.refs_2_.refs_0_), channel_id=1, source_target_pairs={{8,0},{16,24},{9,1},{17,25},{10,2},{18,26},{11,3},{19,27},{12,4},{... | collective-permute-start | bytes 1400840 | tf_op jit(solution)/shard_map/ppermute | solution.py:315
  (102 other events, 477.3 us)
Sparse Core Ops, SparseCore 0:
  10.2 118.0 all-gather.2
  130.5 61.7 all-gather.4
  194.5 109.3 reduce-scatter.2
  307.3 73.4 reduce-scatter.4

commit v3 on v2

--- a/solution.py
+++ b/solution.py
@@ -15,10 +15,10 @@
 ROOT = 0.7978845608028654
 COST = dict(
     prepare=3, attend=16, widen=9, dispatch=10, expert_rows=4, expert=20, expert_last=10, expert_grads=6, gate_back=10, widen_back=12, fold=1,
-    second_back=17, attend_back=2, fold_again=1, fold_wait=12, project_back=2, tokens_back=2, fold_last=1, joined=1,
+    second_back=17, attend_back=2, fold_again=1, fold_wait=12, project_back=2, tokens_back=2, fold_last=1, joined=6,
     combine=1, finish=1, settle=1,
 )
-WIDE = ("attend", "widen", "dispatch", "expert", "expert_last", "widen_back", "settle")
+WIDE = ("attend", "widen", "dispatch", "expert", "expert_last", "expert_grads", "widen_back", "settle")
 VMEM_LIMIT = 60 * 1024 * 1024
 
 
@@ -909,7 +909,7 @@
         part = slice(start, start + wide)
         return jnp.concatenate([expert_up[0][:, part], expert_down[0][:, part]], axis=0)
 
-    chunks = [512, 256] if own_hidden == 768 and m == 4 else [own_hidden]
+    chunks = [640, 128] if own_hidden == 768 and m == 4 else [own_hidden]
     gathered, start = [], 0
     for wide in chunks:
         whole = lax.all_gather(chunk(start, wide), "dp", axis=0, tiled=True)
@@ -995,19 +995,19 @@
     output = combine(returned, slots, hidden, gates)
     down = links.joined(down, down_got)
     down_got = links.middle(down)
-    down = links.joined(down, down_got)
-    down_got = links.outward(down)
     up = links.joined(up, up_got)
     up_got = links.middle(up)
     inner = links.joined(inner, inner_got)
     inner_got = links.middle(inner)
+    down = links.joined(down, down_got)
+    down_got = links.outward(down)
     up = links.joined(up, up_got)
     up_got = links.outward(up)
     inner = links.joined(inner, inner_got)
     inner_got = links.outward(inner)
     expert_sums = finish(summed)
+    down_sum = links.settled(down, down_got)
     units, columns = dense_up.shape[1], project_in.shape[1]
-    down_sum = links.settled(down, down_got)
     up_sum, out_sum = links.settled_across(up, up_got, units)
     inner_sum = links.settled(inner, inner_got)
     small_sum = inner_sum[columns:, :cols]

time: 474 us -> 452 us (0.954)
  blocking collectives: 22.5 us -> 0 us
  local copies, waits for them, and re-layouts: 54.2 us -> 42.8 us
  Pallas kernels: 144 us -> 152 us
  waiting for transfers between devices: 166 us -> 171 us
    all_to_all x1 -> x0, blocking collectives: 22.5 us -> none  [exchange(): lax.all_to_all(blocks, 'expert', split_axis=0, concat_axis=0, tiled=True)]
    all_to_all x3 -> x4, waiting for transfers between devices: 16.6 us -> 38.2 us  [exchange(): lax.all_to_all(blocks, 'expert', split_axis=0, concat_axis=0, tiled=True)]
    unnamed x213 -> x173, local copies, waits for them, and re-layouts: 40.9 us -> 29 us
    ppermute x9, waiting for transfers between devices: 65 us -> 56.4 us  [along(): return lax.ppermute(value, 'dp', pairs)]
    ppermute x44, waiting for transfers between devices: 65.1 us -> 56.7 us  [hop(): return lax.ppermute(value, 'expert', [(i, i ^ bit) for i in range(self.n)])]
    pallas_call x34, Pallas kernels: 144 us -> 152 us  [call(): pl.pallas_call(body, out_shape=outs, in_specs=[pl.BlockSpec(memory_space=...]
    all_to_all x3 -> x4, starting transfers between devices: 11.6 us -> 15.5 us  [exchange(): lax.all_to_all(blocks, 'expert', split_axis=0, concat_axis=0, tiled=True)]
  transfers between devices with their start and end apart: 60 -> 61, of which waited for: 24 -> 26; matrix products, arithmetic and copies ran while one was open for 2% -> 2% of each run, Pallas kernels for 30% -> 34%
where the time goes in v3:
time: 452 us; the launch traced here: 445 us
  waiting for transfers between devices  171 us (38%)
  Pallas kernels  152 us (34%)
  starting transfers between devices  61.9 us (14%)
  local copies, waits for them, and re-layouts  42.8 us (9%)
  between operations  15 us (3%)
    pallas_call x34, Pallas kernels, call(): pl.pallas_call(body, out_shape=outs, in_specs=[pl.BlockSpec(memory_space=...  152 us
    ppermute x44, waiting for transfers between devices, hop(): return lax.ppermute(value, 'expert', [(i, i ^ bit) for i in range(self.n)])  56.7 us
    ppermute x9, waiting for transfers between devices, along(): return lax.ppermute(value, 'dp', pairs)  56.4 us
    all_to_all x4, waiting for transfers between devices, exchange(): lax.all_to_all(blocks, 'expert', split_axis=0, concat_axis=0, tiled=True)  38.2 us
    ppermute x44, starting transfers between devices, hop(): return lax.ppermute(value, 'expert', [(i, i ^ bit) for i in range(self.n)])  32 us
    unnamed x173, local copies, waits for them, and re-layouts  29 us
    all_to_all x4, starting transfers between devices, exchange(): lax.all_to_all(blocks, 'expert', split_axis=0, concat_axis=0, tiled=True)  15.5 us
    all_gather x2, waiting for transfers between devices, on_device(): whole = lax.all_gather(chunk(start, wide), 'dp', axis=0, tiled=True)  15 us
  transfers between devices with their start and end apart: 61, of which 26 were waited for; matrix products, arithmetic and copies ran while one was open for 2% of the time, Pallas kernels for 34%

profile of v3, /device:TPU:0, one launch (start us, length us, event | category | flops | bytes accessed | tf_op | source)
XLA Modules:
  0.0 445.0 jit_solution(15697932168320802058)
XLA Ops:
  8.8 1.6 pad_maximum_fusion
  11.6 3.0 collective-permute-start.1
  14.6 1.5 collective-permute-start.3
  16.1 12.3 %collective-permute-done.1.refs_5_.refs_13_.refs_23_.refs_7_.refs_9_ = bf16[400,768]{1,0:T(8,128)(2,1)S(1)} collective-permute-done((bf16[400,768]{1,0:T(8,128)(2,1)S(1)}, bf16[400,768]{1,0:T(8,128)(2,1)S(1)}, u32[]{:S(2)}, u32[]{:S(2)}) %collective-permute-start.1) | collective-permute-done | bytes 614432 | tf_op jit(solution)/shard_map/ppermute | solution.py:171
  29.2 1.8 collective-permute-start.5
  31.8 1.5 collective-permute-start.7
  34.8 4.9 %collective-permute-done.7.refs_17_.refs_13_ = bf16[192,768]{1,0:T(8,128)(2,1)S(1)} collective-permute-done((bf16[192,768]{1,0:T(8,128)(2,1)}, bf16[192,768]{1,0:T(8,128)(2,1)S(1)}, u32[]{:S(2)}, u32[]{:S(2)}) %collective-permute-start.7) | collective-permute-done | bytes 294944 | tf_op jit(solution)/shard_map/ppermute | solution.py:171
  41.3 1.9 prepare.1
  43.9 1.5 collective-permute-start.9
  48.7 15.9 %attend.1 = (bf16[384,768]{1,0:T(8,128)(2,1)}, bf16[384,2304]{1,0:T(8,128)(2,1)}, bf16[384,768]{1,0:T(8,128)(2,1)}, f32[384,128]{1,0:T(8,128)}, f32[384,768]{1,0...) custom-call(bf16[384,768]{1,0:T(8,128)(2,1)} %refs_1_.3, s32[384,1]{1,0:T(8,128)} %copy.28.refs_1_.refs_3_, ...), custom_call_target="tpu_custom_call" | custom-call | flops 18400000000 | bytes 1000 | tf_op jit(solution)/shard_map/attend/pallas_call | solution.py:111
  65.9 1.6 collective-permute-start.14
  68.0 5.0 %collective-permute-done.18.refs_7_.refs_5_ = bf16[96,3072]{1,0:T(8,128)(2,1)} collective-permute-done((bf16[96,3072]{1,0:T(8,128)(2,1)}, bf16[96,3072]{1,0:T(8,128)(2,1)}, u32[]{:S(2)}, u32[]{:S(2)}) %collective-permute-start.18) | collective-permute-done | bytes 589856 | tf_op jit(solution)/shard_map/ppermute | solution.py:171
  73.1 1.5 collective-permute-done.19.refs_9_.refs_7_
  77.8 1.5 collective-permute-done.14.refs_7_.refs_11_
  79.3 1.6 collective-permute-done.15.refs_8_.refs_12_
  80.9 3.9 collective-permute-done.23.refs_11_.refs_9_
  86.7 4.1 all-to-all-start
  92.7 9.5 %widen.1 = (bf16[384,3072]{1,0:T(8,128)(2,1)}, bf16[384,3072]{1,0:T(8,128)(2,1)}) custom-call(bf16[384,768]{1,0:T(8,128)(2,1)} %get-tuple-element.97.refs_0_.refs_2_, bf16[768,384]{1,0:T(8,128)(2,1)} %refs_5_.2, bf16[768,384]{1,0:T(8,128)(2,1)} %copy-done.46, bf16[768,384]{1,0:T(8,128)(2,1)} %copy-done.31, bf16[768,384]{1,0:T(8,128)(2,1)} %copy-done.48, ...), custom_call_target="tpu_custom_call" | custom-call | flops 10350000128 | bytes 1000 | tf_op jit(solution)/shard_map/widen/pallas_call | solution.py:111
  102.3 5.3 %all-to-all-done = bf16[8,96,768]{2,1,0:T(8,128)(2,1)S(1)} async-done(((bf16[8,96,768]{2,1,0:T(8,128)(2,1)}), bf16[8,96,768]{2,1,0:T(8,128)(2,1)S(1)}, u32[]{:S(2)}, u32[]{:S(2)}) %all-to-all-start) | async-done | bytes 1179680 | tf_op jit(solution)/shard_map/all_to_all | solution.py:234
  108.6 9.9 %dispatch.1 = (f32[384,768]{1,0:T(8,128)}, f32[384,1]{1,0:T(8,128)}, bf16[768,896]{1,0:T(8,128)(2,1)}) custom-call(bf16[384,3072]{1,0:T(8,128)(2,1)} %get-tuple-element.103.refs_0_.refs_16_.refs_6_, f32[384,768]{1,0:T(8,128)} %get-tuple-element.104.refs_1_, f32[16,768]{1,0:T(8,128)} %get-tuple-element.99.refs_11_.refs_2_.refs_4_.refs_3_, ...), custom_call_target="tpu_custom_call" | custom-call | flops 11500000256 | bytes 1000 | tf_op jit(solution)/shard_map/dispatch/pallas_call | solution.py:111
  118.5 3.7 all-to-all-start.1
  125.2 15.9 %all-to-all-done.1 = bf16[8,96,896]{2,1,0:T(8,128)(2,1)S(1)} async-done(((bf16[8,96,896]{2,1,0:T(8,128)(2,1)}), bf16[8,96,896]{2,1,0:T(8,128)(2,1)S(1)}, u32[]{:S(2)}, u32[]{:S(2)}) %all-to-all-start.1) | async-done | bytes 1376288 | tf_op jit(solution)/shard_map/all_to_all | solution.py:234
  146.2 8.2 %all-gather.3.cloned.1.call-done = bf16[6144,640]{1,0:T(8,128)(2,1)} async-done(((bf16[1536,640]{1,0:T(8,128)(2,1)}), bf16[6144,640]{1,0:T(8,128)(2,1)}) %all-gather.3.cloned.1.call-update) | async-done | bytes 7864336 | tf_op jit(solution)/shard_map/all_gather | solution.py:915
  154.4 30.7 %expert.1 = (bf16[4,2,768,640]{3,2,1,0:T(8,128)(2,1)}, f32[768,768]{1,0:T(8,128)}, f32[768,768]{1,0:T(8,128)}) custom-call(bf16[768,768]{1,0:T(8,128)(2,1)} %copy-done.67, bf16[768,768]{1,0:T(8,128)(2,1)} %copy-done.68, bf16[768,768]{1,0:T(8,128)(2,1)} %copy-done.65, bf16[768,768]{1,0:T(8,128)(2,1)} %copy-done.66, bf16[4,2,768,640]{3,2,1,0:T(8,128)(2,1)} %bitcast.51, ...), custom_call_target="tpu_custom_call" | custom-call | flops 23000000512 | bytes 1000 | tf_op jit(solution)/shard_map/expert/pallas_call | solution.py:111
  185.2 6.7 %all-gather.5.cloned.1.call-done = bf16[6144,128]{1,0:T(8,128)(2,1)} async-done(((bf16[1536,128]{1,0:T(8,128)(2,1)}), bf16[6144,128]{1,0:T(8,128)(2,1)}) %all-gather.5.cloned.1.call-update) | async-done | bytes 1572880 | tf_op jit(solution)/shard_map/all_gather | solution.py:915
  191.9 12.9 %expert_last.1 = (bf16[768,896]{1,0:T(8,128)(2,1)}, bf16[768,768]{1,0:T(8,128)(2,1)}, bf16[4,768,128]{2,1,0:T(8,128)(2,1)}, bf16[4,768,128]{2,1,0:T(8,128)(2,1)}) custom-call(bf16[768,768]{1,0:T(8,128)(2,1)} %copy-done.67, bf16[768,768]{1,0:T(8,128)(2,1)} %copy-done.68, bf16[768,768]{1,0:T(8,128)(2,1)} %copy-done.65, bf16[768,768]{1,0:T(8,128)(2,1)} %copy-done.66, ...), custom_call_target="tpu_custom_call" | custom-call | flops 11500000256 | bytes 1000 | tf_op jit(solution)/shard_map/expert_last/pallas_call | solution.py:111
  204.8 4.1 all-to-all-start.2
  208.9 6.1 %expert_grads.1.refs_8_ = bf16[4,2,768,128]{3,2,1,0:T(8,128)(2,1)} custom-call(bf16[768,768]{1,0:T(8,128)(2,1)} %copy-done.65, bf16[768,768]{1,0:T(8,128)(2,1)} %copy-done.66, bf16[4,768,128]{2,1,0:T(8,128)(2,1)} %get-tuple-element.123.refs_2_.refs_4_, bf16[4,768,128]{2,1,0:T(8,128)(2,1)} %get-tuple-element.124.refs_3_, ...), custom_call_target="tpu_custom_call" | custom-call | flops 6899999744 | bytes 1000 | tf_op jit(solution)/shard_map/expert_grads/pallas_call | solution.py:111
  215.0 12.8 %all-to-all-done.2 = bf16[8,96,896]{2,1,0:T(8,128)(2,1)S(1)} async-done(((bf16[8,96,896]{2,1,0:T(8,128)(2,1)}), bf16[8,96,896]{2,1,0:T(8,128)(2,1)S(1)}, u32[]{:S(2)}, u32[]{:S(2)}) %all-to-all-start.2) | async-done | bytes 1376288 | tf_op jit(solution)/shard_map/all_to_all | solution.py:234
  231.0 1.7 copy-done.69
  232.7 6.3 %gate_back.1 = (f32[384,768]{1,0:T(8,128)S(1)}, bf16[384,768]{1,0:T(8,128)(2,1)S(1)}, f32[2,768]{1,0:T(2,128)S(1)}, f32[8,768]{1,0:T(8,128)S(1)}, bf16[4,96,3072...) custom-call(s32[384,1]{1,0:T(8,128)S(1)} %copy-done.59, s32[384,1]{1,0:T(8,128)S(1)} %copy-done.29, ...), custom_call_target="tpu_custom_call" | custom-call | flops 11500000256 | bytes 1000 | tf_op jit(solution)/shard_map/gate_back/pallas_call | solution.py:111
  239.0 1.5 copy-done.9
  243.4 3.6 all-to-all-start.3
  247.1 11.9 %widen_back.1 = (bf16[384,3072]{1,0:T(8,128)(2,1)}, bf16[4,384,768]{2,1,0:T(8,128)(2,1)}, bf16[4,384,768]{2,1,0:T(8,128)(2,1)}) custom-call(bf16[384,768]{1,0:T(8,128)(2,1)} %copy-done.73, bf16[384,3072]{1,0:T(8,128)(2,1)} %get-tuple-element.126.refs_1_, bf16[384,768]{1,0:T(8,128)(2,1)} %get-tuple-element.97.refs_0_.refs_2_, ...), custom_call_target="tpu_custom_call" | custom-call | flops 13799999488 | bytes 1000 | tf_op jit(solution)/shard_map/widen_back/pallas_call | solution.py:111
  259.5 4.2 all-to-all-done.3
  263.8 1.7 copy-done.10
  265.4 1.7 copy-done.11
  267.2 2.4 fold.3
  271.0 6.8 %second_back.1 = (f32[384,768]{1,0:T(8,128)S(1)}, bf16[384,768]{1,0:T(8,128)(2,1)S(1)}, f32[2,768]{1,0:T(2,128)S(1)}, bf16[4,96,768]{2,1,0:T(8,128)(2,1)S(1)}, bf16[4,96,768]{2,1,0:T(8,128)(2,1)S(1)}) custom-call(bf16[384,3072]{1,0:T(8,128)(2,1)S(1)} %copy-done.12, f32[384,768]{1,0:T(8,128)S(1)} %copy-done.70, f32[384,768]{1,0:T(8,128)S(1)} %copy-done.72, ...), custom_call_target="tpu_custom_call" | custom-call | flops 19549999104 | bytes 1000 | tf_op jit(solution)/shard_map/second_back/pallas_call | solution.py:111
  279.2 12.4 %attend_back.1.refs_4_.refs_0_ = bf16[384,2304]{1,0:T(8,128)(2,1)S(1)} custom-call(bf16[384,768]{1,0:T(8,128)(2,1)S(1)} %get-tuple-element.134.refs_0_, bf16[384,2304]{1,0:T(8,128)(2,1)S(1)} %copy-done.13, f32[384,128]{1,0:T(8,128)S(1)} %copy-done.30, s32[384,1]{1,0:T(8,128)S(1)} %copy-done.21, s32[1,384]{1,0:T(1,128)S(1)} %copy-done.40, ...), custom_call_target="tpu_custom_call" | custom-call | flops 2300000000 | bytes 1000 | tf_op jit(solution)/shard_map/attend_back/pallas_call | solution.py:111
  292.4 1.6 collective-permute-start.34
  296.5 5.5 %tokens_back.1 = (f32[384,768]{1,0:T(8,128)}, bf16[4,16,768]{2,1,0:T(8,128)(2,1)S(1)}, bf16[4,16,768]{2,1,0:T(8,128)(2,1)S(1)}) custom-call(bf16[384,2304]{1,0:T(8,128)(2,1)S(1)} %attend_back.1.refs_4_.refs_0_, bf16[384,768]{1,0:T(8,128)(2,1)S(1)} %copy-done.23, f32[384,768]{1,0:T(8,128)S(1)} %get-tuple-element.139.refs_2_, f32[16,768]{1,0:T(8,128)S(1)} %copy-done.34, ...), custom_call_target="tpu_custom_call" | custom-call | flops 2300000000 | bytes 1000 | tf_op jit(solution)/shard_map/tokens_back/pallas_call | solution.py:111
  302.0 2.3 project_back.1
  304.9 5.8 %collective-permute-done.34.refs_1_ = bf16[2,240,768]{2,1,0:T(8,128)(2,1)S(1)} collective-permute-done((bf16[2,240,768]{2,1,0:T(8,128)(2,1)S(1)}, bf16[2,240,768]{2,1,0:T(8,128)(2,1)S(1)}, u32[]{:S(2)}, u32[]{:S(2)}) %collective-permute-start.34) | collective-permute-done | bytes 737312 | tf_op jit(solution)/shard_map/ppermute | solution.py:171
  315.3 1.5 collective-permute-start.39
  318.2 15.1 %collective-permute-done.38.refs_1_ = bf16[48,3072]{1,0:T(8,128)(2,1)S(1)} collective-permute-done((bf16[48,3072]{1,0:T(8,128)(2,1)S(1)}, bf16[48,3072]{1,0:T(8,128)(2,1)S(1)}, u32[]{:S(2)}, u32[]{:S(2)}) %collective-permute-start.38) | collective-permute-done | bytes 294944 | tf_op jit(solution)/shard_map/ppermute | solution.py:171
  333.9 2.5 collective-permute-start.46
  338.1 1.6 collective-permute-start.40
  339.6 1.5 collective-permute-done.42.refs_1_
  342.2 2.3 collective-permute-start.45
  345.6 3.0 collective-permute-start.44
  348.6 1.5 combine.1.refs_2_
  352.1 18.1 %collective-permute-done.45.refs_1_ = bf16[480,768]{1,0:T(8,128)(2,1)S(1)} collective-permute-done((bf16[480,768]{1,0:T(8,128)(2,1)S(1)}, bf16[480,768]{1,0:T(8,128)(2,1)S(1)}, u32[]{:S(2)}, u32[]{:S(2)}) %collective-permute-start.45) | collective-permute-done | bytes 737312 | tf_op jit(solution)/shard_map/ppermute | solution.py:315
  371.1 14.2 %collective-permute-done.44.refs_1_ = bf16[304,768]{1,0:T(8,128)(2,1)} collective-permute-done((bf16[304,768]{1,0:T(8,128)(2,1)}, bf16[304,768]{1,0:T(8,128)(2,1)}, u32[]{:S(2)}, u32[]{:S(2)}) %collective-permute-start.44) | collective-permute-done | bytes 466976 | tf_op jit(solution)/shard_map/ppermute | solution.py:315
  390.9 1.6 collective-permute-start.51
  394.6 4.1 reduce-scatter.5.cloned.1.call-done
  399.7 2.5 finish.1
  402.2 2.4 collective-permute-done.52.refs_1_
  404.7 2.3 settle.3.refs_2_
  407.0 19.3 %collective-permute-done.51.refs_1_ = bf16[480,768]{1,0:T(8,128)(2,1)} collective-permute-done((bf16[480,768]{1,0:T(8,128)(2,1)S(1)}, bf16[480,768]{1,0:T(8,128)(2,1)}, u32[]{:S(2)}, u32[]{:S(2)}) %collective-permute-start.51) | collective-permute-done | bytes 737312 | tf_op jit(solution)/shard_map/ppermute | solution.py:315
  426.3 2.7 settle.4
  429.0 2.3 collective-permute-done.50.refs_1_
  431.3 2.2 settle.5
  434.8 2.1 slice_bitcast_fusion
  (287 shorter events, 67.0 us)
Async XLA Ops:
  7.2 147.2 %all-gather.3.cloned.1.call-start = ((), (), s32[]{:S(2)}) async-start(), calls=%async_computation.6 | async-start | bytes 9830400 | tf_op jit(solution)/shard_map/all_gather | solution.py:915
  10.4 23.4 %copy-start.41 = (s32[384,1]{0,1:T(1,128)S(1)}, s32[384,1]{0,1:T(1,128)}, u32[]{:S(2)}) copy-start(s32[384,1]{0,1:T(1,128)} %param.15) | copy-start | bytes 4612
  11.1 22.8 %copy-start.39 = (s32[1,384]{1,0:T(1,128)S(1)}, s32[1,384]{1,0:T(1,128)}, u32[]{:S(2)}) copy-start(s32[1,384]{1,0:T(1,128)} %refs_4_.2) | copy-start | bytes 4612
  11.5 31.7 %copy-start = (bf16[400,768]{1,0:T(8,128)(2,1)}, bf16[400,768]{1,0:T(8,128)(2,1)S(1)}, u32[]{:S(2)}) copy-start(bf16[400,768]{1,0:T(8,128)(2,1)S(1)} %pad_maximum_fusion.1.refs_3_.refs_11_.refs_21_.refs_5_.refs_7_) | copy-start | bytes 1843204
  11.6 16.9 %collective-permute-start.1 = (bf16[400,768]{1,0:T(8,128)(2,1)S(1)}, bf16[400,768]{1,0:T(8,128)(2,1)S(1)}, u32[]{:S(2)}, u32[]{:S(2)}) collective-permute-start(bf16[400,768]{1,0:T(8,128)(2,1)S(1)} %pad_maximum_fusion.1.refs_3_.refs_11_.refs_21_.refs_5_.refs_7_), channel_id=1, source_target_pairs={{0,2},{1,3},{2,0},{3,1},{4,6},{5,7},{6,4},{7,5},{8,10},{9,11},{10,... | collective-permute-start | bytes 1843208 | tf_op jit(solution)/shard_map/ppermute | solution.py:171
  14.6 16.4 %collective-permute-start.3 = (bf16[400,768]{1,0:T(8,128)(2,1)S(1)}, bf16[400,768]{1,0:T(8,128)(2,1)S(1)}, u32[]{:S(2)}, u32[]{:S(2)}) collective-permute-start(bf16[400,768]{1,0:T(8,128)(2,1)S(1)} %pad_maximum_fusion.1.refs_3_.refs_11_.refs_21_.refs_5_.refs_7_), channel_id=1, source_target_pairs={{0,4},{1,5},{2,6},{3,7},{4,0},{5,1},{6,2},{7,3},{8,12},{9,13},{10,... | collective-permute-start | bytes 1843208 | tf_op jit(solution)/shard_map/ppermute | solution.py:171
  29.2 10.5 %collective-permute-start.5 = (bf16[208,768]{1,0:T(8,128)(2,1)}, bf16[208,768]{1,0:T(8,128)(2,1)S(1)}, u32[]{:S(2)}, u32[]{:S(2)}) collective-permute-start(bf16[208,768]{1,0:T(8,128)(2,1)} %slice.60), channel_id=1, source_target_pairs={{0,4},{1,5},{2,6},{3,7},{4,0},{5,1},{6,2},{7,3},{8,12},{9,13},{10,... | collective-permute-start | bytes 958472 | tf_op jit(solution)/shard_map/ppermute | solution.py:171
  31.8 7.9 %collective-permute-start.7 = (bf16[192,768]{1,0:T(8,128)(2,1)}, bf16[192,768]{1,0:T(8,128)(2,1)S(1)}, u32[]{:S(2)}, u32[]{:S(2)}) collective-permute-start(bf16[192,768]{1,0:T(8,128)(2,1)} %slice.61), channel_id=1, source_target_pairs={{0,2},{1,3},{2,0},{3,1},{4,6},{5,7},{6,4},{7,5},{8,10},{9,11},{10,... | collective-permute-start | bytes 884744 | tf_op jit(solution)/shard_map/ppermute | solution.py:171
  33.3 10.7 %collective-permute-start = (bf16[400,768]{1,0:T(8,128)(2,1)S(1)}, bf16[400,768]{1,0:T(8,128)(2,1)S(1)}, u32[]{:S(2)}, u32[]{:S(2)}) collective-permute-start(bf16[400,768]{1,0:T(8,128)(2,1)S(1)} %pad_maximum_fusion.1.refs_3_.refs_11_.refs_21_.refs_5_.refs_7_), channel_id=1, source_target_pairs={{0,1},{1,0},{2,3},{3,2},{4,5},{5,4},{6,7},{7,6},{8,9},{9,8},{10,11... | collective-permute-start | bytes 1843208 | tf_op jit(solution)/shard_map/ppermute | solution.py:171
  33.3 12.7 %collective-permute-start.2 = (bf16[400,768]{1,0:T(8,128)(2,1)S(1)}, bf16[400,768]{1,0:T(8,128)(2,1)}, u32[]{:S(2)}, u32[]{:S(2)}) collective-permute-start(bf16[400,768]{1,0:T(8,128)(2,1)S(1)} %collective-permute-done.1.refs_5_.refs_13_.refs_23_.refs_7_.refs_9_), channel_id=1, source_target_pairs={{0,1},{1,0},{2,3},{3,2},{4,5},{5,4},{6,7},{7,6},{8,9},{9,8},{10,11... | collective-permute-start | bytes 1843208 | tf_op jit(solution)/shard_map/ppermute | solution.py:171
  33.8 12.8 %collective-permute-start.4 = (bf16[400,768]{1,0:T(8,128)(2,1)S(1)}, bf16[400,768]{1,0:T(8,128)(2,1)}, u32[]{:S(2)}, u32[]{:S(2)}) collective-permute-start(bf16[400,768]{1,0:T(8,128)(2,1)S(1)} %collective-permute-done.3.refs_7_.refs_15_.refs_25_.refs_9_.refs_11_), channel_id=1, source_target_pairs={{0,1},{1,0},{2,3},{3,2},{4,5},{5,4},{6,7},{7,6},{8,9},{9,8},{10,11... | collective-permute-start | bytes 1843208 | tf_op jit(solution)/shard_map/ppermute | solution.py:171
  39.7 5.7 %collective-permute-start.8 = (bf16[192,768]{1,0:T(8,128)(2,1)S(1)}, bf16[192,768]{1,0:T(8,128)(2,1)S(1)}, u32[]{:S(2)}, u32[]{:S(2)}) collective-permute-start(bf16[192,768]{1,0:T(8,128)(2,1)S(1)} %collective-permute-done.7.refs_17_.refs_13_), channel_id=1, source_target_pairs={{0,1},{1,0},{2,3},{3,2},{4,5},{5,4},{6,7},{7,6},{8,9},{9,8},{10,11... | collective-permute-start | bytes 884744 | tf_op jit(solution)/shard_map/ppermute | solution.py:171
  39.7 8.3 %collective-permute-start.6 = (bf16[208,768]{1,0:T(8,128)(2,1)S(1)}, bf16[208,768]{1,0:T(8,128)(2,1)S(1)}, u32[]{:S(2)}, u32[]{:S(2)}) collective-permute-start(bf16[208,768]{1,0:T(8,128)(2,1)S(1)} %collective-permute-done.5.refs_9_.refs_18_.refs_27_.refs_11_.refs_14_), channel_id=1, source_target_pairs={{0,1},{1,0},{2,3},{3,2},{4,5},{5,4},{6,7},{7,6},{8,9},{9,8},{10,11... | collective-permute-start | bytes 958472 | tf_op jit(solution)/shard_map/ppermute | solution.py:171
  43.9 20.7 %collective-permute-start.9 = (bf16[768,384]{1,0:T(8,128)(2,1)}, bf16[768,384]{1,0:T(8,128)(2,1)S(1)}, u32[]{:S(2)}, u32[]{:S(2)}) collective-permute-start(bf16[768,384]{1,0:T(8,128)(2,1)} %refs_5_.2), channel_id=1, source_target_pairs={{0,2},{1,3},{2,0},{3,1},{4,6},{5,7},{6,4},{7,5},{8,10},{9,11},{10,... | collective-permute-start | bytes 1769480 | tf_op jit(solution)/shard_map/ppermute | solution.py:171
  45.4 19.2 %collective-permute-start.10 = (bf16[768,384]{1,0:T(8,128)(2,1)}, bf16[768,384]{1,0:T(8,128)(2,1)}, u32[]{:S(2)}, u32[]{:S(2)}) collective-permute-start(bf16[768,384]{1,0:T(8,128)(2,1)} %refs_5_.2), channel_id=1, source_target_pairs={{0,4},{1,5},{2,6},{3,7},{4,0},{5,1},{6,2},{7,3},{8,12},{9,13},{10,... | collective-permute-start | bytes 1769480 | tf_op jit(solution)/shard_map/ppermute | solution.py:171
  45.9 27.1 %collective-permute-start.18 = (bf16[96,3072]{1,0:T(8,128)(2,1)}, bf16[96,3072]{1,0:T(8,128)(2,1)}, u32[]{:S(2)}, u32[]{:S(2)}) collective-permute-start(bf16[96,3072]{1,0:T(8,128)(2,1)} %bitcast.4.refs_5_.refs_3_), channel_id=1, source_target_pairs={{0,2},{1,3},{2,0},{3,1},{4,6},{5,7},{6,4},{7,5},{8,10},{9,11},{10,... | collective-permute-start | bytes 1769480 | tf_op jit(solution)/shard_map/ppermute | solution.py:171
  46.5 28.1 %collective-permute-start.19 = (bf16[96,3072]{1,0:T(8,128)(2,1)}, bf16[96,3072]{1,0:T(8,128)(2,1)}, u32[]{:S(2)}, u32[]{:S(2)}) collective-permute-start(bf16[96,3072]{1,0:T(8,128)(2,1)} %bitcast.4.refs_5_.refs_3_), channel_id=1, source_target_pairs={{0,4},{1,5},{2,6},{3,7},{4,0},{5,1},{6,2},{7,3},{8,12},{9,13},{10,... | collective-permute-start | bytes 1769480 | tf_op jit(solution)/shard_map/ppermute | solution.py:171
  65.9 13.4 %collective-permute-start.14 = (bf16[384,384]{1,0:T(8,128)(2,1)S(1)}, bf16[384,384]{1,0:T(8,128)(2,1)S(1)}, u32[]{:S(2)}, u32[]{:S(2)}) collective-permute-start(bf16[384,384]{1,0:T(8,128)(2,1)S(1)} %slice.48), channel_id=1, source_target_pairs={{0,2},{1,3},{2,0},{3,1},{4,6},{5,7},{6,4},{7,5},{8,10},{9,11},{10,... | collective-permute-start | bytes 884744 | tf_op jit(solution)/shard_map/ppermute | solution.py:171
  67.5 13.4 %collective-permute-start.15 = (bf16[384,384]{1,0:T(8,128)(2,1)S(1)}, bf16[384,384]{1,0:T(8,128)(2,1)}, u32[]{:S(2)}, u32[]{:S(2)}) collective-permute-start(bf16[384,384]{1,0:T(8,128)(2,1)S(1)} %slice.49), channel_id=1, source_target_pairs={{0,4},{1,5},{2,6},{3,7},{4,0},{5,1},{6,2},{7,3},{8,12},{9,13},{10,... | collective-permute-start | bytes 884744 | tf_op jit(solution)/shard_map/ppermute | solution.py:171
  75.6 9.2 %collective-permute-start.23 = (bf16[48,3072]{1,0:T(8,128)(2,1)S(1)}, bf16[48,3072]{1,0:T(8,128)(2,1)S(1)}, u32[]{:S(2)}, u32[]{:S(2)}) collective-permute-start(bf16[48,3072]{1,0:T(8,128)(2,1)S(1)} %slice.50), channel_id=1, source_target_pairs={{0,2},{1,3},{2,0},{3,1},{4,6},{5,7},{6,4},{7,5},{8,10},{9,11},{10,... | collective-permute-start | bytes 884744 | tf_op jit(solution)/shard_map/ppermute | solution.py:171
  77.2 8.8 %collective-permute-start.24 = (bf16[48,3072]{1,0:T(8,128)(2,1)S(1)}, bf16[48,3072]{1,0:T(8,128)(2,1)S(1)}, u32[]{:S(2)}, u32[]{:S(2)}) collective-permute-start(bf16[48,3072]{1,0:T(8,128)(2,1)S(1)} %slice.51), channel_id=1, source_target_pairs={{0,4},{1,5},{2,6},{3,7},{4,0},{5,1},{6,2},{7,3},{8,12},{9,13},{10,... | collective-permute-start | bytes 884744 | tf_op jit(solution)/shard_map/ppermute | solution.py:171
  77.8 13.6 %collective-permute-start.11 = (bf16[768,384]{1,0:T(8,128)(2,1)}, bf16[768,384]{1,0:T(8,128)(2,1)S(1)}, u32[]{:S(2)}, u32[]{:S(2)}) collective-permute-start(bf16[768,384]{1,0:T(8,128)(2,1)} %refs_5_.2), channel_id=1, source_target_pairs={{0,1},{1,0},{2,3},{3,2},{4,5},{5,4},{6,7},{7,6},{8,9},{9,8},{10,11... | collective-permute-start | bytes 1769480 | tf_op jit(solution)/shard_map/ppermute | solution.py:171
  79.3 12.6 %collective-permute-start.12 = (bf16[768,384]{1,0:T(8,128)(2,1)S(1)}, bf16[768,384]{1,0:T(8,128)(2,1)S(1)}, u32[]{:S(2)}, u32[]{:S(2)}) collective-permute-start(bf16[768,384]{1,0:T(8,128)(2,1)S(1)} %collective-permute-done.9.refs_3_.refs_7_), channel_id=1, source_target_pairs={{0,1},{1,0},{2,3},{3,2},{4,5},{5,4},{6,7},{7,6},{8,9},{9,8},{10,11... | collective-permute-start | bytes 1769480 | tf_op jit(solution)/shard_map/ppermute | solution.py:171
  80.9 11.0 %collective-permute-start.13 = (bf16[768,384]{1,0:T(8,128)(2,1)}, bf16[768,384]{1,0:T(8,128)(2,1)}, u32[]{:S(2)}, u32[]{:S(2)}) collective-permute-start(bf16[768,384]{1,0:T(8,128)(2,1)} %collective-permute-done.10.refs_5_.refs_9_), channel_id=1, source_target_pairs={{0,1},{1,0},{2,3},{3,2},{4,5},{5,4},{6,7},{7,6},{8,9},{9,8},{10,11... | collective-permute-start | bytes 1769480 | tf_op jit(solution)/shard_map/ppermute | solution.py:171
  84.8 6.0 %collective-permute-start.16 = (bf16[384,384]{1,0:T(8,128)(2,1)S(1)}, bf16[384,384]{1,0:T(8,128)(2,1)}, u32[]{:S(2)}, u32[]{:S(2)}) collective-permute-start(bf16[384,384]{1,0:T(8,128)(2,1)S(1)} %collective-permute-done.14.refs_7_.refs_11_), channel_id=1, source_target_pairs={{0,1},{1,0},{2,3},{3,2},{4,5},{5,4},{6,7},{7,6},{8,9},{9,8},{10,11... | collective-permute-start | bytes 884744 | tf_op jit(solution)/shard_map/ppermute | solution.py:171
  86.0 5.3 %collective-permute-start.17 = (bf16[384,384]{1,0:T(8,128)(2,1)}, bf16[384,384]{1,0:T(8,128)(2,1)}, u32[]{:S(2)}, u32[]{:S(2)}) collective-permute-start(bf16[384,384]{1,0:T(8,128)(2,1)} %collective-permute-done.15.refs_8_.refs_12_), channel_id=1, source_target_pairs={{0,1},{1,0},{2,3},{3,2},{4,5},{5,4},{6,7},{7,6},{8,9},{9,8},{10,11... | collective-permute-start | bytes 884744 | tf_op jit(solution)/shard_map/ppermute | solution.py:171
  86.7 20.8 %all-to-all-start = ((bf16[8,96,768]{2,1,0:T(8,128)(2,1)}), bf16[8,96,768]{2,1,0:T(8,128)(2,1)S(1)}, u32[]{:S(2)}, u32[]{:S(2)}) async-start(bf16[8,96,768]{2,1,0:T(8,128)(2,1)} %bitcast.5), calls=%async_computation | async-start | bytes 2359296 | tf_op jit(solution)/shard_map/all_to_all | solution.py:234
  90.8 11.4 %collective-permute-start.21 = (bf16[96,3072]{1,0:T(8,128)(2,1)}, bf16[96,3072]{1,0:T(8,128)(2,1)}, u32[]{:S(2)}, u32[]{:S(2)}) collective-permute-start(bf16[96,3072]{1,0:T(8,128)(2,1)} %collective-permute-done.18.refs_7_.refs_5_), channel_id=1, source_target_pairs={{0,1},{1,0},{2,3},{3,2},{4,5},{5,4},{6,7},{7,6},{8,9},{9,8},{10,11... | collective-permute-start | bytes 1769480 | tf_op jit(solution)/shard_map/ppermute | solution.py:171
  91.3 10.9 %collective-permute-start.22 = (bf16[96,3072]{1,0:T(8,128)(2,1)}, bf16[96,3072]{1,0:T(8,128)(2,1)}, u32[]{:S(2)}, u32[]{:S(2)}) collective-permute-start(bf16[96,3072]{1,0:T(8,128)(2,1)} %collective-permute-done.19.refs_9_.refs_7_), channel_id=1, source_target_pairs={{0,1},{1,0},{2,3},{3,2},{4,5},{5,4},{6,7},{7,6},{8,9},{9,8},{10,11... | collective-permute-start | bytes 1769480 | tf_op jit(solution)/shard_map/ppermute | solution.py:171
  91.4 10.8 %collective-permute-start.20 = (bf16[96,3072]{1,0:T(8,128)(2,1)}, bf16[96,3072]{1,0:T(8,128)(2,1)}, u32[]{:S(2)}, u32[]{:S(2)}) collective-permute-start(bf16[96,3072]{1,0:T(8,128)(2,1)} %bitcast.4.refs_5_.refs_3_), channel_id=1, source_target_pairs={{0,1},{1,0},{2,3},{3,2},{4,5},{5,4},{6,7},{7,6},{8,9},{9,8},{10,11... | collective-permute-start | bytes 1769480 | tf_op jit(solution)/shard_map/ppermute | solution.py:171
  91.9 10.3 %collective-permute-start.25 = (bf16[48,3072]{1,0:T(8,128)(2,1)}, bf16[48,3072]{1,0:T(8,128)(2,1)S(1)}, u32[]{:S(2)}, u32[]{:S(2)}) collective-permute-start(bf16[48,3072]{1,0:T(8,128)(2,1)} %copy-done.82), channel_id=1, source_target_pairs={{0,1},{1,0},{2,3},{3,2},{4,5},{5,4},{6,7},{7,6},{8,9},{9,8},{10,11... | collective-permute-start | bytes 884744 | tf_op jit(solution)/shard_map/ppermute | solution.py:171
  92.0 10.3 %collective-permute-start.26 = (bf16[48,3072]{1,0:T(8,128)(2,1)}, bf16[48,3072]{1,0:T(8,128)(2,1)S(1)}, u32[]{:S(2)}, u32[]{:S(2)}) collective-permute-start(bf16[48,3072]{1,0:T(8,128)(2,1)} %copy-done.83), channel_id=1, source_target_pairs={{0,1},{1,0},{2,3},{3,2},{4,5},{5,4},{6,7},{7,6},{8,9},{9,8},{10,11... | collective-permute-start | bytes 884744 | tf_op jit(solution)/shard_map/ppermute | solution.py:171
  118.5 22.6 %all-to-all-start.1 = ((bf16[8,96,896]{2,1,0:T(8,128)(2,1)}), bf16[8,96,896]{2,1,0:T(8,128)(2,1)S(1)}, u32[]{:S(2)}, u32[]{:S(2)}) async-start(bf16[8,96,896]{2,1,0:T(8,128)(2,1)} %bitcast.41), calls=%async_computation.1 | async-start | bytes 2752512 | tf_op jit(solution)/shard_map/all_to_all | solution.py:234
  122.2 69.7 %all-gather.5.cloned.1.call-start = ((), (), s32[]{:S(2)}) async-start(), calls=%async_computation.7 | async-start | bytes 1966080 | tf_op jit(solution)/shard_map/all_gather | solution.py:915
  125.0 227.1 %reduce-scatter.3.cloned.1.call-start = ((), (), s32[]{:S(2)}) async-start(), calls=%async_computation.8 | async-start | bytes 9830400 | tf_op jit(solution)/shard_map/reduce_scatter | solution.py:952
  204.8 23.0 %all-to-all-start.2 = ((bf16[8,96,896]{2,1,0:T(8,128)(2,1)}), bf16[8,96,896]{2,1,0:T(8,128)(2,1)S(1)}, u32[]{:S(2)}, u32[]{:S(2)}) async-start(bf16[8,96,896]{2,1,0:T(8,128)(2,1)} %bitcast.42), calls=%async_computation.2 | async-start | bytes 2752512 | tf_op jit(solution)/shard_map/all_to_all | solution.py:234
  243.4 20.3 %collective-permute-start.27 = (bf16[4,96,3072]{2,1,0:T(8,128)(2,1)}, bf16[4,96,3072]{2,1,0:T(8,128)(2,1)}, u32[]{:S(2)}, u32[]{:S(2)}) collective-permute-start(bf16[4,96,3072]{2,1,0:T(8,128)(2,1)} %get-tuple-element.132), channel_id=1, source_target_pairs={{0,1},{1,0},{2,3},{3,2},{4,5},{5,4},{6,7},{7,6},{8,9},{9,8},{10,11... | collective-permute-start | bytes 7077896 | tf_op jit(solution)/shard_map/ppermute | solution.py:171
  243.4 20.3 %all-to-all-start.3 = ((bf16[8,96,768]{2,1,0:T(8,128)(2,1)}), bf16[8,96,768]{2,1,0:T(8,128)(2,1)S(1)}, u32[]{:S(2)}, u32[]{:S(2)}) async-start(bf16[8,96,768]{2,1,0:T(8,128)(2,1)} %bitcast.47), calls=%async_computation.3 | async-start | bytes 2359296 | tf_op jit(solution)/shard_map/all_to_all | solution.py:234
  247.0 151.7 %reduce-scatter.5.cloned.1.call-start = ((), (), s32[]{:S(2)}) async-start(), calls=%async_computation.9 | async-start | bytes 1966080 | tf_op jit(solution)/shard_map/reduce_scatter | solution.py:952
  259.0 32.7 %collective-permute-start.30 = (bf16[4,384,768]{2,1,0:T(8,128)(2,1)}, bf16[4,384,768]{2,1,0:T(8,128)(2,1)S(1)}, u32[]{:S(2)}, u32[]{:S(2)}) collective-permute-start(bf16[4,384,768]{2,1,0:T(8,128)(2,1)} %get-tuple-element.146), channel_id=1, source_target_pairs={{0,1},{1,0},{2,3},{3,2},{4,5},{5,4},{6,7},{7,6},{8,9},{9,8},{10,11... | collective-permute-start | bytes 7077896 | tf_op jit(solution)/shard_map/ppermute | solution.py:171
  277.8 13.9 %collective-permute-start.31 = (bf16[4,96,768]{2,1,0:T(8,128)(2,1)S(1)}, bf16[4,96,768]{2,1,0:T(8,128)(2,1)S(1)}, u32[]{:S(2)}, u32[]{:S(2)}) collective-permute-start(bf16[4,96,768]{2,1,0:T(8,128)(2,1)S(1)} %get-tuple-element.147), channel_id=1, source_target_pairs={{0,1},{1,0},{2,3},{3,2},{4,5},{5,4},{6,7},{7,6},{8,9},{9,8},{10,11... | collective-permute-start | bytes 1769480 | tf_op jit(solution)/shard_map/ppermute | solution.py:171
  277.9 17.4 %collective-permute-start.28 = (bf16[2,48,3072]{2,1,0:T(8,128)(2,1)S(1)}, bf16[2,48,3072]{2,1,0:T(8,128)(2,1)S(1)}, u32[]{:S(2)}, u32[]{:S(2)}) collective-permute-start(bf16[2,48,3072]{2,1,0:T(8,128)(2,1)S(1)} %get-tuple-element.141), channel_id=1, source_target_pairs={{0,2},{1,3},{2,0},{3,1},{4,6},{5,7},{6,4},{7,5},{8,10},{9,11},{10,... | collective-permute-start | bytes 1769480 | tf_op jit(solution)/shard_map/ppermute | solution.py:171
  278.7 16.6 %collective-permute-start.29 = (bf16[2,48,3072]{2,1,0:T(8,128)(2,1)S(1)}, bf16[2,48,3072]{2,1,0:T(8,128)(2,1)S(1)}, u32[]{:S(2)}, u32[]{:S(2)}) collective-permute-start(bf16[2,48,3072]{2,1,0:T(8,128)(2,1)S(1)} %get-tuple-element.143), channel_id=1, source_target_pairs={{0,4},{1,5},{2,6},{3,7},{4,0},{5,1},{6,2},{7,3},{8,12},{9,13},{10,... | collective-permute-start | bytes 1769480 | tf_op jit(solution)/shard_map/ppermute | solution.py:171
  292.4 18.3 %collective-permute-start.34 = (bf16[2,240,768]{2,1,0:T(8,128)(2,1)S(1)}, bf16[2,240,768]{2,1,0:T(8,128)(2,1)S(1)}, u32[]{:S(2)}, u32[]{:S(2)}) collective-permute-start(bf16[2,240,768]{2,1,0:T(8,128)(2,1)S(1)} %get-tuple-element.154), channel_id=1, source_target_pairs={{0,2},{1,3},{2,0},{3,1},{4,6},{5,7},{6,4},{7,5},{8,10},{9,11},{10,... | collective-permute-start | bytes 2211848 | tf_op jit(solution)/shard_map/ppermute | solution.py:171
  293.9 18.0 %collective-permute-start.35 = (bf16[2,240,768]{2,1,0:T(8,128)(2,1)S(1)}, bf16[2,240,768]{2,1,0:T(8,128)(2,1)S(1)}, u32[]{:S(2)}, u32[]{:S(2)}) collective-permute-start(bf16[2,240,768]{2,1,0:T(8,128)(2,1)S(1)} %get-tuple-element.156), channel_id=1, source_target_pairs={{0,4},{1,5},{2,6},{3,7},{4,0},{5,1},{6,2},{7,3},{8,12},{9,13},{10,... | collective-permute-start | bytes 2211848 | tf_op jit(solution)/shard_map/ppermute | solution.py:171
  304.3 8.0 %collective-permute-start.32 = (bf16[4,288,768]{2,1,0:T(8,128)(2,1)S(1)}, bf16[4,288,768]{2,1,0:T(8,128)(2,1)S(1)}, u32[]{:S(2)}, u32[]{:S(2)}) collective-permute-start(bf16[4,288,768]{2,1,0:T(8,128)(2,1)S(1)} %get-tuple-element.152), channel_id=1, source_target_pairs={{0,1},{1,0},{2,3},{3,2},{4,5},{5,4},{6,7},{7,6},{8,9},{9,8},{10,11... | collective-permute-start | bytes 5308424 | tf_op jit(solution)/shard_map/ppermute | solution.py:171
  304.4 7.9 %collective-permute-start.33 = (bf16[4,16,768]{2,1,0:T(8,128)(2,1)S(1)}, bf16[4,16,768]{2,1,0:T(8,128)(2,1)S(1)}, u32[]{:S(2)}, u32[]{:S(2)}) collective-permute-start(bf16[4,16,768]{2,1,0:T(8,128)(2,1)S(1)} %get-tuple-element.153), channel_id=1, source_target_pairs={{0,1},{1,0},{2,3},{3,2},{4,5},{5,4},{6,7},{7,6},{8,9},{9,8},{10,11... | collective-permute-start | bytes 294920 | tf_op jit(solution)/shard_map/ppermute | solution.py:171
  312.7 23.7 %collective-permute-start.37 = (bf16[2,160,768]{2,1,0:T(8,128)(2,1)S(1)}, bf16[2,160,768]{2,1,0:T(8,128)(2,1)S(1)}, u32[]{:S(2)}, u32[]{:S(2)}) collective-permute-start(bf16[2,160,768]{2,1,0:T(8,128)(2,1)S(1)} %get-tuple-element.161), channel_id=1, source_target_pairs={{0,4},{1,5},{2,6},{3,7},{4,0},{5,1},{6,2},{7,3},{8,12},{9,13},{10,... | collective-permute-start | bytes 1474568 | tf_op jit(solution)/shard_map/ppermute | solution.py:171
  314.1 22.3 %collective-permute-start.36 = (bf16[2,144,768]{2,1,0:T(8,128)(2,1)S(1)}, bf16[2,144,768]{2,1,0:T(8,128)(2,1)S(1)}, u32[]{:S(2)}, u32[]{:S(2)}) collective-permute-start(bf16[2,144,768]{2,1,0:T(8,128)(2,1)S(1)} %get-tuple-element.159), channel_id=1, source_target_pairs={{0,2},{1,3},{2,0},{3,1},{4,6},{5,7},{6,4},{7,5},{8,10},{9,11},{10,... | collective-permute-start | bytes 1327112 | tf_op jit(solution)/shard_map/ppermute | solution.py:171
  314.8 18.5 %collective-permute-start.38 = (bf16[48,3072]{1,0:T(8,128)(2,1)S(1)}, bf16[48,3072]{1,0:T(8,128)(2,1)S(1)}, u32[]{:S(2)}, u32[]{:S(2)}) collective-permute-start(bf16[48,3072]{1,0:T(8,128)(2,1)S(1)} %get-tuple-element.162), channel_id=1, source_target_pairs={{0,4},{1,5},{2,6},{3,7},{4,0},{5,1},{6,2},{7,3},{8,12},{9,13},{10,... | collective-permute-start | bytes 884744 | tf_op jit(solution)/shard_map/ppermute | solution.py:171
  315.3 18.5 %collective-permute-start.39 = (bf16[48,3072]{1,0:T(8,128)(2,1)S(1)}, bf16[48,3072]{1,0:T(8,128)(2,1)S(1)}, u32[]{:S(2)}, u32[]{:S(2)}) collective-permute-start(bf16[48,3072]{1,0:T(8,128)(2,1)S(1)} %get-tuple-element.164), channel_id=1, source_target_pairs={{0,2},{1,3},{2,0},{3,1},{4,6},{5,7},{6,4},{7,5},{8,10},{9,11},{10,... | collective-permute-start | bytes 884744 | tf_op jit(solution)/shard_map/ppermute | solution.py:171
  316.8 24.3 %collective-permute-start.42 = (bf16[240,768]{1,0:T(8,128)(2,1)S(1)}, bf16[240,768]{1,0:T(8,128)(2,1)S(1)}, u32[]{:S(2)}, u32[]{:S(2)}) collective-permute-start(bf16[240,768]{1,0:T(8,128)(2,1)S(1)} %get-tuple-element.169), channel_id=1, source_target_pairs={{0,4},{1,5},{2,6},{3,7},{4,0},{5,1},{6,2},{7,3},{8,12},{9,13},{10,... | collective-permute-start | bytes 1105928 | tf_op jit(solution)/shard_map/ppermute | solution.py:171
  333.3 8.8 %collective-permute-start.43 = (bf16[240,768]{1,0:T(8,128)(2,1)S(1)}, bf16[240,768]{1,0:T(8,128)(2,1)S(1)}, u32[]{:S(2)}, u32[]{:S(2)}) collective-permute-start(bf16[240,768]{1,0:T(8,128)(2,1)S(1)} %get-tuple-element.171), channel_id=1, source_target_pairs={{0,2},{1,3},{2,0},{3,1},{4,6},{5,7},{6,4},{7,5},{8,10},{9,11},{10,... | collective-permute-start | bytes 1105928 | tf_op jit(solution)/shard_map/ppermute | solution.py:171
  333.9 16.2 %collective-permute-start.46 = (bf16[96,3072]{1,0:T(8,128)(2,1)S(1)}, bf16[96,3072]{1,0:T(8,128)(2,1)S(1)}, u32[]{:S(2)}, u32[]{:S(2)}) collective-permute-start(bf16[96,3072]{1,0:T(8,128)(2,1)S(1)} %fold_last.3.refs_4_.refs_0_), channel_id=1, source_target_pairs={{0,8},{24,16},{1,9},{25,17},{2,10},{26,18},{3,11},{27,19},{4,12},{... | collective-permute-start | bytes 1769480 | tf_op jit(solution)/shard_map/ppermute | solution.py:315
  336.7 8.0 %collective-permute-start.41 = (bf16[160,768]{1,0:T(8,128)(2,1)S(1)}, bf16[160,768]{1,0:T(8,128)(2,1)S(1)}, u32[]{:S(2)}, u32[]{:S(2)}) collective-permute-start(bf16[160,768]{1,0:T(8,128)(2,1)S(1)} %get-tuple-element.168), channel_id=1, source_target_pairs={{0,2},{1,3},{2,0},{3,1},{4,6},{5,7},{6,4},{7,5},{8,10},{9,11},{10,... | collective-permute-start | bytes 737288 | tf_op jit(solution)/shard_map/ppermute | solution.py:171
  338.1 6.5 %collective-permute-start.40 = (bf16[144,768]{1,0:T(8,128)(2,1)S(1)}, bf16[144,768]{1,0:T(8,128)(2,1)S(1)}, u32[]{:S(2)}, u32[]{:S(2)}) collective-permute-start(bf16[144,768]{1,0:T(8,128)(2,1)S(1)} %get-tuple-element.166), channel_id=1, source_target_pairs={{0,4},{1,5},{2,6},{3,7},{4,0},{5,1},{6,2},{7,3},{8,12},{9,13},{10,... | collective-permute-start | bytes 663560 | tf_op jit(solution)/shard_map/ppermute | solution.py:171
  342.2 28.0 %collective-permute-start.45 = (bf16[480,768]{1,0:T(8,128)(2,1)S(1)}, bf16[480,768]{1,0:T(8,128)(2,1)S(1)}, u32[]{:S(2)}, u32[]{:S(2)}) collective-permute-start(bf16[480,768]{1,0:T(8,128)(2,1)S(1)} %fold_last.4.refs_4_.refs_0_), channel_id=1, source_target_pairs={{0,8},{24,16},{1,9},{25,17},{2,10},{26,18},{3,11},{27,19},{4,12},{... | collective-permute-start | bytes 2211848 | tf_op jit(solution)/shard_map/ppermute | solution.py:315
  345.6 39.8 %collective-permute-start.44 = (bf16[304,768]{1,0:T(8,128)(2,1)}, bf16[304,768]{1,0:T(8,128)(2,1)}, u32[]{:S(2)}, u32[]{:S(2)}) collective-permute-start(bf16[304,768]{1,0:T(8,128)(2,1)} %fold_last.5.refs_4_.refs_0_), channel_id=1, source_target_pairs={{0,8},{24,16},{1,9},{25,17},{2,10},{26,18},{3,11},{27,19},{4,12},{... | collective-permute-start | bytes 1400840 | tf_op jit(solution)/shard_map/ppermute | solution.py:315
  351.3 36.0 %collective-permute-start.49 = (bf16[96,3072]{1,0:T(8,128)(2,1)S(1)}, bf16[96,3072]{1,0:T(8,128)(2,1)S(1)}, u32[]{:S(2)}, u32[]{:S(2)}) collective-permute-start(bf16[96,3072]{1,0:T(8,128)(2,1)S(1)} %joined.6.refs_2_.refs_0_), channel_id=1, source_target_pairs={{8,16},{16,8},{9,17},{17,9},{10,18},{18,10},{11,19},{19,11},{12,20... | collective-permute-start | bytes 1769480 | tf_op jit(solution)/shard_map/ppermute | solution.py:315
  370.4 20.3 %collective-permute-start.48 = (bf16[480,768]{1,0:T(8,128)(2,1)S(1)}, bf16[480,768]{1,0:T(8,128)(2,1)S(1)}, u32[]{:S(2)}, u32[]{:S(2)}) collective-permute-start(bf16[480,768]{1,0:T(8,128)(2,1)S(1)} %joined.7.refs_2_.refs_0_), channel_id=1, source_target_pairs={{8,16},{16,8},{9,17},{17,9},{10,18},{18,10},{11,19},{19,11},{12,20... | collective-permute-start | bytes 2211848 | tf_op jit(solution)/shard_map/ppermute | solution.py:315
  386.6 5.8 %collective-permute-start.47 = (bf16[304,768]{1,0:T(8,128)(2,1)S(1)}, bf16[304,768]{1,0:T(8,128)(2,1)S(1)}, u32[]{:S(2)}, u32[]{:S(2)}) collective-permute-start(bf16[304,768]{1,0:T(8,128)(2,1)S(1)} %joined.8.refs_2_.refs_0_), channel_id=1, source_target_pairs={{8,16},{16,8},{9,17},{17,9},{10,18},{18,10},{11,19},{19,11},{12,20... | collective-permute-start | bytes 1400840 | tf_op jit(solution)/shard_map/ppermute | solution.py:315
  389.3 15.3 %collective-permute-start.52 = (bf16[96,3072]{1,0:T(8,128)(2,1)S(1)}, bf16[96,3072]{1,0:T(8,128)(2,1)}, u32[]{:S(2)}, u32[]{:S(2)}) collective-permute-start(bf16[96,3072]{1,0:T(8,128)(2,1)S(1)} %joined.9.refs_2_.refs_0_), channel_id=1, source_target_pairs={{8,0},{16,24},{9,1},{17,25},{10,2},{18,26},{11,3},{19,27},{12,4},{... | collective-permute-start | bytes 1769480 | tf_op jit(solution)/shard_map/ppermute | solution.py:315
  390.9 35.4 %collective-permute-start.51 = (bf16[480,768]{1,0:T(8,128)(2,1)S(1)}, bf16[480,768]{1,0:T(8,128)(2,1)}, u32[]{:S(2)}, u32[]{:S(2)}) collective-permute-start(bf16[480,768]{1,0:T(8,128)(2,1)S(1)} %joined.10.refs_2_.refs_0_), channel_id=1, source_target_pairs={{8,0},{16,24},{9,1},{17,25},{10,2},{18,26},{11,3},{19,27},{12,4},{... | collective-permute-start | bytes 2211848 | tf_op jit(solution)/shard_map/ppermute | solution.py:315
  393.3 38.0 %collective-permute-start.50 = (bf16[304,768]{1,0:T(8,128)(2,1)}, bf16[304,768]{1,0:T(8,128)(2,1)}, u32[]{:S(2)}, u32[]{:S(2)}) collective-permute-start(bf16[304,768]{1,0:T(8,128)(2,1)} %joined.11.refs_2_.refs_0_), channel_id=1, source_target_pairs={{8,0},{16,24},{9,1},{17,25},{10,2},{18,26},{11,3},{19,27},{12,4},{... | collective-permute-start | bytes 1400840 | tf_op jit(solution)/shard_map/ppermute | solution.py:315
  (83 other events, 410.8 us)
Sparse Core Ops, SparseCore 0:
  10.6 143.7 all-gather.2
  156.5 35.3 all-gather.4
  194.2 135.1 reduce-scatter.2
  352.2 46.4 reduce-scatter.4

commit v4 on v3

--- a/solution.py
+++ b/solution.py
@@ -14,11 +14,11 @@
 I32 = jnp.int32
 ROOT = 0.7978845608028654
 COST = dict(
-    prepare=3, attend=16, widen=9, dispatch=10, expert_rows=4, expert=20, expert_last=10, expert_grads=6, gate_back=10, widen_back=12, fold=1,
+    prepare=3, attend=16, widen=9, dispatch=10, expert_rows=4, expert=20, expert_last=10, expert_grads=6, gate_back=10, widen_back=12, fold=1, fold_wide=1,
     second_back=17, attend_back=2, fold_again=1, fold_wait=12, project_back=2, tokens_back=2, fold_last=1, joined=6,
     combine=1, finish=1, settle=1,
 )
-WIDE = ("attend", "widen", "dispatch", "expert", "expert_last", "expert_grads", "widen_back", "settle")
+WIDE = ("attend", "widen", "dispatch", "expert", "expert_last", "expert_grads", "gate_back", "fold_wide", "widen_back", "settle")
 VMEM_LIMIT = 60 * 1024 * 1024
 
 
@@ -252,7 +252,7 @@
     def twins(self, blocks):
         return [self.hop(blocks[1], 1)] if self.cube else []
 
-    def fold(self, groups, twins, after=()):
+    def fold(self, groups, twins, name="fold"):
         if not self.cube:
             return [jnp.concatenate([g[0] for g in groups], axis=1)]
         rows = [g[0].shape[1] for g in groups]
@@ -277,7 +277,7 @@
         outs = [jax.ShapeDtypeStruct((2, half, columns), BF)] * 2
         outs += [jax.ShapeDtypeStruct((2, total - half, columns), BF)] * 2
         args = [g[0] for g in groups] + list(twins)
-        return list(call(kernel, outs, args, "v" * len(args), [], "fold", 0, 0, after))
+        return list(call(kernel, outs, args, "v" * len(args), [], name, 0, 0))
 
     def across(self, kept):
         return [self.hop(kept[1], 2), self.hop(kept[3], 4)] if self.cube else []
@@ -349,6 +349,30 @@
 
         outs = [jax.ShapeDtypeStruct(value.shape, F32)]
         return call(kernel, outs, [value, got[0]], "vv", [], "settle", 0, 0)[0]
+
+    def settled_small(self, value, got, columns, cols):
+        n = self.n
+        rows = [(columns, 3), (columns + 3, 3), (columns + 6, n)]
+        if not self.line:
+            value = lax.psum(value, "dp").astype(F32)
+            return [value[:columns]] + [value[i : i + size, :cols] for i, size in rows]
+
+        def kernel(mine, other, out, *smalls):
+            place = lax.axis_index("dp")
+
+            def write(ref):
+                out[...] = ref[:columns].astype(F32)
+                rest = ref[columns:, :128].astype(F32)
+                for (i, size), small in zip(rows, smalls):
+                    small[...] = rest[i - columns : i - columns + size, :cols]
+
+            middle = (place == 1) | (place == 2)
+            pl.when(middle)(lambda: write(mine))
+            pl.when(jnp.logical_not(middle))(lambda: write(other))
+
+        outs = [jax.ShapeDtypeStruct((columns, value.shape[1]), F32)]
+        outs += [jax.ShapeDtypeStruct((size, cols), F32) for _, size in rows]
+        return call(kernel, outs, [value, got[0]], "vv", [], "settle", 0, 0)
 
     def settled_across(self, value, got, units):
         if not self.line:
@@ -573,6 +597,8 @@
     total, width = rows.shape
     m, _, _, wide = weights.shape
     last, started = cot is not None, sums is not None
+    group = m if last and m * wide <= 512 else 1
+    steps, span = m // group, group * wide
 
     def kernel(rows_ref, grads_ref, rows_across, grads_across, *refs):
         refs = list(refs)
@@ -586,13 +612,17 @@
         else:
             (w_grads,), outs = take(1), take(2)
             held, sems, out_sum, row_sum, grad_held, out_sems = refs
-        entering = [pltpu.make_async_copy(weight_ref.at[i], held.at[i], sems.at[i]) for i in range(m)]
+        entering = []
+        for i in range(m):
+            place = held.at[i // group, :, :, pl.ds(i % group * wide, wide)]
+            entering.append(pltpu.make_async_copy(weight_ref.at[i], place, sems.at[i]))
         for copy in entering:
             copy.start()
         r, g = rows_ref[...], grads_ref[...]
         leaving = []
-        for i in range(m):
-            entering[i].wait()
+        for i in range(steps):
+            for copy in entering[i * group : (i + 1) * group]:
+                copy.wait()
             up, down = held[i, 0], held[i, 1]
             value, slope = smooth_and_slope(mm(r, up))
             act = value.astype(BF)
@@ -628,25 +658,30 @@
     args = [rows, grads, *across] + (sums if started else []) + ([cot] if last else [])
     spaces = "v" * len(args) + "a"
     scratch = [
-        pltpu.VMEM((m, 2, width, wide), BF), pltpu.SemaphoreType.DMA((m,)),
+        pltpu.VMEM((steps, 2, width, span), BF), pltpu.SemaphoreType.DMA((m,)),
         pltpu.VMEM((total, width), F32), pltpu.VMEM((total, width), F32),
     ]
     if last:
-        outs = [shape((total, width + EXTRA), BF), shape((total, width), BF)] + [shape((m, total, wide), BF)] * 2
+        outs = [shape((total, width + EXTRA), BF), shape((total, width), BF)] + [shape((steps, total, span), BF)] * 2
         return call(kernel, outs, args + [weights], spaces, scratch, "expert_last", 0, 0)
     outs = [shape((m, 2, width, wide), BF)] + [shape((total, width), F32)] * 2
     scratch += [pltpu.VMEM((m, 2, width, wide), BF), pltpu.SemaphoreType.DMA((m,))]
     return call(kernel, outs, args + [weights], spaces, scratch, "expert", 0, 0, [], "avv")
 
 
-def expert_grads(across, acts, pre_grads):
-    m, _, wide = acts.shape
+def expert_grads(m, across, acts, pre_grads):
+    steps, _, span = acts.shape
     width = across[0].shape[0]
+    group = m // steps
+    wide = span // group
 
     def kernel(rows_across, grads_across, acts_ref, pre_ref, out):
-        for i in range(m):
-            out[i, 0] = mm(rows_across[...], pre_ref[i]).astype(BF)
-            out[i, 1] = mm(grads_across[...], acts_ref[i]).astype(BF)
+        for i in range(steps):
+            ups = mm(rows_across[...], pre_ref[i]).astype(BF)
+            downs = mm(grads_across[...], acts_ref[i]).astype(BF)
+            for j in range(group):
+                out[i * group + j, 0] = ups[:, j * wide : (j + 1) * wide]
+                out[i * group + j, 1] = downs[:, j * wide : (j + 1) * wide]
 
     outs = [jax.ShapeDtypeStruct((m, 2, width, wide), BF)]
     return call(kernel, outs, [*across, acts, pre_grads], "vvvv", [], "expert_grads", 0, 0)[0]
@@ -946,7 +981,7 @@
         else:
             back, results, acts, pre_grads = expert(rows, grads, across, whole, sums, cots)
     back = links.exchange(back)
-    expert_sums.append(expert_grads(across, acts, pre_grads))
+    expert_sums.append(expert_grads(m, across, acts, pre_grads))
 
     def own_sum(grads):
         sums = lax.psum_scatter(grads.reshape(-1, grads.shape[-1]), "dp", scatter_dimension=0, tiled=True)
@@ -961,10 +996,10 @@
     twin_down = links.twins(sums_down)
     widened_grad, sums_up = widen_back(links, down_in, slope, second_in, weight_down)
     twin_up = links.twins(sums_up)
-    down = links.fold([sums_down], twin_down, [returned])
+    down = links.fold([sums_down], twin_down, "fold_wide")
     down_got = links.across(down)
     after_grad, attn_grad, small_2, sums_out = second_back(
-        links, widened_grad, after_attn, hidden_grad, mixed, small, weight_up, []
+        links, widened_grad, after_attn, hidden_grad, mixed, small, weight_up, [returned]
     )
     twin_out = links.twins(sums_out)
     projected_grad = attend_back(attn_grad, projected, lse, segments, weight_out, [])
@@ -1009,12 +1044,11 @@
     down_sum = links.settled(down, down_got)
     units, columns = dense_up.shape[1], project_in.shape[1]
     up_sum, out_sum = links.settled_across(up, up_got, units)
-    inner_sum = links.settled(inner, inner_got)
-    small_sum = inner_sum[columns:, :cols]
+    in_sum, gains_sum, shifts_sum, centroids_sum = links.settled_small(inner, inner_got, columns, cols)
 
     return (
-        output, tokens_grad, small_sum[:3], small_sum[3:6], inner_sum[:columns].T, out_sum.T, up_sum,
-        down_sum.T, small_sum[6 : 6 + n], expert_sums[0][None], expert_sums[1][None],
+        output, tokens_grad, gains_sum, shifts_sum, in_sum.T, out_sum.T, up_sum,
+        down_sum.T, centroids_sum, expert_sums[0][None], expert_sums[1][None],
     )
 
 

time: 452 us -> 449 us (level)
  local copies, waits for them, and re-layouts: 42.8 us -> 34.7 us
    unnamed x173 -> x155, local copies, waits for them, and re-layouts: 29 us -> 26.7 us
  transfers between devices with their start and end apart: 61 -> 61, of which waited for: 26 -> 25; matrix products, arithmetic and copies ran while one was open for 2% -> 2% of each run, Pallas kernels for 34% -> 35%
where the time goes in v4:
time: 449 us; the launch traced here: 442 us
  waiting for transfers between devices  173 us (39%)
  Pallas kernels  156 us (35%)
  starting transfers between devices  60.8 us (14%)
  local copies, waits for them, and re-layouts  34.7 us (8%)
  between operations  14.9 us (3%)
    pallas_call x34, Pallas kernels, call(): pl.pallas_call(body, out_shape=outs, in_specs=[pl.BlockSpec(memory_space=...  156 us
    ppermute x9, waiting for transfers between devices, along(): return lax.ppermute(value, 'dp', pairs)  60.4 us
    ppermute x44, waiting for transfers between devices, hop(): return lax.ppermute(value, 'expert', [(i, i ^ bit) for i in range(self.n)])  59.1 us
    all_to_all x4, waiting for transfers between devices, exchange(): lax.all_to_all(blocks, 'expert', split_axis=0, concat_axis=0, tiled=True)  35.4 us
    ppermute x44, starting transfers between devices, hop(): return lax.ppermute(value, 'expert', [(i, i ^ bit) for i in range(self.n)])  30.3 us
    unnamed x155, local copies, waits for them, and re-layouts  26.7 us
    all_to_all x4, starting transfers between devices, exchange(): lax.all_to_all(blocks, 'expert', split_axis=0, concat_axis=0, tiled=True)  15.5 us
    ppermute x9, starting transfers between devices, along(): return lax.ppermute(value, 'dp', pairs)  14.8 us
  transfers between devices with their start and end apart: 61, of which 25 were waited for; matrix products, arithmetic and copies ran while one was open for 2% of the time, Pallas kernels for 35%

profile of v4, /device:TPU:0, one launch (start us, length us, event | category | flops | bytes accessed | tf_op | source)
XLA Modules:
  0.0 441.5 jit_solution(7190559383922356089)
XLA Ops:
  7.2 1.4 slice.43
  8.8 1.5 pad_maximum_fusion
  11.5 3.0 collective-permute-start.1
  14.5 1.5 collective-permute-start.3
  16.1 12.3 %collective-permute-done.1.refs_5_.refs_13_.refs_23_.refs_7_.refs_9_ = bf16[400,768]{1,0:T(8,128)(2,1)S(1)} collective-permute-done((bf16[400,768]{1,0:T(8,128)(2,1)S(1)}, bf16[400,768]{1,0:T(8,128)(2,1)S(1)}, u32[]{:S(2)}, u32[]{:S(2)}) %collective-permute-start.1) | collective-permute-done | bytes 614432 | tf_op jit(solution)/shard_map/ppermute | solution.py:171
  29.2 1.8 collective-permute-start.5
  31.7 1.5 collective-permute-start.7
  35.4 4.4 collective-permute-done.7.refs_17_.refs_13_
  42.3 1.9 prepare.1
  44.9 1.5 collective-permute-start.9
  47.5 1.4 collective-permute-start.19
  49.7 15.9 %attend.1 = (bf16[384,768]{1,0:T(8,128)(2,1)}, bf16[384,2304]{1,0:T(8,128)(2,1)}, bf16[384,768]{1,0:T(8,128)(2,1)}, f32[384,128]{1,0:T(8,128)}, f32[384,768]{1,0...) custom-call(bf16[384,768]{1,0:T(8,128)(2,1)} %refs_1_.3, s32[384,1]{1,0:T(8,128)} %copy.28.refs_1_.refs_3_, ...), custom_call_target="tpu_custom_call" | custom-call | flops 18400000000 | bytes 1000 | tf_op jit(solution)/shard_map/attend/pallas_call | solution.py:111
  66.8 1.5 collective-permute-start.14
  69.0 4.9 %collective-permute-done.18.refs_7_.refs_5_ = bf16[96,3072]{1,0:T(8,128)(2,1)S(1)} collective-permute-done((bf16[96,3072]{1,0:T(8,128)(2,1)}, bf16[96,3072]{1,0:T(8,128)(2,1)S(1)}, u32[]{:S(2)}, u32[]{:S(2)}) %collective-permute-start.18) | collective-permute-done | bytes 589856 | tf_op jit(solution)/shard_map/ppermute | solution.py:171
  73.9 1.6 collective-permute-done.19.refs_9_.refs_7_
  77.8 2.4 collective-permute-done.14.refs_7_.refs_11_
  80.2 1.6 collective-permute-done.15.refs_8_.refs_12_
  81.9 3.9 collective-permute-done.23.refs_11_.refs_9_
  87.7 4.1 all-to-all-start
  93.6 9.6 %widen.1 = (bf16[384,3072]{1,0:T(8,128)(2,1)}, bf16[384,3072]{1,0:T(8,128)(2,1)}) custom-call(bf16[384,768]{1,0:T(8,128)(2,1)} %get-tuple-element.101.refs_0_.refs_2_, bf16[768,384]{1,0:T(8,128)(2,1)} %refs_5_.2, bf16[768,384]{1,0:T(8,128)(2,1)} %copy-done.38, bf16[768,384]{1,0:T(8,128)(2,1)} %copy-done.26, bf16[768,384]{1,0:T(8,128)(2,1)} %copy-done.40, ...), custom_call_target="tpu_custom_call" | custom-call | flops 10350000128 | bytes 1000 | tf_op jit(solution)/shard_map/widen/pallas_call | solution.py:111
  103.3 5.2 %all-to-all-done = bf16[8,96,768]{2,1,0:T(8,128)(2,1)S(1)} async-done(((bf16[8,96,768]{2,1,0:T(8,128)(2,1)}), bf16[8,96,768]{2,1,0:T(8,128)(2,1)S(1)}, u32[]{:S(2)}, u32[]{:S(2)}) %all-to-all-start) | async-done | bytes 1179680 | tf_op jit(solution)/shard_map/all_to_all | solution.py:234
  109.5 9.9 %dispatch.1 = (f32[384,768]{1,0:T(8,128)}, f32[384,1]{1,0:T(8,128)}, bf16[768,896]{1,0:T(8,128)(2,1)}) custom-call(bf16[384,3072]{1,0:T(8,128)(2,1)} %get-tuple-element.107.refs_0_.refs_16_.refs_6_, f32[384,768]{1,0:T(8,128)} %get-tuple-element.108.refs_1_, f32[16,768]{1,0:T(8,128)} %get-tuple-element.103.refs_11_.refs_2_.refs_4_.refs_3_, ...), custom_call_target="tpu_custom_call" | custom-call | flops 11500000256 | bytes 1000 | tf_op jit(solution)/shard_map/dispatch/pallas_call | solution.py:111
  119.4 3.7 all-to-all-start.1
  126.1 15.9 %all-to-all-done.1 = bf16[8,96,896]{2,1,0:T(8,128)(2,1)S(1)} async-done(((bf16[8,96,896]{2,1,0:T(8,128)(2,1)}), bf16[8,96,896]{2,1,0:T(8,128)(2,1)S(1)}, u32[]{:S(2)}, u32[]{:S(2)}) %all-to-all-start.1) | async-done | bytes 1376288 | tf_op jit(solution)/shard_map/all_to_all | solution.py:234
  147.1 7.3 %all-gather.3.cloned.1.call-done = bf16[6144,640]{1,0:T(8,128)(2,1)} async-done(((bf16[1536,640]{1,0:T(8,128)(2,1)}), bf16[6144,640]{1,0:T(8,128)(2,1)}) %all-gather.3.cloned.1.call-update) | async-done | bytes 7864336 | tf_op jit(solution)/shard_map/all_gather | solution.py:950
  154.4 30.7 %expert.1 = (bf16[4,2,768,640]{3,2,1,0:T(8,128)(2,1)}, f32[768,768]{1,0:T(8,128)}, f32[768,768]{1,0:T(8,128)}) custom-call(bf16[768,768]{1,0:T(8,128)(2,1)} %copy-done.56, bf16[768,768]{1,0:T(8,128)(2,1)} %copy-done.57, bf16[768,768]{1,0:T(8,128)(2,1)} %copy-done.54, bf16[768,768]{1,0:T(8,128)(2,1)} %copy-done.55, bf16[4,2,768,640]{3,2,1,0:T(8,128)(2,1)} %bitcast.50, ...), custom_call_target="tpu_custom_call" | custom-call | flops 23000000512 | bytes 1000 | tf_op jit(solution)/shard_map/expert/pallas_call | solution.py:111
  185.1 6.7 %all-gather.5.cloned.1.call-done = bf16[6144,128]{1,0:T(8,128)(2,1)} async-done(((bf16[1536,128]{1,0:T(8,128)(2,1)}), bf16[6144,128]{1,0:T(8,128)(2,1)}) %all-gather.5.cloned.1.call-update) | async-done | bytes 1572880 | tf_op jit(solution)/shard_map/all_gather | solution.py:950
  191.9 10.4 %expert_last.1 = (bf16[768,896]{1,0:T(8,128)(2,1)}, bf16[768,768]{1,0:T(8,128)(2,1)}, bf16[1,768,512]{2,1,0:T(8,128)(2,1)}, bf16[1,768,512]{2,1,0:T(8,128)(2,1)}) custom-call(bf16[768,768]{1,0:T(8,128)(2,1)} %copy-done.56, bf16[768,768]{1,0:T(8,128)(2,1)} %copy-done.57, bf16[768,768]{1,0:T(8,128)(2,1)} %copy-done.54, bf16[768,768]{1,0:T(8,128)(2,1)} %copy-done.55, ...), custom_call_target="tpu_custom_call" | custom-call | flops 11500000256 | bytes 1000 | tf_op jit(solution)/shard_map/expert_last/pallas_call | solution.py:111
  202.3 4.1 all-to-all-start.2
  206.4 4.7 %expert_grads.1.refs_8_ = bf16[4,2,768,128]{3,2,1,0:T(8,128)(2,1)} custom-call(bf16[768,768]{1,0:T(8,128)(2,1)} %copy-done.54, bf16[768,768]{1,0:T(8,128)(2,1)} %copy-done.55, bf16[1,768,512]{2,1,0:T(8,128)(2,1)} %get-tuple-element.127.refs_2_.refs_4_, bf16[1,768,512]{2,1,0:T(8,128)(2,1)} %get-tuple-element.128.refs_3_, ...), custom_call_target="tpu_custom_call" | custom-call | flops 6899999744 | bytes 1000 | tf_op jit(solution)/shard_map/expert_grads/pallas_call | solution.py:111
  211.0 14.2 %all-to-all-done.2 = bf16[8,96,896]{2,1,0:T(8,128)(2,1)S(1)} async-done(((bf16[8,96,896]{2,1,0:T(8,128)(2,1)}), bf16[8,96,896]{2,1,0:T(8,128)(2,1)S(1)}, u32[]{:S(2)}, u32[]{:S(2)}) %all-to-all-start.2) | async-done | bytes 1376288 | tf_op jit(solution)/shard_map/all_to_all | solution.py:234
  226.3 9.8 %gate_back.1 = (f32[384,768]{1,0:T(8,128)}, bf16[384,768]{1,0:T(8,128)(2,1)}, f32[2,768]{1,0:T(2,128)}, f32[8,768]{1,0:T(8,128)}, bf16[4,96,3072]{2,1,0:T(8,128)(2,1)}, /*index=5*/bf16[4,96,3072]{2,1,0:T(8,128)(2,1)}) custom-call(s32[384,1]{1,0:T(8,128)} %copy-done.49, s32[384,1]{1,0:T(8,128)} %copy.27.refs_0_.refs_4_.refs_1_, ...), custom_call_target="tpu_custom_call" | custom-call | flops 11500000256 | bytes 1000 | tf_op jit(solution)/shard_map/gate_back/pallas_call | solution.py:111
  236.1 3.6 all-to-all-start.3
  239.7 12.0 %widen_back.1 = (bf16[384,3072]{1,0:T(8,128)(2,1)}, bf16[4,384,768]{2,1,0:T(8,128)(2,1)}, bf16[4,384,768]{2,1,0:T(8,128)(2,1)}) custom-call(bf16[384,768]{1,0:T(8,128)(2,1)} %get-tuple-element.129.refs_0_, bf16[384,3072]{1,0:T(8,128)(2,1)} %get-tuple-element.130.refs_1_, bf16[384,768]{1,0:T(8,128)(2,1)} %get-tuple-element.101.refs_0_.refs_2_, ...), custom_call_target="tpu_custom_call" | custom-call | flops 13799999488 | bytes 1000 | tf_op jit(solution)/shard_map/widen_back/pallas_call | solution.py:111
  252.3 1.4 copy-done.62
  253.7 4.1 fold_wide.1
  267.5 6.8 %second_back.1 = (f32[384,768]{1,0:T(8,128)S(1)}, bf16[384,768]{1,0:T(8,128)(2,1)S(1)}, f32[2,768]{1,0:T(2,128)S(1)}, bf16[4,96,768]{2,1,0:T(8,128)(2,1)S(1)}, bf16[4,96,768]{2,1,0:T(8,128)(2,1)S(1)}) custom-call(bf16[384,3072]{1,0:T(8,128)(2,1)S(1)} %copy-done.10, f32[384,768]{1,0:T(8,128)S(1)} %copy-done.58, f32[384,768]{1,0:T(8,128)S(1)} %copy-done.59, ...), custom_call_target="tpu_custom_call" | custom-call | flops 19549999104 | bytes 1000 | tf_op jit(solution)/shard_map/second_back/pallas_call | solution.py:111
  274.4 1.9 collective-permute-start.28
  276.2 1.5 collective-permute-start.29
  277.8 12.6 %attend_back.1.refs_4_.refs_0_ = bf16[384,2304]{1,0:T(8,128)(2,1)S(1)} custom-call(bf16[384,768]{1,0:T(8,128)(2,1)S(1)} %get-tuple-element.138.refs_0_, bf16[384,2304]{1,0:T(8,128)(2,1)S(1)} %copy-done.12, f32[384,128]{1,0:T(8,128)S(1)} %copy-done.25, s32[384,1]{1,0:T(8,128)S(1)} %copy-done.19, s32[1,384]{1,0:T(1,128)S(1)} %copy-done.33, ...), custom_call_target="tpu_custom_call" | custom-call | flops 2300000000 | bytes 1000 | tf_op jit(solution)/shard_map/attend_back/pallas_call | solution.py:111
  290.5 2.4 fold.2
  294.8 5.7 %tokens_back.1 = (f32[384,768]{1,0:T(8,128)}, bf16[4,16,768]{2,1,0:T(8,128)(2,1)S(1)}, bf16[4,16,768]{2,1,0:T(8,128)(2,1)S(1)}) custom-call(bf16[384,2304]{1,0:T(8,128)(2,1)S(1)} %attend_back.1.refs_4_.refs_0_, bf16[384,768]{1,0:T(8,128)(2,1)S(1)} %copy-done.21, f32[384,768]{1,0:T(8,128)S(1)} %get-tuple-element.143.refs_2_, f32[16,768]{1,0:T(8,128)S(1)} %copy-done.29, ...), custom_call_target="tpu_custom_call" | custom-call | flops 2300000000 | bytes 1000 | tf_op jit(solution)/shard_map/tokens_back/pallas_call | solution.py:111
  300.5 2.3 project_back.1
  303.4 7.6 %collective-permute-done.34.refs_1_ = bf16[2,240,768]{2,1,0:T(8,128)(2,1)S(1)} collective-permute-done((bf16[2,240,768]{2,1,0:T(8,128)(2,1)S(1)}, bf16[2,240,768]{2,1,0:T(8,128)(2,1)S(1)}, u32[]{:S(2)}, u32[]{:S(2)}) %collective-permute-start.34) | collective-permute-done | bytes 737312 | tf_op jit(solution)/shard_map/ppermute | solution.py:171
  312.5 1.6 collective-permute-start.36
  314.1 1.5 collective-permute-start.38
  316.6 16.0 %collective-permute-done.38.refs_1_ = bf16[48,3072]{1,0:T(8,128)(2,1)S(1)} collective-permute-done((bf16[48,3072]{1,0:T(8,128)(2,1)S(1)}, bf16[48,3072]{1,0:T(8,128)(2,1)S(1)}, u32[]{:S(2)}, u32[]{:S(2)}) %collective-permute-start.38) | collective-permute-done | bytes 294944 | tf_op jit(solution)/shard_map/ppermute | solution.py:171
  332.5 1.5 collective-permute-start.43
  334.2 2.8 collective-permute-start.46
  338.3 2.0 collective-permute-done.42.refs_1_
  341.2 2.7 collective-permute-start.45
  344.8 3.1 collective-permute-start.44
  348.0 1.5 combine.1.refs_2_
  352.5 19.7 %collective-permute-done.45.refs_1_ = bf16[480,768]{1,0:T(8,128)(2,1)S(1)} collective-permute-done((bf16[480,768]{1,0:T(8,128)(2,1)S(1)}, bf16[480,768]{1,0:T(8,128)(2,1)S(1)}, u32[]{:S(2)}, u32[]{:S(2)}) %collective-permute-start.45) | collective-permute-done | bytes 737312 | tf_op jit(solution)/shard_map/ppermute | solution.py:315
  373.1 14.2 %collective-permute-done.44.refs_1_ = bf16[304,768]{1,0:T(8,128)(2,1)} collective-permute-done((bf16[304,768]{1,0:T(8,128)(2,1)}, bf16[304,768]{1,0:T(8,128)(2,1)}, u32[]{:S(2)}, u32[]{:S(2)}) %collective-permute-start.44) | collective-permute-done | bytes 466976 | tf_op jit(solution)/shard_map/ppermute | solution.py:315
  391.0 1.6 collective-permute-start.51
  394.7 4.0 reduce-scatter.5.cloned.1.call-done
  399.7 2.5 finish.1
  402.2 1.5 collective-permute-done.52.refs_1_
  403.7 2.3 settle.3.refs_2_
  406.0 21.6 %collective-permute-done.51.refs_1_ = bf16[480,768]{1,0:T(8,128)(2,1)} collective-permute-done((bf16[480,768]{1,0:T(8,128)(2,1)S(1)}, bf16[480,768]{1,0:T(8,128)(2,1)}, u32[]{:S(2)}, u32[]{:S(2)}) %collective-permute-start.51) | collective-permute-done | bytes 737312 | tf_op jit(solution)/shard_map/ppermute | solution.py:315
  427.6 2.7 settle.4
  430.3 2.3 collective-permute-done.50.refs_1_
  432.6 2.1 settle.5
  (266 shorter events, 57.4 us)
Async XLA Ops:
  7.2 147.2 %all-gather.3.cloned.1.call-start = ((), (), s32[]{:S(2)}) async-start(), calls=%async_computation.6 | async-start | bytes 9830400 | tf_op jit(solution)/shard_map/all_gather | solution.py:950
  10.4 23.3 %copy-start.34 = (s32[384,1]{0,1:T(1,128)S(1)}, s32[384,1]{0,1:T(1,128)}, u32[]{:S(2)}) copy-start(s32[384,1]{0,1:T(1,128)} %param.15) | copy-start | bytes 4612
  11.1 23.5 %copy-start.32 = (s32[1,384]{1,0:T(1,128)S(1)}, s32[1,384]{1,0:T(1,128)}, u32[]{:S(2)}) copy-start(s32[1,384]{1,0:T(1,128)} %refs_4_.2) | copy-start | bytes 4612
  11.5 32.7 %copy-start = (bf16[400,768]{1,0:T(8,128)(2,1)}, bf16[400,768]{1,0:T(8,128)(2,1)S(1)}, u32[]{:S(2)}) copy-start(bf16[400,768]{1,0:T(8,128)(2,1)S(1)} %pad_maximum_fusion.1.refs_3_.refs_11_.refs_21_.refs_5_.refs_7_) | copy-start | bytes 1843204
  11.5 16.9 %collective-permute-start.1 = (bf16[400,768]{1,0:T(8,128)(2,1)S(1)}, bf16[400,768]{1,0:T(8,128)(2,1)S(1)}, u32[]{:S(2)}, u32[]{:S(2)}) collective-permute-start(bf16[400,768]{1,0:T(8,128)(2,1)S(1)} %pad_maximum_fusion.1.refs_3_.refs_11_.refs_21_.refs_5_.refs_7_), channel_id=1, source_target_pairs={{0,2},{1,3},{2,0},{3,1},{4,6},{5,7},{6,4},{7,5},{8,10},{9,11},{10,... | collective-permute-start | bytes 1843208 | tf_op jit(solution)/shard_map/ppermute | solution.py:171
  14.5 16.4 %collective-permute-start.3 = (bf16[400,768]{1,0:T(8,128)(2,1)S(1)}, bf16[400,768]{1,0:T(8,128)(2,1)S(1)}, u32[]{:S(2)}, u32[]{:S(2)}) collective-permute-start(bf16[400,768]{1,0:T(8,128)(2,1)S(1)} %pad_maximum_fusion.1.refs_3_.refs_11_.refs_21_.refs_5_.refs_7_), channel_id=1, source_target_pairs={{0,4},{1,5},{2,6},{3,7},{4,0},{5,1},{6,2},{7,3},{8,12},{9,13},{10,... | collective-permute-start | bytes 1843208 | tf_op jit(solution)/shard_map/ppermute | solution.py:171
  29.2 10.6 %collective-permute-start.5 = (bf16[208,768]{1,0:T(8,128)(2,1)}, bf16[208,768]{1,0:T(8,128)(2,1)S(1)}, u32[]{:S(2)}, u32[]{:S(2)}) collective-permute-start(bf16[208,768]{1,0:T(8,128)(2,1)} %slice.40), channel_id=1, source_target_pairs={{0,4},{1,5},{2,6},{3,7},{4,0},{5,1},{6,2},{7,3},{8,12},{9,13},{10,... | collective-permute-start | bytes 958472 | tf_op jit(solution)/shard_map/ppermute | solution.py:171
  31.7 8.0 %collective-permute-start.7 = (bf16[192,768]{1,0:T(8,128)(2,1)}, bf16[192,768]{1,0:T(8,128)(2,1)}, u32[]{:S(2)}, u32[]{:S(2)}) collective-permute-start(bf16[192,768]{1,0:T(8,128)(2,1)} %slice.41), channel_id=1, source_target_pairs={{0,2},{1,3},{2,0},{3,1},{4,6},{5,7},{6,4},{7,5},{8,10},{9,11},{10,... | collective-permute-start | bytes 884744 | tf_op jit(solution)/shard_map/ppermute | solution.py:171
  33.2 11.6 %collective-permute-start = (bf16[400,768]{1,0:T(8,128)(2,1)S(1)}, bf16[400,768]{1,0:T(8,128)(2,1)S(1)}, u32[]{:S(2)}, u32[]{:S(2)}) collective-permute-start(bf16[400,768]{1,0:T(8,128)(2,1)S(1)} %pad_maximum_fusion.1.refs_3_.refs_11_.refs_21_.refs_5_.refs_7_), channel_id=1, source_target_pairs={{0,1},{1,0},{2,3},{3,2},{4,5},{5,4},{6,7},{7,6},{8,9},{9,8},{10,11... | collective-permute-start | bytes 1843208 | tf_op jit(solution)/shard_map/ppermute | solution.py:171
  33.2 13.7 %collective-permute-start.2 = (bf16[400,768]{1,0:T(8,128)(2,1)S(1)}, bf16[400,768]{1,0:T(8,128)(2,1)S(1)}, u32[]{:S(2)}, u32[]{:S(2)}) collective-permute-start(bf16[400,768]{1,0:T(8,128)(2,1)S(1)} %collective-permute-done.1.refs_5_.refs_13_.refs_23_.refs_7_.refs_9_), channel_id=1, source_target_pairs={{0,1},{1,0},{2,3},{3,2},{4,5},{5,4},{6,7},{7,6},{8,9},{9,8},{10,11... | collective-permute-start | bytes 1843208 | tf_op jit(solution)/shard_map/ppermute | solution.py:171
  33.7 13.8 %collective-permute-start.4 = (bf16[400,768]{1,0:T(8,128)(2,1)S(1)}, bf16[400,768]{1,0:T(8,128)(2,1)}, u32[]{:S(2)}, u32[]{:S(2)}) collective-permute-start(bf16[400,768]{1,0:T(8,128)(2,1)S(1)} %collective-permute-done.3.refs_7_.refs_15_.refs_25_.refs_9_.refs_11_), channel_id=1, source_target_pairs={{0,1},{1,0},{2,3},{3,2},{4,5},{5,4},{6,7},{7,6},{8,9},{9,8},{10,11... | collective-permute-start | bytes 1843208 | tf_op jit(solution)/shard_map/ppermute | solution.py:171
  39.8 6.6 %collective-permute-start.8 = (bf16[192,768]{1,0:T(8,128)(2,1)}, bf16[192,768]{1,0:T(8,128)(2,1)S(1)}, u32[]{:S(2)}, u32[]{:S(2)}) collective-permute-start(bf16[192,768]{1,0:T(8,128)(2,1)} %collective-permute-done.7.refs_17_.refs_13_), channel_id=1, source_target_pairs={{0,1},{1,0},{2,3},{3,2},{4,5},{5,4},{6,7},{7,6},{8,9},{9,8},{10,11... | collective-permute-start | bytes 884744 | tf_op jit(solution)/shard_map/ppermute | solution.py:171
  39.8 9.2 %collective-permute-start.6 = (bf16[208,768]{1,0:T(8,128)(2,1)S(1)}, bf16[208,768]{1,0:T(8,128)(2,1)S(1)}, u32[]{:S(2)}, u32[]{:S(2)}) collective-permute-start(bf16[208,768]{1,0:T(8,128)(2,1)S(1)} %collective-permute-done.5.refs_9_.refs_18_.refs_27_.refs_11_.refs_14_), channel_id=1, source_target_pairs={{0,1},{1,0},{2,3},{3,2},{4,5},{5,4},{6,7},{7,6},{8,9},{9,8},{10,11... | collective-permute-start | bytes 958472 | tf_op jit(solution)/shard_map/ppermute | solution.py:171
  44.9 20.7 %collective-permute-start.9 = (bf16[768,384]{1,0:T(8,128)(2,1)}, bf16[768,384]{1,0:T(8,128)(2,1)S(1)}, u32[]{:S(2)}, u32[]{:S(2)}) collective-permute-start(bf16[768,384]{1,0:T(8,128)(2,1)} %refs_5_.2), channel_id=1, source_target_pairs={{0,2},{1,3},{2,0},{3,1},{4,6},{5,7},{6,4},{7,5},{8,10},{9,11},{10,... | collective-permute-start | bytes 1769480 | tf_op jit(solution)/shard_map/ppermute | solution.py:171
  46.4 19.2 %collective-permute-start.10 = (bf16[768,384]{1,0:T(8,128)(2,1)}, bf16[768,384]{1,0:T(8,128)(2,1)}, u32[]{:S(2)}, u32[]{:S(2)}) collective-permute-start(bf16[768,384]{1,0:T(8,128)(2,1)} %refs_5_.2), channel_id=1, source_target_pairs={{0,4},{1,5},{2,6},{3,7},{4,0},{5,1},{6,2},{7,3},{8,12},{9,13},{10,... | collective-permute-start | bytes 1769480 | tf_op jit(solution)/shard_map/ppermute | solution.py:171
  46.9 27.0 %collective-permute-start.18 = (bf16[96,3072]{1,0:T(8,128)(2,1)}, bf16[96,3072]{1,0:T(8,128)(2,1)S(1)}, u32[]{:S(2)}, u32[]{:S(2)}) collective-permute-start(bf16[96,3072]{1,0:T(8,128)(2,1)} %bitcast.4.refs_5_.refs_3_), channel_id=1, source_target_pairs={{0,2},{1,3},{2,0},{3,1},{4,6},{5,7},{6,4},{7,5},{8,10},{9,11},{10,... | collective-permute-start | bytes 1769480 | tf_op jit(solution)/shard_map/ppermute | solution.py:171
  47.5 28.0 %collective-permute-start.19 = (bf16[96,3072]{1,0:T(8,128)(2,1)}, bf16[96,3072]{1,0:T(8,128)(2,1)}, u32[]{:S(2)}, u32[]{:S(2)}) collective-permute-start(bf16[96,3072]{1,0:T(8,128)(2,1)} %bitcast.4.refs_5_.refs_3_), channel_id=1, source_target_pairs={{0,4},{1,5},{2,6},{3,7},{4,0},{5,1},{6,2},{7,3},{8,12},{9,13},{10,... | collective-permute-start | bytes 1769480 | tf_op jit(solution)/shard_map/ppermute | solution.py:171
  66.8 13.4 %collective-permute-start.14 = (bf16[384,384]{1,0:T(8,128)(2,1)S(1)}, bf16[384,384]{1,0:T(8,128)(2,1)S(1)}, u32[]{:S(2)}, u32[]{:S(2)}) collective-permute-start(bf16[384,384]{1,0:T(8,128)(2,1)S(1)} %slice.32), channel_id=1, source_target_pairs={{0,2},{1,3},{2,0},{3,1},{4,6},{5,7},{6,4},{7,5},{8,10},{9,11},{10,... | collective-permute-start | bytes 884744 | tf_op jit(solution)/shard_map/ppermute | solution.py:171
  68.4 13.5 %collective-permute-start.15 = (bf16[384,384]{1,0:T(8,128)(2,1)S(1)}, bf16[384,384]{1,0:T(8,128)(2,1)}, u32[]{:S(2)}, u32[]{:S(2)}) collective-permute-start(bf16[384,384]{1,0:T(8,128)(2,1)S(1)} %slice.33), channel_id=1, source_target_pairs={{0,4},{1,5},{2,6},{3,7},{4,0},{5,1},{6,2},{7,3},{8,12},{9,13},{10,... | collective-permute-start | bytes 884744 | tf_op jit(solution)/shard_map/ppermute | solution.py:171
  76.5 9.2 %collective-permute-start.23 = (bf16[48,3072]{1,0:T(8,128)(2,1)S(1)}, bf16[48,3072]{1,0:T(8,128)(2,1)S(1)}, u32[]{:S(2)}, u32[]{:S(2)}) collective-permute-start(bf16[48,3072]{1,0:T(8,128)(2,1)S(1)} %slice.34), channel_id=1, source_target_pairs={{0,2},{1,3},{2,0},{3,1},{4,6},{5,7},{6,4},{7,5},{8,10},{9,11},{10,... | collective-permute-start | bytes 884744 | tf_op jit(solution)/shard_map/ppermute | solution.py:171
  77.2 9.8 %collective-permute-start.24 = (bf16[48,3072]{1,0:T(8,128)(2,1)S(1)}, bf16[48,3072]{1,0:T(8,128)(2,1)S(1)}, u32[]{:S(2)}, u32[]{:S(2)}) collective-permute-start(bf16[48,3072]{1,0:T(8,128)(2,1)S(1)} %slice.35), channel_id=1, source_target_pairs={{0,4},{1,5},{2,6},{3,7},{4,0},{5,1},{6,2},{7,3},{8,12},{9,13},{10,... | collective-permute-start | bytes 884744 | tf_op jit(solution)/shard_map/ppermute | solution.py:171
  77.8 14.6 %collective-permute-start.11 = (bf16[768,384]{1,0:T(8,128)(2,1)}, bf16[768,384]{1,0:T(8,128)(2,1)S(1)}, u32[]{:S(2)}, u32[]{:S(2)}) collective-permute-start(bf16[768,384]{1,0:T(8,128)(2,1)} %refs_5_.2), channel_id=1, source_target_pairs={{0,1},{1,0},{2,3},{3,2},{4,5},{5,4},{6,7},{7,6},{8,9},{9,8},{10,11... | collective-permute-start | bytes 1769480 | tf_op jit(solution)/shard_map/ppermute | solution.py:171
  80.2 12.6 %collective-permute-start.12 = (bf16[768,384]{1,0:T(8,128)(2,1)S(1)}, bf16[768,384]{1,0:T(8,128)(2,1)S(1)}, u32[]{:S(2)}, u32[]{:S(2)}) collective-permute-start(bf16[768,384]{1,0:T(8,128)(2,1)S(1)} %collective-permute-done.9.refs_3_.refs_7_), channel_id=1, source_target_pairs={{0,1},{1,0},{2,3},{3,2},{4,5},{5,4},{6,7},{7,6},{8,9},{9,8},{10,11... | collective-permute-start | bytes 1769480 | tf_op jit(solution)/shard_map/ppermute | solution.py:171
  81.9 11.0 %collective-permute-start.13 = (bf16[768,384]{1,0:T(8,128)(2,1)}, bf16[768,384]{1,0:T(8,128)(2,1)}, u32[]{:S(2)}, u32[]{:S(2)}) collective-permute-start(bf16[768,384]{1,0:T(8,128)(2,1)} %collective-permute-done.10.refs_5_.refs_9_), channel_id=1, source_target_pairs={{0,1},{1,0},{2,3},{3,2},{4,5},{5,4},{6,7},{7,6},{8,9},{9,8},{10,11... | collective-permute-start | bytes 1769480 | tf_op jit(solution)/shard_map/ppermute | solution.py:171
  85.7 6.0 %collective-permute-start.16 = (bf16[384,384]{1,0:T(8,128)(2,1)S(1)}, bf16[384,384]{1,0:T(8,128)(2,1)}, u32[]{:S(2)}, u32[]{:S(2)}) collective-permute-start(bf16[384,384]{1,0:T(8,128)(2,1)S(1)} %collective-permute-done.14.refs_7_.refs_11_), channel_id=1, source_target_pairs={{0,1},{1,0},{2,3},{3,2},{4,5},{5,4},{6,7},{7,6},{8,9},{9,8},{10,11... | collective-permute-start | bytes 884744 | tf_op jit(solution)/shard_map/ppermute | solution.py:171
  87.0 5.3 %collective-permute-start.17 = (bf16[384,384]{1,0:T(8,128)(2,1)}, bf16[384,384]{1,0:T(8,128)(2,1)}, u32[]{:S(2)}, u32[]{:S(2)}) collective-permute-start(bf16[384,384]{1,0:T(8,128)(2,1)} %collective-permute-done.15.refs_8_.refs_12_), channel_id=1, source_target_pairs={{0,1},{1,0},{2,3},{3,2},{4,5},{5,4},{6,7},{7,6},{8,9},{9,8},{10,11... | collective-permute-start | bytes 884744 | tf_op jit(solution)/shard_map/ppermute | solution.py:171
  87.7 20.8 %all-to-all-start = ((bf16[8,96,768]{2,1,0:T(8,128)(2,1)}), bf16[8,96,768]{2,1,0:T(8,128)(2,1)S(1)}, u32[]{:S(2)}, u32[]{:S(2)}) async-start(bf16[8,96,768]{2,1,0:T(8,128)(2,1)} %bitcast.5), calls=%async_computation | async-start | bytes 2359296 | tf_op jit(solution)/shard_map/all_to_all | solution.py:234
  91.8 11.5 %collective-permute-start.21 = (bf16[96,3072]{1,0:T(8,128)(2,1)}, bf16[96,3072]{1,0:T(8,128)(2,1)}, u32[]{:S(2)}, u32[]{:S(2)}) collective-permute-start(bf16[96,3072]{1,0:T(8,128)(2,1)} %copy-done.67), channel_id=1, source_target_pairs={{0,1},{1,0},{2,3},{3,2},{4,5},{5,4},{6,7},{7,6},{8,9},{9,8},{10,11... | collective-permute-start | bytes 1769480 | tf_op jit(solution)/shard_map/ppermute | solution.py:171
  92.3 11.0 %collective-permute-start.22 = (bf16[96,3072]{1,0:T(8,128)(2,1)}, bf16[96,3072]{1,0:T(8,128)(2,1)}, u32[]{:S(2)}, u32[]{:S(2)}) collective-permute-start(bf16[96,3072]{1,0:T(8,128)(2,1)} %collective-permute-done.19.refs_9_.refs_7_), channel_id=1, source_target_pairs={{0,1},{1,0},{2,3},{3,2},{4,5},{5,4},{6,7},{7,6},{8,9},{9,8},{10,11... | collective-permute-start | bytes 1769480 | tf_op jit(solution)/shard_map/ppermute | solution.py:171
  92.4 10.9 %collective-permute-start.20 = (bf16[96,3072]{1,0:T(8,128)(2,1)}, bf16[96,3072]{1,0:T(8,128)(2,1)}, u32[]{:S(2)}, u32[]{:S(2)}) collective-permute-start(bf16[96,3072]{1,0:T(8,128)(2,1)} %bitcast.4.refs_5_.refs_3_), channel_id=1, source_target_pairs={{0,1},{1,0},{2,3},{3,2},{4,5},{5,4},{6,7},{7,6},{8,9},{9,8},{10,11... | collective-permute-start | bytes 1769480 | tf_op jit(solution)/shard_map/ppermute | solution.py:171
  92.8 10.4 %collective-permute-start.25 = (bf16[48,3072]{1,0:T(8,128)(2,1)}, bf16[48,3072]{1,0:T(8,128)(2,1)S(1)}, u32[]{:S(2)}, u32[]{:S(2)}) collective-permute-start(bf16[48,3072]{1,0:T(8,128)(2,1)} %copy-done.73), channel_id=1, source_target_pairs={{0,1},{1,0},{2,3},{3,2},{4,5},{5,4},{6,7},{7,6},{8,9},{9,8},{10,11... | collective-permute-start | bytes 884744 | tf_op jit(solution)/shard_map/ppermute | solution.py:171
  92.9 10.3 %collective-permute-start.26 = (bf16[48,3072]{1,0:T(8,128)(2,1)}, bf16[48,3072]{1,0:T(8,128)(2,1)S(1)}, u32[]{:S(2)}, u32[]{:S(2)}) collective-permute-start(bf16[48,3072]{1,0:T(8,128)(2,1)} %copy-done.74), channel_id=1, source_target_pairs={{0,1},{1,0},{2,3},{3,2},{4,5},{5,4},{6,7},{7,6},{8,9},{9,8},{10,11... | collective-permute-start | bytes 884744 | tf_op jit(solution)/shard_map/ppermute | solution.py:171
  119.4 22.6 %all-to-all-start.1 = ((bf16[8,96,896]{2,1,0:T(8,128)(2,1)}), bf16[8,96,896]{2,1,0:T(8,128)(2,1)S(1)}, u32[]{:S(2)}, u32[]{:S(2)}) async-start(bf16[8,96,896]{2,1,0:T(8,128)(2,1)} %bitcast.39), calls=%async_computation.1 | async-start | bytes 2752512 | tf_op jit(solution)/shard_map/all_to_all | solution.py:234
  123.2 68.7 %all-gather.5.cloned.1.call-start = ((), (), s32[]{:S(2)}) async-start(), calls=%async_computation.7 | async-start | bytes 1966080 | tf_op jit(solution)/shard_map/all_gather | solution.py:950
  125.9 226.6 %reduce-scatter.3.cloned.1.call-start = ((), (), s32[]{:S(2)}) async-start(), calls=%async_computation.8 | async-start | bytes 9830400 | tf_op jit(solution)/shard_map/reduce_scatter | solution.py:987
  202.3 23.0 %all-to-all-start.2 = ((bf16[8,96,896]{2,1,0:T(8,128)(2,1)}), bf16[8,96,896]{2,1,0:T(8,128)(2,1)S(1)}, u32[]{:S(2)}, u32[]{:S(2)}) async-start(bf16[8,96,896]{2,1,0:T(8,128)(2,1)} %bitcast.41), calls=%async_computation.2 | async-start | bytes 2752512 | tf_op jit(solution)/shard_map/all_to_all | solution.py:234
  236.1 16.2 %collective-permute-start.27 = (bf16[4,96,3072]{2,1,0:T(8,128)(2,1)}, bf16[4,96,3072]{2,1,0:T(8,128)(2,1)S(1)}, u32[]{:S(2)}, u32[]{:S(2)}) collective-permute-start(bf16[4,96,3072]{2,1,0:T(8,128)(2,1)} %get-tuple-element.136), channel_id=1, source_target_pairs={{0,1},{1,0},{2,3},{3,2},{4,5},{5,4},{6,7},{7,6},{8,9},{9,8},{10,11... | collective-permute-start | bytes 7077896 | tf_op jit(solution)/shard_map/ppermute | solution.py:171
  236.1 21.6 %all-to-all-start.3 = ((bf16[8,96,768]{2,1,0:T(8,128)(2,1)}), bf16[8,96,768]{2,1,0:T(8,128)(2,1)S(1)}, u32[]{:S(2)}, u32[]{:S(2)}) async-start(bf16[8,96,768]{2,1,0:T(8,128)(2,1)} %bitcast.46), calls=%async_computation.3 | async-start | bytes 2359296 | tf_op jit(solution)/shard_map/all_to_all | solution.py:234
  239.7 159.0 %reduce-scatter.5.cloned.1.call-start = ((), (), s32[]{:S(2)}) async-start(), calls=%async_computation.9 | async-start | bytes 1966080 | tf_op jit(solution)/shard_map/reduce_scatter | solution.py:987
  251.7 38.7 %collective-permute-start.30 = (bf16[4,384,768]{2,1,0:T(8,128)(2,1)}, bf16[4,384,768]{2,1,0:T(8,128)(2,1)}, u32[]{:S(2)}, u32[]{:S(2)}) collective-permute-start(bf16[4,384,768]{2,1,0:T(8,128)(2,1)} %get-tuple-element.150), channel_id=1, source_target_pairs={{0,1},{1,0},{2,3},{3,2},{4,5},{5,4},{6,7},{7,6},{8,9},{9,8},{10,11... | collective-permute-start | bytes 7077896 | tf_op jit(solution)/shard_map/ppermute | solution.py:171
  274.3 16.2 %collective-permute-start.31 = (bf16[4,96,768]{2,1,0:T(8,128)(2,1)S(1)}, bf16[4,96,768]{2,1,0:T(8,128)(2,1)S(1)}, u32[]{:S(2)}, u32[]{:S(2)}) collective-permute-start(bf16[4,96,768]{2,1,0:T(8,128)(2,1)S(1)} %get-tuple-element.151), channel_id=1, source_target_pairs={{0,1},{1,0},{2,3},{3,2},{4,5},{5,4},{6,7},{7,6},{8,9},{9,8},{10,11... | collective-permute-start | bytes 1769480 | tf_op jit(solution)/shard_map/ppermute | solution.py:171
  274.4 19.3 %collective-permute-start.28 = (bf16[2,48,3072]{2,1,0:T(8,128)(2,1)S(1)}, bf16[2,48,3072]{2,1,0:T(8,128)(2,1)S(1)}, u32[]{:S(2)}, u32[]{:S(2)}) collective-permute-start(bf16[2,48,3072]{2,1,0:T(8,128)(2,1)S(1)} %copy-done.72), channel_id=1, source_target_pairs={{0,2},{1,3},{2,0},{3,1},{4,6},{5,7},{6,4},{7,5},{8,10},{9,11},{10,... | collective-permute-start | bytes 1769480 | tf_op jit(solution)/shard_map/ppermute | solution.py:171
  276.2 17.4 %collective-permute-start.29 = (bf16[2,48,3072]{2,1,0:T(8,128)(2,1)S(1)}, bf16[2,48,3072]{2,1,0:T(8,128)(2,1)S(1)}, u32[]{:S(2)}, u32[]{:S(2)}) collective-permute-start(bf16[2,48,3072]{2,1,0:T(8,128)(2,1)S(1)} %copy-done.71), channel_id=1, source_target_pairs={{0,4},{1,5},{2,6},{3,7},{4,0},{5,1},{6,2},{7,3},{8,12},{9,13},{10,... | collective-permute-start | bytes 1769480 | tf_op jit(solution)/shard_map/ppermute | solution.py:171
  292.9 18.1 %collective-permute-start.34 = (bf16[2,240,768]{2,1,0:T(8,128)(2,1)S(1)}, bf16[2,240,768]{2,1,0:T(8,128)(2,1)S(1)}, u32[]{:S(2)}, u32[]{:S(2)}) collective-permute-start(bf16[2,240,768]{2,1,0:T(8,128)(2,1)S(1)} %get-tuple-element.158), channel_id=1, source_target_pairs={{0,2},{1,3},{2,0},{3,1},{4,6},{5,7},{6,4},{7,5},{8,10},{9,11},{10,... | collective-permute-start | bytes 2211848 | tf_op jit(solution)/shard_map/ppermute | solution.py:171
  293.5 17.7 %collective-permute-start.35 = (bf16[2,240,768]{2,1,0:T(8,128)(2,1)S(1)}, bf16[2,240,768]{2,1,0:T(8,128)(2,1)S(1)}, u32[]{:S(2)}, u32[]{:S(2)}) collective-permute-start(bf16[2,240,768]{2,1,0:T(8,128)(2,1)S(1)} %get-tuple-element.160), channel_id=1, source_target_pairs={{0,4},{1,5},{2,6},{3,7},{4,0},{5,1},{6,2},{7,3},{8,12},{9,13},{10,... | collective-permute-start | bytes 2211848 | tf_op jit(solution)/shard_map/ppermute | solution.py:171
  302.8 8.8 %collective-permute-start.32 = (bf16[4,288,768]{2,1,0:T(8,128)(2,1)S(1)}, bf16[4,288,768]{2,1,0:T(8,128)(2,1)S(1)}, u32[]{:S(2)}, u32[]{:S(2)}) collective-permute-start(bf16[4,288,768]{2,1,0:T(8,128)(2,1)S(1)} %get-tuple-element.156), channel_id=1, source_target_pairs={{0,1},{1,0},{2,3},{3,2},{4,5},{5,4},{6,7},{7,6},{8,9},{9,8},{10,11... | collective-permute-start | bytes 5308424 | tf_op jit(solution)/shard_map/ppermute | solution.py:171
  302.9 8.7 %collective-permute-start.33 = (bf16[4,16,768]{2,1,0:T(8,128)(2,1)S(1)}, bf16[4,16,768]{2,1,0:T(8,128)(2,1)S(1)}, u32[]{:S(2)}, u32[]{:S(2)}) collective-permute-start(bf16[4,16,768]{2,1,0:T(8,128)(2,1)S(1)} %get-tuple-element.157), channel_id=1, source_target_pairs={{0,1},{1,0},{2,3},{3,2},{4,5},{5,4},{6,7},{7,6},{8,9},{9,8},{10,11... | collective-permute-start | bytes 294920 | tf_op jit(solution)/shard_map/ppermute | solution.py:171
  312.0 24.9 %collective-permute-start.37 = (bf16[2,160,768]{2,1,0:T(8,128)(2,1)S(1)}, bf16[2,160,768]{2,1,0:T(8,128)(2,1)S(1)}, u32[]{:S(2)}, u32[]{:S(2)}) collective-permute-start(bf16[2,160,768]{2,1,0:T(8,128)(2,1)S(1)} %get-tuple-element.165), channel_id=1, source_target_pairs={{0,4},{1,5},{2,6},{3,7},{4,0},{5,1},{6,2},{7,3},{8,12},{9,13},{10,... | collective-permute-start | bytes 1474568 | tf_op jit(solution)/shard_map/ppermute | solution.py:171
  312.5 24.4 %collective-permute-start.36 = (bf16[2,144,768]{2,1,0:T(8,128)(2,1)S(1)}, bf16[2,144,768]{2,1,0:T(8,128)(2,1)S(1)}, u32[]{:S(2)}, u32[]{:S(2)}) collective-permute-start(bf16[2,144,768]{2,1,0:T(8,128)(2,1)S(1)} %get-tuple-element.163), channel_id=1, source_target_pairs={{0,2},{1,3},{2,0},{3,1},{4,6},{5,7},{6,4},{7,5},{8,10},{9,11},{10,... | collective-permute-start | bytes 1327112 | tf_op jit(solution)/shard_map/ppermute | solution.py:171
  314.1 18.5 %collective-permute-start.38 = (bf16[48,3072]{1,0:T(8,128)(2,1)S(1)}, bf16[48,3072]{1,0:T(8,128)(2,1)S(1)}, u32[]{:S(2)}, u32[]{:S(2)}) collective-permute-start(bf16[48,3072]{1,0:T(8,128)(2,1)S(1)} %get-tuple-element.166), channel_id=1, source_target_pairs={{0,4},{1,5},{2,6},{3,7},{4,0},{5,1},{6,2},{7,3},{8,12},{9,13},{10,... | collective-permute-start | bytes 884744 | tf_op jit(solution)/shard_map/ppermute | solution.py:171
  315.6 18.5 %collective-permute-start.39 = (bf16[48,3072]{1,0:T(8,128)(2,1)S(1)}, bf16[48,3072]{1,0:T(8,128)(2,1)S(1)}, u32[]{:S(2)}, u32[]{:S(2)}) collective-permute-start(bf16[48,3072]{1,0:T(8,128)(2,1)S(1)} %get-tuple-element.168), channel_id=1, source_target_pairs={{0,2},{1,3},{2,0},{3,1},{4,6},{5,7},{6,4},{7,5},{8,10},{9,11},{10,... | collective-permute-start | bytes 884744 | tf_op jit(solution)/shard_map/ppermute | solution.py:171
  316.1 24.2 %collective-permute-start.42 = (bf16[240,768]{1,0:T(8,128)(2,1)S(1)}, bf16[240,768]{1,0:T(8,128)(2,1)S(1)}, u32[]{:S(2)}, u32[]{:S(2)}) collective-permute-start(bf16[240,768]{1,0:T(8,128)(2,1)S(1)} %get-tuple-element.173), channel_id=1, source_target_pairs={{0,4},{1,5},{2,6},{3,7},{4,0},{5,1},{6,2},{7,3},{8,12},{9,13},{10,... | collective-permute-start | bytes 1105928 | tf_op jit(solution)/shard_map/ppermute | solution.py:171
  332.5 8.5 %collective-permute-start.43 = (bf16[240,768]{1,0:T(8,128)(2,1)S(1)}, bf16[240,768]{1,0:T(8,128)(2,1)S(1)}, u32[]{:S(2)}, u32[]{:S(2)}) collective-permute-start(bf16[240,768]{1,0:T(8,128)(2,1)S(1)} %get-tuple-element.175), channel_id=1, source_target_pairs={{0,2},{1,3},{2,0},{3,1},{4,6},{5,7},{6,4},{7,5},{8,10},{9,11},{10,... | collective-permute-start | bytes 1105928 | tf_op jit(solution)/shard_map/ppermute | solution.py:171
  334.2 16.4 %collective-permute-start.46 = (bf16[96,3072]{1,0:T(8,128)(2,1)S(1)}, bf16[96,3072]{1,0:T(8,128)(2,1)S(1)}, u32[]{:S(2)}, u32[]{:S(2)}) collective-permute-start(bf16[96,3072]{1,0:T(8,128)(2,1)S(1)} %fold_last.3.refs_4_.refs_0_), channel_id=1, source_target_pairs={{0,8},{24,16},{1,9},{25,17},{2,10},{26,18},{3,11},{27,19},{4,12},{... | collective-permute-start | bytes 1769480 | tf_op jit(solution)/shard_map/ppermute | solution.py:315
  337.2 6.7 %collective-permute-start.41 = (bf16[160,768]{1,0:T(8,128)(2,1)S(1)}, bf16[160,768]{1,0:T(8,128)(2,1)S(1)}, u32[]{:S(2)}, u32[]{:S(2)}) collective-permute-start(bf16[160,768]{1,0:T(8,128)(2,1)S(1)} %get-tuple-element.172), channel_id=1, source_target_pairs={{0,2},{1,3},{2,0},{3,1},{4,6},{5,7},{6,4},{7,5},{8,10},{9,11},{10,... | collective-permute-start | bytes 737288 | tf_op jit(solution)/shard_map/ppermute | solution.py:171
  337.8 6.1 %collective-permute-start.40 = (bf16[144,768]{1,0:T(8,128)(2,1)S(1)}, bf16[144,768]{1,0:T(8,128)(2,1)S(1)}, u32[]{:S(2)}, u32[]{:S(2)}) collective-permute-start(bf16[144,768]{1,0:T(8,128)(2,1)S(1)} %get-tuple-element.170), channel_id=1, source_target_pairs={{0,4},{1,5},{2,6},{3,7},{4,0},{5,1},{6,2},{7,3},{8,12},{9,13},{10,... | collective-permute-start | bytes 663560 | tf_op jit(solution)/shard_map/ppermute | solution.py:171
  341.2 30.9 %collective-permute-start.45 = (bf16[480,768]{1,0:T(8,128)(2,1)S(1)}, bf16[480,768]{1,0:T(8,128)(2,1)S(1)}, u32[]{:S(2)}, u32[]{:S(2)}) collective-permute-start(bf16[480,768]{1,0:T(8,128)(2,1)S(1)} %fold_last.4.refs_4_.refs_0_), channel_id=1, source_target_pairs={{0,8},{24,16},{1,9},{25,17},{2,10},{26,18},{3,11},{27,19},{4,12},{... | collective-permute-start | bytes 2211848 | tf_op jit(solution)/shard_map/ppermute | solution.py:315
  344.8 42.4 %collective-permute-start.44 = (bf16[304,768]{1,0:T(8,128)(2,1)}, bf16[304,768]{1,0:T(8,128)(2,1)}, u32[]{:S(2)}, u32[]{:S(2)}) collective-permute-start(bf16[304,768]{1,0:T(8,128)(2,1)} %fold_last.5.refs_4_.refs_0_), channel_id=1, source_target_pairs={{0,8},{24,16},{1,9},{25,17},{2,10},{26,18},{3,11},{27,19},{4,12},{... | collective-permute-start | bytes 1400840 | tf_op jit(solution)/shard_map/ppermute | solution.py:315
  351.7 37.5 %collective-permute-start.49 = (bf16[96,3072]{1,0:T(8,128)(2,1)S(1)}, bf16[96,3072]{1,0:T(8,128)(2,1)S(1)}, u32[]{:S(2)}, u32[]{:S(2)}) collective-permute-start(bf16[96,3072]{1,0:T(8,128)(2,1)S(1)} %joined.6.refs_2_.refs_0_), channel_id=1, source_target_pairs={{8,16},{16,8},{9,17},{17,9},{10,18},{18,10},{11,19},{19,11},{12,20... | collective-permute-start | bytes 1769480 | tf_op jit(solution)/shard_map/ppermute | solution.py:315
  372.3 18.4 %collective-permute-start.48 = (bf16[480,768]{1,0:T(8,128)(2,1)S(1)}, bf16[480,768]{1,0:T(8,128)(2,1)S(1)}, u32[]{:S(2)}, u32[]{:S(2)}) collective-permute-start(bf16[480,768]{1,0:T(8,128)(2,1)S(1)} %joined.7.refs_2_.refs_0_), channel_id=1, source_target_pairs={{8,16},{16,8},{9,17},{17,9},{10,18},{18,10},{11,19},{19,11},{12,20... | collective-permute-start | bytes 2211848 | tf_op jit(solution)/shard_map/ppermute | solution.py:315
  388.6 4.0 collective-permute-start.47
  389.4 14.3 %collective-permute-start.52 = (bf16[96,3072]{1,0:T(8,128)(2,1)S(1)}, bf16[96,3072]{1,0:T(8,128)(2,1)}, u32[]{:S(2)}, u32[]{:S(2)}) collective-permute-start(bf16[96,3072]{1,0:T(8,128)(2,1)S(1)} %joined.9.refs_2_.refs_0_), channel_id=1, source_target_pairs={{8,0},{16,24},{9,1},{17,25},{10,2},{18,26},{11,3},{19,27},{12,4},{... | collective-permute-start | bytes 1769480 | tf_op jit(solution)/shard_map/ppermute | solution.py:315
  391.0 36.7 %collective-permute-start.51 = (bf16[480,768]{1,0:T(8,128)(2,1)S(1)}, bf16[480,768]{1,0:T(8,128)(2,1)}, u32[]{:S(2)}, u32[]{:S(2)}) collective-permute-start(bf16[480,768]{1,0:T(8,128)(2,1)S(1)} %joined.10.refs_2_.refs_0_), channel_id=1, source_target_pairs={{8,0},{16,24},{9,1},{17,25},{10,2},{18,26},{11,3},{19,27},{12,4},{... | collective-permute-start | bytes 2211848 | tf_op jit(solution)/shard_map/ppermute | solution.py:315
  393.5 39.2 %collective-permute-start.50 = (bf16[304,768]{1,0:T(8,128)(2,1)}, bf16[304,768]{1,0:T(8,128)(2,1)}, u32[]{:S(2)}, u32[]{:S(2)}) collective-permute-start(bf16[304,768]{1,0:T(8,128)(2,1)} %joined.11.refs_2_.refs_0_), channel_id=1, source_target_pairs={{8,0},{16,24},{9,1},{17,25},{10,2},{18,26},{11,3},{19,27},{12,4},{... | collective-permute-start | bytes 1400840 | tf_op jit(solution)/shard_map/ppermute | solution.py:315
  (74 other events, 357.5 us)
Sparse Core Ops, SparseCore 0:
  10.6 143.7 all-gather.2
  156.5 35.3 all-gather.4
  194.2 135.0 reduce-scatter.2
  352.6 46.0 reduce-scatter.4

commit v5 on v4

--- a/solution.py
+++ b/solution.py
@@ -14,11 +14,11 @@
 I32 = jnp.int32
 ROOT = 0.7978845608028654
 COST = dict(
-    prepare=3, attend=16, widen=9, dispatch=10, expert_rows=4, expert=20, expert_last=10, expert_grads=6, gate_back=10, widen_back=12, fold=1, fold_wide=1,
-    second_back=17, attend_back=2, fold_again=1, fold_wait=12, project_back=2, tokens_back=2, fold_last=1, joined=6,
+    prepare=3, attend=16, widen=9, dispatch=10, expert_rows=4, expert=20, expert_last=10, expert_grads=6, gate_back=10, widen_back=12, fold=1,
+    second_back=17, attend_back=2, fold_again=1, fold_wait=20, project_back=2, tokens_back=2, fold_last=1, joined=6,
     combine=1, finish=1, settle=1,
 )
-WIDE = ("attend", "widen", "dispatch", "expert", "expert_last", "expert_grads", "gate_back", "fold_wide", "widen_back", "settle")
+WIDE = ("attend", "widen", "dispatch", "expert", "expert_last", "expert_grads", "gate_back", "widen_back", "settle")
 VMEM_LIMIT = 60 * 1024 * 1024
 
 
@@ -252,7 +252,7 @@
     def twins(self, blocks):
         return [self.hop(blocks[1], 1)] if self.cube else []
 
-    def fold(self, groups, twins, name="fold"):
+    def fold(self, groups, twins):
         if not self.cube:
             return [jnp.concatenate([g[0] for g in groups], axis=1)]
         rows = [g[0].shape[1] for g in groups]
@@ -277,7 +277,7 @@
         outs = [jax.ShapeDtypeStruct((2, half, columns), BF)] * 2
         outs += [jax.ShapeDtypeStruct((2, total - half, columns), BF)] * 2
         args = [g[0] for g in groups] + list(twins)
-        return list(call(kernel, outs, args, "v" * len(args), [], name, 0, 0))
+        return list(call(kernel, outs, args, "v" * len(args), [], "fold", 0, 0))
 
     def across(self, kept):
         return [self.hop(kept[1], 2), self.hop(kept[3], 4)] if self.cube else []
@@ -996,7 +996,7 @@
     twin_down = links.twins(sums_down)
     widened_grad, sums_up = widen_back(links, down_in, slope, second_in, weight_down)
     twin_up = links.twins(sums_up)
-    down = links.fold([sums_down], twin_down, "fold_wide")
+    down = links.fold([sums_down], twin_down)
     down_got = links.across(down)
     after_grad, attn_grad, small_2, sums_out = second_back(
         links, widened_grad, after_attn, hidden_grad, mixed, small, weight_up, [returned]
@@ -1015,12 +1015,12 @@
         summed.append(own_sum(links.gated(grads, summed + [sums_small[0]])))
     sums_in = project_back(links, projected_grad, first_in, [])
     twin_in = links.twins(sums_in)
+    down = links.fold_last(down, down_got)
+    down_got = links.inward(down)
     up = links.fold_again(up, up_got, "fold_wait")
     up_got = links.across_again(up)
     inner = links.fold([sums_in, sums_small], twin_in + twin_small)
     inner_got = links.across(inner)
-    down = links.fold_last(down, down_got)
-    down_got = links.inward(down)
     inner = links.fold_again(inner, inner_got)
     inner_got = links.across_again(inner)
     up = links.fold_last(up, up_got)

time: 449 us -> 457 us (1.018)
  local copies, waits for them, and re-layouts: 34.7 us -> 42.1 us
    unnamed x155 -> x171, local copies, waits for them, and re-layouts: 26.7 us -> 34.2 us
    reduce_scatter x2, waiting for transfers between devices: 3.99 us -> 8.63 us  [own_sum(): lax.psum_scatter(grads.reshape(-1, grads.shape[-1]), 'dp', scatter_dimens...]
  transfers between devices with their start and end apart: 61 -> 61, of which waited for: 25 -> 25; matrix products, arithmetic and copies ran while one was open for 2% -> 2% of each run, Pallas kernels for 35% -> 33%
where the time goes in v5:
time: 457 us; the launch traced here: 449 us
  waiting for transfers between devices  174 us (38%)
  Pallas kernels  153 us (33%)
  starting transfers between devices  63.6 us (14%)
  local copies, waits for them, and re-layouts  42.1 us (9%)
  between operations  14.9 us (3%)
    pallas_call x34, Pallas kernels, call(): pl.pallas_call(body, out_shape=outs, in_specs=[pl.BlockSpec(memory_space=...  153 us
    ppermute x44, waiting for transfers between devices, hop(): return lax.ppermute(value, 'expert', [(i, i ^ bit) for i in range(self.n)])  58.6 us
    ppermute x9, waiting for transfers between devices, along(): return lax.ppermute(value, 'dp', pairs)  56.9 us
    all_to_all x4, waiting for transfers between devices, exchange(): lax.all_to_all(blocks, 'expert', split_axis=0, concat_axis=0, tiled=True)  35.4 us
    unnamed x171, local copies, waits for them, and re-layouts  34.2 us
    ppermute x44, starting transfers between devices, hop(): return lax.ppermute(value, 'expert', [(i, i ^ bit) for i in range(self.n)])  32.8 us
    all_to_all x4, starting transfers between devices, exchange(): lax.all_to_all(blocks, 'expert', split_axis=0, concat_axis=0, tiled=True)  15.5 us
    ppermute x9, starting transfers between devices, along(): return lax.ppermute(value, 'dp', pairs)  15.1 us
  transfers between devices with their start and end apart: 61, of which 25 were waited for; matrix products, arithmetic and copies ran while one was open for 2% of the time, Pallas kernels for 33%

profile of v5, /device:TPU:0, one launch (start us, length us, event | category | flops | bytes accessed | tf_op | source)
XLA Modules:
  0.0 449.2 jit_solution(1073345690443598820)
XLA Ops:
  8.8 1.6 pad_maximum_fusion
  11.6 3.0 collective-permute-start.1
  14.6 1.5 collective-permute-start.3
  16.1 12.3 %collective-permute-done.1.refs_5_.refs_13_.refs_23_.refs_7_.refs_9_ = bf16[400,768]{1,0:T(8,128)(2,1)S(1)} collective-permute-done((bf16[400,768]{1,0:T(8,128)(2,1)S(1)}, bf16[400,768]{1,0:T(8,128)(2,1)S(1)}, u32[]{:S(2)}, u32[]{:S(2)}) %collective-permute-start.1) | collective-permute-done | bytes 614432 | tf_op jit(solution)/shard_map/ppermute | solution.py:171
  29.2 1.8 collective-permute-start.5
  31.8 1.5 collective-permute-start.7
  35.4 4.3 collective-permute-done.7.refs_17_.refs_13_
  42.3 1.9 prepare.1
  44.9 1.5 collective-permute-start.9
  49.7 15.9 %attend.1 = (bf16[384,768]{1,0:T(8,128)(2,1)}, bf16[384,2304]{1,0:T(8,128)(2,1)}, bf16[384,768]{1,0:T(8,128)(2,1)}, f32[384,128]{1,0:T(8,128)}, f32[384,768]{1,0...) custom-call(bf16[384,768]{1,0:T(8,128)(2,1)} %refs_1_.3, s32[384,1]{1,0:T(8,128)} %copy.28.refs_1_.refs_3_, ...), custom_call_target="tpu_custom_call" | custom-call | flops 18400000000 | bytes 1000 | tf_op jit(solution)/shard_map/attend/pallas_call | solution.py:111
  66.9 1.5 collective-permute-start.14
  69.1 4.9 %collective-permute-done.18.refs_7_.refs_5_ = bf16[96,3072]{1,0:T(8,128)(2,1)S(1)} collective-permute-done((bf16[96,3072]{1,0:T(8,128)(2,1)}, bf16[96,3072]{1,0:T(8,128)(2,1)S(1)}, u32[]{:S(2)}, u32[]{:S(2)}) %collective-permute-start.18) | collective-permute-done | bytes 589856 | tf_op jit(solution)/shard_map/ppermute | solution.py:171
  73.9 1.6 collective-permute-done.19.refs_9_.refs_7_
  77.9 2.4 collective-permute-done.14.refs_7_.refs_11_
  80.3 1.6 collective-permute-done.15.refs_8_.refs_12_
  81.9 3.9 collective-permute-done.23.refs_11_.refs_9_
  87.7 4.1 all-to-all-start
  93.7 9.5 %widen.1 = (bf16[384,3072]{1,0:T(8,128)(2,1)}, bf16[384,3072]{1,0:T(8,128)(2,1)}) custom-call(bf16[384,768]{1,0:T(8,128)(2,1)} %get-tuple-element.101.refs_0_.refs_2_, bf16[768,384]{1,0:T(8,128)(2,1)} %refs_5_.2, bf16[768,384]{1,0:T(8,128)(2,1)} %copy-done.42, bf16[768,384]{1,0:T(8,128)(2,1)} %copy-done.30, bf16[768,384]{1,0:T(8,128)(2,1)} %copy-done.44, ...), custom_call_target="tpu_custom_call" | custom-call | flops 10350000128 | bytes 1000 | tf_op jit(solution)/shard_map/widen/pallas_call | solution.py:111
  103.3 5.3 %all-to-all-done = bf16[8,96,768]{2,1,0:T(8,128)(2,1)S(1)} async-done(((bf16[8,96,768]{2,1,0:T(8,128)(2,1)}), bf16[8,96,768]{2,1,0:T(8,128)(2,1)S(1)}, u32[]{:S(2)}, u32[]{:S(2)}) %all-to-all-start) | async-done | bytes 1179680 | tf_op jit(solution)/shard_map/all_to_all | solution.py:234
  109.6 9.9 %dispatch.1 = (f32[384,768]{1,0:T(8,128)}, f32[384,1]{1,0:T(8,128)}, bf16[768,896]{1,0:T(8,128)(2,1)}) custom-call(bf16[384,3072]{1,0:T(8,128)(2,1)} %get-tuple-element.107.refs_0_.refs_16_.refs_6_, f32[384,768]{1,0:T(8,128)} %get-tuple-element.108.refs_1_, f32[16,768]{1,0:T(8,128)} %get-tuple-element.103.refs_11_.refs_2_.refs_4_.refs_3_, ...), custom_call_target="tpu_custom_call" | custom-call | flops 11500000256 | bytes 1000 | tf_op jit(solution)/shard_map/dispatch/pallas_call | solution.py:111
  119.5 3.7 all-to-all-start.1
  126.2 15.9 %all-to-all-done.1 = bf16[8,96,896]{2,1,0:T(8,128)(2,1)S(1)} async-done(((bf16[8,96,896]{2,1,0:T(8,128)(2,1)}), bf16[8,96,896]{2,1,0:T(8,128)(2,1)S(1)}, u32[]{:S(2)}, u32[]{:S(2)}) %all-to-all-start.1) | async-done | bytes 1376288 | tf_op jit(solution)/shard_map/all_to_all | solution.py:234
  147.1 7.3 %all-gather.3.cloned.1.call-done = bf16[6144,640]{1,0:T(8,128)(2,1)} async-done(((bf16[1536,640]{1,0:T(8,128)(2,1)}), bf16[6144,640]{1,0:T(8,128)(2,1)}) %all-gather.3.cloned.1.call-update) | async-done | bytes 7864336 | tf_op jit(solution)/shard_map/all_gather | solution.py:950
  154.4 30.8 %expert.1 = (bf16[4,2,768,640]{3,2,1,0:T(8,128)(2,1)}, f32[768,768]{1,0:T(8,128)}, f32[768,768]{1,0:T(8,128)}) custom-call(bf16[768,768]{1,0:T(8,128)(2,1)} %copy-done.67, bf16[768,768]{1,0:T(8,128)(2,1)} %copy-done.68, bf16[768,768]{1,0:T(8,128)(2,1)} %copy-done.65, bf16[768,768]{1,0:T(8,128)(2,1)} %copy-done.66, bf16[4,2,768,640]{3,2,1,0:T(8,128)(2,1)} %bitcast.50, ...), custom_call_target="tpu_custom_call" | custom-call | flops 23000000512 | bytes 1000 | tf_op jit(solution)/shard_map/expert/pallas_call | solution.py:111
  185.2 6.7 %all-gather.5.cloned.1.call-done = bf16[6144,128]{1,0:T(8,128)(2,1)} async-done(((bf16[1536,128]{1,0:T(8,128)(2,1)}), bf16[6144,128]{1,0:T(8,128)(2,1)}) %all-gather.5.cloned.1.call-update) | async-done | bytes 1572880 | tf_op jit(solution)/shard_map/all_gather | solution.py:950
  191.9 10.4 %expert_last.1 = (bf16[768,896]{1,0:T(8,128)(2,1)}, bf16[768,768]{1,0:T(8,128)(2,1)}, bf16[1,768,512]{2,1,0:T(8,128)(2,1)}, bf16[1,768,512]{2,1,0:T(8,128)(2,1)}) custom-call(bf16[768,768]{1,0:T(8,128)(2,1)} %copy-done.67, bf16[768,768]{1,0:T(8,128)(2,1)} %copy-done.68, bf16[768,768]{1,0:T(8,128)(2,1)} %copy-done.65, bf16[768,768]{1,0:T(8,128)(2,1)} %copy-done.66, ...), custom_call_target="tpu_custom_call" | custom-call | flops 11500000256 | bytes 1000 | tf_op jit(solution)/shard_map/expert_last/pallas_call | solution.py:111
  202.3 4.1 all-to-all-start.2
  206.4 4.6 %expert_grads.1.refs_8_ = bf16[4,2,768,128]{3,2,1,0:T(8,128)(2,1)} custom-call(bf16[768,768]{1,0:T(8,128)(2,1)} %copy-done.65, bf16[768,768]{1,0:T(8,128)(2,1)} %copy-done.66, bf16[1,768,512]{2,1,0:T(8,128)(2,1)} %get-tuple-element.127.refs_2_.refs_4_, bf16[1,768,512]{2,1,0:T(8,128)(2,1)} %get-tuple-element.128.refs_3_, ...), custom_call_target="tpu_custom_call" | custom-call | flops 6899999744 | bytes 1000 | tf_op jit(solution)/shard_map/expert_grads/pallas_call | solution.py:111
  211.0 14.2 %all-to-all-done.2 = bf16[8,96,896]{2,1,0:T(8,128)(2,1)S(1)} async-done(((bf16[8,96,896]{2,1,0:T(8,128)(2,1)}), bf16[8,96,896]{2,1,0:T(8,128)(2,1)S(1)}, u32[]{:S(2)}, u32[]{:S(2)}) %all-to-all-start.2) | async-done | bytes 1376288 | tf_op jit(solution)/shard_map/all_to_all | solution.py:234
  226.3 9.8 %gate_back.1 = (f32[384,768]{1,0:T(8,128)}, bf16[384,768]{1,0:T(8,128)(2,1)}, f32[2,768]{1,0:T(2,128)}, f32[8,768]{1,0:T(8,128)}, bf16[4,96,3072]{2,1,0:T(8,128)(2,1)}, /*index=5*/bf16[4,96,3072]{2,1,0:T(8,128)(2,1)}) custom-call(s32[384,1]{1,0:T(8,128)} %copy-done.60, s32[384,1]{1,0:T(8,128)} %copy.27.refs_0_.refs_4_.refs_1_, ...), custom_call_target="tpu_custom_call" | custom-call | flops 11500000256 | bytes 1000 | tf_op jit(solution)/shard_map/gate_back/pallas_call | solution.py:111
  236.1 3.6 all-to-all-start.3
  239.7 12.0 %widen_back.1 = (bf16[384,3072]{1,0:T(8,128)(2,1)}, bf16[4,384,768]{2,1,0:T(8,128)(2,1)}, bf16[4,384,768]{2,1,0:T(8,128)(2,1)}) custom-call(bf16[384,768]{1,0:T(8,128)(2,1)} %get-tuple-element.129.refs_0_, bf16[384,3072]{1,0:T(8,128)(2,1)} %get-tuple-element.130.refs_1_, bf16[384,768]{1,0:T(8,128)(2,1)} %get-tuple-element.101.refs_0_.refs_2_, ...), custom_call_target="tpu_custom_call" | custom-call | flops 13799999488 | bytes 1000 | tf_op jit(solution)/shard_map/widen_back/pallas_call | solution.py:111
  253.6 1.7 copy-done.10
  255.3 1.7 copy-done.12
  257.0 1.7 copy-done.14
  272.2 6.9 %second_back.1 = (f32[384,768]{1,0:T(8,128)S(1)}, bf16[384,768]{1,0:T(8,128)(2,1)S(1)}, f32[2,768]{1,0:T(2,128)S(1)}, bf16[4,96,768]{2,1,0:T(8,128)(2,1)S(1)}, bf16[4,96,768]{2,1,0:T(8,128)(2,1)S(1)}) custom-call(bf16[384,3072]{1,0:T(8,128)(2,1)S(1)} %copy-done.11, f32[384,768]{1,0:T(8,128)S(1)} %copy-done.69, f32[384,768]{1,0:T(8,128)S(1)} %copy-done.70, ...), custom_call_target="tpu_custom_call" | custom-call | flops 19549999104 | bytes 1000 | tf_op jit(solution)/shard_map/second_back/pallas_call | solution.py:111
  279.2 1.9 collective-permute-start.28
  282.7 12.6 %attend_back.1.refs_4_.refs_0_ = bf16[384,2304]{1,0:T(8,128)(2,1)S(1)} custom-call(bf16[384,768]{1,0:T(8,128)(2,1)S(1)} %get-tuple-element.138.refs_0_, bf16[384,2304]{1,0:T(8,128)(2,1)S(1)} %copy-done.16, f32[384,128]{1,0:T(8,128)S(1)} %copy-done.29, s32[384,1]{1,0:T(8,128)S(1)} %copy-done.23, s32[1,384]{1,0:T(1,128)S(1)} %copy-done.37, ...), custom_call_target="tpu_custom_call" | custom-call | flops 2300000000 | bytes 1000 | tf_op jit(solution)/shard_map/attend_back/pallas_call | solution.py:111
  295.4 2.4 fold.4
  298.9 2.0 collective-permute-start.36
  300.9 1.5 collective-permute-start.37
  302.4 5.7 %tokens_back.1 = (f32[384,768]{1,0:T(8,128)}, bf16[4,16,768]{2,1,0:T(8,128)(2,1)S(1)}, bf16[4,16,768]{2,1,0:T(8,128)(2,1)S(1)}) custom-call(bf16[384,2304]{1,0:T(8,128)(2,1)S(1)} %attend_back.1.refs_4_.refs_0_, bf16[384,768]{1,0:T(8,128)(2,1)S(1)} %copy-done.25, f32[384,768]{1,0:T(8,128)S(1)} %get-tuple-element.143.refs_2_, f32[16,768]{1,0:T(8,128)S(1)} %copy-done.33, ...), custom_call_target="tpu_custom_call" | custom-call | flops 2300000000 | bytes 1000 | tf_op jit(solution)/shard_map/tokens_back/pallas_call | solution.py:111
  308.1 2.3 project_back.1
  310.5 11.9 %collective-permute-done.36.refs_1_ = bf16[48,3072]{1,0:T(8,128)(2,1)S(1)} collective-permute-done((bf16[48,3072]{1,0:T(8,128)(2,1)S(1)}, bf16[48,3072]{1,0:T(8,128)(2,1)S(1)}, u32[]{:S(2)}, u32[]{:S(2)}) %collective-permute-start.36) | collective-permute-done | bytes 294944 | tf_op jit(solution)/shard_map/ppermute | solution.py:171
  324.7 1.5 collective-permute-start.38
  326.2 1.5 collective-permute-start.42
  328.3 2.7 collective-permute-start.46
  331.0 6.8 %collective-permute-done.38.refs_1_ = bf16[2,144,768]{2,1,0:T(8,128)(2,1)S(1)} collective-permute-done((bf16[2,144,768]{2,1,0:T(8,128)(2,1)S(1)}, bf16[2,144,768]{2,1,0:T(8,128)(2,1)S(1)}, u32[]{:S(2)}, u32[]{:S(2)}) %collective-permute-start.38) | collective-permute-done | bytes 442400 | tf_op jit(solution)/shard_map/ppermute | solution.py:171
  338.5 1.5 collective-permute-start.41
  341.1 5.1 %collective-permute-done.42.refs_1_ = bf16[240,768]{1,0:T(8,128)(2,1)S(1)} collective-permute-done((bf16[240,768]{1,0:T(8,128)(2,1)S(1)}, bf16[240,768]{1,0:T(8,128)(2,1)S(1)}, u32[]{:S(2)}, u32[]{:S(2)}) %collective-permute-start.42) | collective-permute-done | bytes 368672 | tf_op jit(solution)/shard_map/ppermute | solution.py:171
  346.3 2.7 collective-permute-start.45
  351.0 3.4 collective-permute-start.44
  354.5 1.5 combine.1.refs_2_
  358.0 10.2 %collective-permute-done.45.refs_1_ = bf16[480,768]{1,0:T(8,128)(2,1)S(1)} collective-permute-done((bf16[480,768]{1,0:T(8,128)(2,1)S(1)}, bf16[480,768]{1,0:T(8,128)(2,1)S(1)}, u32[]{:S(2)}, u32[]{:S(2)}) %collective-permute-start.45) | collective-permute-done | bytes 737312 | tf_op jit(solution)/shard_map/ppermute | solution.py:315
  369.1 16.7 %collective-permute-done.44.refs_1_ = bf16[304,768]{1,0:T(8,128)(2,1)} collective-permute-done((bf16[304,768]{1,0:T(8,128)(2,1)}, bf16[304,768]{1,0:T(8,128)(2,1)}, u32[]{:S(2)}, u32[]{:S(2)}) %collective-permute-start.44) | collective-permute-done | bytes 466976 | tf_op jit(solution)/shard_map/ppermute | solution.py:315
  389.5 1.6 collective-permute-start.51
  393.3 8.6 %reduce-scatter.5.cloned.1.call-done = bf16[1536,128]{1,0:T(8,128)(2,1)} async-done(((bf16[6144,128]{1,0:T(8,128)(2,1)}), bf16[1536,128]{1,0:T(8,128)(2,1)}) %reduce-scatter.5.cloned.1.call-update) | async-done | bytes 393232 | tf_op jit(solution)/shard_map/reduce_scatter | solution.py:987
  402.9 2.5 finish.1
  405.3 4.4 collective-permute-done.52.refs_1_
  409.7 2.3 settle.3.refs_2_
  412.1 22.3 %collective-permute-done.51.refs_1_ = bf16[480,768]{1,0:T(8,128)(2,1)} collective-permute-done((bf16[480,768]{1,0:T(8,128)(2,1)S(1)}, bf16[480,768]{1,0:T(8,128)(2,1)}, u32[]{:S(2)}, u32[]{:S(2)}) %collective-permute-start.51) | collective-permute-done | bytes 737312 | tf_op jit(solution)/shard_map/ppermute | solution.py:315
  434.3 2.7 settle.4
  437.0 3.3 collective-permute-done.50.refs_1_
  440.3 2.1 settle.5
  (282 shorter events, 65.5 us)
Async XLA Ops:
  7.2 147.2 %all-gather.3.cloned.1.call-start = ((), (), s32[]{:S(2)}) async-start(), calls=%async_computation.6 | async-start | bytes 9830400 | tf_op jit(solution)/shard_map/all_gather | solution.py:950
  10.4 23.3 %copy-start.38 = (s32[384,1]{0,1:T(1,128)S(1)}, s32[384,1]{0,1:T(1,128)}, u32[]{:S(2)}) copy-start(s32[384,1]{0,1:T(1,128)} %param.15) | copy-start | bytes 4612
  11.1 23.5 %copy-start.36 = (s32[1,384]{1,0:T(1,128)S(1)}, s32[1,384]{1,0:T(1,128)}, u32[]{:S(2)}) copy-start(s32[1,384]{1,0:T(1,128)} %refs_4_.2) | copy-start | bytes 4612
  11.6 32.7 %copy-start = (bf16[400,768]{1,0:T(8,128)(2,1)}, bf16[400,768]{1,0:T(8,128)(2,1)S(1)}, u32[]{:S(2)}) copy-start(bf16[400,768]{1,0:T(8,128)(2,1)S(1)} %pad_maximum_fusion.1.refs_3_.refs_11_.refs_21_.refs_5_.refs_7_) | copy-start | bytes 1843204
  11.6 16.9 %collective-permute-start.1 = (bf16[400,768]{1,0:T(8,128)(2,1)S(1)}, bf16[400,768]{1,0:T(8,128)(2,1)S(1)}, u32[]{:S(2)}, u32[]{:S(2)}) collective-permute-start(bf16[400,768]{1,0:T(8,128)(2,1)S(1)} %pad_maximum_fusion.1.refs_3_.refs_11_.refs_21_.refs_5_.refs_7_), channel_id=1, source_target_pairs={{0,2},{1,3},{2,0},{3,1},{4,6},{5,7},{6,4},{7,5},{8,10},{9,11},{10,... | collective-permute-start | bytes 1843208 | tf_op jit(solution)/shard_map/ppermute | solution.py:171
  14.6 16.4 %collective-permute-start.3 = (bf16[400,768]{1,0:T(8,128)(2,1)S(1)}, bf16[400,768]{1,0:T(8,128)(2,1)S(1)}, u32[]{:S(2)}, u32[]{:S(2)}) collective-permute-start(bf16[400,768]{1,0:T(8,128)(2,1)S(1)} %pad_maximum_fusion.1.refs_3_.refs_11_.refs_21_.refs_5_.refs_7_), channel_id=1, source_target_pairs={{0,4},{1,5},{2,6},{3,7},{4,0},{5,1},{6,2},{7,3},{8,12},{9,13},{10,... | collective-permute-start | bytes 1843208 | tf_op jit(solution)/shard_map/ppermute | solution.py:171
  29.2 10.6 %collective-permute-start.5 = (bf16[208,768]{1,0:T(8,128)(2,1)}, bf16[208,768]{1,0:T(8,128)(2,1)S(1)}, u32[]{:S(2)}, u32[]{:S(2)}) collective-permute-start(bf16[208,768]{1,0:T(8,128)(2,1)} %slice.40), channel_id=1, source_target_pairs={{0,4},{1,5},{2,6},{3,7},{4,0},{5,1},{6,2},{7,3},{8,12},{9,13},{10,... | collective-permute-start | bytes 958472 | tf_op jit(solution)/shard_map/ppermute | solution.py:171
  31.8 8.0 %collective-permute-start.7 = (bf16[192,768]{1,0:T(8,128)(2,1)}, bf16[192,768]{1,0:T(8,128)(2,1)}, u32[]{:S(2)}, u32[]{:S(2)}) collective-permute-start(bf16[192,768]{1,0:T(8,128)(2,1)} %slice.41), channel_id=1, source_target_pairs={{0,2},{1,3},{2,0},{3,1},{4,6},{5,7},{6,4},{7,5},{8,10},{9,11},{10,... | collective-permute-start | bytes 884744 | tf_op jit(solution)/shard_map/ppermute | solution.py:171
  33.3 11.7 %collective-permute-start = (bf16[400,768]{1,0:T(8,128)(2,1)S(1)}, bf16[400,768]{1,0:T(8,128)(2,1)S(1)}, u32[]{:S(2)}, u32[]{:S(2)}) collective-permute-start(bf16[400,768]{1,0:T(8,128)(2,1)S(1)} %pad_maximum_fusion.1.refs_3_.refs_11_.refs_21_.refs_5_.refs_7_), channel_id=1, source_target_pairs={{0,1},{1,0},{2,3},{3,2},{4,5},{5,4},{6,7},{7,6},{8,9},{9,8},{10,11... | collective-permute-start | bytes 1843208 | tf_op jit(solution)/shard_map/ppermute | solution.py:171
  33.3 13.7 %collective-permute-start.2 = (bf16[400,768]{1,0:T(8,128)(2,1)S(1)}, bf16[400,768]{1,0:T(8,128)(2,1)S(1)}, u32[]{:S(2)}, u32[]{:S(2)}) collective-permute-start(bf16[400,768]{1,0:T(8,128)(2,1)S(1)} %collective-permute-done.1.refs_5_.refs_13_.refs_23_.refs_7_.refs_9_), channel_id=1, source_target_pairs={{0,1},{1,0},{2,3},{3,2},{4,5},{5,4},{6,7},{7,6},{8,9},{9,8},{10,11... | collective-permute-start | bytes 1843208 | tf_op jit(solution)/shard_map/ppermute | solution.py:171
  33.8 13.8 %collective-permute-start.4 = (bf16[400,768]{1,0:T(8,128)(2,1)S(1)}, bf16[400,768]{1,0:T(8,128)(2,1)}, u32[]{:S(2)}, u32[]{:S(2)}) collective-permute-start(bf16[400,768]{1,0:T(8,128)(2,1)S(1)} %collective-permute-done.3.refs_7_.refs_15_.refs_25_.refs_9_.refs_11_), channel_id=1, source_target_pairs={{0,1},{1,0},{2,3},{3,2},{4,5},{5,4},{6,7},{7,6},{8,9},{9,8},{10,11... | collective-permute-start | bytes 1843208 | tf_op jit(solution)/shard_map/ppermute | solution.py:171
  39.8 6.6 %collective-permute-start.8 = (bf16[192,768]{1,0:T(8,128)(2,1)}, bf16[192,768]{1,0:T(8,128)(2,1)S(1)}, u32[]{:S(2)}, u32[]{:S(2)}) collective-permute-start(bf16[192,768]{1,0:T(8,128)(2,1)} %collective-permute-done.7.refs_17_.refs_13_), channel_id=1, source_target_pairs={{0,1},{1,0},{2,3},{3,2},{4,5},{5,4},{6,7},{7,6},{8,9},{9,8},{10,11... | collective-permute-start | bytes 884744 | tf_op jit(solution)/shard_map/ppermute | solution.py:171
  39.8 9.2 %collective-permute-start.6 = (bf16[208,768]{1,0:T(8,128)(2,1)S(1)}, bf16[208,768]{1,0:T(8,128)(2,1)S(1)}, u32[]{:S(2)}, u32[]{:S(2)}) collective-permute-start(bf16[208,768]{1,0:T(8,128)(2,1)S(1)} %collective-permute-done.5.refs_9_.refs_18_.refs_27_.refs_11_.refs_14_), channel_id=1, source_target_pairs={{0,1},{1,0},{2,3},{3,2},{4,5},{5,4},{6,7},{7,6},{8,9},{9,8},{10,11... | collective-permute-start | bytes 958472 | tf_op jit(solution)/shard_map/ppermute | solution.py:171
  44.9 20.7 %collective-permute-start.9 = (bf16[768,384]{1,0:T(8,128)(2,1)}, bf16[768,384]{1,0:T(8,128)(2,1)S(1)}, u32[]{:S(2)}, u32[]{:S(2)}) collective-permute-start(bf16[768,384]{1,0:T(8,128)(2,1)} %refs_5_.2), channel_id=1, source_target_pairs={{0,2},{1,3},{2,0},{3,1},{4,6},{5,7},{6,4},{7,5},{8,10},{9,11},{10,... | collective-permute-start | bytes 1769480 | tf_op jit(solution)/shard_map/ppermute | solution.py:171
  46.4 19.3 %collective-permute-start.10 = (bf16[768,384]{1,0:T(8,128)(2,1)}, bf16[768,384]{1,0:T(8,128)(2,1)}, u32[]{:S(2)}, u32[]{:S(2)}) collective-permute-start(bf16[768,384]{1,0:T(8,128)(2,1)} %refs_5_.2), channel_id=1, source_target_pairs={{0,4},{1,5},{2,6},{3,7},{4,0},{5,1},{6,2},{7,3},{8,12},{9,13},{10,... | collective-permute-start | bytes 1769480 | tf_op jit(solution)/shard_map/ppermute | solution.py:171
  46.9 27.0 %collective-permute-start.18 = (bf16[96,3072]{1,0:T(8,128)(2,1)}, bf16[96,3072]{1,0:T(8,128)(2,1)S(1)}, u32[]{:S(2)}, u32[]{:S(2)}) collective-permute-start(bf16[96,3072]{1,0:T(8,128)(2,1)} %bitcast.4.refs_5_.refs_3_), channel_id=1, source_target_pairs={{0,2},{1,3},{2,0},{3,1},{4,6},{5,7},{6,4},{7,5},{8,10},{9,11},{10,... | collective-permute-start | bytes 1769480 | tf_op jit(solution)/shard_map/ppermute | solution.py:171
  47.5 28.0 %collective-permute-start.19 = (bf16[96,3072]{1,0:T(8,128)(2,1)}, bf16[96,3072]{1,0:T(8,128)(2,1)}, u32[]{:S(2)}, u32[]{:S(2)}) collective-permute-start(bf16[96,3072]{1,0:T(8,128)(2,1)} %bitcast.4.refs_5_.refs_3_), channel_id=1, source_target_pairs={{0,4},{1,5},{2,6},{3,7},{4,0},{5,1},{6,2},{7,3},{8,12},{9,13},{10,... | collective-permute-start | bytes 1769480 | tf_op jit(solution)/shard_map/ppermute | solution.py:171
  66.9 13.4 %collective-permute-start.14 = (bf16[384,384]{1,0:T(8,128)(2,1)S(1)}, bf16[384,384]{1,0:T(8,128)(2,1)S(1)}, u32[]{:S(2)}, u32[]{:S(2)}) collective-permute-start(bf16[384,384]{1,0:T(8,128)(2,1)S(1)} %slice.32), channel_id=1, source_target_pairs={{0,2},{1,3},{2,0},{3,1},{4,6},{5,7},{6,4},{7,5},{8,10},{9,11},{10,... | collective-permute-start | bytes 884744 | tf_op jit(solution)/shard_map/ppermute | solution.py:171
  68.5 13.4 %collective-permute-start.15 = (bf16[384,384]{1,0:T(8,128)(2,1)S(1)}, bf16[384,384]{1,0:T(8,128)(2,1)}, u32[]{:S(2)}, u32[]{:S(2)}) collective-permute-start(bf16[384,384]{1,0:T(8,128)(2,1)S(1)} %slice.33), channel_id=1, source_target_pairs={{0,4},{1,5},{2,6},{3,7},{4,0},{5,1},{6,2},{7,3},{8,12},{9,13},{10,... | collective-permute-start | bytes 884744 | tf_op jit(solution)/shard_map/ppermute | solution.py:171
  76.6 9.2 %collective-permute-start.23 = (bf16[48,3072]{1,0:T(8,128)(2,1)S(1)}, bf16[48,3072]{1,0:T(8,128)(2,1)S(1)}, u32[]{:S(2)}, u32[]{:S(2)}) collective-permute-start(bf16[48,3072]{1,0:T(8,128)(2,1)S(1)} %slice.34), channel_id=1, source_target_pairs={{0,2},{1,3},{2,0},{3,1},{4,6},{5,7},{6,4},{7,5},{8,10},{9,11},{10,... | collective-permute-start | bytes 884744 | tf_op jit(solution)/shard_map/ppermute | solution.py:171
  77.2 9.8 %collective-permute-start.24 = (bf16[48,3072]{1,0:T(8,128)(2,1)S(1)}, bf16[48,3072]{1,0:T(8,128)(2,1)S(1)}, u32[]{:S(2)}, u32[]{:S(2)}) collective-permute-start(bf16[48,3072]{1,0:T(8,128)(2,1)S(1)} %slice.35), channel_id=1, source_target_pairs={{0,4},{1,5},{2,6},{3,7},{4,0},{5,1},{6,2},{7,3},{8,12},{9,13},{10,... | collective-permute-start | bytes 884744 | tf_op jit(solution)/shard_map/ppermute | solution.py:171
  77.9 14.6 %collective-permute-start.11 = (bf16[768,384]{1,0:T(8,128)(2,1)}, bf16[768,384]{1,0:T(8,128)(2,1)S(1)}, u32[]{:S(2)}, u32[]{:S(2)}) collective-permute-start(bf16[768,384]{1,0:T(8,128)(2,1)} %refs_5_.2), channel_id=1, source_target_pairs={{0,1},{1,0},{2,3},{3,2},{4,5},{5,4},{6,7},{7,6},{8,9},{9,8},{10,11... | collective-permute-start | bytes 1769480 | tf_op jit(solution)/shard_map/ppermute | solution.py:171
  80.3 12.6 %collective-permute-start.12 = (bf16[768,384]{1,0:T(8,128)(2,1)S(1)}, bf16[768,384]{1,0:T(8,128)(2,1)S(1)}, u32[]{:S(2)}, u32[]{:S(2)}) collective-permute-start(bf16[768,384]{1,0:T(8,128)(2,1)S(1)} %collective-permute-done.9.refs_3_.refs_7_), channel_id=1, source_target_pairs={{0,1},{1,0},{2,3},{3,2},{4,5},{5,4},{6,7},{7,6},{8,9},{9,8},{10,11... | collective-permute-start | bytes 1769480 | tf_op jit(solution)/shard_map/ppermute | solution.py:171
  81.9 11.0 %collective-permute-start.13 = (bf16[768,384]{1,0:T(8,128)(2,1)}, bf16[768,384]{1,0:T(8,128)(2,1)}, u32[]{:S(2)}, u32[]{:S(2)}) collective-permute-start(bf16[768,384]{1,0:T(8,128)(2,1)} %collective-permute-done.10.refs_5_.refs_9_), channel_id=1, source_target_pairs={{0,1},{1,0},{2,3},{3,2},{4,5},{5,4},{6,7},{7,6},{8,9},{9,8},{10,11... | collective-permute-start | bytes 1769480 | tf_op jit(solution)/shard_map/ppermute | solution.py:171
  85.8 6.0 %collective-permute-start.16 = (bf16[384,384]{1,0:T(8,128)(2,1)S(1)}, bf16[384,384]{1,0:T(8,128)(2,1)}, u32[]{:S(2)}, u32[]{:S(2)}) collective-permute-start(bf16[384,384]{1,0:T(8,128)(2,1)S(1)} %collective-permute-done.14.refs_7_.refs_11_), channel_id=1, source_target_pairs={{0,1},{1,0},{2,3},{3,2},{4,5},{5,4},{6,7},{7,6},{8,9},{9,8},{10,11... | collective-permute-start | bytes 884744 | tf_op jit(solution)/shard_map/ppermute | solution.py:171
  87.0 5.3 %collective-permute-start.17 = (bf16[384,384]{1,0:T(8,128)(2,1)}, bf16[384,384]{1,0:T(8,128)(2,1)}, u32[]{:S(2)}, u32[]{:S(2)}) collective-permute-start(bf16[384,384]{1,0:T(8,128)(2,1)} %collective-permute-done.15.refs_8_.refs_12_), channel_id=1, source_target_pairs={{0,1},{1,0},{2,3},{3,2},{4,5},{5,4},{6,7},{7,6},{8,9},{9,8},{10,11... | collective-permute-start | bytes 884744 | tf_op jit(solution)/shard_map/ppermute | solution.py:171
  87.7 20.8 %all-to-all-start = ((bf16[8,96,768]{2,1,0:T(8,128)(2,1)}), bf16[8,96,768]{2,1,0:T(8,128)(2,1)S(1)}, u32[]{:S(2)}, u32[]{:S(2)}) async-start(bf16[8,96,768]{2,1,0:T(8,128)(2,1)} %bitcast.5), calls=%async_computation | async-start | bytes 2359296 | tf_op jit(solution)/shard_map/all_to_all | solution.py:234
  91.8 11.4 %collective-permute-start.21 = (bf16[96,3072]{1,0:T(8,128)(2,1)}, bf16[96,3072]{1,0:T(8,128)(2,1)}, u32[]{:S(2)}, u32[]{:S(2)}) collective-permute-start(bf16[96,3072]{1,0:T(8,128)(2,1)} %copy-done.77), channel_id=1, source_target_pairs={{0,1},{1,0},{2,3},{3,2},{4,5},{5,4},{6,7},{7,6},{8,9},{9,8},{10,11... | collective-permute-start | bytes 1769480 | tf_op jit(solution)/shard_map/ppermute | solution.py:171
  92.3 11.0 %collective-permute-start.22 = (bf16[96,3072]{1,0:T(8,128)(2,1)}, bf16[96,3072]{1,0:T(8,128)(2,1)}, u32[]{:S(2)}, u32[]{:S(2)}) collective-permute-start(bf16[96,3072]{1,0:T(8,128)(2,1)} %collective-permute-done.19.refs_9_.refs_7_), channel_id=1, source_target_pairs={{0,1},{1,0},{2,3},{3,2},{4,5},{5,4},{6,7},{7,6},{8,9},{9,8},{10,11... | collective-permute-start | bytes 1769480 | tf_op jit(solution)/shard_map/ppermute | solution.py:171
  92.4 10.8 %collective-permute-start.20 = (bf16[96,3072]{1,0:T(8,128)(2,1)}, bf16[96,3072]{1,0:T(8,128)(2,1)}, u32[]{:S(2)}, u32[]{:S(2)}) collective-permute-start(bf16[96,3072]{1,0:T(8,128)(2,1)} %bitcast.4.refs_5_.refs_3_), channel_id=1, source_target_pairs={{0,1},{1,0},{2,3},{3,2},{4,5},{5,4},{6,7},{7,6},{8,9},{9,8},{10,11... | collective-permute-start | bytes 1769480 | tf_op jit(solution)/shard_map/ppermute | solution.py:171
  92.9 10.4 %collective-permute-start.25 = (bf16[48,3072]{1,0:T(8,128)(2,1)}, bf16[48,3072]{1,0:T(8,128)(2,1)S(1)}, u32[]{:S(2)}, u32[]{:S(2)}) collective-permute-start(bf16[48,3072]{1,0:T(8,128)(2,1)} %copy-done.81), channel_id=1, source_target_pairs={{0,1},{1,0},{2,3},{3,2},{4,5},{5,4},{6,7},{7,6},{8,9},{9,8},{10,11... | collective-permute-start | bytes 884744 | tf_op jit(solution)/shard_map/ppermute | solution.py:171
  93.0 10.3 %collective-permute-start.26 = (bf16[48,3072]{1,0:T(8,128)(2,1)}, bf16[48,3072]{1,0:T(8,128)(2,1)S(1)}, u32[]{:S(2)}, u32[]{:S(2)}) collective-permute-start(bf16[48,3072]{1,0:T(8,128)(2,1)} %copy-done.82), channel_id=1, source_target_pairs={{0,1},{1,0},{2,3},{3,2},{4,5},{5,4},{6,7},{7,6},{8,9},{9,8},{10,11... | collective-permute-start | bytes 884744 | tf_op jit(solution)/shard_map/ppermute | solution.py:171
  119.5 22.6 %all-to-all-start.1 = ((bf16[8,96,896]{2,1,0:T(8,128)(2,1)}), bf16[8,96,896]{2,1,0:T(8,128)(2,1)S(1)}, u32[]{:S(2)}, u32[]{:S(2)}) async-start(bf16[8,96,896]{2,1,0:T(8,128)(2,1)} %bitcast.39), calls=%async_computation.1 | async-start | bytes 2752512 | tf_op jit(solution)/shard_map/all_to_all | solution.py:234
  123.2 68.7 %all-gather.5.cloned.1.call-start = ((), (), s32[]{:S(2)}) async-start(), calls=%async_computation.7 | async-start | bytes 1966080 | tf_op jit(solution)/shard_map/all_gather | solution.py:950
  126.0 232.0 %reduce-scatter.3.cloned.1.call-start = ((), (), s32[]{:S(2)}) async-start(), calls=%async_computation.8 | async-start | bytes 9830400 | tf_op jit(solution)/shard_map/reduce_scatter | solution.py:987
  202.3 23.0 %all-to-all-start.2 = ((bf16[8,96,896]{2,1,0:T(8,128)(2,1)}), bf16[8,96,896]{2,1,0:T(8,128)(2,1)S(1)}, u32[]{:S(2)}, u32[]{:S(2)}) async-start(bf16[8,96,896]{2,1,0:T(8,128)(2,1)} %bitcast.41), calls=%async_computation.2 | async-start | bytes 2752512 | tf_op jit(solution)/shard_map/all_to_all | solution.py:234
  236.1 16.1 %collective-permute-start.27 = (bf16[4,96,3072]{2,1,0:T(8,128)(2,1)}, bf16[4,96,3072]{2,1,0:T(8,128)(2,1)S(1)}, u32[]{:S(2)}, u32[]{:S(2)}) collective-permute-start(bf16[4,96,3072]{2,1,0:T(8,128)(2,1)} %get-tuple-element.136), channel_id=1, source_target_pairs={{0,1},{1,0},{2,3},{3,2},{4,5},{5,4},{6,7},{7,6},{8,9},{9,8},{10,11... | collective-permute-start | bytes 7077896 | tf_op jit(solution)/shard_map/ppermute | solution.py:171
  236.1 26.3 %all-to-all-start.3 = ((bf16[8,96,768]{2,1,0:T(8,128)(2,1)}), bf16[8,96,768]{2,1,0:T(8,128)(2,1)S(1)}, u32[]{:S(2)}, u32[]{:S(2)}) async-start(bf16[8,96,768]{2,1,0:T(8,128)(2,1)} %bitcast.46), calls=%async_computation.3 | async-start | bytes 2359296 | tf_op jit(solution)/shard_map/all_to_all | solution.py:234
  239.7 162.2 %reduce-scatter.5.cloned.1.call-start = ((), (), s32[]{:S(2)}) async-start(), calls=%async_computation.9 | async-start | bytes 1966080 | tf_op jit(solution)/shard_map/reduce_scatter | solution.py:987
  251.7 43.6 %collective-permute-start.30 = (bf16[4,384,768]{2,1,0:T(8,128)(2,1)}, bf16[4,384,768]{2,1,0:T(8,128)(2,1)}, u32[]{:S(2)}, u32[]{:S(2)}) collective-permute-start(bf16[4,384,768]{2,1,0:T(8,128)(2,1)} %get-tuple-element.150), channel_id=1, source_target_pairs={{0,1},{1,0},{2,3},{3,2},{4,5},{5,4},{6,7},{7,6},{8,9},{9,8},{10,11... | collective-permute-start | bytes 7077896 | tf_op jit(solution)/shard_map/ppermute | solution.py:171
  279.1 16.2 %collective-permute-start.31 = (bf16[4,96,768]{2,1,0:T(8,128)(2,1)S(1)}, bf16[4,96,768]{2,1,0:T(8,128)(2,1)S(1)}, u32[]{:S(2)}, u32[]{:S(2)}) collective-permute-start(bf16[4,96,768]{2,1,0:T(8,128)(2,1)S(1)} %get-tuple-element.151), channel_id=1, source_target_pairs={{0,1},{1,0},{2,3},{3,2},{4,5},{5,4},{6,7},{7,6},{8,9},{9,8},{10,11... | collective-permute-start | bytes 1769480 | tf_op jit(solution)/shard_map/ppermute | solution.py:171
  279.2 19.3 %collective-permute-start.28 = (bf16[2,48,3072]{2,1,0:T(8,128)(2,1)S(1)}, bf16[2,48,3072]{2,1,0:T(8,128)(2,1)S(1)}, u32[]{:S(2)}, u32[]{:S(2)}) collective-permute-start(bf16[2,48,3072]{2,1,0:T(8,128)(2,1)S(1)} %copy-done.54), channel_id=1, source_target_pairs={{0,2},{1,3},{2,0},{3,1},{4,6},{5,7},{6,4},{7,5},{8,10},{9,11},{10,... | collective-permute-start | bytes 1769480 | tf_op jit(solution)/shard_map/ppermute | solution.py:171
  281.2 17.4 %collective-permute-start.29 = (bf16[2,48,3072]{2,1,0:T(8,128)(2,1)S(1)}, bf16[2,48,3072]{2,1,0:T(8,128)(2,1)S(1)}, u32[]{:S(2)}, u32[]{:S(2)}) collective-permute-start(bf16[2,48,3072]{2,1,0:T(8,128)(2,1)S(1)} %copy-done.52), channel_id=1, source_target_pairs={{0,4},{1,5},{2,6},{3,7},{4,0},{5,1},{6,2},{7,3},{8,12},{9,13},{10,... | collective-permute-start | bytes 1769480 | tf_op jit(solution)/shard_map/ppermute | solution.py:171
  297.8 24.7 %collective-permute-start.34 = (bf16[2,240,768]{2,1,0:T(8,128)(2,1)S(1)}, bf16[2,240,768]{2,1,0:T(8,128)(2,1)S(1)}, u32[]{:S(2)}, u32[]{:S(2)}) collective-permute-start(bf16[2,240,768]{2,1,0:T(8,128)(2,1)S(1)} %get-tuple-element.158), channel_id=1, source_target_pairs={{0,2},{1,3},{2,0},{3,1},{4,6},{5,7},{6,4},{7,5},{8,10},{9,11},{10,... | collective-permute-start | bytes 2211848 | tf_op jit(solution)/shard_map/ppermute | solution.py:171
  298.5 24.1 %collective-permute-start.35 = (bf16[2,240,768]{2,1,0:T(8,128)(2,1)S(1)}, bf16[2,240,768]{2,1,0:T(8,128)(2,1)S(1)}, u32[]{:S(2)}, u32[]{:S(2)}) collective-permute-start(bf16[2,240,768]{2,1,0:T(8,128)(2,1)S(1)} %get-tuple-element.160), channel_id=1, source_target_pairs={{0,4},{1,5},{2,6},{3,7},{4,0},{5,1},{6,2},{7,3},{8,12},{9,13},{10,... | collective-permute-start | bytes 2211848 | tf_op jit(solution)/shard_map/ppermute | solution.py:171
  298.9 23.5 %collective-permute-start.36 = (bf16[48,3072]{1,0:T(8,128)(2,1)S(1)}, bf16[48,3072]{1,0:T(8,128)(2,1)S(1)}, u32[]{:S(2)}, u32[]{:S(2)}) collective-permute-start(bf16[48,3072]{1,0:T(8,128)(2,1)S(1)} %get-tuple-element.161), channel_id=1, source_target_pairs={{0,4},{1,5},{2,6},{3,7},{4,0},{5,1},{6,2},{7,3},{8,12},{9,13},{10,... | collective-permute-start | bytes 884744 | tf_op jit(solution)/shard_map/ppermute | solution.py:171
  300.9 21.5 %collective-permute-start.37 = (bf16[48,3072]{1,0:T(8,128)(2,1)S(1)}, bf16[48,3072]{1,0:T(8,128)(2,1)S(1)}, u32[]{:S(2)}, u32[]{:S(2)}) collective-permute-start(bf16[48,3072]{1,0:T(8,128)(2,1)S(1)} %get-tuple-element.163), channel_id=1, source_target_pairs={{0,2},{1,3},{2,0},{3,1},{4,6},{5,7},{6,4},{7,5},{8,10},{9,11},{10,... | collective-permute-start | bytes 884744 | tf_op jit(solution)/shard_map/ppermute | solution.py:171
  310.4 13.3 %collective-permute-start.32 = (bf16[4,288,768]{2,1,0:T(8,128)(2,1)S(1)}, bf16[4,288,768]{2,1,0:T(8,128)(2,1)S(1)}, u32[]{:S(2)}, u32[]{:S(2)}) collective-permute-start(bf16[4,288,768]{2,1,0:T(8,128)(2,1)S(1)} %get-tuple-element.156), channel_id=1, source_target_pairs={{0,1},{1,0},{2,3},{3,2},{4,5},{5,4},{6,7},{7,6},{8,9},{9,8},{10,11... | collective-permute-start | bytes 5308424 | tf_op jit(solution)/shard_map/ppermute | solution.py:171
  322.4 1.3 collective-permute-start.33
  324.1 14.1 %collective-permute-start.39 = (bf16[2,160,768]{2,1,0:T(8,128)(2,1)S(1)}, bf16[2,160,768]{2,1,0:T(8,128)(2,1)S(1)}, u32[]{:S(2)}, u32[]{:S(2)}) collective-permute-start(bf16[2,160,768]{2,1,0:T(8,128)(2,1)S(1)} %get-tuple-element.168), channel_id=1, source_target_pairs={{0,4},{1,5},{2,6},{3,7},{4,0},{5,1},{6,2},{7,3},{8,12},{9,13},{10,... | collective-permute-start | bytes 1474568 | tf_op jit(solution)/shard_map/ppermute | solution.py:171
  324.7 13.1 %collective-permute-start.38 = (bf16[2,144,768]{2,1,0:T(8,128)(2,1)S(1)}, bf16[2,144,768]{2,1,0:T(8,128)(2,1)S(1)}, u32[]{:S(2)}, u32[]{:S(2)}) collective-permute-start(bf16[2,144,768]{2,1,0:T(8,128)(2,1)S(1)} %get-tuple-element.166), channel_id=1, source_target_pairs={{0,2},{1,3},{2,0},{3,1},{4,6},{5,7},{6,4},{7,5},{8,10},{9,11},{10,... | collective-permute-start | bytes 1327112 | tf_op jit(solution)/shard_map/ppermute | solution.py:171
  326.2 19.9 %collective-permute-start.42 = (bf16[240,768]{1,0:T(8,128)(2,1)S(1)}, bf16[240,768]{1,0:T(8,128)(2,1)S(1)}, u32[]{:S(2)}, u32[]{:S(2)}) collective-permute-start(bf16[240,768]{1,0:T(8,128)(2,1)S(1)} %get-tuple-element.173), channel_id=1, source_target_pairs={{0,4},{1,5},{2,6},{3,7},{4,0},{5,1},{6,2},{7,3},{8,12},{9,13},{10,... | collective-permute-start | bytes 1105928 | tf_op jit(solution)/shard_map/ppermute | solution.py:171
  327.7 18.5 %collective-permute-start.43 = (bf16[240,768]{1,0:T(8,128)(2,1)S(1)}, bf16[240,768]{1,0:T(8,128)(2,1)S(1)}, u32[]{:S(2)}, u32[]{:S(2)}) collective-permute-start(bf16[240,768]{1,0:T(8,128)(2,1)S(1)} %get-tuple-element.175), channel_id=1, source_target_pairs={{0,2},{1,3},{2,0},{3,1},{4,6},{5,7},{6,4},{7,5},{8,10},{9,11},{10,... | collective-permute-start | bytes 1105928 | tf_op jit(solution)/shard_map/ppermute | solution.py:171
  328.3 27.7 %collective-permute-start.46 = (bf16[96,3072]{1,0:T(8,128)(2,1)S(1)}, bf16[96,3072]{1,0:T(8,128)(2,1)S(1)}, u32[]{:S(2)}, u32[]{:S(2)}) collective-permute-start(bf16[96,3072]{1,0:T(8,128)(2,1)S(1)} %fold_last.3.refs_4_.refs_0_), channel_id=1, source_target_pairs={{0,8},{24,16},{1,9},{25,17},{2,10},{26,18},{3,11},{27,19},{4,12},{... | collective-permute-start | bytes 1769480 | tf_op jit(solution)/shard_map/ppermute | solution.py:315
  338.5 11.6 %collective-permute-start.41 = (bf16[160,768]{1,0:T(8,128)(2,1)S(1)}, bf16[160,768]{1,0:T(8,128)(2,1)S(1)}, u32[]{:S(2)}, u32[]{:S(2)}) collective-permute-start(bf16[160,768]{1,0:T(8,128)(2,1)S(1)} %get-tuple-element.172), channel_id=1, source_target_pairs={{0,2},{1,3},{2,0},{3,1},{4,6},{5,7},{6,4},{7,5},{8,10},{9,11},{10,... | collective-permute-start | bytes 737288 | tf_op jit(solution)/shard_map/ppermute | solution.py:171
  340.0 10.1 %collective-permute-start.40 = (bf16[144,768]{1,0:T(8,128)(2,1)S(1)}, bf16[144,768]{1,0:T(8,128)(2,1)S(1)}, u32[]{:S(2)}, u32[]{:S(2)}) collective-permute-start(bf16[144,768]{1,0:T(8,128)(2,1)S(1)} %get-tuple-element.170), channel_id=1, source_target_pairs={{0,4},{1,5},{2,6},{3,7},{4,0},{5,1},{6,2},{7,3},{8,12},{9,13},{10,... | collective-permute-start | bytes 663560 | tf_op jit(solution)/shard_map/ppermute | solution.py:171
  346.3 21.9 %collective-permute-start.45 = (bf16[480,768]{1,0:T(8,128)(2,1)S(1)}, bf16[480,768]{1,0:T(8,128)(2,1)S(1)}, u32[]{:S(2)}, u32[]{:S(2)}) collective-permute-start(bf16[480,768]{1,0:T(8,128)(2,1)S(1)} %fold_last.4.refs_4_.refs_0_), channel_id=1, source_target_pairs={{0,8},{24,16},{1,9},{25,17},{2,10},{26,18},{3,11},{27,19},{4,12},{... | collective-permute-start | bytes 2211848 | tf_op jit(solution)/shard_map/ppermute | solution.py:315
  351.0 34.8 %collective-permute-start.44 = (bf16[304,768]{1,0:T(8,128)(2,1)}, bf16[304,768]{1,0:T(8,128)(2,1)}, u32[]{:S(2)}, u32[]{:S(2)}) collective-permute-start(bf16[304,768]{1,0:T(8,128)(2,1)} %fold_last.5.refs_4_.refs_0_), channel_id=1, source_target_pairs={{0,8},{24,16},{1,9},{25,17},{2,10},{26,18},{3,11},{27,19},{4,12},{... | collective-permute-start | bytes 1400840 | tf_op jit(solution)/shard_map/ppermute | solution.py:315
  357.2 30.6 %collective-permute-start.49 = (bf16[96,3072]{1,0:T(8,128)(2,1)S(1)}, bf16[96,3072]{1,0:T(8,128)(2,1)S(1)}, u32[]{:S(2)}, u32[]{:S(2)}) collective-permute-start(bf16[96,3072]{1,0:T(8,128)(2,1)S(1)} %joined.6.refs_2_.refs_0_), channel_id=1, source_target_pairs={{8,16},{16,8},{9,17},{17,9},{10,18},{18,10},{11,19},{19,11},{12,20... | collective-permute-start | bytes 1769480 | tf_op jit(solution)/shard_map/ppermute | solution.py:315
  368.4 20.9 %collective-permute-start.48 = (bf16[480,768]{1,0:T(8,128)(2,1)S(1)}, bf16[480,768]{1,0:T(8,128)(2,1)S(1)}, u32[]{:S(2)}, u32[]{:S(2)}) collective-permute-start(bf16[480,768]{1,0:T(8,128)(2,1)S(1)} %joined.7.refs_2_.refs_0_), channel_id=1, source_target_pairs={{8,16},{16,8},{9,17},{17,9},{10,18},{18,10},{11,19},{19,11},{12,20... | collective-permute-start | bytes 2211848 | tf_op jit(solution)/shard_map/ppermute | solution.py:315
  387.1 4.0 collective-permute-start.47
  388.0 21.7 %collective-permute-start.52 = (bf16[96,3072]{1,0:T(8,128)(2,1)S(1)}, bf16[96,3072]{1,0:T(8,128)(2,1)}, u32[]{:S(2)}, u32[]{:S(2)}) collective-permute-start(bf16[96,3072]{1,0:T(8,128)(2,1)S(1)} %joined.9.refs_2_.refs_0_), channel_id=1, source_target_pairs={{8,0},{16,24},{9,1},{17,25},{10,2},{18,26},{11,3},{19,27},{12,4},{... | collective-permute-start | bytes 1769480 | tf_op jit(solution)/shard_map/ppermute | solution.py:315
  389.5 44.8 %collective-permute-start.51 = (bf16[480,768]{1,0:T(8,128)(2,1)S(1)}, bf16[480,768]{1,0:T(8,128)(2,1)}, u32[]{:S(2)}, u32[]{:S(2)}) collective-permute-start(bf16[480,768]{1,0:T(8,128)(2,1)S(1)} %joined.10.refs_2_.refs_0_), channel_id=1, source_target_pairs={{8,0},{16,24},{9,1},{17,25},{10,2},{18,26},{11,3},{19,27},{12,4},{... | collective-permute-start | bytes 2211848 | tf_op jit(solution)/shard_map/ppermute | solution.py:315
  392.0 48.3 %collective-permute-start.50 = (bf16[304,768]{1,0:T(8,128)(2,1)}, bf16[304,768]{1,0:T(8,128)(2,1)}, u32[]{:S(2)}, u32[]{:S(2)}) collective-permute-start(bf16[304,768]{1,0:T(8,128)(2,1)} %joined.11.refs_2_.refs_0_), channel_id=1, source_target_pairs={{8,0},{16,24},{9,1},{17,25},{10,2},{18,26},{11,3},{19,27},{12,4},{... | collective-permute-start | bytes 1400840 | tf_op jit(solution)/shard_map/ppermute | solution.py:315
  (82 other events, 389.6 us)
Sparse Core Ops, SparseCore 0:
  10.6 143.7 all-gather.2
  156.5 35.3 all-gather.4
  194.2 135.0 reduce-scatter.2
  358.1 43.7 reduce-scatter.4

commit v6 on v4

--- a/solution.py
+++ b/solution.py
@@ -15,7 +15,7 @@
 ROOT = 0.7978845608028654
 COST = dict(
     prepare=3, attend=16, widen=9, dispatch=10, expert_rows=4, expert=20, expert_last=10, expert_grads=6, gate_back=10, widen_back=12, fold=1, fold_wide=1,
-    second_back=17, attend_back=2, fold_again=1, fold_wait=12, project_back=2, tokens_back=2, fold_last=1, joined=6,
+    second_back=17, attend_back=2, fold_again=1, fold_wait=12, project_back=2, tokens_back=2, fold_last=1, joined=4,
     combine=1, finish=1, settle=1,
 )
 WIDE = ("attend", "widen", "dispatch", "expert", "expert_last", "expert_grads", "gate_back", "fold_wide", "widen_back", "settle")

time: 449 us -> 452 us (level)
  local copies, waits for them, and re-layouts: 34.7 us -> 41 us
  waiting for transfers between devices: 173 us -> 168 us
    unnamed x155 -> x175, local copies, waits for them, and re-layouts: 26.7 us -> 33 us
    ppermute x44, waiting for transfers between devices: 59.1 us -> 54.1 us  [hop(): return lax.ppermute(value, 'expert', [(i, i ^ bit) for i in range(self.n)])]
  transfers between devices with their start and end apart: 61 -> 61, of which waited for: 25 -> 22; matrix products, arithmetic and copies ran while one was open for 2% -> 2% of each run, Pallas kernels for 35% -> 35%
where the time goes in v6:
time: 452 us; the launch traced here: 444 us
  waiting for transfers between devices  168 us (37%)
  Pallas kernels  156 us (35%)
  starting transfers between devices  61.4 us (14%)
  local copies, waits for them, and re-layouts  41 us (9%)
  between operations  15 us (3%)
    pallas_call x34, Pallas kernels, call(): pl.pallas_call(body, out_shape=outs, in_specs=[pl.BlockSpec(memory_space=...  156 us
    ppermute x9, waiting for transfers between devices, along(): return lax.ppermute(value, 'dp', pairs)  64.6 us
    ppermute x44, waiting for transfers between devices, hop(): return lax.ppermute(value, 'expert', [(i, i ^ bit) for i in range(self.n)])  54.1 us
    all_to_all x4, waiting for transfers between devices, exchange(): lax.all_to_all(blocks, 'expert', split_axis=0, concat_axis=0, tiled=True)  35.4 us
    ppermute x44, starting transfers between devices, hop(): return lax.ppermute(value, 'expert', [(i, i ^ bit) for i in range(self.n)])  33.8 us
    unnamed x175, local copies, waits for them, and re-layouts  33 us
    all_to_all x4, starting transfers between devices, exchange(): lax.all_to_all(blocks, 'expert', split_axis=0, concat_axis=0, tiled=True)  15.5 us
    all_gather x2, waiting for transfers between devices, on_device(): whole = lax.all_gather(chunk(start, wide), 'dp', axis=0, tiled=True)  13.9 us
  transfers between devices with their start and end apart: 61, of which 22 were waited for; matrix products, arithmetic and copies ran while one was open for 2% of the time, Pallas kernels for 35%

profile of v6, /device:TPU:0, one launch (start us, length us, event | category | flops | bytes accessed | tf_op | source)
XLA Modules:
  0.0 444.3 jit_solution(1690205349414687228)
XLA Ops:
  8.8 1.5 pad_maximum_fusion
  11.5 3.0 collective-permute-start.1
  14.5 1.5 collective-permute-start.3
  16.0 12.3 %collective-permute-done.1.refs_5_.refs_13_.refs_23_.refs_7_.refs_9_ = bf16[400,768]{1,0:T(8,128)(2,1)S(1)} collective-permute-done((bf16[400,768]{1,0:T(8,128)(2,1)S(1)}, bf16[400,768]{1,0:T(8,128)(2,1)S(1)}, u32[]{:S(2)}, u32[]{:S(2)}) %collective-permute-start.1) | collective-permute-done | bytes 614432 | tf_op jit(solution)/shard_map/ppermute | solution.py:171
  29.1 1.8 collective-permute-start.5
  31.7 1.5 collective-permute-start.7
  35.4 4.3 collective-permute-done.7.refs_17_.refs_13_
  42.2 1.9 prepare.1
  44.8 1.5 collective-permute-start.9
  47.5 1.4 collective-permute-start.19
  49.7 15.9 %attend.1 = (bf16[384,768]{1,0:T(8,128)(2,1)}, bf16[384,2304]{1,0:T(8,128)(2,1)}, bf16[384,768]{1,0:T(8,128)(2,1)}, f32[384,128]{1,0:T(8,128)}, f32[384,768]{1,0...) custom-call(bf16[384,768]{1,0:T(8,128)(2,1)} %refs_1_.3, s32[384,1]{1,0:T(8,128)} %copy.28.refs_1_.refs_3_, ...), custom_call_target="tpu_custom_call" | custom-call | flops 18400000000 | bytes 1000 | tf_op jit(solution)/shard_map/attend/pallas_call | solution.py:111
  66.8 1.6 collective-permute-start.14
  69.0 4.9 %collective-permute-done.18.refs_7_.refs_5_ = bf16[96,3072]{1,0:T(8,128)(2,1)S(1)} collective-permute-done((bf16[96,3072]{1,0:T(8,128)(2,1)}, bf16[96,3072]{1,0:T(8,128)(2,1)S(1)}, u32[]{:S(2)}, u32[]{:S(2)}) %collective-permute-start.18) | collective-permute-done | bytes 589856 | tf_op jit(solution)/shard_map/ppermute | solution.py:171
  73.9 1.6 collective-permute-done.19.refs_9_.refs_7_
  77.8 2.4 collective-permute-done.14.refs_7_.refs_11_
  80.2 1.6 collective-permute-done.15.refs_8_.refs_12_
  81.8 3.9 collective-permute-done.23.refs_11_.refs_9_
  87.7 4.1 all-to-all-start
  93.6 9.6 %widen.1 = (bf16[384,3072]{1,0:T(8,128)(2,1)}, bf16[384,3072]{1,0:T(8,128)(2,1)}) custom-call(bf16[384,768]{1,0:T(8,128)(2,1)} %get-tuple-element.101.refs_0_.refs_2_, bf16[768,384]{1,0:T(8,128)(2,1)} %refs_5_.2, bf16[768,384]{1,0:T(8,128)(2,1)} %copy-done.38, bf16[768,384]{1,0:T(8,128)(2,1)} %copy-done.26, bf16[768,384]{1,0:T(8,128)(2,1)} %copy-done.40, ...), custom_call_target="tpu_custom_call" | custom-call | flops 10350000128 | bytes 1000 | tf_op jit(solution)/shard_map/widen/pallas_call | solution.py:111
  103.2 5.3 %all-to-all-done = bf16[8,96,768]{2,1,0:T(8,128)(2,1)S(1)} async-done(((bf16[8,96,768]{2,1,0:T(8,128)(2,1)}), bf16[8,96,768]{2,1,0:T(8,128)(2,1)S(1)}, u32[]{:S(2)}, u32[]{:S(2)}) %all-to-all-start) | async-done | bytes 1179680 | tf_op jit(solution)/shard_map/all_to_all | solution.py:234
  109.5 9.9 %dispatch.1 = (f32[384,768]{1,0:T(8,128)}, f32[384,1]{1,0:T(8,128)}, bf16[768,896]{1,0:T(8,128)(2,1)}) custom-call(bf16[384,3072]{1,0:T(8,128)(2,1)} %get-tuple-element.107.refs_0_.refs_16_.refs_6_, f32[384,768]{1,0:T(8,128)} %get-tuple-element.108.refs_1_, f32[16,768]{1,0:T(8,128)} %get-tuple-element.103.refs_11_.refs_2_.refs_4_.refs_3_, ...), custom_call_target="tpu_custom_call" | custom-call | flops 11500000256 | bytes 1000 | tf_op jit(solution)/shard_map/dispatch/pallas_call | solution.py:111
  119.4 3.7 all-to-all-start.1
  126.1 15.9 %all-to-all-done.1 = bf16[8,96,896]{2,1,0:T(8,128)(2,1)S(1)} async-done(((bf16[8,96,896]{2,1,0:T(8,128)(2,1)}), bf16[8,96,896]{2,1,0:T(8,128)(2,1)S(1)}, u32[]{:S(2)}, u32[]{:S(2)}) %all-to-all-start.1) | async-done | bytes 1376288 | tf_op jit(solution)/shard_map/all_to_all | solution.py:234
  147.1 7.3 %all-gather.3.cloned.1.call-done = bf16[6144,640]{1,0:T(8,128)(2,1)} async-done(((bf16[1536,640]{1,0:T(8,128)(2,1)}), bf16[6144,640]{1,0:T(8,128)(2,1)}) %all-gather.3.cloned.1.call-update) | async-done | bytes 7864336 | tf_op jit(solution)/shard_map/all_gather | solution.py:950
  154.3 30.8 %expert.1 = (bf16[4,2,768,640]{3,2,1,0:T(8,128)(2,1)}, f32[768,768]{1,0:T(8,128)}, f32[768,768]{1,0:T(8,128)}) custom-call(bf16[768,768]{1,0:T(8,128)(2,1)} %copy-done.66, bf16[768,768]{1,0:T(8,128)(2,1)} %copy-done.67, bf16[768,768]{1,0:T(8,128)(2,1)} %copy-done.64, bf16[768,768]{1,0:T(8,128)(2,1)} %copy-done.65, bf16[4,2,768,640]{3,2,1,0:T(8,128)(2,1)} %bitcast.50, ...), custom_call_target="tpu_custom_call" | custom-call | flops 23000000512 | bytes 1000 | tf_op jit(solution)/shard_map/expert/pallas_call | solution.py:111
  185.1 6.7 %all-gather.5.cloned.1.call-done = bf16[6144,128]{1,0:T(8,128)(2,1)} async-done(((bf16[1536,128]{1,0:T(8,128)(2,1)}), bf16[6144,128]{1,0:T(8,128)(2,1)}) %all-gather.5.cloned.1.call-update) | async-done | bytes 1572880 | tf_op jit(solution)/shard_map/all_gather | solution.py:950
  191.8 10.4 %expert_last.1 = (bf16[768,896]{1,0:T(8,128)(2,1)}, bf16[768,768]{1,0:T(8,128)(2,1)}, bf16[1,768,512]{2,1,0:T(8,128)(2,1)}, bf16[1,768,512]{2,1,0:T(8,128)(2,1)}) custom-call(bf16[768,768]{1,0:T(8,128)(2,1)} %copy-done.66, bf16[768,768]{1,0:T(8,128)(2,1)} %copy-done.67, bf16[768,768]{1,0:T(8,128)(2,1)} %copy-done.64, bf16[768,768]{1,0:T(8,128)(2,1)} %copy-done.65, ...), custom_call_target="tpu_custom_call" | custom-call | flops 11500000256 | bytes 1000 | tf_op jit(solution)/shard_map/expert_last/pallas_call | solution.py:111
  202.2 4.1 all-to-all-start.2
  206.3 4.6 %expert_grads.1.refs_8_ = bf16[4,2,768,128]{3,2,1,0:T(8,128)(2,1)} custom-call(bf16[768,768]{1,0:T(8,128)(2,1)} %copy-done.64, bf16[768,768]{1,0:T(8,128)(2,1)} %copy-done.65, bf16[1,768,512]{2,1,0:T(8,128)(2,1)} %get-tuple-element.127.refs_2_.refs_4_, bf16[1,768,512]{2,1,0:T(8,128)(2,1)} %get-tuple-element.128.refs_3_, ...), custom_call_target="tpu_custom_call" | custom-call | flops 6899999744 | bytes 1000 | tf_op jit(solution)/shard_map/expert_grads/pallas_call | solution.py:111
  210.9 14.3 %all-to-all-done.2 = bf16[8,96,896]{2,1,0:T(8,128)(2,1)S(1)} async-done(((bf16[8,96,896]{2,1,0:T(8,128)(2,1)}), bf16[8,96,896]{2,1,0:T(8,128)(2,1)S(1)}, u32[]{:S(2)}, u32[]{:S(2)}) %all-to-all-start.2) | async-done | bytes 1376288 | tf_op jit(solution)/shard_map/all_to_all | solution.py:234
  226.3 9.8 %gate_back.1 = (f32[384,768]{1,0:T(8,128)}, bf16[384,768]{1,0:T(8,128)(2,1)}, f32[2,768]{1,0:T(2,128)}, f32[8,768]{1,0:T(8,128)}, bf16[4,96,3072]{2,1,0:T(8,128)(2,1)}, /*index=5*/bf16[4,96,3072]{2,1,0:T(8,128)(2,1)}) custom-call(s32[384,1]{1,0:T(8,128)} %copy-done.53, s32[384,1]{1,0:T(8,128)} %copy.27.refs_0_.refs_4_.refs_1_, ...), custom_call_target="tpu_custom_call" | custom-call | flops 11500000256 | bytes 1000 | tf_op jit(solution)/shard_map/gate_back/pallas_call | solution.py:111
  236.1 3.6 all-to-all-start.3
  239.7 12.0 %widen_back.1 = (bf16[384,3072]{1,0:T(8,128)(2,1)}, bf16[4,384,768]{2,1,0:T(8,128)(2,1)}, bf16[4,384,768]{2,1,0:T(8,128)(2,1)}) custom-call(bf16[384,768]{1,0:T(8,128)(2,1)} %get-tuple-element.129.refs_0_, bf16[384,3072]{1,0:T(8,128)(2,1)} %get-tuple-element.130.refs_1_, bf16[384,768]{1,0:T(8,128)(2,1)} %get-tuple-element.101.refs_0_.refs_2_, ...), custom_call_target="tpu_custom_call" | custom-call | flops 13799999488 | bytes 1000 | tf_op jit(solution)/shard_map/widen_back/pallas_call | solution.py:111
  252.2 1.4 copy-done.72
  253.6 4.1 fold_wide.1
  267.4 6.8 %second_back.1 = (f32[384,768]{1,0:T(8,128)S(1)}, bf16[384,768]{1,0:T(8,128)(2,1)S(1)}, f32[2,768]{1,0:T(2,128)S(1)}, bf16[4,96,768]{2,1,0:T(8,128)(2,1)S(1)}, bf16[4,96,768]{2,1,0:T(8,128)(2,1)S(1)}) custom-call(bf16[384,3072]{1,0:T(8,128)(2,1)S(1)} %copy-done.10, f32[384,768]{1,0:T(8,128)S(1)} %copy-done.68, f32[384,768]{1,0:T(8,128)S(1)} %copy-done.69, ...), custom_call_target="tpu_custom_call" | custom-call | flops 19549999104 | bytes 1000 | tf_op jit(solution)/shard_map/second_back/pallas_call | solution.py:111
  274.3 1.9 collective-permute-start.28
  276.2 1.5 collective-permute-start.29
  277.7 12.6 %attend_back.1.refs_4_.refs_0_ = bf16[384,2304]{1,0:T(8,128)(2,1)S(1)} custom-call(bf16[384,768]{1,0:T(8,128)(2,1)S(1)} %get-tuple-element.138.refs_0_, bf16[384,2304]{1,0:T(8,128)(2,1)S(1)} %copy-done.12, f32[384,128]{1,0:T(8,128)S(1)} %copy-done.25, s32[384,1]{1,0:T(8,128)S(1)} %copy-done.19, s32[1,384]{1,0:T(1,128)S(1)} %copy-done.33, ...), custom_call_target="tpu_custom_call" | custom-call | flops 2300000000 | bytes 1000 | tf_op jit(solution)/shard_map/attend_back/pallas_call | solution.py:111
  290.4 2.4 fold.2
  294.8 5.7 %tokens_back.1 = (f32[384,768]{1,0:T(8,128)}, bf16[4,16,768]{2,1,0:T(8,128)(2,1)S(1)}, bf16[4,16,768]{2,1,0:T(8,128)(2,1)S(1)}) custom-call(bf16[384,2304]{1,0:T(8,128)(2,1)S(1)} %attend_back.1.refs_4_.refs_0_, bf16[384,768]{1,0:T(8,128)(2,1)S(1)} %copy-done.21, f32[384,768]{1,0:T(8,128)S(1)} %get-tuple-element.143.refs_2_, f32[16,768]{1,0:T(8,128)S(1)} %copy-done.29, ...), custom_call_target="tpu_custom_call" | custom-call | flops 2300000000 | bytes 1000 | tf_op jit(solution)/shard_map/tokens_back/pallas_call | solution.py:111
  300.5 2.3 project_back.1
  303.3 1.9 collective-permute-start.38
  305.2 5.7 %collective-permute-done.34.refs_1_ = bf16[2,240,768]{2,1,0:T(8,128)(2,1)S(1)} collective-permute-done((bf16[2,240,768]{2,1,0:T(8,128)(2,1)S(1)}, bf16[2,240,768]{2,1,0:T(8,128)(2,1)S(1)}, u32[]{:S(2)}, u32[]{:S(2)}) %collective-permute-start.34) | collective-permute-done | bytes 737312 | tf_op jit(solution)/shard_map/ppermute | solution.py:171
  310.9 2.0 collective-permute-done.35.refs_3_
  315.0 1.8 collective-permute-start.36
  317.0 1.9 collective-permute-start.42
  319.2 1.5 collective-permute-start.43
  320.6 13.8 %collective-permute-done.39.refs_3_ = bf16[48,3072]{1,0:T(8,128)(2,1)S(1)} collective-permute-done((bf16[48,3072]{1,0:T(8,128)(2,1)S(1)}, bf16[48,3072]{1,0:T(8,128)(2,1)S(1)}, u32[]{:S(2)}, u32[]{:S(2)}) %collective-permute-start.39) | collective-permute-done | bytes 294944 | tf_op jit(solution)/shard_map/ppermute | solution.py:171
  334.6 2.8 collective-permute-start.46
  339.6 1.8 collective-permute-start.41
  341.4 1.5 collective-permute-start.40
  350.3 1.5 collective-permute-start.44
  351.8 1.5 combine.1.refs_2_
  355.2 25.9 %collective-permute-done.45.refs_1_ = bf16[480,768]{1,0:T(8,128)(2,1)S(1)} collective-permute-done((bf16[480,768]{1,0:T(8,128)(2,1)S(1)}, bf16[480,768]{1,0:T(8,128)(2,1)S(1)}, u32[]{:S(2)}, u32[]{:S(2)}) %collective-permute-start.45) | collective-permute-done | bytes 737312 | tf_op jit(solution)/shard_map/ppermute | solution.py:315
  382.0 13.8 %collective-permute-done.44.refs_1_ = bf16[304,768]{1,0:T(8,128)(2,1)S(1)} collective-permute-done((bf16[304,768]{1,0:T(8,128)(2,1)S(1)}, bf16[304,768]{1,0:T(8,128)(2,1)S(1)}, u32[]{:S(2)}, u32[]{:S(2)}) %collective-permute-start.44) | collective-permute-done | bytes 466976 | tf_op jit(solution)/shard_map/ppermute | solution.py:315
  398.3 1.6 collective-permute-start.51
  403.1 2.5 finish.1
  405.6 12.0 %collective-permute-done.52.refs_1_ = bf16[96,3072]{1,0:T(8,128)(2,1)} collective-permute-done((bf16[96,3072]{1,0:T(8,128)(2,1)S(1)}, bf16[96,3072]{1,0:T(8,128)(2,1)}, u32[]{:S(2)}, u32[]{:S(2)}) %collective-permute-start.52) | collective-permute-done | bytes 589856 | tf_op jit(solution)/shard_map/ppermute | solution.py:315
  417.5 2.3 settle.3.refs_2_
  419.9 10.6 %collective-permute-done.51.refs_1_ = bf16[480,768]{1,0:T(8,128)(2,1)} collective-permute-done((bf16[480,768]{1,0:T(8,128)(2,1)S(1)}, bf16[480,768]{1,0:T(8,128)(2,1)}, u32[]{:S(2)}, u32[]{:S(2)}) %collective-permute-start.51) | collective-permute-done | bytes 737312 | tf_op jit(solution)/shard_map/ppermute | solution.py:315
  430.4 2.7 settle.4
  433.1 2.3 collective-permute-done.50.refs_1_
  435.4 2.1 settle.5
  (286 shorter events, 63.1 us)
Async XLA Ops:
  7.2 147.1 %all-gather.3.cloned.1.call-start = ((), (), s32[]{:S(2)}) async-start(), calls=%async_computation.6 | async-start | bytes 9830400 | tf_op jit(solution)/shard_map/all_gather | solution.py:950
  10.4 23.3 %copy-start.34 = (s32[384,1]{0,1:T(1,128)S(1)}, s32[384,1]{0,1:T(1,128)}, u32[]{:S(2)}) copy-start(s32[384,1]{0,1:T(1,128)} %param.15) | copy-start | bytes 4612
  11.1 23.5 %copy-start.32 = (s32[1,384]{1,0:T(1,128)S(1)}, s32[1,384]{1,0:T(1,128)}, u32[]{:S(2)}) copy-start(s32[1,384]{1,0:T(1,128)} %refs_4_.2) | copy-start | bytes 4612
  11.5 32.7 %copy-start = (bf16[400,768]{1,0:T(8,128)(2,1)}, bf16[400,768]{1,0:T(8,128)(2,1)S(1)}, u32[]{:S(2)}) copy-start(bf16[400,768]{1,0:T(8,128)(2,1)S(1)} %pad_maximum_fusion.1.refs_3_.refs_11_.refs_21_.refs_5_.refs_7_) | copy-start | bytes 1843204
  11.5 16.9 %collective-permute-start.1 = (bf16[400,768]{1,0:T(8,128)(2,1)S(1)}, bf16[400,768]{1,0:T(8,128)(2,1)S(1)}, u32[]{:S(2)}, u32[]{:S(2)}) collective-permute-start(bf16[400,768]{1,0:T(8,128)(2,1)S(1)} %pad_maximum_fusion.1.refs_3_.refs_11_.refs_21_.refs_5_.refs_7_), channel_id=1, source_target_pairs={{0,2},{1,3},{2,0},{3,1},{4,6},{5,7},{6,4},{7,5},{8,10},{9,11},{10,... | collective-permute-start | bytes 1843208 | tf_op jit(solution)/shard_map/ppermute | solution.py:171
  14.5 16.4 %collective-permute-start.3 = (bf16[400,768]{1,0:T(8,128)(2,1)S(1)}, bf16[400,768]{1,0:T(8,128)(2,1)S(1)}, u32[]{:S(2)}, u32[]{:S(2)}) collective-permute-start(bf16[400,768]{1,0:T(8,128)(2,1)S(1)} %pad_maximum_fusion.1.refs_3_.refs_11_.refs_21_.refs_5_.refs_7_), channel_id=1, source_target_pairs={{0,4},{1,5},{2,6},{3,7},{4,0},{5,1},{6,2},{7,3},{8,12},{9,13},{10,... | collective-permute-start | bytes 1843208 | tf_op jit(solution)/shard_map/ppermute | solution.py:171
  29.1 10.6 %collective-permute-start.5 = (bf16[208,768]{1,0:T(8,128)(2,1)}, bf16[208,768]{1,0:T(8,128)(2,1)S(1)}, u32[]{:S(2)}, u32[]{:S(2)}) collective-permute-start(bf16[208,768]{1,0:T(8,128)(2,1)} %slice.40), channel_id=1, source_target_pairs={{0,4},{1,5},{2,6},{3,7},{4,0},{5,1},{6,2},{7,3},{8,12},{9,13},{10,... | collective-permute-start | bytes 958472 | tf_op jit(solution)/shard_map/ppermute | solution.py:171
  31.7 8.0 %collective-permute-start.7 = (bf16[192,768]{1,0:T(8,128)(2,1)}, bf16[192,768]{1,0:T(8,128)(2,1)}, u32[]{:S(2)}, u32[]{:S(2)}) collective-permute-start(bf16[192,768]{1,0:T(8,128)(2,1)} %slice.41), channel_id=1, source_target_pairs={{0,2},{1,3},{2,0},{3,1},{4,6},{5,7},{6,4},{7,5},{8,10},{9,11},{10,... | collective-permute-start | bytes 884744 | tf_op jit(solution)/shard_map/ppermute | solution.py:171
  33.2 11.7 %collective-permute-start = (bf16[400,768]{1,0:T(8,128)(2,1)S(1)}, bf16[400,768]{1,0:T(8,128)(2,1)S(1)}, u32[]{:S(2)}, u32[]{:S(2)}) collective-permute-start(bf16[400,768]{1,0:T(8,128)(2,1)S(1)} %pad_maximum_fusion.1.refs_3_.refs_11_.refs_21_.refs_5_.refs_7_), channel_id=1, source_target_pairs={{0,1},{1,0},{2,3},{3,2},{4,5},{5,4},{6,7},{7,6},{8,9},{9,8},{10,11... | collective-permute-start | bytes 1843208 | tf_op jit(solution)/shard_map/ppermute | solution.py:171
  33.2 13.7 %collective-permute-start.2 = (bf16[400,768]{1,0:T(8,128)(2,1)S(1)}, bf16[400,768]{1,0:T(8,128)(2,1)S(1)}, u32[]{:S(2)}, u32[]{:S(2)}) collective-permute-start(bf16[400,768]{1,0:T(8,128)(2,1)S(1)} %collective-permute-done.1.refs_5_.refs_13_.refs_23_.refs_7_.refs_9_), channel_id=1, source_target_pairs={{0,1},{1,0},{2,3},{3,2},{4,5},{5,4},{6,7},{7,6},{8,9},{9,8},{10,11... | collective-permute-start | bytes 1843208 | tf_op jit(solution)/shard_map/ppermute | solution.py:171
  33.7 13.8 %collective-permute-start.4 = (bf16[400,768]{1,0:T(8,128)(2,1)S(1)}, bf16[400,768]{1,0:T(8,128)(2,1)}, u32[]{:S(2)}, u32[]{:S(2)}) collective-permute-start(bf16[400,768]{1,0:T(8,128)(2,1)S(1)} %collective-permute-done.3.refs_7_.refs_15_.refs_25_.refs_9_.refs_11_), channel_id=1, source_target_pairs={{0,1},{1,0},{2,3},{3,2},{4,5},{5,4},{6,7},{7,6},{8,9},{9,8},{10,11... | collective-permute-start | bytes 1843208 | tf_op jit(solution)/shard_map/ppermute | solution.py:171
  39.7 6.6 %collective-permute-start.8 = (bf16[192,768]{1,0:T(8,128)(2,1)}, bf16[192,768]{1,0:T(8,128)(2,1)S(1)}, u32[]{:S(2)}, u32[]{:S(2)}) collective-permute-start(bf16[192,768]{1,0:T(8,128)(2,1)} %collective-permute-done.7.refs_17_.refs_13_), channel_id=1, source_target_pairs={{0,1},{1,0},{2,3},{3,2},{4,5},{5,4},{6,7},{7,6},{8,9},{9,8},{10,11... | collective-permute-start | bytes 884744 | tf_op jit(solution)/shard_map/ppermute | solution.py:171
  39.7 9.2 %collective-permute-start.6 = (bf16[208,768]{1,0:T(8,128)(2,1)S(1)}, bf16[208,768]{1,0:T(8,128)(2,1)S(1)}, u32[]{:S(2)}, u32[]{:S(2)}) collective-permute-start(bf16[208,768]{1,0:T(8,128)(2,1)S(1)} %collective-permute-done.5.refs_9_.refs_18_.refs_27_.refs_11_.refs_14_), channel_id=1, source_target_pairs={{0,1},{1,0},{2,3},{3,2},{4,5},{5,4},{6,7},{7,6},{8,9},{9,8},{10,11... | collective-permute-start | bytes 958472 | tf_op jit(solution)/shard_map/ppermute | solution.py:171
  44.8 20.7 %collective-permute-start.9 = (bf16[768,384]{1,0:T(8,128)(2,1)}, bf16[768,384]{1,0:T(8,128)(2,1)S(1)}, u32[]{:S(2)}, u32[]{:S(2)}) collective-permute-start(bf16[768,384]{1,0:T(8,128)(2,1)} %refs_5_.2), channel_id=1, source_target_pairs={{0,2},{1,3},{2,0},{3,1},{4,6},{5,7},{6,4},{7,5},{8,10},{9,11},{10,... | collective-permute-start | bytes 1769480 | tf_op jit(solution)/shard_map/ppermute | solution.py:171
  46.3 19.3 %collective-permute-start.10 = (bf16[768,384]{1,0:T(8,128)(2,1)}, bf16[768,384]{1,0:T(8,128)(2,1)}, u32[]{:S(2)}, u32[]{:S(2)}) collective-permute-start(bf16[768,384]{1,0:T(8,128)(2,1)} %refs_5_.2), channel_id=1, source_target_pairs={{0,4},{1,5},{2,6},{3,7},{4,0},{5,1},{6,2},{7,3},{8,12},{9,13},{10,... | collective-permute-start | bytes 1769480 | tf_op jit(solution)/shard_map/ppermute | solution.py:171
  46.9 27.0 %collective-permute-start.18 = (bf16[96,3072]{1,0:T(8,128)(2,1)}, bf16[96,3072]{1,0:T(8,128)(2,1)S(1)}, u32[]{:S(2)}, u32[]{:S(2)}) collective-permute-start(bf16[96,3072]{1,0:T(8,128)(2,1)} %bitcast.4.refs_5_.refs_3_), channel_id=1, source_target_pairs={{0,2},{1,3},{2,0},{3,1},{4,6},{5,7},{6,4},{7,5},{8,10},{9,11},{10,... | collective-permute-start | bytes 1769480 | tf_op jit(solution)/shard_map/ppermute | solution.py:171
  47.5 28.0 %collective-permute-start.19 = (bf16[96,3072]{1,0:T(8,128)(2,1)}, bf16[96,3072]{1,0:T(8,128)(2,1)}, u32[]{:S(2)}, u32[]{:S(2)}) collective-permute-start(bf16[96,3072]{1,0:T(8,128)(2,1)} %bitcast.4.refs_5_.refs_3_), channel_id=1, source_target_pairs={{0,4},{1,5},{2,6},{3,7},{4,0},{5,1},{6,2},{7,3},{8,12},{9,13},{10,... | collective-permute-start | bytes 1769480 | tf_op jit(solution)/shard_map/ppermute | solution.py:171
  66.8 13.4 %collective-permute-start.14 = (bf16[384,384]{1,0:T(8,128)(2,1)S(1)}, bf16[384,384]{1,0:T(8,128)(2,1)S(1)}, u32[]{:S(2)}, u32[]{:S(2)}) collective-permute-start(bf16[384,384]{1,0:T(8,128)(2,1)S(1)} %slice.32), channel_id=1, source_target_pairs={{0,2},{1,3},{2,0},{3,1},{4,6},{5,7},{6,4},{7,5},{8,10},{9,11},{10,... | collective-permute-start | bytes 884744 | tf_op jit(solution)/shard_map/ppermute | solution.py:171
  68.4 13.4 %collective-permute-start.15 = (bf16[384,384]{1,0:T(8,128)(2,1)S(1)}, bf16[384,384]{1,0:T(8,128)(2,1)}, u32[]{:S(2)}, u32[]{:S(2)}) collective-permute-start(bf16[384,384]{1,0:T(8,128)(2,1)S(1)} %slice.33), channel_id=1, source_target_pairs={{0,4},{1,5},{2,6},{3,7},{4,0},{5,1},{6,2},{7,3},{8,12},{9,13},{10,... | collective-permute-start | bytes 884744 | tf_op jit(solution)/shard_map/ppermute | solution.py:171
  76.5 9.2 %collective-permute-start.23 = (bf16[48,3072]{1,0:T(8,128)(2,1)S(1)}, bf16[48,3072]{1,0:T(8,128)(2,1)S(1)}, u32[]{:S(2)}, u32[]{:S(2)}) collective-permute-start(bf16[48,3072]{1,0:T(8,128)(2,1)S(1)} %slice.34), channel_id=1, source_target_pairs={{0,2},{1,3},{2,0},{3,1},{4,6},{5,7},{6,4},{7,5},{8,10},{9,11},{10,... | collective-permute-start | bytes 884744 | tf_op jit(solution)/shard_map/ppermute | solution.py:171
  77.1 9.8 %collective-permute-start.24 = (bf16[48,3072]{1,0:T(8,128)(2,1)S(1)}, bf16[48,3072]{1,0:T(8,128)(2,1)S(1)}, u32[]{:S(2)}, u32[]{:S(2)}) collective-permute-start(bf16[48,3072]{1,0:T(8,128)(2,1)S(1)} %slice.35), channel_id=1, source_target_pairs={{0,4},{1,5},{2,6},{3,7},{4,0},{5,1},{6,2},{7,3},{8,12},{9,13},{10,... | collective-permute-start | bytes 884744 | tf_op jit(solution)/shard_map/ppermute | solution.py:171
  77.8 14.6 %collective-permute-start.11 = (bf16[768,384]{1,0:T(8,128)(2,1)}, bf16[768,384]{1,0:T(8,128)(2,1)S(1)}, u32[]{:S(2)}, u32[]{:S(2)}) collective-permute-start(bf16[768,384]{1,0:T(8,128)(2,1)} %refs_5_.2), channel_id=1, source_target_pairs={{0,1},{1,0},{2,3},{3,2},{4,5},{5,4},{6,7},{7,6},{8,9},{9,8},{10,11... | collective-permute-start | bytes 1769480 | tf_op jit(solution)/shard_map/ppermute | solution.py:171
  80.2 12.6 %collective-permute-start.12 = (bf16[768,384]{1,0:T(8,128)(2,1)S(1)}, bf16[768,384]{1,0:T(8,128)(2,1)S(1)}, u32[]{:S(2)}, u32[]{:S(2)}) collective-permute-start(bf16[768,384]{1,0:T(8,128)(2,1)S(1)} %collective-permute-done.9.refs_3_.refs_7_), channel_id=1, source_target_pairs={{0,1},{1,0},{2,3},{3,2},{4,5},{5,4},{6,7},{7,6},{8,9},{9,8},{10,11... | collective-permute-start | bytes 1769480 | tf_op jit(solution)/shard_map/ppermute | solution.py:171
  81.8 11.0 %collective-permute-start.13 = (bf16[768,384]{1,0:T(8,128)(2,1)}, bf16[768,384]{1,0:T(8,128)(2,1)}, u32[]{:S(2)}, u32[]{:S(2)}) collective-permute-start(bf16[768,384]{1,0:T(8,128)(2,1)} %collective-permute-done.10.refs_5_.refs_9_), channel_id=1, source_target_pairs={{0,1},{1,0},{2,3},{3,2},{4,5},{5,4},{6,7},{7,6},{8,9},{9,8},{10,11... | collective-permute-start | bytes 1769480 | tf_op jit(solution)/shard_map/ppermute | solution.py:171
  85.7 6.1 %collective-permute-start.16 = (bf16[384,384]{1,0:T(8,128)(2,1)S(1)}, bf16[384,384]{1,0:T(8,128)(2,1)}, u32[]{:S(2)}, u32[]{:S(2)}) collective-permute-start(bf16[384,384]{1,0:T(8,128)(2,1)S(1)} %collective-permute-done.14.refs_7_.refs_11_), channel_id=1, source_target_pairs={{0,1},{1,0},{2,3},{3,2},{4,5},{5,4},{6,7},{7,6},{8,9},{9,8},{10,11... | collective-permute-start | bytes 884744 | tf_op jit(solution)/shard_map/ppermute | solution.py:171
  86.9 5.3 %collective-permute-start.17 = (bf16[384,384]{1,0:T(8,128)(2,1)}, bf16[384,384]{1,0:T(8,128)(2,1)}, u32[]{:S(2)}, u32[]{:S(2)}) collective-permute-start(bf16[384,384]{1,0:T(8,128)(2,1)} %collective-permute-done.15.refs_8_.refs_12_), channel_id=1, source_target_pairs={{0,1},{1,0},{2,3},{3,2},{4,5},{5,4},{6,7},{7,6},{8,9},{9,8},{10,11... | collective-permute-start | bytes 884744 | tf_op jit(solution)/shard_map/ppermute | solution.py:171
  87.7 20.8 %all-to-all-start = ((bf16[8,96,768]{2,1,0:T(8,128)(2,1)}), bf16[8,96,768]{2,1,0:T(8,128)(2,1)S(1)}, u32[]{:S(2)}, u32[]{:S(2)}) async-start(bf16[8,96,768]{2,1,0:T(8,128)(2,1)} %bitcast.5), calls=%async_computation | async-start | bytes 2359296 | tf_op jit(solution)/shard_map/all_to_all | solution.py:234
  91.8 11.5 %collective-permute-start.21 = (bf16[96,3072]{1,0:T(8,128)(2,1)}, bf16[96,3072]{1,0:T(8,128)(2,1)}, u32[]{:S(2)}, u32[]{:S(2)}) collective-permute-start(bf16[96,3072]{1,0:T(8,128)(2,1)} %copy-done.77), channel_id=1, source_target_pairs={{0,1},{1,0},{2,3},{3,2},{4,5},{5,4},{6,7},{7,6},{8,9},{9,8},{10,11... | collective-permute-start | bytes 1769480 | tf_op jit(solution)/shard_map/ppermute | solution.py:171
  92.3 11.0 %collective-permute-start.22 = (bf16[96,3072]{1,0:T(8,128)(2,1)}, bf16[96,3072]{1,0:T(8,128)(2,1)}, u32[]{:S(2)}, u32[]{:S(2)}) collective-permute-start(bf16[96,3072]{1,0:T(8,128)(2,1)} %collective-permute-done.19.refs_9_.refs_7_), channel_id=1, source_target_pairs={{0,1},{1,0},{2,3},{3,2},{4,5},{5,4},{6,7},{7,6},{8,9},{9,8},{10,11... | collective-permute-start | bytes 1769480 | tf_op jit(solution)/shard_map/ppermute | solution.py:171
  92.4 10.8 %collective-permute-start.20 = (bf16[96,3072]{1,0:T(8,128)(2,1)}, bf16[96,3072]{1,0:T(8,128)(2,1)}, u32[]{:S(2)}, u32[]{:S(2)}) collective-permute-start(bf16[96,3072]{1,0:T(8,128)(2,1)} %bitcast.4.refs_5_.refs_3_), channel_id=1, source_target_pairs={{0,1},{1,0},{2,3},{3,2},{4,5},{5,4},{6,7},{7,6},{8,9},{9,8},{10,11... | collective-permute-start | bytes 1769480 | tf_op jit(solution)/shard_map/ppermute | solution.py:171
  92.8 10.4 %collective-permute-start.25 = (bf16[48,3072]{1,0:T(8,128)(2,1)}, bf16[48,3072]{1,0:T(8,128)(2,1)S(1)}, u32[]{:S(2)}, u32[]{:S(2)}) collective-permute-start(bf16[48,3072]{1,0:T(8,128)(2,1)} %copy-done.83), channel_id=1, source_target_pairs={{0,1},{1,0},{2,3},{3,2},{4,5},{5,4},{6,7},{7,6},{8,9},{9,8},{10,11... | collective-permute-start | bytes 884744 | tf_op jit(solution)/shard_map/ppermute | solution.py:171
  92.9 10.3 %collective-permute-start.26 = (bf16[48,3072]{1,0:T(8,128)(2,1)}, bf16[48,3072]{1,0:T(8,128)(2,1)S(1)}, u32[]{:S(2)}, u32[]{:S(2)}) collective-permute-start(bf16[48,3072]{1,0:T(8,128)(2,1)} %copy-done.84), channel_id=1, source_target_pairs={{0,1},{1,0},{2,3},{3,2},{4,5},{5,4},{6,7},{7,6},{8,9},{9,8},{10,11... | collective-permute-start | bytes 884744 | tf_op jit(solution)/shard_map/ppermute | solution.py:171
  119.4 22.6 %all-to-all-start.1 = ((bf16[8,96,896]{2,1,0:T(8,128)(2,1)}), bf16[8,96,896]{2,1,0:T(8,128)(2,1)S(1)}, u32[]{:S(2)}, u32[]{:S(2)}) async-start(bf16[8,96,896]{2,1,0:T(8,128)(2,1)} %bitcast.39), calls=%async_computation.1 | async-start | bytes 2752512 | tf_op jit(solution)/shard_map/all_to_all | solution.py:234
  123.1 68.7 %all-gather.5.cloned.1.call-start = ((), (), s32[]{:S(2)}) async-start(), calls=%async_computation.7 | async-start | bytes 1966080 | tf_op jit(solution)/shard_map/all_gather | solution.py:950
  125.9 217.0 %reduce-scatter.3.cloned.1.call-start = ((), (), s32[]{:S(2)}) async-start(), calls=%async_computation.8 | async-start | bytes 9830400 | tf_op jit(solution)/shard_map/reduce_scatter | solution.py:987
  202.2 23.0 %all-to-all-start.2 = ((bf16[8,96,896]{2,1,0:T(8,128)(2,1)}), bf16[8,96,896]{2,1,0:T(8,128)(2,1)S(1)}, u32[]{:S(2)}, u32[]{:S(2)}) async-start(bf16[8,96,896]{2,1,0:T(8,128)(2,1)} %bitcast.41), calls=%async_computation.2 | async-start | bytes 2752512 | tf_op jit(solution)/shard_map/all_to_all | solution.py:234
  236.1 16.1 %collective-permute-start.27 = (bf16[4,96,3072]{2,1,0:T(8,128)(2,1)}, bf16[4,96,3072]{2,1,0:T(8,128)(2,1)S(1)}, u32[]{:S(2)}, u32[]{:S(2)}) collective-permute-start(bf16[4,96,3072]{2,1,0:T(8,128)(2,1)} %get-tuple-element.136), channel_id=1, source_target_pairs={{0,1},{1,0},{2,3},{3,2},{4,5},{5,4},{6,7},{7,6},{8,9},{9,8},{10,11... | collective-permute-start | bytes 7077896 | tf_op jit(solution)/shard_map/ppermute | solution.py:171
  236.1 21.6 %all-to-all-start.3 = ((bf16[8,96,768]{2,1,0:T(8,128)(2,1)}), bf16[8,96,768]{2,1,0:T(8,128)(2,1)S(1)}, u32[]{:S(2)}, u32[]{:S(2)}) async-start(bf16[8,96,768]{2,1,0:T(8,128)(2,1)} %bitcast.46), calls=%async_computation.3 | async-start | bytes 2359296 | tf_op jit(solution)/shard_map/all_to_all | solution.py:234
  239.6 162.4 %reduce-scatter.5.cloned.1.call-start = ((), (), s32[]{:S(2)}) async-start(), calls=%async_computation.9 | async-start | bytes 1966080 | tf_op jit(solution)/shard_map/reduce_scatter | solution.py:987
  251.6 38.7 %collective-permute-start.30 = (bf16[4,384,768]{2,1,0:T(8,128)(2,1)}, bf16[4,384,768]{2,1,0:T(8,128)(2,1)}, u32[]{:S(2)}, u32[]{:S(2)}) collective-permute-start(bf16[4,384,768]{2,1,0:T(8,128)(2,1)} %get-tuple-element.150), channel_id=1, source_target_pairs={{0,1},{1,0},{2,3},{3,2},{4,5},{5,4},{6,7},{7,6},{8,9},{9,8},{10,11... | collective-permute-start | bytes 7077896 | tf_op jit(solution)/shard_map/ppermute | solution.py:171
  274.2 16.2 %collective-permute-start.31 = (bf16[4,96,768]{2,1,0:T(8,128)(2,1)S(1)}, bf16[4,96,768]{2,1,0:T(8,128)(2,1)S(1)}, u32[]{:S(2)}, u32[]{:S(2)}) collective-permute-start(bf16[4,96,768]{2,1,0:T(8,128)(2,1)S(1)} %get-tuple-element.151), channel_id=1, source_target_pairs={{0,1},{1,0},{2,3},{3,2},{4,5},{5,4},{6,7},{7,6},{8,9},{9,8},{10,11... | collective-permute-start | bytes 1769480 | tf_op jit(solution)/shard_map/ppermute | solution.py:171
  274.3 19.3 %collective-permute-start.28 = (bf16[2,48,3072]{2,1,0:T(8,128)(2,1)S(1)}, bf16[2,48,3072]{2,1,0:T(8,128)(2,1)S(1)}, u32[]{:S(2)}, u32[]{:S(2)}) collective-permute-start(bf16[2,48,3072]{2,1,0:T(8,128)(2,1)S(1)} %copy-done.82), channel_id=1, source_target_pairs={{0,2},{1,3},{2,0},{3,1},{4,6},{5,7},{6,4},{7,5},{8,10},{9,11},{10,... | collective-permute-start | bytes 1769480 | tf_op jit(solution)/shard_map/ppermute | solution.py:171
  276.2 17.4 %collective-permute-start.29 = (bf16[2,48,3072]{2,1,0:T(8,128)(2,1)S(1)}, bf16[2,48,3072]{2,1,0:T(8,128)(2,1)S(1)}, u32[]{:S(2)}, u32[]{:S(2)}) collective-permute-start(bf16[2,48,3072]{2,1,0:T(8,128)(2,1)S(1)} %copy-done.81), channel_id=1, source_target_pairs={{0,4},{1,5},{2,6},{3,7},{4,0},{5,1},{6,2},{7,3},{8,12},{9,13},{10,... | collective-permute-start | bytes 1769480 | tf_op jit(solution)/shard_map/ppermute | solution.py:171
  292.8 18.1 %collective-permute-start.34 = (bf16[2,240,768]{2,1,0:T(8,128)(2,1)S(1)}, bf16[2,240,768]{2,1,0:T(8,128)(2,1)S(1)}, u32[]{:S(2)}, u32[]{:S(2)}) collective-permute-start(bf16[2,240,768]{2,1,0:T(8,128)(2,1)S(1)} %get-tuple-element.158), channel_id=1, source_target_pairs={{0,2},{1,3},{2,0},{3,1},{4,6},{5,7},{6,4},{7,5},{8,10},{9,11},{10,... | collective-permute-start | bytes 2211848 | tf_op jit(solution)/shard_map/ppermute | solution.py:171
  293.4 19.4 %collective-permute-start.35 = (bf16[2,240,768]{2,1,0:T(8,128)(2,1)S(1)}, bf16[2,240,768]{2,1,0:T(8,128)(2,1)S(1)}, u32[]{:S(2)}, u32[]{:S(2)}) collective-permute-start(bf16[2,240,768]{2,1,0:T(8,128)(2,1)S(1)} %get-tuple-element.160), channel_id=1, source_target_pairs={{0,4},{1,5},{2,6},{3,7},{4,0},{5,1},{6,2},{7,3},{8,12},{9,13},{10,... | collective-permute-start | bytes 2211848 | tf_op jit(solution)/shard_map/ppermute | solution.py:171
  302.7 11.3 %collective-permute-start.32 = (bf16[4,288,768]{2,1,0:T(8,128)(2,1)S(1)}, bf16[4,288,768]{2,1,0:T(8,128)(2,1)S(1)}, u32[]{:S(2)}, u32[]{:S(2)}) collective-permute-start(bf16[4,288,768]{2,1,0:T(8,128)(2,1)S(1)} %get-tuple-element.156), channel_id=1, source_target_pairs={{0,1},{1,0},{2,3},{3,2},{4,5},{5,4},{6,7},{7,6},{8,9},{9,8},{10,11... | collective-permute-start | bytes 5308424 | tf_op jit(solution)/shard_map/ppermute | solution.py:171
  302.8 11.2 %collective-permute-start.33 = (bf16[4,16,768]{2,1,0:T(8,128)(2,1)S(1)}, bf16[4,16,768]{2,1,0:T(8,128)(2,1)S(1)}, u32[]{:S(2)}, u32[]{:S(2)}) collective-permute-start(bf16[4,16,768]{2,1,0:T(8,128)(2,1)S(1)} %get-tuple-element.157), channel_id=1, source_target_pairs={{0,1},{1,0},{2,3},{3,2},{4,5},{5,4},{6,7},{7,6},{8,9},{9,8},{10,11... | collective-permute-start | bytes 294920 | tf_op jit(solution)/shard_map/ppermute | solution.py:171
  303.3 15.9 %collective-permute-start.38 = (bf16[48,3072]{1,0:T(8,128)(2,1)S(1)}, bf16[48,3072]{1,0:T(8,128)(2,1)S(1)}, u32[]{:S(2)}, u32[]{:S(2)}) collective-permute-start(bf16[48,3072]{1,0:T(8,128)(2,1)S(1)} %get-tuple-element.166), channel_id=1, source_target_pairs={{0,4},{1,5},{2,6},{3,7},{4,0},{5,1},{6,2},{7,3},{8,12},{9,13},{10,... | collective-permute-start | bytes 884744 | tf_op jit(solution)/shard_map/ppermute | solution.py:171
  314.8 22.5 %collective-permute-start.37 = (bf16[2,160,768]{2,1,0:T(8,128)(2,1)S(1)}, bf16[2,160,768]{2,1,0:T(8,128)(2,1)S(1)}, u32[]{:S(2)}, u32[]{:S(2)}) collective-permute-start(bf16[2,160,768]{2,1,0:T(8,128)(2,1)S(1)} %get-tuple-element.165), channel_id=1, source_target_pairs={{0,4},{1,5},{2,6},{3,7},{4,0},{5,1},{6,2},{7,3},{8,12},{9,13},{10,... | collective-permute-start | bytes 1474568 | tf_op jit(solution)/shard_map/ppermute | solution.py:171
  315.0 22.4 %collective-permute-start.36 = (bf16[2,144,768]{2,1,0:T(8,128)(2,1)S(1)}, bf16[2,144,768]{2,1,0:T(8,128)(2,1)S(1)}, u32[]{:S(2)}, u32[]{:S(2)}) collective-permute-start(bf16[2,144,768]{2,1,0:T(8,128)(2,1)S(1)} %get-tuple-element.163), channel_id=1, source_target_pairs={{0,2},{1,3},{2,0},{3,1},{4,6},{5,7},{6,4},{7,5},{8,10},{9,11},{10,... | collective-permute-start | bytes 1327112 | tf_op jit(solution)/shard_map/ppermute | solution.py:171
  316.8 17.6 %collective-permute-start.39 = (bf16[48,3072]{1,0:T(8,128)(2,1)S(1)}, bf16[48,3072]{1,0:T(8,128)(2,1)S(1)}, u32[]{:S(2)}, u32[]{:S(2)}) collective-permute-start(bf16[48,3072]{1,0:T(8,128)(2,1)S(1)} %get-tuple-element.168), channel_id=1, source_target_pairs={{0,2},{1,3},{2,0},{3,1},{4,6},{5,7},{6,4},{7,5},{8,10},{9,11},{10,... | collective-permute-start | bytes 884744 | tf_op jit(solution)/shard_map/ppermute | solution.py:171
  317.0 25.9 %collective-permute-start.42 = (bf16[240,768]{1,0:T(8,128)(2,1)}, bf16[240,768]{1,0:T(8,128)(2,1)}, u32[]{:S(2)}, u32[]{:S(2)}) collective-permute-start(bf16[240,768]{1,0:T(8,128)(2,1)} %get-tuple-element.173), channel_id=1, source_target_pairs={{0,4},{1,5},{2,6},{3,7},{4,0},{5,1},{6,2},{7,3},{8,12},{9,13},{10,... | collective-permute-start | bytes 1105928 | tf_op jit(solution)/shard_map/ppermute | solution.py:171
  319.2 23.8 %collective-permute-start.43 = (bf16[240,768]{1,0:T(8,128)(2,1)}, bf16[240,768]{1,0:T(8,128)(2,1)}, u32[]{:S(2)}, u32[]{:S(2)}) collective-permute-start(bf16[240,768]{1,0:T(8,128)(2,1)} %get-tuple-element.175), channel_id=1, source_target_pairs={{0,2},{1,3},{2,0},{3,1},{4,6},{5,7},{6,4},{7,5},{8,10},{9,11},{10,... | collective-permute-start | bytes 1105928 | tf_op jit(solution)/shard_map/ppermute | solution.py:171
  334.6 18.8 %collective-permute-start.46 = (bf16[96,3072]{1,0:T(8,128)(2,1)S(1)}, bf16[96,3072]{1,0:T(8,128)(2,1)S(1)}, u32[]{:S(2)}, u32[]{:S(2)}) collective-permute-start(bf16[96,3072]{1,0:T(8,128)(2,1)S(1)} %fold_last.3.refs_4_.refs_0_), channel_id=1, source_target_pairs={{0,8},{24,16},{1,9},{25,17},{2,10},{26,18},{3,11},{27,19},{4,12},{... | collective-permute-start | bytes 1769480 | tf_op jit(solution)/shard_map/ppermute | solution.py:315
  339.6 9.7 %collective-permute-start.41 = (bf16[160,768]{1,0:T(8,128)(2,1)S(1)}, bf16[160,768]{1,0:T(8,128)(2,1)S(1)}, u32[]{:S(2)}, u32[]{:S(2)}) collective-permute-start(bf16[160,768]{1,0:T(8,128)(2,1)S(1)} %get-tuple-element.172), channel_id=1, source_target_pairs={{0,2},{1,3},{2,0},{3,1},{4,6},{5,7},{6,4},{7,5},{8,10},{9,11},{10,... | collective-permute-start | bytes 737288 | tf_op jit(solution)/shard_map/ppermute | solution.py:171
  341.4 7.2 %collective-permute-start.40 = (bf16[144,768]{1,0:T(8,128)(2,1)}, bf16[144,768]{1,0:T(8,128)(2,1)S(1)}, u32[]{:S(2)}, u32[]{:S(2)}) collective-permute-start(bf16[144,768]{1,0:T(8,128)(2,1)} %get-tuple-element.170), channel_id=1, source_target_pairs={{0,4},{1,5},{2,6},{3,7},{4,0},{5,1},{6,2},{7,3},{8,12},{9,13},{10,... | collective-permute-start | bytes 663560 | tf_op jit(solution)/shard_map/ppermute | solution.py:171
  347.2 33.9 %collective-permute-start.45 = (bf16[480,768]{1,0:T(8,128)(2,1)S(1)}, bf16[480,768]{1,0:T(8,128)(2,1)S(1)}, u32[]{:S(2)}, u32[]{:S(2)}) collective-permute-start(bf16[480,768]{1,0:T(8,128)(2,1)S(1)} %fold_last.4.refs_4_.refs_0_), channel_id=1, source_target_pairs={{0,8},{24,16},{1,9},{25,17},{2,10},{26,18},{3,11},{27,19},{4,12},{... | collective-permute-start | bytes 2211848 | tf_op jit(solution)/shard_map/ppermute | solution.py:315
  350.3 45.5 %collective-permute-start.44 = (bf16[304,768]{1,0:T(8,128)(2,1)S(1)}, bf16[304,768]{1,0:T(8,128)(2,1)S(1)}, u32[]{:S(2)}, u32[]{:S(2)}) collective-permute-start(bf16[304,768]{1,0:T(8,128)(2,1)S(1)} %fold_last.5.refs_4_.refs_0_), channel_id=1, source_target_pairs={{0,8},{24,16},{1,9},{25,17},{2,10},{26,18},{3,11},{27,19},{4,12},{... | collective-permute-start | bytes 1400840 | tf_op jit(solution)/shard_map/ppermute | solution.py:315
  354.5 42.1 %collective-permute-start.49 = (bf16[96,3072]{1,0:T(8,128)(2,1)S(1)}, bf16[96,3072]{1,0:T(8,128)(2,1)S(1)}, u32[]{:S(2)}, u32[]{:S(2)}) collective-permute-start(bf16[96,3072]{1,0:T(8,128)(2,1)S(1)} %joined.6.refs_2_.refs_0_), channel_id=1, source_target_pairs={{8,16},{16,8},{9,17},{17,9},{10,18},{18,10},{11,19},{19,11},{12,20... | collective-permute-start | bytes 1769480 | tf_op jit(solution)/shard_map/ppermute | solution.py:315
  381.3 16.8 %collective-permute-start.48 = (bf16[480,768]{1,0:T(8,128)(2,1)S(1)}, bf16[480,768]{1,0:T(8,128)(2,1)S(1)}, u32[]{:S(2)}, u32[]{:S(2)}) collective-permute-start(bf16[480,768]{1,0:T(8,128)(2,1)S(1)} %joined.7.refs_2_.refs_0_), channel_id=1, source_target_pairs={{8,16},{16,8},{9,17},{17,9},{10,18},{18,10},{11,19},{19,11},{12,20... | collective-permute-start | bytes 2211848 | tf_op jit(solution)/shard_map/ppermute | solution.py:315
  395.9 4.0 collective-permute-start.47
  396.8 20.8 %collective-permute-start.52 = (bf16[96,3072]{1,0:T(8,128)(2,1)S(1)}, bf16[96,3072]{1,0:T(8,128)(2,1)}, u32[]{:S(2)}, u32[]{:S(2)}) collective-permute-start(bf16[96,3072]{1,0:T(8,128)(2,1)S(1)} %joined.9.refs_2_.refs_0_), channel_id=1, source_target_pairs={{8,0},{16,24},{9,1},{17,25},{10,2},{18,26},{11,3},{19,27},{12,4},{... | collective-permute-start | bytes 1769480 | tf_op jit(solution)/shard_map/ppermute | solution.py:315
  398.3 32.1 %collective-permute-start.51 = (bf16[480,768]{1,0:T(8,128)(2,1)S(1)}, bf16[480,768]{1,0:T(8,128)(2,1)}, u32[]{:S(2)}, u32[]{:S(2)}) collective-permute-start(bf16[480,768]{1,0:T(8,128)(2,1)S(1)} %joined.10.refs_2_.refs_0_), channel_id=1, source_target_pairs={{8,0},{16,24},{9,1},{17,25},{10,2},{18,26},{11,3},{19,27},{12,4},{... | collective-permute-start | bytes 2211848 | tf_op jit(solution)/shard_map/ppermute | solution.py:315
  400.8 34.7 %collective-permute-start.50 = (bf16[304,768]{1,0:T(8,128)(2,1)}, bf16[304,768]{1,0:T(8,128)(2,1)}, u32[]{:S(2)}, u32[]{:S(2)}) collective-permute-start(bf16[304,768]{1,0:T(8,128)(2,1)} %joined.11.refs_2_.refs_0_), channel_id=1, source_target_pairs={{8,0},{16,24},{9,1},{17,25},{10,2},{18,26},{11,3},{19,27},{12,4},{... | collective-permute-start | bytes 1400840 | tf_op jit(solution)/shard_map/ppermute | solution.py:315
  (84 other events, 357.2 us)
Sparse Core Ops, SparseCore 0:
  10.5 143.7 all-gather.2
  156.5 35.3 all-gather.4
  194.1 135.0 reduce-scatter.2
  343.0 54.3 reduce-scatter.4

commit v7 on v4

--- a/solution.py
+++ b/solution.py
@@ -18,7 +18,7 @@
     second_back=17, attend_back=2, fold_again=1, fold_wait=12, project_back=2, tokens_back=2, fold_last=1, joined=6,
     combine=1, finish=1, settle=1,
 )
-WIDE = ("attend", "widen", "dispatch", "expert", "expert_last", "expert_grads", "gate_back", "fold_wide", "widen_back", "settle")
+WIDE = ("attend", "widen", "dispatch", "expert", "expert_last", "expert_grads", "gate_back", "fold_wide", "widen_back", "second_back", "attend_back", "tokens_back", "settle")
 VMEM_LIMIT = 60 * 1024 * 1024
 
 

time: 449 us -> 450 us (level)
  local copies, waits for them, and re-layouts: 34.7 us -> 24.2 us
  Pallas kernels: 156 us -> 166 us
    pallas_call x34, Pallas kernels: 156 us -> 166 us  [call(): pl.pallas_call(body, out_shape=outs, in_specs=[pl.BlockSpec(memory_space=...]
    unnamed x155 -> x131, local copies, waits for them, and re-layouts: 26.7 us -> 18.3 us
  transfers between devices with their start and end apart: 61 -> 61, of which waited for: 25 -> 25; matrix products, arithmetic and copies ran while one was open for 2% -> 1% of each run, Pallas kernels for 35% -> 37%
where the time goes in v7:
time: 450 us; the launch traced here: 443 us
  waiting for transfers between devices  173 us (38%)
  Pallas kernels  166 us (37%)
  starting transfers between devices  63.1 us (14%)
  local copies, waits for them, and re-layouts  24.2 us (5%)
  between operations  14.8 us (3%)
    pallas_call x34, Pallas kernels, call(): pl.pallas_call(body, out_shape=outs, in_specs=[pl.BlockSpec(memory_space=...  166 us
    ppermute x9, waiting for transfers between devices, along(): return lax.ppermute(value, 'dp', pairs)  58.8 us
    ppermute x44, waiting for transfers between devices, hop(): return lax.ppermute(value, 'expert', [(i, i ^ bit) for i in range(self.n)])  57.4 us
    all_to_all x4, waiting for transfers between devices, exchange(): lax.all_to_all(blocks, 'expert', split_axis=0, concat_axis=0, tiled=True)  35.8 us
    ppermute x44, starting transfers between devices, hop(): return lax.ppermute(value, 'expert', [(i, i ^ bit) for i in range(self.n)])  32.2 us
    unnamed x131, local copies, waits for them, and re-layouts  18.3 us
    all_gather x2, waiting for transfers between devices, on_device(): whole = lax.all_gather(chunk(start, wide), 'dp', axis=0, tiled=True)  15.6 us
    ppermute x9, starting transfers between devices, along(): return lax.ppermute(value, 'dp', pairs)  15.2 us
  transfers between devices with their start and end apart: 61, of which 25 were waited for; matrix products, arithmetic and copies ran while one was open for 1% of the time, Pallas kernels for 37%

profile of v7, /device:TPU:0, one launch (start us, length us, event | category | flops | bytes accessed | tf_op | source)
XLA Modules:
  0.0 443.1 jit_solution(9150167473421780218)
XLA Ops:
  8.8 1.5 pad_maximum_fusion
  11.5 3.0 collective-permute-start.1
  14.5 1.5 collective-permute-start.3
  16.0 12.3 %collective-permute-done.1.refs_5_.refs_13_.refs_23_.refs_7_.refs_9_ = bf16[400,768]{1,0:T(8,128)(2,1)S(1)} collective-permute-done((bf16[400,768]{1,0:T(8,128)(2,1)S(1)}, bf16[400,768]{1,0:T(8,128)(2,1)S(1)}, u32[]{:S(2)}, u32[]{:S(2)}) %collective-permute-start.1) | collective-permute-done | bytes 614432 | tf_op jit(solution)/shard_map/ppermute | solution.py:171
  29.2 1.8 collective-permute-start.5
  31.7 1.5 collective-permute-start.7
  34.7 5.0 %collective-permute-done.7.refs_17_.refs_13_ = bf16[192,768]{1,0:T(8,128)(2,1)} collective-permute-done((bf16[192,768]{1,0:T(8,128)(2,1)}, bf16[192,768]{1,0:T(8,128)(2,1)}, u32[]{:S(2)}, u32[]{:S(2)}) %collective-permute-start.7) | collective-permute-done | bytes 294944 | tf_op jit(solution)/shard_map/ppermute | solution.py:171
  40.2 1.9 prepare.1
  43.4 1.5 collective-permute-start.9
  46.0 1.5 collective-permute-start.19
  48.2 15.9 %attend.1 = (bf16[384,768]{1,0:T(8,128)(2,1)}, bf16[384,2304]{1,0:T(8,128)(2,1)}, bf16[384,768]{1,0:T(8,128)(2,1)}, f32[384,128]{1,0:T(8,128)}, f32[384,768]{1,0...) custom-call(bf16[384,768]{1,0:T(8,128)(2,1)} %refs_1_.3, s32[384,1]{1,0:T(8,128)} %copy.28.refs_1_.refs_3_, ...), custom_call_target="tpu_custom_call" | custom-call | flops 18400000000 | bytes 1000 | tf_op jit(solution)/shard_map/attend/pallas_call | solution.py:111
  64.3 1.6 collective-permute-start.14
  66.4 6.1 %collective-permute-done.18.refs_7_.refs_5_ = bf16[96,3072]{1,0:T(8,128)(2,1)S(1)} collective-permute-done((bf16[96,3072]{1,0:T(8,128)(2,1)}, bf16[96,3072]{1,0:T(8,128)(2,1)S(1)}, u32[]{:S(2)}, u32[]{:S(2)}) %collective-permute-start.18) | collective-permute-done | bytes 589856 | tf_op jit(solution)/shard_map/ppermute | solution.py:171
  72.5 1.5 collective-permute-done.19.refs_9_.refs_7_
  75.3 3.5 collective-permute-done.14.refs_7_.refs_11_
  78.8 1.6 collective-permute-done.15.refs_8_.refs_12_
  80.4 3.7 collective-permute-done.23.refs_11_.refs_9_
  86.1 4.0 all-to-all-start
  91.7 9.5 %widen.1 = (bf16[384,3072]{1,0:T(8,128)(2,1)}, bf16[384,3072]{1,0:T(8,128)(2,1)}) custom-call(bf16[384,768]{1,0:T(8,128)(2,1)} %get-tuple-element.101.refs_0_.refs_2_, bf16[768,384]{1,0:T(8,128)(2,1)} %refs_5_.2, bf16[768,384]{1,0:T(8,128)(2,1)} %collective-permute-done.11.refs_2_.refs_6_, bf16[768,384]{1,0:T(8,128)(2,1)} %copy-done.51, ...), custom_call_target="tpu_custom_call" | custom-call | flops 10350000128 | bytes 1000 | tf_op jit(solution)/shard_map/widen/pallas_call | solution.py:111
  101.3 5.6 %all-to-all-done = bf16[8,96,768]{2,1,0:T(8,128)(2,1)S(1)} async-done(((bf16[8,96,768]{2,1,0:T(8,128)(2,1)}), bf16[8,96,768]{2,1,0:T(8,128)(2,1)S(1)}, u32[]{:S(2)}, u32[]{:S(2)}) %all-to-all-start) | async-done | bytes 1179680 | tf_op jit(solution)/shard_map/all_to_all | solution.py:234
  107.9 9.8 %dispatch.1 = (f32[384,768]{1,0:T(8,128)}, f32[384,1]{1,0:T(8,128)}, bf16[768,896]{1,0:T(8,128)(2,1)}) custom-call(bf16[384,3072]{1,0:T(8,128)(2,1)} %get-tuple-element.107.refs_0_.refs_16_.refs_6_, f32[384,768]{1,0:T(8,128)} %get-tuple-element.108.refs_1_, f32[16,768]{1,0:T(8,128)} %get-tuple-element.103.refs_11_.refs_2_.refs_4_.refs_3_, ...), custom_call_target="tpu_custom_call" | custom-call | flops 11500000256 | bytes 1000 | tf_op jit(solution)/shard_map/dispatch/pallas_call | solution.py:111
  117.8 3.7 all-to-all-start.1
  124.4 15.9 %all-to-all-done.1 = bf16[8,96,896]{2,1,0:T(8,128)(2,1)S(1)} async-done(((bf16[8,96,896]{2,1,0:T(8,128)(2,1)}), bf16[8,96,896]{2,1,0:T(8,128)(2,1)S(1)}, u32[]{:S(2)}, u32[]{:S(2)}) %all-to-all-start.1) | async-done | bytes 1376288 | tf_op jit(solution)/shard_map/all_to_all | solution.py:234
  145.4 8.9 %all-gather.3.cloned.1.call-done = bf16[6144,640]{1,0:T(8,128)(2,1)} async-done(((bf16[1536,640]{1,0:T(8,128)(2,1)}), bf16[6144,640]{1,0:T(8,128)(2,1)}) %all-gather.3.cloned.1.call-update) | async-done | bytes 7864336 | tf_op jit(solution)/shard_map/all_gather | solution.py:950
  154.3 30.8 %expert.1 = (bf16[4,2,768,640]{3,2,1,0:T(8,128)(2,1)}, f32[768,768]{1,0:T(8,128)}, f32[768,768]{1,0:T(8,128)}) custom-call(bf16[768,768]{1,0:T(8,128)(2,1)} %copy-done.38, bf16[768,768]{1,0:T(8,128)(2,1)} %copy-done.39, bf16[768,768]{1,0:T(8,128)(2,1)} %copy-done.36, bf16[768,768]{1,0:T(8,128)(2,1)} %copy-done.37, bf16[4,2,768,640]{3,2,1,0:T(8,128)(2,1)} %bitcast.50, ...), custom_call_target="tpu_custom_call" | custom-call | flops 23000000512 | bytes 1000 | tf_op jit(solution)/shard_map/expert/pallas_call | solution.py:111
  185.1 6.7 %all-gather.5.cloned.1.call-done = bf16[6144,128]{1,0:T(8,128)(2,1)} async-done(((bf16[1536,128]{1,0:T(8,128)(2,1)}), bf16[6144,128]{1,0:T(8,128)(2,1)}) %all-gather.5.cloned.1.call-update) | async-done | bytes 1572880 | tf_op jit(solution)/shard_map/all_gather | solution.py:950
  191.8 10.4 %expert_last.1 = (bf16[768,896]{1,0:T(8,128)(2,1)}, bf16[768,768]{1,0:T(8,128)(2,1)}, bf16[1,768,512]{2,1,0:T(8,128)(2,1)}, bf16[1,768,512]{2,1,0:T(8,128)(2,1)}) custom-call(bf16[768,768]{1,0:T(8,128)(2,1)} %copy-done.38, bf16[768,768]{1,0:T(8,128)(2,1)} %copy-done.39, bf16[768,768]{1,0:T(8,128)(2,1)} %copy-done.36, bf16[768,768]{1,0:T(8,128)(2,1)} %copy-done.37, ...), custom_call_target="tpu_custom_call" | custom-call | flops 11500000256 | bytes 1000 | tf_op jit(solution)/shard_map/expert_last/pallas_call | solution.py:111
  202.2 3.7 all-to-all-start.2
  205.9 4.6 %expert_grads.1.refs_8_ = bf16[4,2,768,128]{3,2,1,0:T(8,128)(2,1)} custom-call(bf16[768,768]{1,0:T(8,128)(2,1)} %copy-done.36, bf16[768,768]{1,0:T(8,128)(2,1)} %copy-done.37, bf16[1,768,512]{2,1,0:T(8,128)(2,1)} %get-tuple-element.127.refs_2_.refs_4_, bf16[1,768,512]{2,1,0:T(8,128)(2,1)} %get-tuple-element.128.refs_3_, ...), custom_call_target="tpu_custom_call" | custom-call | flops 6899999744 | bytes 1000 | tf_op jit(solution)/shard_map/expert_grads/pallas_call | solution.py:111
  210.5 14.3 %all-to-all-done.2 = bf16[8,96,896]{2,1,0:T(8,128)(2,1)S(1)} async-done(((bf16[8,96,896]{2,1,0:T(8,128)(2,1)}), bf16[8,96,896]{2,1,0:T(8,128)(2,1)S(1)}, u32[]{:S(2)}, u32[]{:S(2)}) %all-to-all-start.2) | async-done | bytes 1376288 | tf_op jit(solution)/shard_map/all_to_all | solution.py:234
  225.9 9.8 %gate_back.1 = (f32[384,768]{1,0:T(8,128)}, bf16[384,768]{1,0:T(8,128)(2,1)}, f32[2,768]{1,0:T(2,128)}, f32[8,768]{1,0:T(8,128)}, bf16[4,96,3072]{2,1,0:T(8,128)(2,1)}, /*index=5*/bf16[4,96,3072]{2,1,0:T(8,128)(2,1)}) custom-call(s32[384,1]{1,0:T(8,128)} %copy-done.29, s32[384,1]{1,0:T(8,128)} %copy-done.11, f32[384,768]{1,0:T(8,128)} %get-tuple-element.115.refs_2_.refs_1_, ...), custom_call_target="tpu_custom_call" | custom-call | flops 11500000256 | bytes 1000 | tf_op jit(solution)/shard_map/gate_back/pallas_call | solution.py:111
  235.7 3.6 all-to-all-start.3
  239.8 12.0 %widen_back.1 = (bf16[384,3072]{1,0:T(8,128)(2,1)}, bf16[4,384,768]{2,1,0:T(8,128)(2,1)}, bf16[4,384,768]{2,1,0:T(8,128)(2,1)}) custom-call(bf16[384,768]{1,0:T(8,128)(2,1)} %get-tuple-element.129.refs_0_, bf16[384,3072]{1,0:T(8,128)(2,1)} %get-tuple-element.130.refs_1_, bf16[384,768]{1,0:T(8,128)(2,1)} %get-tuple-element.101.refs_0_.refs_2_, ...), custom_call_target="tpu_custom_call" | custom-call | flops 13799999488 | bytes 1000 | tf_op jit(solution)/shard_map/widen_back/pallas_call | solution.py:111
  252.3 4.1 fold_wide.1
  257.4 10.2 %second_back.1 = (f32[384,768]{1,0:T(8,128)}, bf16[384,768]{1,0:T(8,128)(2,1)}, f32[2,768]{1,0:T(2,128)}, bf16[4,96,768]{2,1,0:T(8,128)(2,1)}, bf16[4,96,768]{2,1,0:T(8,128)(2,1)}) custom-call(bf16[384,3072]{1,0:T(8,128)(2,1)} %get-tuple-element.132.refs_2_.refs_0_, f32[384,768]{1,0:T(8,128)} %get-tuple-element.108.refs_1_, ...), custom_call_target="tpu_custom_call" | custom-call | flops 19549999104 | bytes 1000 | tf_op jit(solution)/shard_map/second_back/pallas_call | solution.py:111
  267.7 1.8 collective-permute-start.28
  269.6 1.5 collective-permute-start.29
  271.1 15.3 %attend_back.1.refs_4_.refs_0_ = bf16[384,2304]{1,0:T(8,128)(2,1)} custom-call(bf16[384,768]{1,0:T(8,128)(2,1)} %get-tuple-element.138.refs_0_, bf16[384,2304]{1,0:T(8,128)(2,1)} %get-tuple-element.139.refs_1_, f32[384,128]{1,0:T(8,128)} %get-tuple-element.140.refs_2_, s32[384,1]{1,0:T(8,128)} %copy.28.refs_1_.refs_3_, s32[1,384]{1,0:T(1,128)} %refs_4_.2, ...), custom_call_target="tpu_custom_call" | custom-call | flops 2300000000 | bytes 1000 | tf_op jit(solution)/shard_map/attend_back/pallas_call | solution.py:111
  286.5 1.5 copy-done
  287.9 3.1 fold.2
  295.4 7.6 %tokens_back.1 = (f32[384,768]{1,0:T(8,128)}, bf16[4,16,768]{2,1,0:T(8,128)(2,1)}, bf16[4,16,768]{2,1,0:T(8,128)(2,1)}) custom-call(bf16[384,2304]{1,0:T(8,128)(2,1)} %attend_back.1.refs_4_.refs_0_, bf16[384,768]{1,0:T(8,128)(2,1)} %refs_1_.3, f32[384,768]{1,0:T(8,128)} %get-tuple-element.143.refs_2_, ...), custom_call_target="tpu_custom_call" | custom-call | flops 2300000000 | bytes 1000 | tf_op jit(solution)/shard_map/tokens_back/pallas_call | solution.py:111
  303.9 2.3 project_back.1
  306.7 2.5 collective-permute-done.34.refs_1_
  310.8 1.5 collective-permute-start.37
  312.3 1.6 collective-permute-start.36
  316.4 15.0 %collective-permute-done.38.refs_1_ = bf16[48,3072]{1,0:T(8,128)(2,1)S(1)} collective-permute-done((bf16[48,3072]{1,0:T(8,128)(2,1)S(1)}, bf16[48,3072]{1,0:T(8,128)(2,1)S(1)}, u32[]{:S(2)}, u32[]{:S(2)}) %collective-permute-start.38) | collective-permute-done | bytes 294944 | tf_op jit(solution)/shard_map/ppermute | solution.py:171
  331.3 1.5 collective-permute-start.43
  333.0 2.7 collective-permute-start.46
  336.6 1.5 collective-permute-start.40
  339.2 3.2 collective-permute-done.43.refs_3_
  342.6 2.9 collective-permute-start.45
  346.5 3.3 collective-permute-start.44
  349.8 1.5 combine.1.refs_2_
  353.3 17.5 %collective-permute-done.45.refs_1_ = bf16[480,768]{1,0:T(8,128)(2,1)S(1)} collective-permute-done((bf16[480,768]{1,0:T(8,128)(2,1)S(1)}, bf16[480,768]{1,0:T(8,128)(2,1)S(1)}, u32[]{:S(2)}, u32[]{:S(2)}) %collective-permute-start.45) | collective-permute-done | bytes 737312 | tf_op jit(solution)/shard_map/ppermute | solution.py:315
  371.7 16.4 %collective-permute-done.44.refs_1_ = bf16[304,768]{1,0:T(8,128)(2,1)} collective-permute-done((bf16[304,768]{1,0:T(8,128)(2,1)}, bf16[304,768]{1,0:T(8,128)(2,1)}, u32[]{:S(2)}, u32[]{:S(2)}) %collective-permute-start.44) | collective-permute-done | bytes 466976 | tf_op jit(solution)/shard_map/ppermute | solution.py:315
  391.8 1.6 collective-permute-start.51
  395.5 5.4 %reduce-scatter.5.cloned.1.call-done = bf16[1536,128]{1,0:T(8,128)(2,1)} async-done(((bf16[6144,128]{1,0:T(8,128)(2,1)}), bf16[1536,128]{1,0:T(8,128)(2,1)}) %reduce-scatter.5.cloned.1.call-update) | async-done | bytes 393232 | tf_op jit(solution)/shard_map/reduce_scatter | solution.py:987
  401.9 2.5 finish.1
  404.3 5.8 %collective-permute-done.52.refs_1_ = bf16[96,3072]{1,0:T(8,128)(2,1)} collective-permute-done((bf16[96,3072]{1,0:T(8,128)(2,1)S(1)}, bf16[96,3072]{1,0:T(8,128)(2,1)}, u32[]{:S(2)}, u32[]{:S(2)}) %collective-permute-start.52) | collective-permute-done | bytes 589856 | tf_op jit(solution)/shard_map/ppermute | solution.py:315
  410.2 2.3 settle.3.refs_2_
  412.5 16.2 %collective-permute-done.51.refs_1_ = bf16[480,768]{1,0:T(8,128)(2,1)} collective-permute-done((bf16[480,768]{1,0:T(8,128)(2,1)S(1)}, bf16[480,768]{1,0:T(8,128)(2,1)}, u32[]{:S(2)}, u32[]{:S(2)}) %collective-permute-start.51) | collective-permute-done | bytes 737312 | tf_op jit(solution)/shard_map/ppermute | solution.py:315
  428.7 2.7 settle.4
  431.4 2.9 collective-permute-done.50.refs_1_
  434.3 2.1 settle.5
  (242 shorter events, 49.8 us)
Async XLA Ops:
  7.2 147.1 %all-gather.3.cloned.1.call-start = ((), (), s32[]{:S(2)}) async-start(), calls=%async_computation.6 | async-start | bytes 9830400 | tf_op jit(solution)/shard_map/all_gather | solution.py:950
  10.4 23.3 %copy-start.12 = (s32[384,1]{0,1:T(1,128)S(1)}, s32[384,1]{0,1:T(1,128)}, u32[]{:S(2)}) copy-start(s32[384,1]{0,1:T(1,128)} %param.15) | copy-start | bytes 4612
  11.1 29.2 %copy-start.19 = (bf16[384,768]{1,0:T(8,128)(2,1)S(1)}, bf16[384,768]{1,0:T(8,128)(2,1)}, u32[]{:S(2)}) copy-start(bf16[384,768]{1,0:T(8,128)(2,1)} %refs_5_.1) | copy-start | bytes 1769476
  11.5 30.7 %copy-start.41 = (bf16[400,768]{1,0:T(8,128)(2,1)}, bf16[400,768]{1,0:T(8,128)(2,1)S(1)}, u32[]{:S(2)}) copy-start(bf16[400,768]{1,0:T(8,128)(2,1)S(1)} %pad_maximum_fusion.1.refs_3_.refs_11_.refs_21_.refs_5_.refs_7_) | copy-start | bytes 1843204
  11.5 16.9 %collective-permute-start.1 = (bf16[400,768]{1,0:T(8,128)(2,1)S(1)}, bf16[400,768]{1,0:T(8,128)(2,1)S(1)}, u32[]{:S(2)}, u32[]{:S(2)}) collective-permute-start(bf16[400,768]{1,0:T(8,128)(2,1)S(1)} %pad_maximum_fusion.1.refs_3_.refs_11_.refs_21_.refs_5_.refs_7_), channel_id=1, source_target_pairs={{0,2},{1,3},{2,0},{3,1},{4,6},{5,7},{6,4},{7,5},{8,10},{9,11},{10,... | collective-permute-start | bytes 1843208 | tf_op jit(solution)/shard_map/ppermute | solution.py:171
  14.5 16.4 %collective-permute-start.3 = (bf16[400,768]{1,0:T(8,128)(2,1)S(1)}, bf16[400,768]{1,0:T(8,128)(2,1)S(1)}, u32[]{:S(2)}, u32[]{:S(2)}) collective-permute-start(bf16[400,768]{1,0:T(8,128)(2,1)S(1)} %pad_maximum_fusion.1.refs_3_.refs_11_.refs_21_.refs_5_.refs_7_), channel_id=1, source_target_pairs={{0,4},{1,5},{2,6},{3,7},{4,0},{5,1},{6,2},{7,3},{8,12},{9,13},{10,... | collective-permute-start | bytes 1843208 | tf_op jit(solution)/shard_map/ppermute | solution.py:171
  29.2 10.6 %collective-permute-start.5 = (bf16[208,768]{1,0:T(8,128)(2,1)}, bf16[208,768]{1,0:T(8,128)(2,1)}, u32[]{:S(2)}, u32[]{:S(2)}) collective-permute-start(bf16[208,768]{1,0:T(8,128)(2,1)} %slice.40), channel_id=1, source_target_pairs={{0,4},{1,5},{2,6},{3,7},{4,0},{5,1},{6,2},{7,3},{8,12},{9,13},{10,... | collective-permute-start | bytes 958472 | tf_op jit(solution)/shard_map/ppermute | solution.py:171
  31.7 8.0 %collective-permute-start.7 = (bf16[192,768]{1,0:T(8,128)(2,1)}, bf16[192,768]{1,0:T(8,128)(2,1)}, u32[]{:S(2)}, u32[]{:S(2)}) collective-permute-start(bf16[192,768]{1,0:T(8,128)(2,1)} %slice.41), channel_id=1, source_target_pairs={{0,2},{1,3},{2,0},{3,1},{4,6},{5,7},{6,4},{7,5},{8,10},{9,11},{10,... | collective-permute-start | bytes 884744 | tf_op jit(solution)/shard_map/ppermute | solution.py:171
  33.2 10.2 %collective-permute-start = (bf16[400,768]{1,0:T(8,128)(2,1)S(1)}, bf16[400,768]{1,0:T(8,128)(2,1)S(1)}, u32[]{:S(2)}, u32[]{:S(2)}) collective-permute-start(bf16[400,768]{1,0:T(8,128)(2,1)S(1)} %pad_maximum_fusion.1.refs_3_.refs_11_.refs_21_.refs_5_.refs_7_), channel_id=1, source_target_pairs={{0,1},{1,0},{2,3},{3,2},{4,5},{5,4},{6,7},{7,6},{8,9},{9,8},{10,11... | collective-permute-start | bytes 1843208 | tf_op jit(solution)/shard_map/ppermute | solution.py:171
  33.2 12.2 %collective-permute-start.2 = (bf16[400,768]{1,0:T(8,128)(2,1)S(1)}, bf16[400,768]{1,0:T(8,128)(2,1)}, u32[]{:S(2)}, u32[]{:S(2)}) collective-permute-start(bf16[400,768]{1,0:T(8,128)(2,1)S(1)} %collective-permute-done.1.refs_5_.refs_13_.refs_23_.refs_7_.refs_9_), channel_id=1, source_target_pairs={{0,1},{1,0},{2,3},{3,2},{4,5},{5,4},{6,7},{7,6},{8,9},{9,8},{10,11... | collective-permute-start | bytes 1843208 | tf_op jit(solution)/shard_map/ppermute | solution.py:171
  33.7 12.3 %collective-permute-start.4 = (bf16[400,768]{1,0:T(8,128)(2,1)S(1)}, bf16[400,768]{1,0:T(8,128)(2,1)}, u32[]{:S(2)}, u32[]{:S(2)}) collective-permute-start(bf16[400,768]{1,0:T(8,128)(2,1)S(1)} %collective-permute-done.3.refs_7_.refs_15_.refs_25_.refs_9_.refs_11_), channel_id=1, source_target_pairs={{0,1},{1,0},{2,3},{3,2},{4,5},{5,4},{6,7},{7,6},{8,9},{9,8},{10,11... | collective-permute-start | bytes 1843208 | tf_op jit(solution)/shard_map/ppermute | solution.py:171
  39.7 5.2 %collective-permute-start.8 = (bf16[192,768]{1,0:T(8,128)(2,1)}, bf16[192,768]{1,0:T(8,128)(2,1)S(1)}, u32[]{:S(2)}, u32[]{:S(2)}) collective-permute-start(bf16[192,768]{1,0:T(8,128)(2,1)} %collective-permute-done.7.refs_17_.refs_13_), channel_id=1, source_target_pairs={{0,1},{1,0},{2,3},{3,2},{4,5},{5,4},{6,7},{7,6},{8,9},{9,8},{10,11... | collective-permute-start | bytes 884744 | tf_op jit(solution)/shard_map/ppermute | solution.py:171
  39.7 7.8 %collective-permute-start.6 = (bf16[208,768]{1,0:T(8,128)(2,1)}, bf16[208,768]{1,0:T(8,128)(2,1)S(1)}, u32[]{:S(2)}, u32[]{:S(2)}) collective-permute-start(bf16[208,768]{1,0:T(8,128)(2,1)} %collective-permute-done.5.refs_9_.refs_18_.refs_27_.refs_11_.refs_14_), channel_id=1, source_target_pairs={{0,1},{1,0},{2,3},{3,2},{4,5},{5,4},{6,7},{7,6},{8,9},{9,8},{10,11... | collective-permute-start | bytes 958472 | tf_op jit(solution)/shard_map/ppermute | solution.py:171
  43.4 20.8 %collective-permute-start.9 = (bf16[768,384]{1,0:T(8,128)(2,1)}, bf16[768,384]{1,0:T(8,128)(2,1)S(1)}, u32[]{:S(2)}, u32[]{:S(2)}) collective-permute-start(bf16[768,384]{1,0:T(8,128)(2,1)} %refs_5_.2), channel_id=1, source_target_pairs={{0,2},{1,3},{2,0},{3,1},{4,6},{5,7},{6,4},{7,5},{8,10},{9,11},{10,... | collective-permute-start | bytes 1769480 | tf_op jit(solution)/shard_map/ppermute | solution.py:171
  44.9 19.3 %collective-permute-start.10 = (bf16[768,384]{1,0:T(8,128)(2,1)}, bf16[768,384]{1,0:T(8,128)(2,1)S(1)}, u32[]{:S(2)}, u32[]{:S(2)}) collective-permute-start(bf16[768,384]{1,0:T(8,128)(2,1)} %refs_5_.2), channel_id=1, source_target_pairs={{0,4},{1,5},{2,6},{3,7},{4,0},{5,1},{6,2},{7,3},{8,12},{9,13},{10,... | collective-permute-start | bytes 1769480 | tf_op jit(solution)/shard_map/ppermute | solution.py:171
  45.4 27.0 %collective-permute-start.18 = (bf16[96,3072]{1,0:T(8,128)(2,1)}, bf16[96,3072]{1,0:T(8,128)(2,1)S(1)}, u32[]{:S(2)}, u32[]{:S(2)}) collective-permute-start(bf16[96,3072]{1,0:T(8,128)(2,1)} %bitcast.4.refs_5_.refs_3_), channel_id=1, source_target_pairs={{0,2},{1,3},{2,0},{3,1},{4,6},{5,7},{6,4},{7,5},{8,10},{9,11},{10,... | collective-permute-start | bytes 1769480 | tf_op jit(solution)/shard_map/ppermute | solution.py:171
  46.0 28.0 %collective-permute-start.19 = (bf16[96,3072]{1,0:T(8,128)(2,1)}, bf16[96,3072]{1,0:T(8,128)(2,1)S(1)}, u32[]{:S(2)}, u32[]{:S(2)}) collective-permute-start(bf16[96,3072]{1,0:T(8,128)(2,1)} %bitcast.4.refs_5_.refs_3_), channel_id=1, source_target_pairs={{0,4},{1,5},{2,6},{3,7},{4,0},{5,1},{6,2},{7,3},{8,12},{9,13},{10,... | collective-permute-start | bytes 1769480 | tf_op jit(solution)/shard_map/ppermute | solution.py:171
  64.3 14.5 %collective-permute-start.14 = (bf16[384,384]{1,0:T(8,128)(2,1)S(1)}, bf16[384,384]{1,0:T(8,128)(2,1)S(1)}, u32[]{:S(2)}, u32[]{:S(2)}) collective-permute-start(bf16[384,384]{1,0:T(8,128)(2,1)S(1)} %slice.32), channel_id=1, source_target_pairs={{0,2},{1,3},{2,0},{3,1},{4,6},{5,7},{6,4},{7,5},{8,10},{9,11},{10,... | collective-permute-start | bytes 884744 | tf_op jit(solution)/shard_map/ppermute | solution.py:171
  65.8 14.6 %collective-permute-start.15 = (bf16[384,384]{1,0:T(8,128)(2,1)S(1)}, bf16[384,384]{1,0:T(8,128)(2,1)}, u32[]{:S(2)}, u32[]{:S(2)}) collective-permute-start(bf16[384,384]{1,0:T(8,128)(2,1)S(1)} %slice.33), channel_id=1, source_target_pairs={{0,4},{1,5},{2,6},{3,7},{4,0},{5,1},{6,2},{7,3},{8,12},{9,13},{10,... | collective-permute-start | bytes 884744 | tf_op jit(solution)/shard_map/ppermute | solution.py:171
  74.0 10.1 %collective-permute-start.23 = (bf16[48,3072]{1,0:T(8,128)(2,1)S(1)}, bf16[48,3072]{1,0:T(8,128)(2,1)S(1)}, u32[]{:S(2)}, u32[]{:S(2)}) collective-permute-start(bf16[48,3072]{1,0:T(8,128)(2,1)S(1)} %slice.34), channel_id=1, source_target_pairs={{0,2},{1,3},{2,0},{3,1},{4,6},{5,7},{6,4},{7,5},{8,10},{9,11},{10,... | collective-permute-start | bytes 884744 | tf_op jit(solution)/shard_map/ppermute | solution.py:171
  74.7 10.7 %collective-permute-start.24 = (bf16[48,3072]{1,0:T(8,128)(2,1)S(1)}, bf16[48,3072]{1,0:T(8,128)(2,1)S(1)}, u32[]{:S(2)}, u32[]{:S(2)}) collective-permute-start(bf16[48,3072]{1,0:T(8,128)(2,1)S(1)} %slice.35), channel_id=1, source_target_pairs={{0,4},{1,5},{2,6},{3,7},{4,0},{5,1},{6,2},{7,3},{8,12},{9,13},{10,... | collective-permute-start | bytes 884744 | tf_op jit(solution)/shard_map/ppermute | solution.py:171
  75.3 15.5 %collective-permute-start.11 = (bf16[768,384]{1,0:T(8,128)(2,1)}, bf16[768,384]{1,0:T(8,128)(2,1)}, u32[]{:S(2)}, u32[]{:S(2)}) collective-permute-start(bf16[768,384]{1,0:T(8,128)(2,1)} %refs_5_.2), channel_id=1, source_target_pairs={{0,1},{1,0},{2,3},{3,2},{4,5},{5,4},{6,7},{7,6},{8,9},{9,8},{10,11... | collective-permute-start | bytes 1769480 | tf_op jit(solution)/shard_map/ppermute | solution.py:171
  78.8 12.4 %collective-permute-start.12 = (bf16[768,384]{1,0:T(8,128)(2,1)S(1)}, bf16[768,384]{1,0:T(8,128)(2,1)}, u32[]{:S(2)}, u32[]{:S(2)}) collective-permute-start(bf16[768,384]{1,0:T(8,128)(2,1)S(1)} %collective-permute-done.9.refs_3_.refs_7_), channel_id=1, source_target_pairs={{0,1},{1,0},{2,3},{3,2},{4,5},{5,4},{6,7},{7,6},{8,9},{9,8},{10,11... | collective-permute-start | bytes 1769480 | tf_op jit(solution)/shard_map/ppermute | solution.py:171
  80.4 10.8 %collective-permute-start.13 = (bf16[768,384]{1,0:T(8,128)(2,1)S(1)}, bf16[768,384]{1,0:T(8,128)(2,1)}, u32[]{:S(2)}, u32[]{:S(2)}) collective-permute-start(bf16[768,384]{1,0:T(8,128)(2,1)S(1)} %collective-permute-done.10.refs_5_.refs_9_), channel_id=1, source_target_pairs={{0,1},{1,0},{2,3},{3,2},{4,5},{5,4},{6,7},{7,6},{8,9},{9,8},{10,11... | collective-permute-start | bytes 1769480 | tf_op jit(solution)/shard_map/ppermute | solution.py:171
  84.2 6.0 %collective-permute-start.16 = (bf16[384,384]{1,0:T(8,128)(2,1)S(1)}, bf16[384,384]{1,0:T(8,128)(2,1)}, u32[]{:S(2)}, u32[]{:S(2)}) collective-permute-start(bf16[384,384]{1,0:T(8,128)(2,1)S(1)} %collective-permute-done.14.refs_7_.refs_11_), channel_id=1, source_target_pairs={{0,1},{1,0},{2,3},{3,2},{4,5},{5,4},{6,7},{7,6},{8,9},{9,8},{10,11... | collective-permute-start | bytes 884744 | tf_op jit(solution)/shard_map/ppermute | solution.py:171
  85.4 5.3 %collective-permute-start.17 = (bf16[384,384]{1,0:T(8,128)(2,1)}, bf16[384,384]{1,0:T(8,128)(2,1)}, u32[]{:S(2)}, u32[]{:S(2)}) collective-permute-start(bf16[384,384]{1,0:T(8,128)(2,1)} %collective-permute-done.15.refs_8_.refs_12_), channel_id=1, source_target_pairs={{0,1},{1,0},{2,3},{3,2},{4,5},{5,4},{6,7},{7,6},{8,9},{9,8},{10,11... | collective-permute-start | bytes 884744 | tf_op jit(solution)/shard_map/ppermute | solution.py:171
  86.1 20.8 %all-to-all-start = ((bf16[8,96,768]{2,1,0:T(8,128)(2,1)}), bf16[8,96,768]{2,1,0:T(8,128)(2,1)S(1)}, u32[]{:S(2)}, u32[]{:S(2)}) async-start(bf16[8,96,768]{2,1,0:T(8,128)(2,1)} %bitcast.5), calls=%async_computation | async-start | bytes 2359296 | tf_op jit(solution)/shard_map/all_to_all | solution.py:234
  90.2 11.1 %collective-permute-start.21 = (bf16[96,3072]{1,0:T(8,128)(2,1)S(1)}, bf16[96,3072]{1,0:T(8,128)(2,1)}, u32[]{:S(2)}, u32[]{:S(2)}) collective-permute-start(bf16[96,3072]{1,0:T(8,128)(2,1)S(1)} %collective-permute-done.18.refs_7_.refs_5_), channel_id=1, source_target_pairs={{0,1},{1,0},{2,3},{3,2},{4,5},{5,4},{6,7},{7,6},{8,9},{9,8},{10,11... | collective-permute-start | bytes 1769480 | tf_op jit(solution)/shard_map/ppermute | solution.py:171
  90.7 10.6 %collective-permute-start.22 = (bf16[96,3072]{1,0:T(8,128)(2,1)}, bf16[96,3072]{1,0:T(8,128)(2,1)}, u32[]{:S(2)}, u32[]{:S(2)}) collective-permute-start(bf16[96,3072]{1,0:T(8,128)(2,1)} %copy-done.54), channel_id=1, source_target_pairs={{0,1},{1,0},{2,3},{3,2},{4,5},{5,4},{6,7},{7,6},{8,9},{9,8},{10,11... | collective-permute-start | bytes 1769480 | tf_op jit(solution)/shard_map/ppermute | solution.py:171
  90.8 10.5 %collective-permute-start.20 = (bf16[96,3072]{1,0:T(8,128)(2,1)}, bf16[96,3072]{1,0:T(8,128)(2,1)}, u32[]{:S(2)}, u32[]{:S(2)}) collective-permute-start(bf16[96,3072]{1,0:T(8,128)(2,1)} %bitcast.4.refs_5_.refs_3_), channel_id=1, source_target_pairs={{0,1},{1,0},{2,3},{3,2},{4,5},{5,4},{6,7},{7,6},{8,9},{9,8},{10,11... | collective-permute-start | bytes 1769480 | tf_op jit(solution)/shard_map/ppermute | solution.py:171
  91.2 10.1 %collective-permute-start.25 = (bf16[48,3072]{1,0:T(8,128)(2,1)}, bf16[48,3072]{1,0:T(8,128)(2,1)S(1)}, u32[]{:S(2)}, u32[]{:S(2)}) collective-permute-start(bf16[48,3072]{1,0:T(8,128)(2,1)} %copy-done.60), channel_id=1, source_target_pairs={{0,1},{1,0},{2,3},{3,2},{4,5},{5,4},{6,7},{7,6},{8,9},{9,8},{10,11... | collective-permute-start | bytes 884744 | tf_op jit(solution)/shard_map/ppermute | solution.py:171
  91.3 10.0 %collective-permute-start.26 = (bf16[48,3072]{1,0:T(8,128)(2,1)}, bf16[48,3072]{1,0:T(8,128)(2,1)S(1)}, u32[]{:S(2)}, u32[]{:S(2)}) collective-permute-start(bf16[48,3072]{1,0:T(8,128)(2,1)} %copy-done.61), channel_id=1, source_target_pairs={{0,1},{1,0},{2,3},{3,2},{4,5},{5,4},{6,7},{7,6},{8,9},{9,8},{10,11... | collective-permute-start | bytes 884744 | tf_op jit(solution)/shard_map/ppermute | solution.py:171
  117.8 22.6 %all-to-all-start.1 = ((bf16[8,96,896]{2,1,0:T(8,128)(2,1)}), bf16[8,96,896]{2,1,0:T(8,128)(2,1)S(1)}, u32[]{:S(2)}, u32[]{:S(2)}) async-start(bf16[8,96,896]{2,1,0:T(8,128)(2,1)} %bitcast.38), calls=%async_computation.1 | async-start | bytes 2752512 | tf_op jit(solution)/shard_map/all_to_all | solution.py:234
  121.5 70.3 %all-gather.5.cloned.1.call-start = ((), (), s32[]{:S(2)}) async-start(), calls=%async_computation.7 | async-start | bytes 1966080 | tf_op jit(solution)/shard_map/all_gather | solution.py:950
  124.2 229.1 %reduce-scatter.3.cloned.1.call-start = ((), (), s32[]{:S(2)}) async-start(), calls=%async_computation.8 | async-start | bytes 9830400 | tf_op jit(solution)/shard_map/reduce_scatter | solution.py:987
  202.2 22.6 %all-to-all-start.2 = ((bf16[8,96,896]{2,1,0:T(8,128)(2,1)}), bf16[8,96,896]{2,1,0:T(8,128)(2,1)S(1)}, u32[]{:S(2)}, u32[]{:S(2)}) async-start(bf16[8,96,896]{2,1,0:T(8,128)(2,1)} %bitcast.40), calls=%async_computation.2 | async-start | bytes 2752512 | tf_op jit(solution)/shard_map/all_to_all | solution.py:234
  235.7 16.6 %collective-permute-start.27 = (bf16[4,96,3072]{2,1,0:T(8,128)(2,1)}, bf16[4,96,3072]{2,1,0:T(8,128)(2,1)}, u32[]{:S(2)}, u32[]{:S(2)}) collective-permute-start(bf16[4,96,3072]{2,1,0:T(8,128)(2,1)} %get-tuple-element.136), channel_id=1, source_target_pairs={{0,1},{1,0},{2,3},{3,2},{4,5},{5,4},{6,7},{7,6},{8,9},{9,8},{10,11... | collective-permute-start | bytes 7077896 | tf_op jit(solution)/shard_map/ppermute | solution.py:171
  235.7 20.7 %all-to-all-start.3 = ((bf16[8,96,768]{2,1,0:T(8,128)(2,1)}), bf16[8,96,768]{2,1,0:T(8,128)(2,1)S(1)}, u32[]{:S(2)}, u32[]{:S(2)}) async-start(bf16[8,96,768]{2,1,0:T(8,128)(2,1)} %bitcast.45), calls=%async_computation.3 | async-start | bytes 2359296 | tf_op jit(solution)/shard_map/all_to_all | solution.py:234
  239.3 161.6 %reduce-scatter.5.cloned.1.call-start = ((), (), s32[]{:S(2)}) async-start(), calls=%async_computation.9 | async-start | bytes 1966080 | tf_op jit(solution)/shard_map/reduce_scatter | solution.py:987
  251.7 34.7 %collective-permute-start.30 = (bf16[4,384,768]{2,1,0:T(8,128)(2,1)}, bf16[4,384,768]{2,1,0:T(8,128)(2,1)}, u32[]{:S(2)}, u32[]{:S(2)}) collective-permute-start(bf16[4,384,768]{2,1,0:T(8,128)(2,1)} %get-tuple-element.150), channel_id=1, source_target_pairs={{0,1},{1,0},{2,3},{3,2},{4,5},{5,4},{6,7},{7,6},{8,9},{9,8},{10,11... | collective-permute-start | bytes 7077896 | tf_op jit(solution)/shard_map/ppermute | solution.py:171
  267.6 18.8 %collective-permute-start.31 = (bf16[4,96,768]{2,1,0:T(8,128)(2,1)}, bf16[4,96,768]{2,1,0:T(8,128)(2,1)S(1)}, u32[]{:S(2)}, u32[]{:S(2)}) collective-permute-start(bf16[4,96,768]{2,1,0:T(8,128)(2,1)} %get-tuple-element.151), channel_id=1, source_target_pairs={{0,1},{1,0},{2,3},{3,2},{4,5},{5,4},{6,7},{7,6},{8,9},{9,8},{10,11... | collective-permute-start | bytes 1769480 | tf_op jit(solution)/shard_map/ppermute | solution.py:171
  267.7 24.1 %collective-permute-start.28 = (bf16[2,48,3072]{2,1,0:T(8,128)(2,1)}, bf16[2,48,3072]{2,1,0:T(8,128)(2,1)S(1)}, u32[]{:S(2)}, u32[]{:S(2)}) collective-permute-start(bf16[2,48,3072]{2,1,0:T(8,128)(2,1)} %get-tuple-element.145), channel_id=1, source_target_pairs={{0,2},{1,3},{2,0},{3,1},{4,6},{5,7},{6,4},{7,5},{8,10},{9,11},{10,... | collective-permute-start | bytes 1769480 | tf_op jit(solution)/shard_map/ppermute | solution.py:171
  269.6 22.2 %collective-permute-start.29 = (bf16[2,48,3072]{2,1,0:T(8,128)(2,1)}, bf16[2,48,3072]{2,1,0:T(8,128)(2,1)}, u32[]{:S(2)}, u32[]{:S(2)}) collective-permute-start(bf16[2,48,3072]{2,1,0:T(8,128)(2,1)} %get-tuple-element.147), channel_id=1, source_target_pairs={{0,4},{1,5},{2,6},{3,7},{4,0},{5,1},{6,2},{7,3},{8,12},{9,13},{10,... | collective-permute-start | bytes 1769480 | tf_op jit(solution)/shard_map/ppermute | solution.py:171
  291.0 18.2 %collective-permute-start.34 = (bf16[2,240,768]{2,1,0:T(8,128)(2,1)}, bf16[2,240,768]{2,1,0:T(8,128)(2,1)S(1)}, u32[]{:S(2)}, u32[]{:S(2)}) collective-permute-start(bf16[2,240,768]{2,1,0:T(8,128)(2,1)} %get-tuple-element.158), channel_id=1, source_target_pairs={{0,2},{1,3},{2,0},{3,1},{4,6},{5,7},{6,4},{7,5},{8,10},{9,11},{10,... | collective-permute-start | bytes 2211848 | tf_op jit(solution)/shard_map/ppermute | solution.py:171
  291.5 18.0 %collective-permute-start.35 = (bf16[2,240,768]{2,1,0:T(8,128)(2,1)}, bf16[2,240,768]{2,1,0:T(8,128)(2,1)S(1)}, u32[]{:S(2)}, u32[]{:S(2)}) collective-permute-start(bf16[2,240,768]{2,1,0:T(8,128)(2,1)} %get-tuple-element.160), channel_id=1, source_target_pairs={{0,4},{1,5},{2,6},{3,7},{4,0},{5,1},{6,2},{7,3},{8,12},{9,13},{10,... | collective-permute-start | bytes 2211848 | tf_op jit(solution)/shard_map/ppermute | solution.py:171
  306.1 3.9 collective-permute-start.32
  306.2 3.8 collective-permute-start.33
  310.8 24.9 %collective-permute-start.37 = (bf16[2,160,768]{2,1,0:T(8,128)(2,1)S(1)}, bf16[2,160,768]{2,1,0:T(8,128)(2,1)S(1)}, u32[]{:S(2)}, u32[]{:S(2)}) collective-permute-start(bf16[2,160,768]{2,1,0:T(8,128)(2,1)S(1)} %get-tuple-element.165), channel_id=1, source_target_pairs={{0,4},{1,5},{2,6},{3,7},{4,0},{5,1},{6,2},{7,3},{8,12},{9,13},{10,... | collective-permute-start | bytes 1474568 | tf_op jit(solution)/shard_map/ppermute | solution.py:171
  312.3 23.4 %collective-permute-start.36 = (bf16[2,144,768]{2,1,0:T(8,128)(2,1)S(1)}, bf16[2,144,768]{2,1,0:T(8,128)(2,1)S(1)}, u32[]{:S(2)}, u32[]{:S(2)}) collective-permute-start(bf16[2,144,768]{2,1,0:T(8,128)(2,1)S(1)} %get-tuple-element.163), channel_id=1, source_target_pairs={{0,2},{1,3},{2,0},{3,1},{4,6},{5,7},{6,4},{7,5},{8,10},{9,11},{10,... | collective-permute-start | bytes 1327112 | tf_op jit(solution)/shard_map/ppermute | solution.py:171
  313.9 17.4 %collective-permute-start.38 = (bf16[48,3072]{1,0:T(8,128)(2,1)S(1)}, bf16[48,3072]{1,0:T(8,128)(2,1)S(1)}, u32[]{:S(2)}, u32[]{:S(2)}) collective-permute-start(bf16[48,3072]{1,0:T(8,128)(2,1)S(1)} %copy-done.24), channel_id=1, source_target_pairs={{0,4},{1,5},{2,6},{3,7},{4,0},{5,1},{6,2},{7,3},{8,12},{9,13},{10,... | collective-permute-start | bytes 884744 | tf_op jit(solution)/shard_map/ppermute | solution.py:171
  314.4 18.4 %collective-permute-start.39 = (bf16[48,3072]{1,0:T(8,128)(2,1)S(1)}, bf16[48,3072]{1,0:T(8,128)(2,1)S(1)}, u32[]{:S(2)}, u32[]{:S(2)}) collective-permute-start(bf16[48,3072]{1,0:T(8,128)(2,1)S(1)} %get-tuple-element.168), channel_id=1, source_target_pairs={{0,2},{1,3},{2,0},{3,1},{4,6},{5,7},{6,4},{7,5},{8,10},{9,11},{10,... | collective-permute-start | bytes 884744 | tf_op jit(solution)/shard_map/ppermute | solution.py:171
  315.0 24.3 %collective-permute-start.42 = (bf16[240,768]{1,0:T(8,128)(2,1)S(1)}, bf16[240,768]{1,0:T(8,128)(2,1)S(1)}, u32[]{:S(2)}, u32[]{:S(2)}) collective-permute-start(bf16[240,768]{1,0:T(8,128)(2,1)S(1)} %get-tuple-element.173), channel_id=1, source_target_pairs={{0,4},{1,5},{2,6},{3,7},{4,0},{5,1},{6,2},{7,3},{8,12},{9,13},{10,... | collective-permute-start | bytes 1105928 | tf_op jit(solution)/shard_map/ppermute | solution.py:171
  331.3 11.1 %collective-permute-start.43 = (bf16[240,768]{1,0:T(8,128)(2,1)S(1)}, bf16[240,768]{1,0:T(8,128)(2,1)S(1)}, u32[]{:S(2)}, u32[]{:S(2)}) collective-permute-start(bf16[240,768]{1,0:T(8,128)(2,1)S(1)} %get-tuple-element.175), channel_id=1, source_target_pairs={{0,2},{1,3},{2,0},{3,1},{4,6},{5,7},{6,4},{7,5},{8,10},{9,11},{10,... | collective-permute-start | bytes 1105928 | tf_op jit(solution)/shard_map/ppermute | solution.py:171
  333.0 18.4 %collective-permute-start.46 = (bf16[96,3072]{1,0:T(8,128)(2,1)S(1)}, bf16[96,3072]{1,0:T(8,128)(2,1)S(1)}, u32[]{:S(2)}, u32[]{:S(2)}) collective-permute-start(bf16[96,3072]{1,0:T(8,128)(2,1)S(1)} %fold_last.3.refs_4_.refs_0_), channel_id=1, source_target_pairs={{0,8},{24,16},{1,9},{25,17},{2,10},{26,18},{3,11},{27,19},{4,12},{... | collective-permute-start | bytes 1769480 | tf_op jit(solution)/shard_map/ppermute | solution.py:315
  336.0 9.7 %collective-permute-start.41 = (bf16[160,768]{1,0:T(8,128)(2,1)S(1)}, bf16[160,768]{1,0:T(8,128)(2,1)S(1)}, u32[]{:S(2)}, u32[]{:S(2)}) collective-permute-start(bf16[160,768]{1,0:T(8,128)(2,1)S(1)} %get-tuple-element.172), channel_id=1, source_target_pairs={{0,2},{1,3},{2,0},{3,1},{4,6},{5,7},{6,4},{7,5},{8,10},{9,11},{10,... | collective-permute-start | bytes 737288 | tf_op jit(solution)/shard_map/ppermute | solution.py:171
  336.6 9.0 %collective-permute-start.40 = (bf16[144,768]{1,0:T(8,128)(2,1)S(1)}, bf16[144,768]{1,0:T(8,128)(2,1)S(1)}, u32[]{:S(2)}, u32[]{:S(2)}) collective-permute-start(bf16[144,768]{1,0:T(8,128)(2,1)S(1)} %get-tuple-element.170), channel_id=1, source_target_pairs={{0,4},{1,5},{2,6},{3,7},{4,0},{5,1},{6,2},{7,3},{8,12},{9,13},{10,... | collective-permute-start | bytes 663560 | tf_op jit(solution)/shard_map/ppermute | solution.py:171
  342.6 28.2 %collective-permute-start.45 = (bf16[480,768]{1,0:T(8,128)(2,1)S(1)}, bf16[480,768]{1,0:T(8,128)(2,1)S(1)}, u32[]{:S(2)}, u32[]{:S(2)}) collective-permute-start(bf16[480,768]{1,0:T(8,128)(2,1)S(1)} %fold_last.4.refs_4_.refs_0_), channel_id=1, source_target_pairs={{0,8},{24,16},{1,9},{25,17},{2,10},{26,18},{3,11},{27,19},{4,12},{... | collective-permute-start | bytes 2211848 | tf_op jit(solution)/shard_map/ppermute | solution.py:315
  346.5 41.6 %collective-permute-start.44 = (bf16[304,768]{1,0:T(8,128)(2,1)}, bf16[304,768]{1,0:T(8,128)(2,1)}, u32[]{:S(2)}, u32[]{:S(2)}) collective-permute-start(bf16[304,768]{1,0:T(8,128)(2,1)} %fold_last.5.refs_4_.refs_0_), channel_id=1, source_target_pairs={{0,8},{24,16},{1,9},{25,17},{2,10},{26,18},{3,11},{27,19},{4,12},{... | collective-permute-start | bytes 1400840 | tf_op jit(solution)/shard_map/ppermute | solution.py:315
  352.6 37.5 %collective-permute-start.49 = (bf16[96,3072]{1,0:T(8,128)(2,1)S(1)}, bf16[96,3072]{1,0:T(8,128)(2,1)S(1)}, u32[]{:S(2)}, u32[]{:S(2)}) collective-permute-start(bf16[96,3072]{1,0:T(8,128)(2,1)S(1)} %joined.6.refs_2_.refs_0_), channel_id=1, source_target_pairs={{8,16},{16,8},{9,17},{17,9},{10,18},{18,10},{11,19},{19,11},{12,20... | collective-permute-start | bytes 1769480 | tf_op jit(solution)/shard_map/ppermute | solution.py:315
  371.0 20.6 %collective-permute-start.48 = (bf16[480,768]{1,0:T(8,128)(2,1)S(1)}, bf16[480,768]{1,0:T(8,128)(2,1)S(1)}, u32[]{:S(2)}, u32[]{:S(2)}) collective-permute-start(bf16[480,768]{1,0:T(8,128)(2,1)S(1)} %joined.7.refs_2_.refs_0_), channel_id=1, source_target_pairs={{8,16},{16,8},{9,17},{17,9},{10,18},{18,10},{11,19},{19,11},{12,20... | collective-permute-start | bytes 2211848 | tf_op jit(solution)/shard_map/ppermute | solution.py:315
  389.4 4.0 collective-permute-start.47
  390.2 19.9 %collective-permute-start.52 = (bf16[96,3072]{1,0:T(8,128)(2,1)S(1)}, bf16[96,3072]{1,0:T(8,128)(2,1)}, u32[]{:S(2)}, u32[]{:S(2)}) collective-permute-start(bf16[96,3072]{1,0:T(8,128)(2,1)S(1)} %joined.9.refs_2_.refs_0_), channel_id=1, source_target_pairs={{8,0},{16,24},{9,1},{17,25},{10,2},{18,26},{11,3},{19,27},{12,4},{... | collective-permute-start | bytes 1769480 | tf_op jit(solution)/shard_map/ppermute | solution.py:315
  391.8 36.9 %collective-permute-start.51 = (bf16[480,768]{1,0:T(8,128)(2,1)S(1)}, bf16[480,768]{1,0:T(8,128)(2,1)}, u32[]{:S(2)}, u32[]{:S(2)}) collective-permute-start(bf16[480,768]{1,0:T(8,128)(2,1)S(1)} %joined.10.refs_2_.refs_0_), channel_id=1, source_target_pairs={{8,0},{16,24},{9,1},{17,25},{10,2},{18,26},{11,3},{19,27},{12,4},{... | collective-permute-start | bytes 2211848 | tf_op jit(solution)/shard_map/ppermute | solution.py:315
  394.2 40.0 %collective-permute-start.50 = (bf16[304,768]{1,0:T(8,128)(2,1)}, bf16[304,768]{1,0:T(8,128)(2,1)}, u32[]{:S(2)}, u32[]{:S(2)}) collective-permute-start(bf16[304,768]{1,0:T(8,128)(2,1)} %joined.11.refs_2_.refs_0_), channel_id=1, source_target_pairs={{8,0},{16,24},{9,1},{17,25},{10,2},{18,26},{11,3},{19,27},{12,4},{... | collective-permute-start | bytes 1400840 | tf_op jit(solution)/shard_map/ppermute | solution.py:315
  (62 other events, 379.2 us)
Sparse Core Ops, SparseCore 0:
  10.5 143.7 all-gather.2
  156.5 35.3 all-gather.4
  194.1 135.0 reduce-scatter.2
  353.4 47.3 reduce-scatter.4
